TPU v7x, 32 devices: a whole 2x2x4 slice. The times are simulated.
32 devices in a mesh: tm: 4 (over x, core), gx: 2 (over y), gy: 4 (over z).
Axes of the slice: x: 2, y: 2, z: 4, core: 2. Of those that a mesh axis runs over, the one named last changes fastest.
Arguments:
- velocity: float32 [3, 32, 128, 256], P(None, 'gx', 'gy'), may hold values from -3 to 3
- start_field: float32 [3, 32, 128, 256], P(None, 'gx', 'gy'), may hold values from -6 to 6
- guess: float32 [4, 3, 32, 128, 256], P('tm', None, 'gx', 'gy'), may hold values from -6 to 6
Outputs:
- slab_ends: float32 [4, 3, 32, 128, 256], P('tm', None, 'gx', 'gy')
All inputs are finite; a program needn't handle non-finite values.
Results may differ from a plain program's by a relative error of at most 0.0003.
Values sent between devices are 32-bit elements; how exact they have to be, the bound alone decides.
No kernel may reach another device: no remote copies, remote signals or barrier semaphores. Data moves between devices by JAX's collectives and lax.ppermute only.
A program may use at most 128 MiB of HBM per device.

v0:
```python
import jax
import jax.numpy as jnp
from jax import lax
from jax.sharding import PartitionSpec as P

ITERS = 2


VISCOSITY = 0.25
TIME_STEP = 0.5


def extended(shard, sides, width):
    for axis, dim in sides:
        size, length = (lax.axis_size(axis), shard.shape[dim])
        up = [(i, (i + 1) % size) for i in range(size)]
        down = [(j, i) for i, j in up]
        last = lax.slice_in_dim(shard, length - width, length, axis=dim)
        initial = lax.slice_in_dim(shard, 0, width, axis=dim)
        before = lax.ppermute(last, axis, up)
        after = lax.ppermute(initial, axis, down)
        shard = jnp.concatenate([before, shard, after], axis=dim)
    return shard


def passed_along(shard, axis, by):
    length = lax.axis_size(axis)
    pairs = [(i, i + by) for i in range(length) if 0 <= i + by < length]
    return lax.ppermute(shard, axis, pairs)


def pair_table(fine_len):
    fine_index = lax.broadcasted_iota(jnp.int32, (fine_len, fine_len // 2), 0) // 2
    coarse_index = lax.broadcasted_iota(jnp.int32, (fine_len, fine_len // 2), 1)
    return (fine_index == coarse_index).astype(jnp.float32)


def restrict(field):
    extent = field.shape
    lead = extent[:-3]
    blocks = field.reshape(lead + (extent[-3] // 2, 2, extent[-2] // 2, 2, extent[-1]))
    summed = jnp.sum(blocks, axis=(-4, -2)) * 0.25
    table = pair_table(extent[-1]) * 0.5
    return jnp.einsum("...z,zc->...c", summed, table, precision=lax.Precision.HIGHEST)


def prolong(field):
    extent = field.shape
    lead = extent[:-3]
    table = jnp.transpose(pair_table(extent[-1] * 2))
    along_z = jnp.einsum("...c,cz->...z", field, table, precision=lax.Precision.HIGHEST)
    spread = jnp.broadcast_to(
        along_z[..., :, None, :, None, :], lead + (extent[-3], 2, extent[-2], 2, extent[-1] * 2)
    )
    return spread.reshape(lead + (extent[-3] * 2, extent[-2] * 2, extent[-1] * 2))


def gradients(velocity):
    framed = extended(velocity, (("gx", 1), ("gy", 2)), 1)
    along_x = (framed[:, 2:, 1:-1] - framed[:, :-2, 1:-1]) / 2.0
    along_y = (framed[:, 1:-1, 2:] - framed[:, 1:-1, :-2]) / 2.0
    along_z = (jnp.roll(velocity, -1, 3) - jnp.roll(velocity, 1, 3)) / 2.0
    stacked = jnp.stack([along_x, along_y, along_z], axis=1)
    extent = velocity.shape
    return stacked.reshape((9,) + extent[1:])


def apply_operator(framed, inner, velocity, grads, spacing):
    ahead_x = framed[:, :, 2:, 1:-1]
    behind_x = framed[:, :, :-2, 1:-1]
    ahead_y = framed[:, :, 1:-1, 2:]
    behind_y = framed[:, :, 1:-1, :-2]
    ahead_z = jnp.roll(inner, -1, 4)
    behind_z = jnp.roll(inner, 1, 4)
    laplace = ahead_x + behind_x + ahead_y + behind_y + ahead_z + behind_z - 6.0 * inner
    advect = (
        velocity[0] * (ahead_x - behind_x)
        + velocity[1] * (ahead_y - behind_y)
        + velocity[2] * (ahead_z - behind_z)
    )
    result_term = VISCOSITY / (spacing * spacing) * laplace - advect / (2.0 * spacing)
    extent = grads.shape
    grid = grads.reshape((3, 3) + extent[1:])
    for across in range(3):
        result_term = result_term + inner[:, across : across + 1] * grid[None, :, across]
    return result_term


def fine_rhs(stacked, velocity, grads):
    framed = extended(stacked, (("gx", 2), ("gy", 3)), 1)
    return apply_operator(framed, stacked, velocity, grads, 1.0)


def coarse_rhs(field, velocity, grads):
    stacked = field[None]
    framed = extended(stacked, (("gx", 2), ("gy", 3)), 1)
    return apply_operator(framed, stacked, velocity, grads, 2.0)[0]


def evaluate_all(fields, velocity, grads):
    results = fine_rhs(jnp.stack(fields), velocity, grads)
    return [results[number] for number in range(len(fields))]


def shards(velocity, start_field, guess):
    grads = gradients(velocity)
    coarse_vel = restrict(velocity)
    coarse_grads = restrict(grads)
    coarse_init = restrict(start_field)
    is_first = lax.axis_index("tm") == 0
    rounds = lax.axis_size("tm") - 1
    own_guess = guess[0]
    node_values = [jnp.where(is_first, start_field, own_guess), own_guess, own_guess]
    rhs_values = evaluate_all(node_values, velocity, grads)
    slab_end = own_guess
    for sweep_index in range(ITERS):
        if sweep_index > 0:
            fresh = evaluate_all([node_values[0], node_values[2]], velocity, grads)
            rhs_values = [fresh[0], rhs_values[1], fresh[1]]
        integral = TIME_STEP * (
            rhs_values[0] / 6.0 + rhs_values[1] * (2.0 / 3.0) + rhs_values[2] / 6.0
        )
        coarse_zero = restrict(node_values[0])
        coarse_end = restrict(node_values[2])
        offset = restrict(integral) - TIME_STEP * coarse_rhs(coarse_zero, coarse_vel, coarse_grads)

        def advance(coarse_start):
            return (
                coarse_start
                + TIME_STEP * coarse_rhs(coarse_start, coarse_vel, coarse_grads)
                + offset
            )

        def chain_round(number, coarse_start):
            arrived = passed_along(advance(coarse_start), "tm", 1)
            return jnp.where(is_first, coarse_init, arrived)

        coarse_start = lax.fori_loop(
            0, rounds, chain_round, jnp.where(is_first, coarse_init, coarse_zero)
        )
        finish = advance(coarse_start)
        delta_zero = prolong(coarse_start - coarse_zero)
        delta_end = prolong(finish - coarse_end)
        fixed_zero = node_values[0] + delta_zero
        fixed_mid = node_values[1] + 0.5 * (delta_zero + delta_end)
        fixed_end = node_values[2] + delta_end
        corrected = evaluate_all([fixed_zero, fixed_mid, fixed_end], velocity, grads)
        middle = fixed_zero + TIME_STEP * (
            corrected[0] * (5.0 / 24.0) + corrected[1] / 3.0 - corrected[2] / 24.0
        )
        middle_value = evaluate_all([middle], velocity, grads)[0]
        slab_end = (
            middle
            + 0.5 * TIME_STEP * (middle_value - corrected[1])
            + TIME_STEP * (-corrected[0] / 24.0 + corrected[1] / 3.0 + corrected[2] * (5.0 / 24.0))
        )
        node_values = [fixed_zero, middle, slab_end]
        rhs_values = [corrected[0], middle_value, corrected[2]]
        if sweep_index + 1 < ITERS:
            arrived_end = passed_along(slab_end, "tm", 1)
            node_values[0] = jnp.where(is_first, start_field, arrived_end)
    return slab_end[None]


def solution(mesh):
    in_specs = (
        P(None, "gx", "gy", None),
        P(None, "gx", "gy", None),
        P("tm", None, "gx", "gy", None),
    )
    out_specs = P("tm", None, "gx", "gy", None)
    return jax.shard_map(shards, mesh=mesh, in_specs=in_specs, out_specs=out_specs, check_vma=False)
```

profile of v0, /device:TPU:26, one launch (start us, length us, event | category | flops | bytes accessed | tf_op | source)
XLA Modules:
  0.0 528.6 jit_solution(5287483731045409677)
XLA Ops:
  20.2 4.9 slice_bitcast_fusion.50
  25.1 5.3 %fusion.232 = (f32[3,3,16,32,255]{4,3,2,1,0:T(8,128)}, f32[3,3,16,32,255]{4,3,2,1,0:T(8,128)}) fusion(f32[3,3,16,32,256]{4,3,2,1,0:T(8,128)S(1)} %bitcast.538), kind=kLoop, calls=%fused_computation.560 | loop fusion | bytes 18800640 | tf_op jit(solution)/shard_map/jit(_roll_static)/slice | solution.py:73
  90.9 6.7 %reshape_reshape.3 = f32[9,8,2,16,2,256]{5,4,3,2,1,0:T(2,128)} reshape(f32[3,3,16,32,256]{4,3,2,1,0:T(8,128)} %copy.18) | data formatting | bytes 9437184 | tf_op jit(solution)/shard_map/reshape;reshape | solution.py:41
  97.6 7.3 %reduce_sum.84 = f32[9,8,16,256]{3,2,1,0:T(8,128)} reduce(f32[9,8,2,16,2,256]{5,4,3,2,1,0:T(2,128)} %reshape_reshape.3, f32[]{:T(128)} %constant.121.clone.1), dimensions={2,4}, to_apply=%region_3.4 | reduce | flops 884736 | bytes 5898244 | tf_op jit(solution)/shard_map/reduce_sum | solution.py:42
  116.4 16.2 %multiply_add_fusion.2 = f32[3,3,16,32,256]{4,3,2,1,0:T(8,128)S(1)} fusion(f32[3,3,16,32,255]{4,3,2,1,0:T(8,128)} %get-tuple-element.167, f32[3,3,16,32,1]{4,3,2,1,0:T(8,128)} %get-tuple-element.169, f32[3,3,16,32,1]{4,3,2,1,0:T(8,128)} %get-tuple-element.168, f32[3,3,16,32,255]{4,3,2,1,0:T(8,128)} %get-tuple-element.166, ...), kind=kLoop, calls=%fused_computation.151 | loop fusion | flops 51904512 | bytes 29233152 | tf_op jit(solution)/shard_map/add | solution.py:85
  142.1 54.4 %while.20 = (s32[]{:T(128)}, f32[3,8,16,128]{3,2,1,0:T(8,128)S(1)}, pred[]{:T(512)}, f32[3,8,16,128]{3,2,1,0:T(8,128)S(1)}, f32[9,8,16,128]{3,2,1,0:T(8,128)S(1)...) while((s32[]{:T(128)}, f32[3,8,16,128]{3,2,1,0:T(8,128)S(1)}, pred[]{:T(512)}, ...), condition=%wide.region_6.7_spmd, body=%wide.region_5.6_spmd.sunk | while | flops 1883138 | bytes 5886238 | solution.py:138
  155.5 5.1 collective-permute-done.4
  172.9 5.1 collective-permute-done.4
  191.4 5.1 collective-permute-done.4
  227.1 5.3 %fusion.229 = (f32[3,3,16,32,255]{4,3,2,1,0:T(8,128)}, f32[3,3,16,32,255]{4,3,2,1,0:T(8,128)}) fusion(f32[3,3,16,32,256]{4,3,2,1,0:T(8,128)S(1)} %pad_maximum_fusion.79), kind=kLoop, calls=%fused_computation.557 | loop fusion | bytes 18800640 | tf_op jit(solution)/shard_map/jit(_roll_static)/slice | solution.py:73
  248.0 4.0 collective-permute-done.28
  252.1 14.6 %multiply_add_fusion.1 = f32[3,3,16,32,256]{4,3,2,1,0:T(8,128)S(1)} fusion(f32[3,3,16,32,255]{4,3,2,1,0:T(8,128)} %get-tuple-element.158, f32[3,3,16,32,1]{4,3,2,1,0:T(8,128)} %get-tuple-element.160, f32[3,3,16,32,1]{4,3,2,1,0:T(8,128)} %get-tuple-element.159, f32[3,3,16,32,255]{4,3,2,1,0:T(8,128)} %get-tuple-element.157, ...), kind=kLoop, calls=%fused_computation.150 | loop fusion | flops 51904512 | bytes 30806016 | tf_op jit(solution)/shard_map/add | solution.py:85
  282.6 8.8 %bitcast_add_fusion.5 = (f32[3,16,32,256]{3,2,1,0:T(8,128)S(1)}, f32[1,3,16,32,256]{4,3,2,1,0:T(8,128)}) fusion(f32[3,16,32,256]{3,2,1,0:T(8,128)S(1)} %bitcast_add_fusion.9, f32[3,3,16,32,256]{4,3,2,1,0:T(8,128)S(1)} %multiply_add_fusion.1, f32[16,32,256]{2,1,0:T(8,128)} %get-tuple-element.210, f32[1,3,16,32,255]{4,3,2,1,0:T(8,128)} %get-tuple-element.215, ...), kind=kLoop, calls=%fused_computation.240 | loop fusion | flops 21233664 | bytes 24403968 | tf_op jit(solution)/shard_map/add | solution.py:153
  299.3 14.0 %collective-permute-done.34 = f32[3,16,32,256]{3,2,1,0:T(8,128)} collective-permute-done((f32[3,16,32,256]{3,2,1,0:T(8,128)S(1)}, f32[3,16,32,256]{3,2,1,0:T(8,128)}, u32[]{:S(2)}, u32[]{:S(2)}) %collective-permute-start.34) | collective-permute-done | bytes 1572896 | tf_op jit(solution)/shard_map/ppermute | solution.py:29
  319.2 5.8 %fusion.24 = (f32[2,3,16,32,255]{4,3,2,1,0:T(8,128)}, f32[2,3,16,32,255]{4,3,2,1,0:T(8,128)}) fusion(f32[1,3,16,32,256]{4,3,2,1,0:T(8,128)} %bitcast.531, f32[1,3,16,32,256]{4,3,2,1,0:T(8,128)S(1)} %bitcast.525), kind=kLoop, calls=%fused_computation.152 | loop fusion | flops 1566720 | bytes 9412608 | tf_op jit(solution)/shard_map/stack | solution.py:101
  349.2 11.1 %fusion.32 = f32[2,3,16,32,256]{4,3,2,1,0:T(8,128)} fusion(f32[1,3,16,32,256]{4,3,2,1,0:T(8,128)S(1)} %bitcast.530, f32[1,3,16,32,256]{4,3,2,1,0:T(8,128)S(1)} %bitcast.536, f32[2,3,16,32,255]{4,3,2,1,0:T(8,128)} %get-tuple-element.180, f32[2,3,16,32,1]{4,3,2,1,0:T(8,128)} %get-tuple-element.182, f32[2,3,16,32,1]{4,3,2,1,0:T(8,128)} %get-tuple-element.181, ...), kind=kLoop, calls=%fused_computation.160 | loop fusion | flops 30670848 | bytes 22634496 | tf_op jit(solution)/shard_map/add | solution.py:85
  360.4 4.2 fusion.36
  374.2 63.8 %while.21 = (s32[]{:T(128)}, f32[3,8,16,128]{3,2,1,0:T(8,128)S(1)}, pred[]{:T(512)}, f32[3,8,16,128]{3,2,1,0:T(8,128)S(1)}, f32[9,8,16,128]{3,2,1,0:T(8,128)}, /...) while((s32[]{:T(128)}, f32[3,8,16,128]{3,2,1,0:T(8,128)S(1)}, pred[]{:T(512)}, ...), condition=%wide.region_11.12_spmd, body=%wide.region_10.11_spmd.sunk | while | flops 1883138 | bytes 9818482 | solution.py:138
  383.2 4.1 collective-permute-done.8
  390.2 5.3 collective-permute-done.9
  410.6 5.3 collective-permute-done.9
  431.1 5.3 collective-permute-done.9
  489.2 15.2 %multiply_add_fusion = f32[3,3,16,32,256]{4,3,2,1,0:T(8,128)S(1)} fusion(f32[3,3,16,32,255]{4,3,2,1,0:T(8,128)} %get-tuple-element.149, f32[3,3,16,32,1]{4,3,2,1,0:T(8,128)} %get-tuple-element.151, f32[3,3,16,32,1]{4,3,2,1,0:T(8,128)} %get-tuple-element.150, f32[3,3,16,32,255]{4,3,2,1,0:T(8,128)S(1)} %get-tuple-element.148, ...), kind=kLoop, calls=%fused_computation.149 | loop fusion | flops 51904512 | bytes 30806016 | tf_op jit(solution)/shard_map/add | solution.py:85
  519.9 8.5 %fusion.45 = f32[1,3,16,32,256]{4,3,2,1,0:T(8,128)} fusion(f32[3,16,32,256]{3,2,1,0:T(8,128)S(1)} %bitcast_add_fusion.4, f32[1,3,16,32,255]{4,3,2,1,0:T(8,128)} %get-tuple-element.197, f32[1,3,16,32,1]{4,3,2,1,0:T(8,128)} %get-tuple-element.199, f32[1,3,16,32,1]{4,3,2,1,0:T(8,128)} %get-tuple-element.198, f32[1,3,16,32,255]{4,3,2,1,0:T(8,128)S(1)} %get-tuple-element.196, ...), kind=kLoop, calls=%fused_computation.229 | loop fusion | flops 21233664 | bytes 22831104 | tf_op jit(solution)/shard_map/broadcast_in_dim | solution.py:162
  (524 shorter events, 359.4 us)
Async XLA Ops:
  1.6 75.0 %collective-permute-start.11 = (f32[3,1,32,256]{3,2,1,0:T(8,128)}, f32[3,1,32,256]{3,2,1,0:T(8,128)}, u32[]{:S(2)}, u32[]{:S(2)}) collective-permute-start(f32[3,1,32,256]{3,2,1,0:T(8,128)} %get-tuple-element.224), channel_id=1, source_target_pairs={{0,4},{4,0},{1,5},{5,1},{2,6},{6,2},{3,7},{7,3},{8,12},{12,8},{9,1... | collective-permute-start | bytes 294920 | tf_op jit(solution)/shard_map/ppermute | solution.py:20
  3.1 74.9 %collective-permute-start.10 = (f32[3,1,32,256]{3,2,1,0:T(8,128)}, f32[3,1,32,256]{3,2,1,0:T(8,128)}, u32[]{:S(2)}, u32[]{:S(2)}) collective-permute-start(f32[3,1,32,256]{3,2,1,0:T(8,128)} %get-tuple-element.223), channel_id=1, source_target_pairs={{4,0},{0,4},{5,1},{1,5},{6,2},{2,6},{7,3},{3,7},{12,8},{8,12},{13,... | collective-permute-start | bytes 294920 | tf_op jit(solution)/shard_map/ppermute | solution.py:21
  9.1 95.9 %collective-permute-start.14 = (f32[3,3,1,32,256]{4,3,2,1,0:T(8,128)}, f32[3,3,1,32,256]{4,3,2,1,0:T(8,128)}, u32[]{:S(2)}, u32[]{:S(2)}) collective-permute-start(f32[3,3,1,32,256]{4,3,2,1,0:T(8,128)} %get-tuple-element.165), channel_id=1, source_target_pairs={{4,0},{0,4},{5,1},{1,5},{6,2},{2,6},{7,3},{3,7},{12,8},{8,12},{13,... | collective-permute-start | bytes 884744 | tf_op jit(solution)/shard_map/ppermute | solution.py:21
  10.6 94.4 %collective-permute-start.15 = (f32[3,3,1,32,256]{4,3,2,1,0:T(8,128)}, f32[3,3,1,32,256]{4,3,2,1,0:T(8,128)}, u32[]{:S(2)}, u32[]{:S(2)}) collective-permute-start(f32[3,3,1,32,256]{4,3,2,1,0:T(8,128)} %get-tuple-element.164), channel_id=1, source_target_pairs={{0,4},{4,0},{1,5},{5,1},{2,6},{6,2},{3,7},{7,3},{8,12},{12,8},{9,1... | collective-permute-start | bytes 884744 | tf_op jit(solution)/shard_map/ppermute | solution.py:20
  83.3 56.7 %collective-permute-start.21 = (f32[1,3,10,1,128]{4,3,2,1,0:T(1,128)}, f32[1,3,10,1,128]{4,3,2,1,0:T(1,128)}, u32[]{:S(2)}, u32[]{:S(2)}) collective-permute-start(f32[1,3,10,1,128]{4,3,2,1,0:T(1,128)} %get-tuple-element.234), channel_id=1, source_target_pairs={{0,1},{1,2},{2,3},{3,0},{4,5},{5,6},{6,7},{7,4},{8,9},{9,10},{10,1... | collective-permute-start | bytes 46088 | tf_op jit(solution)/shard_map/ppermute | solution.py:20
  85.3 54.7 %collective-permute-start.20 = (f32[1,3,10,1,128]{4,3,2,1,0:T(1,128)}, f32[1,3,10,1,128]{4,3,2,1,0:T(1,128)}, u32[]{:S(2)}, u32[]{:S(2)}) collective-permute-start(f32[1,3,10,1,128]{4,3,2,1,0:T(1,128)} %get-tuple-element.233), channel_id=1, source_target_pairs={{1,0},{2,1},{3,2},{0,3},{5,4},{6,5},{7,6},{4,7},{9,8},{10,9},{11,1... | collective-permute-start | bytes 46088 | tf_op jit(solution)/shard_map/ppermute | solution.py:21
  106.6 7.1 %collective-permute-start.17 = (f32[3,3,18,1,256]{4,3,2,1,0:T(1,128)S(1)}, f32[3,3,18,1,256]{4,3,2,1,0:T(1,128)S(1)}, u32[]{:S(2)}, u32[]{:S(2)}) collective-permute-start(f32[3,3,18,1,256]{4,3,2,1,0:T(1,128)S(1)} %get-tuple-element.171), channel_id=1, source_target_pairs={{0,1},{1,2},{2,3},{3,0},{4,5},{5,6},{6,7},{7,4},{8,9},{9,10},{10,1... | collective-permute-start | bytes 497672 | tf_op jit(solution)/shard_map/ppermute | solution.py:20
  109.0 7.3 %collective-permute-start.16 = (f32[3,3,18,1,256]{4,3,2,1,0:T(1,128)S(1)}, f32[3,3,18,1,256]{4,3,2,1,0:T(1,128)S(1)}, u32[]{:S(2)}, u32[]{:S(2)}) collective-permute-start(f32[3,3,18,1,256]{4,3,2,1,0:T(1,128)S(1)} %get-tuple-element.170), channel_id=1, source_target_pairs={{1,0},{2,1},{3,2},{0,3},{5,4},{6,5},{7,6},{4,7},{9,8},{10,9},{11,1... | collective-permute-start | bytes 497672 | tf_op jit(solution)/shard_map/ppermute | solution.py:21
  153.6 7.0 %collective-permute-start.4 = (f32[3,8,16,128]{3,2,1,0:T(8,128)S(1)}, f32[3,8,16,128]{3,2,1,0:T(8,128)S(1)}, u32[]{:S(2)}, u32[]{:S(2)}) collective-permute-start(f32[3,8,16,128]{3,2,1,0:T(8,128)S(1)} %fusion.269), channel_id=1, source_target_pairs={{0,8},{8,16},{16,24},{1,9},{9,17},{17,25},{2,10},{10,18},{18,26},{... | collective-permute-start | bytes 589832 | tf_op jit(solution)/shard_map/while/body/eval_jaxpr/ppermute | solution.py:29
  202.1 14.6 %collective-permute-start.25 = (f32[1,3,10,1,128]{4,3,2,1,0:T(1,128)}, f32[1,3,10,1,128]{4,3,2,1,0:T(1,128)}, u32[]{:S(2)}, u32[]{:S(2)}) collective-permute-start(f32[1,3,10,1,128]{4,3,2,1,0:T(1,128)} %get-tuple-element.232), channel_id=1, source_target_pairs={{0,1},{1,2},{2,3},{3,0},{4,5},{5,6},{6,7},{7,4},{8,9},{9,10},{10,1... | collective-permute-start | bytes 46088 | tf_op jit(solution)/shard_map/ppermute | solution.py:20
  202.1 14.6 %collective-permute-start.24 = (f32[1,3,10,1,128]{4,3,2,1,0:T(1,128)}, f32[1,3,10,1,128]{4,3,2,1,0:T(1,128)}, u32[]{:S(2)}, u32[]{:S(2)}) collective-permute-start(f32[1,3,10,1,128]{4,3,2,1,0:T(1,128)} %get-tuple-element.231), channel_id=1, source_target_pairs={{1,0},{2,1},{3,2},{0,3},{5,4},{6,5},{7,6},{4,7},{9,8},{10,9},{11,1... | collective-permute-start | bytes 46088 | tf_op jit(solution)/shard_map/ppermute | solution.py:21
  234.0 8.4 %collective-permute-start.27 = (f32[3,3,1,32,256]{4,3,2,1,0:T(8,128)S(1)}, f32[3,3,1,32,256]{4,3,2,1,0:T(8,128)S(1)}, u32[]{:S(2)}, u32[]{:S(2)}) collective-permute-start(f32[3,3,1,32,256]{4,3,2,1,0:T(8,128)S(1)} %get-tuple-element.155), channel_id=1, source_target_pairs={{0,4},{4,0},{1,5},{5,1},{2,6},{6,2},{3,7},{7,3},{8,12},{12,8},{9,1... | collective-permute-start | bytes 884744 | tf_op jit(solution)/shard_map/ppermute | solution.py:20
  244.6 7.4 %collective-permute-start.28 = (f32[3,3,18,1,256]{4,3,2,1,0:T(1,128)S(1)}, f32[3,3,18,1,256]{4,3,2,1,0:T(1,128)S(1)}, u32[]{:S(2)}, u32[]{:S(2)}) collective-permute-start(f32[3,3,18,1,256]{4,3,2,1,0:T(1,128)S(1)} %get-tuple-element.141), channel_id=1, source_target_pairs={{1,0},{2,1},{3,2},{0,3},{5,4},{6,5},{7,6},{4,7},{9,8},{10,9},{11,1... | collective-permute-start | bytes 497672 | tf_op jit(solution)/shard_map/ppermute | solution.py:21
  291.5 21.8 %collective-permute-start.34 = (f32[3,16,32,256]{3,2,1,0:T(8,128)S(1)}, f32[3,16,32,256]{3,2,1,0:T(8,128)}, u32[]{:S(2)}, u32[]{:S(2)}) collective-permute-start(f32[3,16,32,256]{3,2,1,0:T(8,128)S(1)} %get-tuple-element.109), channel_id=1, source_target_pairs={{0,8},{8,16},{16,24},{1,9},{9,17},{17,25},{2,10},{10,18},{18,26},{... | collective-permute-start | bytes 4718600 | tf_op jit(solution)/shard_map/ppermute | solution.py:29
  333.2 8.0 %collective-permute-start.35 = (f32[2,3,1,32,256]{4,3,2,1,0:T(8,128)S(1)}, f32[2,3,1,32,256]{4,3,2,1,0:T(8,128)S(1)}, u32[]{:S(2)}, u32[]{:S(2)}) collective-permute-start(f32[2,3,1,32,256]{4,3,2,1,0:T(8,128)S(1)} %copy-done.74), channel_id=1, source_target_pairs={{4,0},{0,4},{5,1},{1,5},{6,2},{2,6},{7,3},{3,7},{12,8},{8,12},{13,... | collective-permute-start | bytes 589832 | tf_op jit(solution)/shard_map/ppermute | solution.py:21
  344.7 26.3 %collective-permute-start.42 = (f32[1,3,10,1,128]{4,3,2,1,0:T(1,128)}, f32[1,3,10,1,128]{4,3,2,1,0:T(1,128)}, u32[]{:S(2)}, u32[]{:S(2)}) collective-permute-start(f32[1,3,10,1,128]{4,3,2,1,0:T(1,128)} %get-tuple-element.230), channel_id=1, source_target_pairs={{0,1},{1,2},{2,3},{3,0},{4,5},{5,6},{6,7},{7,4},{8,9},{9,10},{10,1... | collective-permute-start | bytes 46088 | tf_op jit(solution)/shard_map/ppermute | solution.py:20
  346.5 24.5 %collective-permute-start.41 = (f32[1,3,10,1,128]{4,3,2,1,0:T(1,128)}, f32[1,3,10,1,128]{4,3,2,1,0:T(1,128)}, u32[]{:S(2)}, u32[]{:S(2)}) collective-permute-start(f32[1,3,10,1,128]{4,3,2,1,0:T(1,128)} %get-tuple-element.229), channel_id=1, source_target_pairs={{1,0},{2,1},{3,2},{0,3},{5,4},{6,5},{7,6},{4,7},{9,8},{10,9},{11,1... | collective-permute-start | bytes 46088 | tf_op jit(solution)/shard_map/ppermute | solution.py:21
  388.3 7.2 %collective-permute-start.9 = (f32[3,8,16,128]{3,2,1,0:T(8,128)}, f32[3,8,16,128]{3,2,1,0:T(8,128)S(1)}, u32[]{:S(2)}, u32[]{:S(2)}) collective-permute-start(f32[3,8,16,128]{3,2,1,0:T(8,128)} %fusion.273), channel_id=1, source_target_pairs={{0,8},{8,16},{16,24},{1,9},{9,17},{17,25},{2,10},{10,18},{18,26},{... | collective-permute-start | bytes 589832 | tf_op jit(solution)/shard_map/while/body/eval_jaxpr/ppermute | solution.py:29
  408.7 7.2 %collective-permute-start.9 = (f32[3,8,16,128]{3,2,1,0:T(8,128)}, f32[3,8,16,128]{3,2,1,0:T(8,128)S(1)}, u32[]{:S(2)}, u32[]{:S(2)}) collective-permute-start(f32[3,8,16,128]{3,2,1,0:T(8,128)} %fusion.273), channel_id=1, source_target_pairs={{0,8},{8,16},{16,24},{1,9},{9,17},{17,25},{2,10},{10,18},{18,26},{... | collective-permute-start | bytes 589832 | tf_op jit(solution)/shard_map/while/body/eval_jaxpr/ppermute | solution.py:29
  429.2 7.2 %collective-permute-start.9 = (f32[3,8,16,128]{3,2,1,0:T(8,128)}, f32[3,8,16,128]{3,2,1,0:T(8,128)S(1)}, u32[]{:S(2)}, u32[]{:S(2)}) collective-permute-start(f32[3,8,16,128]{3,2,1,0:T(8,128)} %fusion.273), channel_id=1, source_target_pairs={{0,8},{8,16},{16,24},{1,9},{9,17},{17,25},{2,10},{10,18},{18,26},{... | collective-permute-start | bytes 589832 | tf_op jit(solution)/shard_map/while/body/eval_jaxpr/ppermute | solution.py:29
  445.6 8.0 %collective-permute-start.46 = (f32[1,3,10,1,128]{4,3,2,1,0:T(1,128)}, f32[1,3,10,1,128]{4,3,2,1,0:T(1,128)}, u32[]{:S(2)}, u32[]{:S(2)}) collective-permute-start(f32[1,3,10,1,128]{4,3,2,1,0:T(1,128)} %get-tuple-element.228), channel_id=1, source_target_pairs={{0,1},{1,2},{2,3},{3,0},{4,5},{5,6},{6,7},{7,4},{8,9},{9,10},{10,1... | collective-permute-start | bytes 46088 | tf_op jit(solution)/shard_map/ppermute | solution.py:20
  445.6 8.0 %collective-permute-start.45 = (f32[1,3,10,1,128]{4,3,2,1,0:T(1,128)}, f32[1,3,10,1,128]{4,3,2,1,0:T(1,128)}, u32[]{:S(2)}, u32[]{:S(2)}) collective-permute-start(f32[1,3,10,1,128]{4,3,2,1,0:T(1,128)} %get-tuple-element.227), channel_id=1, source_target_pairs={{1,0},{2,1},{3,2},{0,3},{5,4},{6,5},{7,6},{4,7},{9,8},{10,9},{11,1... | collective-permute-start | bytes 46088 | tf_op jit(solution)/shard_map/ppermute | solution.py:21
  470.3 8.8 %collective-permute-start.48 = (f32[3,3,1,32,256]{4,3,2,1,0:T(8,128)S(1)}, f32[3,3,1,32,256]{4,3,2,1,0:T(8,128)S(1)}, u32[]{:S(2)}, u32[]{:S(2)}) collective-permute-start(f32[3,3,1,32,256]{4,3,2,1,0:T(8,128)S(1)} %get-tuple-element.146), channel_id=1, source_target_pairs={{0,4},{4,0},{1,5},{5,1},{2,6},{6,2},{3,7},{7,3},{8,12},{12,8},{9,1... | collective-permute-start | bytes 884744 | tf_op jit(solution)/shard_map/ppermute | solution.py:20
  481.7 7.4 %collective-permute-start.49 = (f32[3,3,18,1,256]{4,3,2,1,0:T(1,128)S(1)}, f32[3,3,18,1,256]{4,3,2,1,0:T(1,128)S(1)}, u32[]{:S(2)}, u32[]{:S(2)}) collective-permute-start(f32[3,3,18,1,256]{4,3,2,1,0:T(1,128)S(1)} %get-tuple-element.139), channel_id=1, source_target_pairs={{1,0},{2,1},{3,2},{0,3},{5,4},{6,5},{7,6},{4,7},{9,8},{10,9},{11,1... | collective-permute-start | bytes 497672 | tf_op jit(solution)/shard_map/ppermute | solution.py:21
  (159 other events, 1076.6 us)
where the time goes:
time: 533 us; the launch traced here: 529 us
  other arithmetic  164 us (31%)
  local copies, waits for them, and re-layouts  133 us (25%)
  waiting for transfers between devices  125 us (23%)
  starting transfers between devices  85.7 us (16%)
  matrix products  19.5 us (4%)
    add x4, other arithmetic, apply_operator(): result_term + inner[:, across:across + 1] * grid[None, :, across]  57.2 us
    ppermute x34, waiting for transfers between devices, extended(): after = lax.ppermute(initial, axis, down)  48.3 us
    ppermute x7, waiting for transfers between devices, passed_along(): return lax.ppermute(shard, axis, pairs)  45 us
    ppermute x34, starting transfers between devices, extended(): after = lax.ppermute(initial, axis, down)  42.8 us
    slice x30, local copies, waits for them, and re-layouts, apply_operator(): ahead_z = jnp.roll(inner, -1, 4)  37.5 us
    reduce_sum x9, other arithmetic, restrict(): summed = jnp.sum(blocks, axis=(-4, -2)) * 0.25  33.1 us
    ppermute x34, waiting for transfers between devices, extended(): before = lax.ppermute(last, axis, up)  31.6 us
    ppermute x34, starting transfers between devices, extended(): before = lax.ppermute(last, axis, up)  29.1 us
  transfers between devices with their start and end apart: 75, of which 55 were waited for; matrix products, arithmetic and copies ran while one was open for 35% of the time, Pallas kernels for 0%

commit v1 on v0

v1 whole, which is shorter than its diff:
```python
import jax
import jax.numpy as jnp
from jax import lax
from jax.experimental import pallas as pl
from jax.experimental.pallas import tpu as pltpu
from jax.sharding import PartitionSpec as P

ITERS = 2
VISCOSITY = 0.25
TIME_STEP = 0.5
PAD = 8
CHUNK = 16
F32 = jnp.float32
BF16 = jnp.bfloat16


def ring(size, by):
    return [(i, (i + by) % size) for i in range(size)]


def both_faces(faces, permute, size):
    if size == 2:
        return permute(faces, 1)
    before = permute(faces[:, 0:1], 1)
    after = permute(faces[:, 1:2], -1)
    return jnp.concatenate([before, after], axis=1)


def swap_faces(faces):
    x_faces, y_last, y_first = faces
    gx, gy = lax.axis_size("gx"), lax.axis_size("gy")
    before_after = both_faces(x_faces, lambda a, by: lax.ppermute(a, "gx", ring(gx, by)), gx)
    behind = lax.ppermute(y_last, "gy", ring(gy, 1))
    ahead = lax.ppermute(y_first, "gy", ring(gy, -1))
    return before_after, behind, ahead


def hand_on(slabs, value, faces):
    gx, gy = lax.axis_size("gx"), lax.axis_size("gy")

    def permute(array, dx, dy):
        pairs = []
        for t in slabs:
            for x in range(gx):
                for y in range(gy):
                    source = (t * gx + x) * gy + y
                    target = ((t + 1) * gx + (x + dx) % gx) * gy + (y + dy) % gy
                    pairs.append((source, target))
        return lax.ppermute(array, ("tm", "gx", "gy"), pairs)

    moved = [] if value is None else [permute(value, 0, 0)]
    x_faces, y_last, y_first = faces
    moved.append(both_faces(x_faces, lambda a, by: permute(a, by, 0), gx))
    moved.append(permute(y_last, 0, 1))
    moved.append(permute(y_first, 0, -1))
    return moved


class Node:
    def __init__(self, main, x_faces, behind, ahead, off=0):
        self.main, self.x_faces, self.behind, self.ahead, self.off = main, x_faces, behind, ahead, off


def total(terms):
    result = terms[0]
    for term in terms[1:]:
        result = result + term
    return result


def fill(ext, parts, spread=()):
    width, length = ext.shape[1] - 2, ext.shape[2] - 2 * PAD
    inner = slice(PAD, PAD + length)
    for c in range(3):
        for k, at in ((0, 0), (1, width + 1)):
            terms = [w * n.x_faces[n.off + c, k] for w, n in parts]
            terms += [w * p[c, k * (width // 2 + 1)] for w, p, _ in spread]
            ext[c, at, inner] = total(terms)

    @pl.loop(0, width // 2)
    def _(i):
        for q in range(2):
            x = 2 * i + q
            for c in range(3):
                terms = [w * n.main[c, x] for w, n in parts]
                terms += [w * p[c, i + 1] for w, p, _ in spread]
                ext[c, x + 1, inner] = total(terms)
                row = pl.ds(x, 1)
                for k, at in ((0, PAD - 1), (1, PAD + length)):
                    terms = [w * (n.ahead if k else n.behind)[n.off + c, row] for w, n in parts]
                    terms += [w * e[k, c, pl.ds(i, 1)] for w, _, e in spread]
                    ext[c, x + 1, at : at + 1] = total(terms)


def turned(value, by):
    return pltpu.roll(value, by % value.shape[-1], value.ndim - 1)


def sides(ext, c, x, r, n):
    here = ext[c, x, r : r + n]
    return (
        here,
        (ext[c, x + 1, r : r + n], ext[c, x, r + 1 : r + 1 + n], turned(here, -1)),
        (ext[c, x - 1, r : r + n], ext[c, x, r - 1 : r - 1 + n], turned(here, 1)),
    )


def slopes(half, x, r, n):
    rows = []
    for a in range(3):
        _, ahead, behind = sides(half, a, x, r, n)
        rows.append([ahead[b] - behind[b] for b in range(3)])
    return rows


def rates(ext, x, r, n, speeds, grads, strength):
    fields = [sides(ext, a, x, r, n) for a in range(3)]
    toward = [strength - speed for speed in speeds]
    away = [strength + speed for speed in speeds]
    outputs = []
    for a in range(3):
        here, ahead, behind = fields[a]
        result = here * (grads[a][a] - 6.0 * strength)
        for b in range(3):
            if b != a:
                result = result + fields[b][0] * grads[a][b]
        for b in range(3):
            result = result + toward[b] * ahead[b] + away[b] * behind[b]
        outputs.append(result)
    return outputs


def fine_rates(ext, half, x, r, n):
    grads = slopes(half, x, r, n)
    speeds = [half[b, x, r : r + n] for b in range(3)]
    return rates(ext, x, r, n, speeds, grads, VISCOSITY), grads


def split(value):
    high = value.astype(BF16)
    low = (value - high.astype(F32)).astype(BF16)
    return high, low


def pair_table(rows, columns, by_row, entry):
    i = lax.broadcasted_iota(jnp.int32, (rows, columns), 0)
    j = lax.broadcasted_iota(jnp.int32, (rows, columns), 1)
    same = (i >> 1) == j if by_row else i == (j >> 1)
    return jnp.where(same, entry, 0.0).astype(BF16)


def squeeze(summed, rows, store, count):
    cx, y, z = summed.shape[1:]
    table = pair_table(z, z // 2, True, 0.125)
    for c in range(count):
        high, low = split(summed[c].reshape(cx * y, z))
        rows[...] = jnp.dot(high, table, preferred_element_type=F32) + jnp.dot(
            low, table, preferred_element_type=F32
        )
        half = cx * y // 2
        value = rows[pl.ds(0, half, stride=2)] + rows[pl.ds(1, half, stride=2)]
        store(c, value.reshape(cx, y // 2, z // 2))


def prolong(field, wide, edge, rows):
    cx, cy, cz = field.main.shape[1:]
    single = pair_table(cz, 2 * cz, False, 1.0)
    table = jnp.concatenate([single, single], axis=0)

    def along_z(value):
        high, low = split(value)
        return jnp.dot(jnp.concatenate([high, low], axis=1), table, preferred_element_type=F32)

    count = (cx + 2) * cy
    edges = []
    for c in range(3):
        layers = [field.x_faces[c, 0:1], field.main[c], field.x_faces[c, 1:2]]
        value = jnp.concatenate(layers, axis=0).reshape(count, cz)
        rows[pl.ds(0, count, stride=2)] = value
        rows[pl.ds(1, count, stride=2)] = value
        wide[c] = along_z(rows[...]).reshape(cx + 2, 2 * cy, 2 * cz)
        edges += [field.behind[c], field.ahead[c]]
    value = along_z(jnp.concatenate(edges, axis=0))
    for c in range(3):
        for k in range(2):
            at = (2 * c + k) * cx
            edge[k, c] = value[at : at + cx]


def emit_faces(main, outs):
    x_faces, y_last, y_first = outs
    width, length = main.shape[1:3]
    for c in range(3):
        x_faces[c, 0] = main[c, width - 1]
        x_faces[c, 1] = main[c, 0]
        for x in range(width):
            y_last[c, x : x + 1] = main[c, x, length - 1 : length]
            y_first[c, x : x + 1] = main[c, x, 0:1]


def coarsen_kernel(first, v, s, g, speed, zero, end, end_x, end_l, end_f, summed, rows):
    f = first[0]

    def run(field, store):
        @pl.loop(0, field.shape[1] // 2)
        def _(i):
            for c in range(3):
                summed[c, i] = field[c, 2 * i] + field[c, 2 * i + 1]

        squeeze(summed, rows, store, 3)

    def store_end(c, value):
        end[c] = value

    def store_zero(c, value):
        zero[c] = f * value + (1.0 - f) * end[c]

    def store_speed(c, value):
        speed[c] = value * 0.25

    run(g, store_end)
    emit_faces(end, (end_x, end_l, end_f))
    run(s, store_zero)
    run(v, store_speed)


def integral_loop(ext, half, summed, grads_summed):
    width, length = ext.shape[1] - 2, ext.shape[2] - 2 * PAD
    n = min(CHUNK, length)

    @pl.loop(0, width // 2)
    def _(i):
        for r in range(0, length, n):
            pair = [fine_rates(ext, half, 2 * i + 1 + q, PAD + r, n) for q in range(2)]
            for a in range(3):
                summed[a, i, r : r + n] = pair[0][0][a] + pair[1][0][a]
                if grads_summed is not None:
                    for b in range(3):
                        value = pair[0][1][a][b] + pair[1][1][a][b]
                        grads_summed[3 * a + b, i, r : r + n] = value


def offset_start_kernel(
    first, v, s, g, x_faces, behind, ahead, zero,
    integral, coarse_grads, end, end_x, end_l, end_f,
    ext, half, summed, grads_summed, rows,
):
    f = first[0]
    fill(half, [(0.5, Node(v, x_faces, behind, ahead))])
    start = Node(s, x_faces, behind, ahead, 6)
    guess = Node(g, x_faces, behind, ahead, 3)
    share = f * (TIME_STEP / 6.0)
    fill(ext, [(share, start), (TIME_STEP - share, guess)])
    integral_loop(ext, half, summed, grads_summed)

    def store(c, value):
        integral[c] = value
        end[c] = zero[c] + value

    squeeze(summed, rows, store, 3)
    emit_faces(end, (end_x, end_l, end_f))

    def store_grads(c, value):
        coarse_grads[c] = value

    squeeze(grads_summed, rows, store_grads, 9)


def offset_later_kernel(
    first, v, s, x_faces, behind, ahead,
    u0, u0_x, u0_b, u0_a, u1, u1_x, u1_b, u1_a, u2, u2_x, u2_b, u2_a,
    integral, zero, end, end_x, end_l, end_f,
    ext, half, summed, rows,
):
    f = first[0]
    fill(half, [(0.5, Node(v, x_faces, behind, ahead))])
    sixth = TIME_STEP / 6.0
    fill(
        ext,
        [
            (f * sixth, Node(s, x_faces, behind, ahead, 6)),
            (sixth, Node(u0, u0_x, u0_b, u0_a)),
            (TIME_STEP * 2.0 / 3.0, Node(u1, u1_x, u1_b, u1_a)),
            (sixth, Node(u2, u2_x, u2_b, u2_a)),
        ],
    )

    @pl.loop(0, s.shape[1] // 2)
    def _(i):
        for c in range(3):
            summed[c, i] = f * (s[c, 2 * i] + s[c, 2 * i + 1]) + (u0[c, 2 * i] + u0[c, 2 * i + 1])

    def store_zero(c, value):
        zero[c] = value

    squeeze(summed, rows, store_zero, 3)
    integral_loop(ext, half, summed, None)

    def store(c, value):
        integral[c] = value
        end[c] = zero[c] + value

    squeeze(summed, rows, store, 3)
    emit_faces(end, (end_x, end_l, end_f))


def chain_kernel(last, arrivals, *refs):
    refs = list(refs)

    def take(count):
        taken = refs[:count]
        del refs[:count]
        return taken

    first, = take(1)
    arrived = [take(4) for _ in range(arrivals)]
    zero, zero_x, zero_b, zero_a, integral, speed, coarse_grads = take(7)
    f = first[0]
    if last:
        end_two, = take(1)
        d0, d0_x, d0_b, d0_a, d2, d2_x, d2_l, d2_f = take(8)
    else:
        end, end_x, end_l, end_f = take(4)
        d0, d0_x, d0_b, d0_a = take(4)
    ext, = take(1)
    rest = 1.0 - f
    width, length = zero.shape[1:3]
    for out, old, k in ((d0, zero, 0), (d0_x, zero_x, 1), (d0_b, zero_b, 2), (d0_a, zero_a, 3)):
        out[...] = rest * (total([a[k][...] for a in arrived]) - old[...])
    fill(ext, [(TIME_STEP, Node(d0, d0_x, d0_b, d0_a))])

    @pl.loop(0, width)
    def _(x):
        speeds = [speed[b, x] for b in range(3)]
        grads = [[coarse_grads[3 * a + b, x] for b in range(3)] for a in range(3)]
        changes = rates(ext, x + 1, PAD, length, speeds, grads, VISCOSITY / 4.0)
        for a in range(3):
            value = zero[a, x] + d0[a, x] + integral[a, x] + changes[a]
            if last:
                d2[a, x] = value - end_two[a, x]
            else:
                end[a, x] = value

    emit_faces(d2 if last else end, (d2_x, d2_l, d2_f) if last else (end_x, end_l, end_f))


def middle_kernel(nodes, *refs):
    first, v, vx, vb, va = refs[:5]
    at = 5
    parts = []
    for _, _, _, own, off in nodes:
        main = refs[at]
        at += 1
        if own:
            x_faces, behind, ahead = refs[at : at + 3]
            at += 3
        else:
            x_faces, behind, ahead = vx, vb, va
        parts.append(Node(main, x_faces, behind, ahead, off))
    d0 = Node(*refs[at : at + 4])
    d2 = Node(*refs[at + 4 : at + 8])
    a1, a1_x, a1_l, a1_f, rest, rest_x, rest_b, rest_a = refs[at + 8 : at + 16]
    ext, half, wide0, edge0, wide2, edge2, rows = refs[at + 16 :]
    f = first[0]
    begin, first_stage, second_stage = [
        [(spec[k][0] * f + spec[k][1], node) for spec, node in zip(nodes, parts)] for k in range(3)
    ]
    fill(half, [(0.5, Node(v, vx, vb, va))])
    prolong(d0, wide0, edge0, rows)
    prolong(d2, wide2, edge2, rows)
    fill(
        ext,
        [(TIME_STEP * w, node) for w, node in first_stage],
        [(TIME_STEP * 0.375, wide0, edge0), (TIME_STEP * 0.125, wide2, edge2)],
    )
    width, length = a1.shape[1:3]
    n = min(CHUNK, length)
    last_cx = width // 2 + 1

    def rest_of(get, p0, p2):
        return total([w * get(node) for w, node in second_stage]) + 0.125 * (p2 - p0)

    for c in range(3):
        for k in range(2):
            rest_x[c, k] = rest_of(
                lambda nd: nd.x_faces[nd.off + c, k], wide0[c, k * last_cx], wide2[c, k * last_cx]
            )

    @pl.loop(0, width // 2)
    def _(i):
        for q in range(2):
            x = 2 * i + q
            row = pl.ds(x, 1)
            for r in range(0, length, n):
                changes, _ = fine_rates(ext, half, x + 1, PAD + r, n)
                for a in range(3):
                    p0, p2 = wide0[a, i + 1, r : r + n], wide2[a, i + 1, r : r + n]
                    start = total([w * nd.main[a, x, r : r + n] for w, nd in begin])
                    a1[a, x, r : r + n] = start + p0 + changes[a]
                    rest[a, x, r : r + n] = rest_of(lambda nd: nd.main[a, x, r : r + n], p0, p2)
            for c in range(3):
                p0, p2 = edge0[0, c, pl.ds(i, 1)], edge2[0, c, pl.ds(i, 1)]
                rest_b[c, row] = rest_of(lambda nd: nd.behind[nd.off + c, row], p0, p2)
                p0, p2 = edge0[1, c, pl.ds(i, 1)], edge2[1, c, pl.ds(i, 1)]
                rest_a[c, row] = rest_of(lambda nd: nd.ahead[nd.off + c, row], p0, p2)

    emit_faces(a1, (a1_x, a1_l, a1_f))


def finish_kernel(last, first, v, vx, vb, va, a1, a1_x, a1_b, a1_a, rest, rest_x, rest_b, rest_a, *refs):
    if last:
        a2, ext, half = refs
    else:
        a2, a2_x, a2_l, a2_f, end, end_x, end_l, end_f, ext, half, summed, rows = refs
    fill(half, [(0.5, Node(v, vx, vb, va))])
    fill(
        ext,
        [
            (TIME_STEP * 0.5, Node(a1, a1_x, a1_b, a1_a)),
            (TIME_STEP, Node(rest, rest_x, rest_b, rest_a)),
        ],
    )
    width, length = a1.shape[1:3]
    n = min(CHUNK, length)

    @pl.loop(0, width // 2)
    def _(i):
        for r in range(0, length, n):
            pair = []
            for q in range(2):
                x = 2 * i + q
                changes, _ = fine_rates(ext, half, x + 1, PAD + r, n)
                pair.append([a1[a, x, r : r + n] + changes[a] for a in range(3)])
                for a in range(3):
                    a2[a, x, r : r + n] = pair[q][a]
            if not last:
                for a in range(3):
                    summed[a, i, r : r + n] = pair[0][a] + pair[1][a]

    if not last:
        emit_faces(a2, (a2_x, a2_l, a2_f))

        def store(c, value):
            end[c] = value

        squeeze(summed, rows, store, 3)
        emit_faces(end, (end_x, end_l, end_f))


def call(kernel, name, first, args, outs, scratch, flops=0):
    moved = sum(4 * a.size for a in args)
    return pl.pallas_call(
        kernel,
        name=name,
        out_shape=[jax.ShapeDtypeStruct(dims, F32) for dims in outs],
        in_specs=[pl.BlockSpec(memory_space=pltpu.SMEM)] + [pl.BlockSpec(memory_space=pltpu.VMEM)] * len(args),
        out_specs=[pl.BlockSpec(memory_space=pltpu.VMEM)] * len(outs),
        scratch_shapes=[pltpu.VMEM(dims, F32) for dims in scratch],
        compiler_params=pltpu.CompilerParams(vmem_limit_bytes=56 << 20),
        cost_estimate=pl.CostEstimate(flops=flops, bytes_accessed=moved, transcendentals=0),
    )(first, *args)


def shards(velocity, start_field, guess):
    own = guess[0]
    _, nx, ny, nz = own.shape
    cx, cy, cz = nx // 2, ny // 2, nz // 2
    slabs = lax.axis_size("tm")
    first = (lax.axis_index("tm") == 0).astype(F32).reshape(1)

    fine, fine_faces = (3, nx, ny, nz), [(3, 2, ny, nz), (3, nx, nz), (3, nx, nz)]
    coarse, coarse_faces = (3, cx, cy, cz), [(3, 2, cy, cz), (3, cx, cz), (3, cx, cz)]
    ext = (3, nx + 2, ny + 2 * PAD, nz)
    coarse_ext = (3, cx + 2, cy + 2 * PAD, cz)
    summed, rows = (3, cx, ny, nz), (cx * ny, cz)
    wide, edge, wide_rows = (3, cx + 2, ny, nz), (2, 3, cx, nz), ((cx + 2) * ny, cz)

    fields = [velocity, own, start_field]
    packed = (
        jnp.concatenate([jnp.concatenate([f[:, nx - 1 :], f[:, :1]], axis=1) for f in fields], axis=0),
        jnp.concatenate([f[:, :, ny - 1] for f in fields], axis=0),
        jnp.concatenate([f[:, :, 0] for f in fields], axis=0),
    )
    layers = swap_faces(packed)
    speed, zero, end_two, *sent = call(
        coarsen_kernel, "coarsen", first, [velocity, start_field, own],
        [coarse, coarse, coarse] + coarse_faces, [summed, rows], 10_000_000,
    )
    zero_faces = swap_faces(sent)
    integral, coarse_grads, end, *sent = call(
        offset_start_kernel, "offset_start", first, [velocity, start_field, own, *layers, zero],
        [coarse, (9, cx, cy, cz), coarse] + coarse_faces,
        [ext, ext, summed, (9, cx, ny, nz), rows], 40_000_000,
    )
    for sweep_index in range(ITERS):
        final = sweep_index + 1 == ITERS
        arrivals = []
        for slab in range(slabs - 1):
            arrivals.append(hand_on([slab], end, sent))
            last = slab + 2 == slabs
            args = [a for group in arrivals for a in group]
            args += [zero, *zero_faces, integral, speed, coarse_grads]
            if last:
                outs = [coarse] + coarse_faces + [coarse] + coarse_faces
                args.append(end_two)
            else:
                outs = [coarse] + coarse_faces + [coarse] + coarse_faces
            count = len(arrivals)
            results = call(
                lambda *refs, last=last, count=count: chain_kernel(last, count, *refs),
                "chain", first, args, outs, [coarse_ext], 2_000_000,
            )
            if not last:
                end, *sent = results[:4]
        d0, d2 = list(results[:4]), [results[4], *swap_faces(results[5:])]

        if sweep_index == 0:
            nodes = (
                ((1.0, 0.0), (5.0 / 24.0, 0.0), (-1.0 / 24.0, 0.0), False, 6),
                ((-1.0, 1.0), (-5.0 / 24.0, 0.5), (1.0 / 24.0, 0.0), False, 3),
            )
            args = [start_field, own]
        else:
            nodes = (
                ((1.0, 0.0), (5.0 / 24.0, 0.0), (-1.0 / 24.0, 0.0), False, 6),
                ((0.0, 1.0), (0.0, 5.0 / 24.0), (0.0, -1.0 / 24.0), True, 0),
                ((0.0, 0.0), (0.0, 1.0 / 3.0), (0.0, -1.0 / 6.0), True, 0),
                ((0.0, 0.0), (0.0, -1.0 / 24.0), (0.0, 5.0 / 24.0), True, 0),
            )
            args = [start_field, *u0, *u1, *u2]
        middle, m_x, m_l, m_f, *rest = call(
            lambda *refs, nodes=nodes: middle_kernel(nodes, *refs),
            "middle", first, [velocity, *layers, *args, *d0, *d2],
            [fine] + fine_faces + [fine] + fine_faces,
            [ext, ext, wide, edge, wide, edge, wide_rows], 60_000_000,
        )
        u1 = [middle, *swap_faces((m_x, m_l, m_f))]
        results = call(
            lambda *refs, final=final: finish_kernel(final, *refs),
            "finish", first, [velocity, *layers, *u1, *rest],
            [fine] if final else [fine] + fine_faces + [coarse] + coarse_faces,
            [ext, ext] if final else [ext, ext, summed, rows], 40_000_000,
        )
        if final:
            return results[0][None]
        value, *faces = results[:4]
        u0 = hand_on(range(slabs - 1), value, faces)
        u2 = [value, *swap_faces(faces)]
        zero_faces = hand_on(range(slabs - 1), None, results[5:])
        end_two = results[4]
        integral, zero, end, *sent = call(
            offset_later_kernel, "offset_later", first,
            [velocity, start_field, *layers, *u0, *u1, *u2],
            [coarse, coarse, coarse] + coarse_faces, [ext, ext, summed, rows], 40_000_000,
        )


def solution(mesh):
    in_specs = (
        P(None, "gx", "gy", None),
        P(None, "gx", "gy", None),
        P("tm", None, "gx", "gy", None),
    )
    out_specs = P("tm", None, "gx", "gy", None)
    return jax.shard_map(shards, mesh=mesh, in_specs=in_specs, out_specs=out_specs, check_vma=False)
```

time: 533 us -> 222 us (0.42)
  other arithmetic: 164 us -> 0.56 us
  local copies, waits for them, and re-layouts: 133 us -> 17.3 us
  Pallas kernels: 0 us -> 73.3 us
  waiting for transfers between devices: 125 us -> 66.9 us
  starting transfers between devices: 85.7 us -> 61.7 us
  matrix products: 19.5 us -> 0 us
    add x15 -> x0, other arithmetic: 77.4 us -> none  [the longest x4 57.2 us: apply_operator(): result_term + inner[:, across:across + 1] * grid[None, :, across]]
    pallas_call x0 -> x13, Pallas kernels: none -> 73.3 us  [call(): pl.pallas_call(kernel, name=name, out_shape=[jax.ShapeDtypeStruct(dims, F...]
    ppermute x75 -> x52, waiting for transfers between devices: 125 us -> 66.9 us  [the longest x31 37.1 us: permute(): return lax.ppermute(array, ('tm', 'gx', 'gy'), pairs)]
    slice x48 -> x9, local copies, waits for them, and re-layouts: 42.2 us -> 4.96 us  [the longest x5 2.38 us: shards(): f[:, nx - 1:]]
    reduce_sum x9 -> x0, other arithmetic: 33.1 us -> none  [restrict(): summed = jnp.sum(blocks, axis=(-4, -2)) * 0.25]
    reshape x10 -> x0, local copies, waits for them, and re-layouts: 28.6 us -> none  [the longest x5 15.9 us: prolong(): spread.reshape(lead + (extent[-3] * 2, extent[-2] * 2, extent[-1] * 2))]
    ppermute x75 -> x52, starting transfers between devices: 85.7 us -> 61.7 us  [the longest x31 39.5 us: permute(): return lax.ppermute(array, ('tm', 'gx', 'gy'), pairs)]
    dot_general x13 -> x0, matrix products: 19.5 us -> none  [the longest x9 16.7 us: restrict(): jnp.einsum('...z,zc->...c', summed, table, precision=lax.Precision.HIGHEST)]
  transfers between devices with their start and end apart: 75 -> 52, of which waited for: 55 -> 27; matrix products, arithmetic and copies ran while one was open for 35% -> 2% of each run, Pallas kernels for 0% -> 2%
where the time goes in v1:
time: 222 us; the launch traced here: 221 us
  Pallas kernels  73.3 us (33%)
  waiting for transfers between devices  66.9 us (30%)
  starting transfers between devices  61.7 us (28%)
  local copies, waits for them, and re-layouts  17.3 us (8%)
    pallas_call x13, Pallas kernels, call(): pl.pallas_call(kernel, name=name, out_shape=[jax.ShapeDtypeStruct(dims, F...  73.3 us
    ppermute x31, starting transfers between devices, permute(): return lax.ppermute(array, ('tm', 'gx', 'gy'), pairs)  39.5 us
    ppermute x31, waiting for transfers between devices, permute(): return lax.ppermute(array, ('tm', 'gx', 'gy'), pairs)  37.1 us
    ppermute x7, waiting for transfers between devices, swap_faces(): ahead = lax.ppermute(y_first, 'gy', ring(gy, -1))  13.4 us
    ppermute x7, waiting for transfers between devices, swap_faces(): behind = lax.ppermute(y_last, 'gy', ring(gy, 1))  12.1 us
    unnamed x117, local copies, waits for them, and re-layouts  11.4 us
    ppermute x7, starting transfers between devices, swap_faces(): lax.ppermute(a, 'gx', ring(gx, by))  8.62 us
    ppermute x7, starting transfers between devices, swap_faces(): ahead = lax.ppermute(y_first, 'gy', ring(gy, -1))  7.89 us
  transfers between devices with their start and end apart: 52, of which 27 were waited for; matrix products, arithmetic and copies ran while one was open for 2% of the time, Pallas kernels for 2%

profile of v1, /device:TPU:26, one launch (start us, length us, event | category | flops | bytes accessed | tf_op | source)
XLA Modules:
  0.0 220.7 jit_solution(3683652228490056225)
XLA Ops:
  10.3 4.6 %coarsen.1 = (f32[3,8,16,128]{3,2,1,0:T(8,128)}, f32[3,8,16,128]{3,2,1,0:T(8,128)}, f32[3,8,16,128]{3,2,1,0:T(8,128)}, f32[3,2,16,128]{3,2,1,0:T(8,128)}, f32[3,8,128]{2,1,0:T(8,128)}, /*index=5*/f32[3,8,128]{2,1,0:T(8,128)}) custom-call(f32[1]{0:T(128)} %bitcast.first.refs_0_, f32[3,16,32,256]{3,2,1,0:T(8,128)} %refs_1_.7, f32[3,16,32,256]{3,2,1,0:T(8,128)} %refs_5_.3, ...), custom_call_target="tpu_custom_call" | custom-call | flops 10000000 | bytes 4718592 | tf_op jit(solution)/shard_map/coarsen/pallas_call | solution.py:452
  14.9 4.3 %collective-permute-done = f32[9,2,32,256]{3,1,0,2:T(2,128)S(1)} collective-permute-done((f32[9,2,32,256]{3,1,0,2:T(2,128)S(1)}, f32[9,2,32,256]{3,1,0,2:T(2,128)S(1)}, u32[]{:S(2)}, u32[]{:S(2)}) %collective-permute-start) | collective-permute-done | bytes 589856 | tf_op jit(solution)/shard_map/ppermute | solution.py:32
  20.9 7.7 %offset_start.1 = (f32[3,8,16,128]{3,2,1,0:T(8,128)}, f32[9,8,16,128]{3,2,1,0:T(8,128)}, f32[3,8,16,128]{3,2,1,0:T(8,128)}, f32[3,2,16,128]{3,2,1,0:T(8,128)}, f...) custom-call(f32[1]{0:T(128)} %bitcast.first.refs_0_, f32[3,16,32,256]{3,2,1,0:T(8,128)} %refs_1_.7, f32[3,16,32,256]{3,2,1,0:T(8,128)} %refs_5_.3, ...), custom_call_target="tpu_custom_call" | custom-call | flops 40000000 | bytes 5799936 | tf_op jit(solution)/shard_map/offset_start/pallas_call | solution.py:452
  38.7 3.1 %chain.6 = (f32[3,8,16,128]{3,2,1,0:T(8,128)}, f32[3,2,16,128]{3,2,1,0:T(8,128)}, f32[3,8,128]{2,1,0:T(8,128)}, f32[3,8,128]{2,1,0:T(8,128)}, f32[3,8,16,128]{3,...) custom-call(f32[1]{0:T(128)} %bitcast.first.refs_0_, ...), custom_call_target="tpu_custom_call" | custom-call | flops 2000000 | bytes 1523712 | tf_op jit(solution)/shard_map/chain/pallas_call | solution.py:452
  47.0 5.4 %collective-permute-done.12.refs_7_ = f32[3,8,128]{2,1,0:T(8,128)S(1)} collective-permute-done((f32[3,8,128]{2,1,0:T(8,128)}, f32[3,8,128]{2,1,0:T(8,128)S(1)}, u32[]{:S(2)}, u32[]{:S(2)}) %collective-permute-start.12) | collective-permute-done | bytes 12320 | tf_op jit(solution)/shard_map/ppermute | solution.py:49
  55.0 3.2 %chain.7 = (f32[3,8,16,128]{3,2,1,0:T(8,128)}, f32[3,2,16,128]{3,2,1,0:T(8,128)}, f32[3,8,128]{2,1,0:T(8,128)}, f32[3,8,128]{2,1,0:T(8,128)}, f32[3,8,16,128]{3,...) custom-call(f32[1]{0:T(128)} %bitcast.first.refs_0_, ...), custom_call_target="tpu_custom_call" | custom-call | flops 2000000 | bytes 1794048 | tf_op jit(solution)/shard_map/chain/pallas_call | solution.py:452
  65.6 3.3 %chain.8 = (f32[3,8,16,128]{3,2,1,0:T(8,128)}, f32[3,2,16,128]{3,2,1,0:T(8,128)}, f32[3,8,128]{2,1,0:T(8,128)}, f32[3,8,128]{2,1,0:T(8,128)}, f32[3,8,16,128]{3,...) custom-call(f32[1]{0:T(128)} %bitcast.first.refs_0_, ...), custom_call_target="tpu_custom_call" | custom-call | flops 2000000 | bytes 2260992 | tf_op jit(solution)/shard_map/chain/pallas_call | solution.py:452
  73.7 3.8 %collective-permute-done.20.refs_14_ = f32[3,8,128]{2,1,0:T(8,128)S(1)} collective-permute-done((f32[3,8,128]{2,1,0:T(8,128)}, f32[3,8,128]{2,1,0:T(8,128)S(1)}, u32[]{:S(2)}, u32[]{:S(2)}) %collective-permute-start.20) | collective-permute-done | bytes 12320 | tf_op jit(solution)/shard_map/ppermute | solution.py:34
  78.1 8.6 %middle.2 = (f32[3,16,32,256]{3,2,1,0:T(8,128)}, f32[3,2,32,256]{3,2,1,0:T(8,128)}, f32[3,16,256]{2,1,0:T(8,128)}, f32[3,16,256]{2,1,0:T(8,128)}, f32[3,16,32,25...) custom-call(f32[1]{0:T(128)} %bitcast.first.refs_0_, ...), custom_call_target="tpu_custom_call" | custom-call | flops 60000000 | bytes 6144000 | tf_op jit(solution)/shard_map/middle/pallas_call | solution.py:452
  90.0 2.7 %collective-permute-done.22.refs_7_.u1_b.refs_12_ = f32[3,16,256]{2,1,0:T(8,128)S(1)} collective-permute-done((f32[3,16,256]{2,1,0:T(8,128)}, f32[3,16,256]{2,1,0:T(8,128)S(1)}, u32[]{:S(2)}, u32[]{:S(2)}) %collective-permute-start.22) | collective-permute-done | bytes 49184 | tf_op jit(solution)/shard_map/ppermute | solution.py:33
  94.8 7.1 %finish.2 = (f32[3,16,32,256]{3,2,1,0:T(8,128)}, f32[3,2,32,256]{3,2,1,0:T(8,128)}, f32[3,16,256]{2,1,0:T(8,128)}, f32[3,16,256]{2,1,0:T(8,128)}, f32[3,8,16,128...) custom-call(f32[1]{0:T(128)} %bitcast.first.refs_0_, ...), custom_call_target="tpu_custom_call" | custom-call | flops 40000000 | bytes 6193152 | tf_op jit(solution)/shard_map/finish/pallas_call | solution.py:452
  111.3 3.0 %collective-permute-done.26.u0_b.refs_8_ = f32[3,16,256]{2,1,0:T(8,128)S(1)} collective-permute-done((f32[3,16,256]{2,1,0:T(8,128)}, f32[3,16,256]{2,1,0:T(8,128)S(1)}, u32[]{:S(2)}, u32[]{:S(2)}) %collective-permute-start.26) | collective-permute-done | bytes 49184 | tf_op jit(solution)/shard_map/ppermute | solution.py:49
  117.3 5.7 %collective-permute-done.27.u0_a.refs_9_ = f32[3,16,256]{2,1,0:T(8,128)S(1)} collective-permute-done((f32[3,16,256]{2,1,0:T(8,128)}, f32[3,16,256]{2,1,0:T(8,128)S(1)}, u32[]{:S(2)}, u32[]{:S(2)}) %collective-permute-start.27) | collective-permute-done | bytes 49184 | tf_op jit(solution)/shard_map/ppermute | solution.py:49
  123.0 4.4 %collective-permute-done.25.u0_x.refs_7_ = f32[3,2,32,256]{3,2,1,0:T(8,128)S(1)} collective-permute-done((f32[3,2,32,256]{3,2,1,0:T(8,128)}, f32[3,2,32,256]{3,2,1,0:T(8,128)S(1)}, u32[]{:S(2)}, u32[]{:S(2)}) %collective-permute-start.25) | collective-permute-done | bytes 196640 | tf_op jit(solution)/shard_map/ppermute | solution.py:49
  129.2 8.8 %offset_later.1 = (f32[3,8,16,128]{3,2,1,0:T(8,128)}, f32[3,8,16,128]{3,2,1,0:T(8,128)}, f32[3,8,16,128]{3,2,1,0:T(8,128)}, f32[3,2,16,128]{3,2,1,0:T(8,128)}, f...) custom-call(f32[1]{0:T(128)} %bitcast.first.refs_0_, f32[3,16,32,256]{3,2,1,0:T(8,128)} %refs_1_.7, f32[3,16,32,256]{3,2,1,0:T(8,128)} %refs_5_.3, ...), custom_call_target="tpu_custom_call" | custom-call | flops 40000000 | bytes 9633792 | tf_op jit(solution)/shard_map/offset_later/pallas_call | solution.py:452
  147.9 3.3 %collective-permute-done.37.refs_8_.refs_12_.refs_16_ = f32[3,8,128]{2,1,0:T(8,128)S(1)} collective-permute-done((f32[3,8,128]{2,1,0:T(8,128)S(1)}, f32[3,8,128]{2,1,0:T(8,128)S(1)}, u32[]{:S(2)}, u32[]{:S(2)}) %collective-permute-start.37) | collective-permute-done | bytes 12320 | tf_op jit(solution)/shard_map/ppermute | solution.py:49
  152.6 3.1 %chain.9 = (f32[3,8,16,128]{3,2,1,0:T(8,128)}, f32[3,2,16,128]{3,2,1,0:T(8,128)}, f32[3,8,128]{2,1,0:T(8,128)}, f32[3,8,128]{2,1,0:T(8,128)}, f32[3,8,16,128]{3,...) custom-call(f32[1]{0:T(128)} %bitcast.first.refs_0_, ...), custom_call_target="tpu_custom_call" | custom-call | flops 2000000 | bytes 1523712 | tf_op jit(solution)/shard_map/chain/pallas_call | solution.py:452
  160.8 6.5 %collective-permute-done.40.refs_7_ = f32[3,8,128]{2,1,0:T(8,128)S(1)} collective-permute-done((f32[3,8,128]{2,1,0:T(8,128)}, f32[3,8,128]{2,1,0:T(8,128)S(1)}, u32[]{:S(2)}, u32[]{:S(2)}) %collective-permute-start.40) | collective-permute-done | bytes 12320 | tf_op jit(solution)/shard_map/ppermute | solution.py:49
  171.2 3.2 %chain.10 = (f32[3,8,16,128]{3,2,1,0:T(8,128)}, f32[3,2,16,128]{3,2,1,0:T(8,128)}, f32[3,8,128]{2,1,0:T(8,128)}, f32[3,8,128]{2,1,0:T(8,128)}, f32[3,8,16,128]{3...) custom-call(f32[1]{0:T(128)} %bitcast.first.refs_0_, ...), custom_call_target="tpu_custom_call" | custom-call | flops 2000000 | bytes 1794048 | tf_op jit(solution)/shard_map/chain/pallas_call | solution.py:452
  181.9 3.3 %chain.11 = (f32[3,8,16,128]{3,2,1,0:T(8,128)}, f32[3,2,16,128]{3,2,1,0:T(8,128)}, f32[3,8,128]{2,1,0:T(8,128)}, f32[3,8,128]{2,1,0:T(8,128)}, f32[3,8,16,128]{3...) custom-call(f32[1]{0:T(128)} %bitcast.first.refs_0_, ...), custom_call_target="tpu_custom_call" | custom-call | flops 2000000 | bytes 2260992 | tf_op jit(solution)/shard_map/chain/pallas_call | solution.py:452
  186.4 2.5 %collective-permute-start.47 = (f32[3,8,128]{2,1,0:T(8,128)}, f32[3,8,128]{2,1,0:T(8,128)S(1)}, u32[]{:S(2)}, u32[]{:S(2)}) collective-permute-start(f32[3,8,128]{2,1,0:T(8,128)} %get-tuple-element.143), channel_id=1, source_target_pairs={{0,1},{1,2},{2,3},{3,0},{4,5},{5,6},{6,7},{7,4},{8,9},{9,10},{10,1... | collective-permute-start | bytes 36872 | tf_op jit(solution)/shard_map/ppermute | solution.py:33
  190.5 4.1 %collective-permute-done.48.refs_25_ = f32[3,8,128]{2,1,0:T(8,128)S(1)} collective-permute-done((f32[3,8,128]{2,1,0:T(8,128)}, f32[3,8,128]{2,1,0:T(8,128)S(1)}, u32[]{:S(2)}, u32[]{:S(2)}) %collective-permute-start.48) | collective-permute-done | bytes 12320 | tf_op jit(solution)/shard_map/ppermute | solution.py:34
  195.3 10.5 %middle.3 = (f32[3,16,32,256]{3,2,1,0:T(8,128)}, f32[3,2,32,256]{3,2,1,0:T(8,128)}, f32[3,16,256]{2,1,0:T(8,128)}, f32[3,16,256]{2,1,0:T(8,128)}, f32[3,16,32,25...) custom-call(f32[1]{0:T(128)} %bitcast.first.refs_0_, ...), custom_call_target="tpu_custom_call" | custom-call | flops 60000000 | bytes 10174464 | tf_op jit(solution)/shard_map/middle/pallas_call | solution.py:452
  213.8 6.9 %finish.3 = f32[3,16,32,256]{3,2,1,0:T(8,128)} custom-call(f32[1]{0:T(128)} %bitcast.first.refs_0_, f32[3,16,32,256]{3,2,1,0:T(8,128)} %refs_1_.7, f32[9,2,32,256]{3,2,1,0:T(8,128)} %copy.21.x_faces.refs_2_, f32[9,16,256]{2,1,0:T(8,128)} %copy-done.2, f32[9,16,256]{2,1,0:T(8,128)} %copy-done.3, f32[3,16,32,256]{3,2,1,0:T(8,128)} %get-tuple-element.145.refs_5_, ...), custom_call_target="tpu_custom_call" | custom-call | flops 40000000 | bytes 6193152 | tf_op jit(solution)/shard_map/finish/pallas_call | solution.py:452
  (226 shorter events, 100.8 us)
Async XLA Ops:
  4.1 15.1 %collective-permute-start = (f32[9,2,32,256]{3,1,0,2:T(2,128)S(1)}, f32[9,2,32,256]{3,1,0,2:T(2,128)S(1)}, u32[]{:S(2)}, u32[]{:S(2)}) collective-permute-start(f32[9,2,32,256]{3,1,0,2:T(2,128)S(1)} %maximum_maximum_fusion), channel_id=1, source_target_pairs={{0,4},{4,0},{1,5},{5,1},{2,6},{6,2},{3,7},{7,3},{8,12},{12,8},{9,1... | collective-permute-start | bytes 1769480 | tf_op jit(solution)/shard_map/ppermute | solution.py:32
  8.1 12.1 %collective-permute-start.1 = (f32[9,16,256]{2,1,0:T(8,128)S(1)}, f32[9,16,256]{2,1,0:T(8,128)S(1)}, u32[]{:S(2)}, u32[]{:S(2)}) collective-permute-start(f32[9,16,256]{2,1,0:T(8,128)S(1)} %pad_maximum_fusion), channel_id=1, source_target_pairs={{0,1},{1,2},{2,3},{3,0},{4,5},{5,6},{6,7},{7,4},{8,9},{9,10},{10,1... | collective-permute-start | bytes 442376 | tf_op jit(solution)/shard_map/ppermute | solution.py:33
  8.4 11.8 %collective-permute-start.2 = (f32[9,16,256]{2,1,0:T(8,128)S(1)}, f32[9,16,256]{2,1,0:T(8,128)S(1)}, u32[]{:S(2)}, u32[]{:S(2)}) collective-permute-start(f32[9,16,256]{2,1,0:T(8,128)S(1)} %pad_maximum_fusion.1), channel_id=1, source_target_pairs={{0,3},{1,0},{2,1},{3,2},{4,7},{5,4},{6,5},{7,6},{8,11},{9,8},{10,9... | collective-permute-start | bytes 442376 | tf_op jit(solution)/shard_map/ppermute | solution.py:34
  28.6 9.5 %collective-permute-start.3 = (f32[3,8,16,128]{3,2,1,0:T(8,128)}, f32[3,8,16,128]{3,2,1,0:T(8,128)S(1)}, u32[]{:S(2)}, u32[]{:S(2)}) collective-permute-start(f32[3,8,16,128]{3,2,1,0:T(8,128)} %get-tuple-element.80), channel_id=1, source_target_pairs={{0,8},{1,9},{2,10},{3,11},{4,12},{5,13},{6,14},{7,15}} | collective-permute-start | bytes 589832 | tf_op jit(solution)/shard_map/ppermute | solution.py:49
  29.3 8.7 %collective-permute-start.7 = (f32[3,2,16,128]{3,2,1,0:T(8,128)S(1)}, f32[3,2,16,128]{3,2,1,0:T(8,128)S(1)}, u32[]{:S(2)}, u32[]{:S(2)}) collective-permute-start(f32[3,2,16,128]{3,2,1,0:T(8,128)S(1)} %copy-done.53), channel_id=1, source_target_pairs={{0,4},{4,0},{1,5},{5,1},{2,6},{6,2},{3,7},{7,3},{8,12},{12,8},{9,1... | collective-permute-start | bytes 147464 | tf_op jit(solution)/shard_map/ppermute | solution.py:32
  41.8 11.8 %collective-permute-start.10 = (f32[3,8,16,128]{3,2,1,0:T(8,128)}, f32[3,8,16,128]{3,2,1,0:T(8,128)S(1)}, u32[]{:S(2)}, u32[]{:S(2)}) collective-permute-start(f32[3,8,16,128]{3,2,1,0:T(8,128)} %get-tuple-element.90), channel_id=1, source_target_pairs={{8,16},{9,17},{10,18},{11,19},{12,20},{13,21},{14,22},{15,23}} | collective-permute-start | bytes 589832 | tf_op jit(solution)/shard_map/ppermute | solution.py:49
  43.1 10.5 %collective-permute-start.11 = (f32[3,2,16,128]{3,2,1,0:T(8,128)}, f32[3,2,16,128]{3,2,1,0:T(8,128)S(1)}, u32[]{:S(2)}, u32[]{:S(2)}) collective-permute-start(f32[3,2,16,128]{3,2,1,0:T(8,128)} %get-tuple-element.91), channel_id=1, source_target_pairs={{8,20},{9,21},{10,22},{11,23},{12,16},{13,17},{14,18},{15,19}} | collective-permute-start | bytes 147464 | tf_op jit(solution)/shard_map/ppermute | solution.py:49
  44.4 8.0 %collective-permute-start.12 = (f32[3,8,128]{2,1,0:T(8,128)}, f32[3,8,128]{2,1,0:T(8,128)S(1)}, u32[]{:S(2)}, u32[]{:S(2)}) collective-permute-start(f32[3,8,128]{2,1,0:T(8,128)} %get-tuple-element.92), channel_id=1, source_target_pairs={{8,17},{9,18},{10,19},{11,16},{12,21},{13,22},{14,23},{15,20}} | collective-permute-start | bytes 36872 | tf_op jit(solution)/shard_map/ppermute | solution.py:49
  45.7 7.9 %collective-permute-start.13 = (f32[3,8,128]{2,1,0:T(8,128)}, f32[3,8,128]{2,1,0:T(8,128)S(1)}, u32[]{:S(2)}, u32[]{:S(2)}) collective-permute-start(f32[3,8,128]{2,1,0:T(8,128)} %get-tuple-element.93), channel_id=1, source_target_pairs={{8,19},{9,16},{10,17},{11,18},{12,23},{13,20},{14,21},{15,22}} | collective-permute-start | bytes 36872 | tf_op jit(solution)/shard_map/ppermute | solution.py:49
  68.9 8.6 %collective-permute-start.18 = (f32[3,2,16,128]{3,2,1,0:T(8,128)}, f32[3,2,16,128]{3,2,1,0:T(8,128)S(1)}, u32[]{:S(2)}, u32[]{:S(2)}) collective-permute-start(f32[3,2,16,128]{3,2,1,0:T(8,128)} %get-tuple-element.104), channel_id=1, source_target_pairs={{0,4},{4,0},{1,5},{5,1},{2,6},{6,2},{3,7},{7,3},{8,12},{12,8},{9,1... | collective-permute-start | bytes 147464 | tf_op jit(solution)/shard_map/ppermute | solution.py:32
  86.7 7.4 %collective-permute-start.21 = (f32[3,2,32,256]{3,2,1,0:T(8,128)}, f32[3,2,32,256]{3,2,1,0:T(8,128)S(1)}, u32[]{:S(2)}, u32[]{:S(2)}) collective-permute-start(f32[3,2,32,256]{3,2,1,0:T(8,128)} %get-tuple-element.108), channel_id=1, source_target_pairs={{0,4},{4,0},{1,5},{5,1},{2,6},{6,2},{3,7},{7,3},{8,12},{12,8},{9,1... | collective-permute-start | bytes 589832 | tf_op jit(solution)/shard_map/ppermute | solution.py:32
  102.0 25.4 %collective-permute-start.24 = (f32[3,16,32,256]{3,2,1,0:T(8,128)}, f32[3,16,32,256]{3,2,1,0:T(8,128)S(1)}, u32[]{:S(2)}, u32[]{:S(2)}) collective-permute-start(f32[3,16,32,256]{3,2,1,0:T(8,128)} %get-tuple-element.115.u2.refs_14_), channel_id=1, source_target_pairs={{0,8},{1,9},{2,10},{3,11},{4,12},{5,13},{6,14},{7,15},{8,16},{9,17... | collective-permute-start | bytes 4718600 | tf_op jit(solution)/shard_map/ppermute | solution.py:49
  103.9 19.1 %collective-permute-start.28 = (f32[3,2,32,256]{3,2,1,0:T(8,128)}, f32[3,2,32,256]{3,2,1,0:T(8,128)S(1)}, u32[]{:S(2)}, u32[]{:S(2)}) collective-permute-start(f32[3,2,32,256]{3,2,1,0:T(8,128)} %get-tuple-element.116), channel_id=1, source_target_pairs={{0,4},{4,0},{1,5},{5,1},{2,6},{6,2},{3,7},{7,3},{8,12},{12,8},{9,1... | collective-permute-start | bytes 589832 | tf_op jit(solution)/shard_map/ppermute | solution.py:32
  104.8 22.5 %collective-permute-start.25 = (f32[3,2,32,256]{3,2,1,0:T(8,128)}, f32[3,2,32,256]{3,2,1,0:T(8,128)S(1)}, u32[]{:S(2)}, u32[]{:S(2)}) collective-permute-start(f32[3,2,32,256]{3,2,1,0:T(8,128)} %get-tuple-element.116), channel_id=1, source_target_pairs={{0,12},{1,13},{2,14},{3,15},{4,8},{5,9},{6,10},{7,11},{8,20},{9,21... | collective-permute-start | bytes 589832 | tf_op jit(solution)/shard_map/ppermute | solution.py:49
  114.3 8.7 %collective-permute-start.27 = (f32[3,16,256]{2,1,0:T(8,128)}, f32[3,16,256]{2,1,0:T(8,128)S(1)}, u32[]{:S(2)}, u32[]{:S(2)}) collective-permute-start(f32[3,16,256]{2,1,0:T(8,128)} %get-tuple-element.118), channel_id=1, source_target_pairs={{0,11},{1,8},{2,9},{3,10},{4,15},{5,12},{6,13},{7,14},{8,19},{9,16... | collective-permute-start | bytes 147464 | tf_op jit(solution)/shard_map/ppermute | solution.py:49
  138.0 13.9 %collective-permute-start.31 = (f32[3,8,16,128]{3,2,1,0:T(8,128)}, f32[3,8,16,128]{3,2,1,0:T(8,128)S(1)}, u32[]{:S(2)}, u32[]{:S(2)}) collective-permute-start(f32[3,8,16,128]{3,2,1,0:T(8,128)} %get-tuple-element.119), channel_id=1, source_target_pairs={{0,8},{1,9},{2,10},{3,11},{4,12},{5,13},{6,14},{7,15}} | collective-permute-start | bytes 589832 | tf_op jit(solution)/shard_map/ppermute | solution.py:49
  138.7 13.1 %collective-permute-start.35 = (f32[3,2,16,128]{3,2,1,0:T(8,128)S(1)}, f32[3,2,16,128]{3,2,1,0:T(8,128)S(1)}, u32[]{:S(2)}, u32[]{:S(2)}) collective-permute-start(f32[3,2,16,128]{3,2,1,0:T(8,128)S(1)} %copy-done.52), channel_id=1, source_target_pairs={{0,12},{1,13},{2,14},{3,15},{4,8},{5,9},{6,10},{7,11},{8,20},{9,21... | collective-permute-start | bytes 147464 | tf_op jit(solution)/shard_map/ppermute | solution.py:49
  140.6 11.2 %collective-permute-start.32 = (f32[3,2,16,128]{3,2,1,0:T(8,128)}, f32[3,2,16,128]{3,2,1,0:T(8,128)S(1)}, u32[]{:S(2)}, u32[]{:S(2)}) collective-permute-start(f32[3,2,16,128]{3,2,1,0:T(8,128)} %get-tuple-element.120), channel_id=1, source_target_pairs={{0,12},{1,13},{2,14},{3,15},{4,8},{5,9},{6,10},{7,11}} | collective-permute-start | bytes 147464 | tf_op jit(solution)/shard_map/ppermute | solution.py:49
  143.2 7.9 %collective-permute-start.37 = (f32[3,8,128]{2,1,0:T(8,128)S(1)}, f32[3,8,128]{2,1,0:T(8,128)S(1)}, u32[]{:S(2)}, u32[]{:S(2)}) collective-permute-start(f32[3,8,128]{2,1,0:T(8,128)S(1)} %copy-done.54), channel_id=1, source_target_pairs={{0,11},{1,8},{2,9},{3,10},{4,15},{5,12},{6,13},{7,14},{8,19},{9,16... | collective-permute-start | bytes 36872 | tf_op jit(solution)/shard_map/ppermute | solution.py:49
  155.6 14.3 %collective-permute-start.38 = (f32[3,8,16,128]{3,2,1,0:T(8,128)}, f32[3,8,16,128]{3,2,1,0:T(8,128)S(1)}, u32[]{:S(2)}, u32[]{:S(2)}) collective-permute-start(f32[3,8,16,128]{3,2,1,0:T(8,128)} %get-tuple-element.128), channel_id=1, source_target_pairs={{8,16},{9,17},{10,18},{11,19},{12,20},{13,21},{14,22},{15,23}} | collective-permute-start | bytes 589832 | tf_op jit(solution)/shard_map/ppermute | solution.py:49
  156.9 13.0 %collective-permute-start.39 = (f32[3,2,16,128]{3,2,1,0:T(8,128)}, f32[3,2,16,128]{3,2,1,0:T(8,128)S(1)}, u32[]{:S(2)}, u32[]{:S(2)}) collective-permute-start(f32[3,2,16,128]{3,2,1,0:T(8,128)} %get-tuple-element.129), channel_id=1, source_target_pairs={{8,20},{9,21},{10,22},{11,23},{12,16},{13,17},{14,18},{15,19}} | collective-permute-start | bytes 147464 | tf_op jit(solution)/shard_map/ppermute | solution.py:49
  158.2 9.1 %collective-permute-start.40 = (f32[3,8,128]{2,1,0:T(8,128)}, f32[3,8,128]{2,1,0:T(8,128)S(1)}, u32[]{:S(2)}, u32[]{:S(2)}) collective-permute-start(f32[3,8,128]{2,1,0:T(8,128)} %get-tuple-element.130), channel_id=1, source_target_pairs={{8,17},{9,18},{10,19},{11,16},{12,21},{13,22},{14,23},{15,20}} | collective-permute-start | bytes 36872 | tf_op jit(solution)/shard_map/ppermute | solution.py:49
  159.5 9.6 %collective-permute-start.41 = (f32[3,8,128]{2,1,0:T(8,128)}, f32[3,8,128]{2,1,0:T(8,128)S(1)}, u32[]{:S(2)}, u32[]{:S(2)}) collective-permute-start(f32[3,8,128]{2,1,0:T(8,128)} %get-tuple-element.131), channel_id=1, source_target_pairs={{8,19},{9,16},{10,17},{11,18},{12,23},{13,20},{14,21},{15,22}} | collective-permute-start | bytes 36872 | tf_op jit(solution)/shard_map/ppermute | solution.py:49
  185.2 9.5 %collective-permute-start.46 = (f32[3,2,16,128]{3,2,1,0:T(8,128)}, f32[3,2,16,128]{3,2,1,0:T(8,128)S(1)}, u32[]{:S(2)}, u32[]{:S(2)}) collective-permute-start(f32[3,2,16,128]{3,2,1,0:T(8,128)} %get-tuple-element.142), channel_id=1, source_target_pairs={{0,4},{4,0},{1,5},{5,1},{2,6},{6,2},{3,7},{7,3},{8,12},{12,8},{9,1... | collective-permute-start | bytes 147464 | tf_op jit(solution)/shard_map/ppermute | solution.py:32
  (86 other events, 352.3 us)

commit v2 on v1

--- a/solution.py
+++ b/solution.py
@@ -9,7 +9,7 @@
 VISCOSITY = 0.25
 TIME_STEP = 0.5
 PAD = 8
-CHUNK = 16
+CHUNK = 8
 F32 = jnp.float32
 BF16 = jnp.bfloat16
 
@@ -68,7 +68,18 @@
     return result
 
 
-def fill(ext, parts, spread=()):
+def each(count, unrolled=False):
+    def wrap(body):
+        if unrolled:
+            for i in range(count):
+                body(i)
+        else:
+            pl.loop(0, count)(body)
+
+    return wrap
+
+
+def fill(ext, parts, spread=(), unrolled=False):
     width, length = ext.shape[1] - 2, ext.shape[2] - 2 * PAD
     inner = slice(PAD, PAD + length)
     for c in range(3):
@@ -77,7 +88,7 @@
             terms += [w * p[c, k * (width // 2 + 1)] for w, p, _ in spread]
             ext[c, at, inner] = total(terms)
 
-    @pl.loop(0, width // 2)
+    @each(width // 2, unrolled)
     def _(i):
         for q in range(2):
             x = 2 * i + q
@@ -105,35 +116,33 @@
     )
 
 
-def slopes(half, x, r, n):
-    rows = []
-    for a in range(3):
-        _, ahead, behind = sides(half, a, x, r, n)
-        rows.append([ahead[b] - behind[b] for b in range(3)])
-    return rows
-
-
-def rates(ext, x, r, n, speeds, grads, strength):
-    fields = [sides(ext, a, x, r, n) for a in range(3)]
+def rates(ext, x, r, n, speeds, grads_of, strength):
+    here = [ext[b, x, r : r + n] for b in range(3)]
     toward = [strength - speed for speed in speeds]
     away = [strength + speed for speed in speeds]
     outputs = []
     for a in range(3):
-        here, ahead, behind = fields[a]
-        result = here * (grads[a][a] - 6.0 * strength)
+        _, ahead, behind = sides(ext, a, x, r, n)
+        grads = grads_of(a)
+        result = here[a] * (grads[a] - 6.0 * strength)
         for b in range(3):
             if b != a:
-                result = result + fields[b][0] * grads[a][b]
-        for b in range(3):
+                result = result + here[b] * grads[b]
             result = result + toward[b] * ahead[b] + away[b] * behind[b]
         outputs.append(result)
     return outputs
 
 
 def fine_rates(ext, half, x, r, n):
-    grads = slopes(half, x, r, n)
+    rows = []
+
+    def grads_of(a):
+        _, ahead, behind = sides(half, a, x, r, n)
+        rows.append([ahead[b] - behind[b] for b in range(3)])
+        return rows[a]
+
     speeds = [half[b, x, r : r + n] for b in range(3)]
-    return rates(ext, x, r, n, speeds, grads, VISCOSITY), grads
+    return rates(ext, x, r, n, speeds, grads_of, VISCOSITY), rows
 
 
 def split(value):
@@ -187,30 +196,69 @@
             edge[k, c] = value[at : at + cx]
 
 
-def emit_faces(main, outs):
+def emit_faces(main, outs, off=0):
     x_faces, y_last, y_first = outs
     width, length = main.shape[1:3]
     for c in range(3):
-        x_faces[c, 0] = main[c, width - 1]
-        x_faces[c, 1] = main[c, 0]
+        x_faces[off + c, 0] = main[c, width - 1]
+        x_faces[off + c, 1] = main[c, 0]
         for x in range(width):
-            y_last[c, x : x + 1] = main[c, x, length - 1 : length]
-            y_first[c, x : x + 1] = main[c, x, 0:1]
-
-
-def coarsen_kernel(first, v, s, g, speed, zero, end, end_x, end_l, end_f, summed, rows):
+            y_last[off + c, x : x + 1] = main[c, x, length - 1 : length]
+            y_first[off + c, x : x + 1] = main[c, x, 0:1]
+
+
+def quadrant(c, rows, columns):
+    up, along = c // 2, c % 2
+    return slice(up * rows, (up + 1) * rows), slice(along * columns, (along + 1) * columns)
+
+
+def emit_coarse_faces(main, outs, comp):
+    x_faces, y_last, y_first = outs
+    cx, cy, cz = main.shape[1:]
+    for c in range(3):
+        x_faces[(comp, 0) + quadrant(c, cy, cz)] = main[c, cx - 1]
+        x_faces[(comp, 1) + quadrant(c, cy, cz)] = main[c, 0]
+        rows, columns = quadrant(c, cx, cz)
+        for i in range(cx):
+            at = slice(rows.start + i, rows.start + i + 1)
+            y_last[comp, at, columns] = main[c, i, cy - 1 : cy]
+            y_first[comp, at, columns] = main[c, i, 0:1]
+
+
+def take_coarse_faces(x_faces, behind, ahead, comp, outs):
+    out_x, out_b, out_a = outs
+    cy, cz = out_x.shape[2:]
+    cx = out_b.shape[1]
+    for c in range(3):
+        for k in range(2):
+            out_x[c, k] = x_faces[(comp, k) + quadrant(c, cy, cz)]
+        out_b[c] = behind[(comp,) + quadrant(c, cx, cz)]
+        out_a[c] = ahead[(comp,) + quadrant(c, cx, cz)]
+
+
+def coarsen(field, summed, rows, store):
+    @pl.loop(0, field.shape[1] // 2)
+    def _(i):
+        for c in range(3):
+            summed[c, i] = field[c, 2 * i] + field[c, 2 * i + 1]
+
+    squeeze(summed, rows, store, 3)
+
+
+def pack_kernel(first, v, s, g, end, x_faces, y_last, y_first, summed, rows):
+    outs = (x_faces, y_last, y_first)
+    for k, field in enumerate((v, g, s)):
+        emit_faces(field, outs, 3 * k)
+
+    def store(c, value):
+        end[c] = value
+
+    coarsen(g, summed, rows, store)
+    emit_coarse_faces(end, outs, 9)
+
+
+def coarsen_kernel(first, v, s, end, speed, zero, summed, rows):
     f = first[0]
-
-    def run(field, store):
-        @pl.loop(0, field.shape[1] // 2)
-        def _(i):
-            for c in range(3):
-                summed[c, i] = field[c, 2 * i] + field[c, 2 * i + 1]
-
-        squeeze(summed, rows, store, 3)
-
-    def store_end(c, value):
-        end[c] = value
 
     def store_zero(c, value):
         zero[c] = f * value + (1.0 - f) * end[c]
@@ -218,10 +266,8 @@
     def store_speed(c, value):
         speed[c] = value * 0.25
 
-    run(g, store_end)
-    emit_faces(end, (end_x, end_l, end_f))
-    run(s, store_zero)
-    run(v, store_speed)
+    coarsen(s, summed, rows, store_zero)
+    coarsen(v, summed, rows, store_speed)
 
 
 def integral_loop(ext, half, summed, grads_summed):
@@ -242,7 +288,7 @@
 
 def offset_start_kernel(
     first, v, s, g, x_faces, behind, ahead, zero,
-    integral, coarse_grads, end, end_x, end_l, end_f,
+    integral, coarse_grads, zero_x, zero_b, zero_a, end, end_x, end_l, end_f,
     ext, half, summed, grads_summed, rows,
 ):
     f = first[0]
@@ -259,6 +305,7 @@
 
     squeeze(summed, rows, store, 3)
     emit_faces(end, (end_x, end_l, end_f))
+    take_coarse_faces(x_faces, behind, ahead, 9, (zero_x, zero_b, zero_a))
 
     def store_grads(c, value):
         coarse_grads[c] = value
@@ -269,7 +316,7 @@
 def offset_later_kernel(
     first, v, s, x_faces, behind, ahead,
     u0, u0_x, u0_b, u0_a, u1, u1_x, u1_b, u1_a, u2, u2_x, u2_b, u2_a,
-    integral, zero, end, end_x, end_l, end_f,
+    integral, zero, zero_x, zero_b, zero_a, end, end_x, end_l, end_f,
     ext, half, summed, rows,
 ):
     f = first[0]
@@ -302,46 +349,50 @@
 
     squeeze(summed, rows, store, 3)
     emit_faces(end, (end_x, end_l, end_f))
-
-
-def chain_kernel(last, arrivals, *refs):
-    refs = list(refs)
-
-    def take(count):
-        taken = refs[:count]
-        del refs[:count]
-        return taken
-
-    first, = take(1)
-    arrived = [take(4) for _ in range(arrivals)]
-    zero, zero_x, zero_b, zero_a, integral, speed, coarse_grads = take(7)
-    f = first[0]
-    if last:
-        end_two, = take(1)
-        d0, d0_x, d0_b, d0_a, d2, d2_x, d2_l, d2_f = take(8)
-    else:
-        end, end_x, end_l, end_f = take(4)
-        d0, d0_x, d0_b, d0_a = take(4)
-    ext, = take(1)
-    rest = 1.0 - f
-    width, length = zero.shape[1:3]
-    for out, old, k in ((d0, zero, 0), (d0_x, zero_x, 1), (d0_b, zero_b, 2), (d0_a, zero_a, 3)):
-        out[...] = rest * (total([a[k][...] for a in arrived]) - old[...])
-    fill(ext, [(TIME_STEP, Node(d0, d0_x, d0_b, d0_a))])
-
-    @pl.loop(0, width)
-    def _(x):
+    take_coarse_faces(u0_x, u0_b, u0_a, 3, (zero_x, zero_b, zero_a))
+
+
+def chain_step(rest, arrived, zero, integral, speed, coarse_grads, d0, ext, store):
+    for k in range(4):
+        d0[k][...] = rest * (total([group[k][...] for group in arrived]) - zero[k][...])
+    fill(ext, [(TIME_STEP, Node(*d0))], unrolled=True)
+    width, length = zero[0].shape[1:3]
+    for x in range(width):
         speeds = [speed[b, x] for b in range(3)]
-        grads = [[coarse_grads[3 * a + b, x] for b in range(3)] for a in range(3)]
-        changes = rates(ext, x + 1, PAD, length, speeds, grads, VISCOSITY / 4.0)
+
+        def grads_of(a):
+            return [coarse_grads[3 * a + b, x] for b in range(3)]
+
+        changes = rates(ext, x + 1, PAD, length, speeds, grads_of, VISCOSITY / 4.0)
         for a in range(3):
-            value = zero[a, x] + d0[a, x] + integral[a, x] + changes[a]
-            if last:
-                d2[a, x] = value - end_two[a, x]
-            else:
-                end[a, x] = value
-
-    emit_faces(d2 if last else end, (d2_x, d2_l, d2_f) if last else (end_x, end_l, end_f))
+            store(a, x, zero[0][a, x] + d0[0][a, x] + integral[a, x] + changes[a])
+
+
+def pass_kernel(turn, first, *refs):
+    arrived, zero = refs[:4], refs[4:8]
+    integral, speed, coarse_grads, end, end_x, end_l, end_f = refs[8:15]
+    d0, ext = refs[15:19], refs[19]
+
+    @pl.when(first[1] == float(turn))
+    def _():
+        def store(a, x, value):
+            end[a, x] = value
+
+        chain_step(1.0, [arrived], zero, integral, speed, coarse_grads, d0, ext, store)
+        emit_faces(end, (end_x, end_l, end_f))
+
+
+def settle_kernel(count, first, *refs):
+    arrived = [refs[4 * k : 4 * k + 4] for k in range(count)]
+    refs = refs[4 * count :]
+    zero, (integral, speed, coarse_grads, end_two) = refs[:4], refs[4:8]
+    d0, (d2, d2_x, d2_l, d2_f, ext) = refs[8:12], refs[12:17]
+
+    def store(a, x, value):
+        d2[a, x] = value - end_two[a, x]
+
+    chain_step(1.0 - first[0], arrived, zero, integral, speed, coarse_grads, d0, ext, store)
+    emit_faces(d2, (d2_x, d2_l, d2_f))
 
 
 def middle_kernel(nodes, *refs):
@@ -411,7 +462,7 @@
     if last:
         a2, ext, half = refs
     else:
-        a2, a2_x, a2_l, a2_f, end, end_x, end_l, end_f, ext, half, summed, rows = refs
+        a2, a2_x, a2_l, a2_f, end, ext, half, summed, rows = refs
     fill(half, [(0.5, Node(v, vx, vb, va))])
     fill(
         ext,
@@ -444,7 +495,7 @@
             end[c] = value
 
         squeeze(summed, rows, store, 3)
-        emit_faces(end, (end_x, end_l, end_f))
+        emit_coarse_faces(end, (a2_x, a2_l, a2_f), 3)
 
 
 def call(kernel, name, first, args, outs, scratch, flops=0):
@@ -466,52 +517,51 @@
     _, nx, ny, nz = own.shape
     cx, cy, cz = nx // 2, ny // 2, nz // 2
     slabs = lax.axis_size("tm")
-    first = (lax.axis_index("tm") == 0).astype(F32).reshape(1)
-
-    fine, fine_faces = (3, nx, ny, nz), [(3, 2, ny, nz), (3, nx, nz), (3, nx, nz)]
-    coarse, coarse_faces = (3, cx, cy, cz), [(3, 2, cy, cz), (3, cx, cz), (3, cx, cz)]
+    number = lax.axis_index("tm")
+    first = jnp.stack([number == 0, number]).astype(F32)
+
+    def layers_of(count):
+        return [(count, 2, ny, nz), (count, nx, nz), (count, nx, nz)]
+
+    fine, coarse = (3, nx, ny, nz), (3, cx, cy, cz)
+    fine_faces, coarse_faces = layers_of(3), [(3, 2, cy, cz), (3, cx, cz), (3, cx, cz)]
     ext = (3, nx + 2, ny + 2 * PAD, nz)
     coarse_ext = (3, cx + 2, cy + 2 * PAD, cz)
     summed, rows = (3, cx, ny, nz), (cx * ny, cz)
     wide, edge, wide_rows = (3, cx + 2, ny, nz), (2, 3, cx, nz), ((cx + 2) * ny, cz)
 
-    fields = [velocity, own, start_field]
-    packed = (
-        jnp.concatenate([jnp.concatenate([f[:, nx - 1 :], f[:, :1]], axis=1) for f in fields], axis=0),
-        jnp.concatenate([f[:, :, ny - 1] for f in fields], axis=0),
-        jnp.concatenate([f[:, :, 0] for f in fields], axis=0),
+    end_two, *packed = call(
+        pack_kernel, "pack", first, [velocity, start_field, own],
+        [coarse] + layers_of(10), [summed, rows], 5_000_000,
     )
     layers = swap_faces(packed)
-    speed, zero, end_two, *sent = call(
-        coarsen_kernel, "coarsen", first, [velocity, start_field, own],
-        [coarse, coarse, coarse] + coarse_faces, [summed, rows], 10_000_000,
-    )
-    zero_faces = swap_faces(sent)
-    integral, coarse_grads, end, *sent = call(
+    speed, zero = call(
+        coarsen_kernel, "coarsen", first, [velocity, start_field, end_two],
+        [coarse, coarse], [summed, rows], 10_000_000,
+    )
+    integral, coarse_grads, *results = call(
         offset_start_kernel, "offset_start", first, [velocity, start_field, own, *layers, zero],
-        [coarse, (9, cx, cy, cz), coarse] + coarse_faces,
+        [coarse, (9, cx, cy, cz)] + coarse_faces + [coarse] + coarse_faces,
         [ext, ext, summed, (9, cx, ny, nz), rows], 40_000_000,
     )
+    zero_faces, end, sent = results[:3], results[3], results[4:]
     for sweep_index in range(ITERS):
         final = sweep_index + 1 == ITERS
         arrivals = []
-        for slab in range(slabs - 1):
-            arrivals.append(hand_on([slab], end, sent))
-            last = slab + 2 == slabs
-            args = [a for group in arrivals for a in group]
-            args += [zero, *zero_faces, integral, speed, coarse_grads]
-            if last:
-                outs = [coarse] + coarse_faces + [coarse] + coarse_faces
-                args.append(end_two)
-            else:
-                outs = [coarse] + coarse_faces + [coarse] + coarse_faces
-            count = len(arrivals)
-            results = call(
-                lambda *refs, last=last, count=count: chain_kernel(last, count, *refs),
-                "chain", first, args, outs, [coarse_ext], 2_000_000,
-            )
-            if not last:
-                end, *sent = results[:4]
+        for turn in range(1, slabs):
+            arrivals.append(hand_on([turn - 1], end, sent))
+            if turn + 1 < slabs:
+                end, *sent = call(
+                    lambda *refs, turn=turn: pass_kernel(turn, *refs), "chain", first,
+                    [*arrivals[-1], zero, *zero_faces, integral, speed, coarse_grads],
+                    [coarse] + coarse_faces, [coarse, *coarse_faces, coarse_ext], 2_000_000,
+                )
+        results = call(
+            lambda *refs, count=len(arrivals): settle_kernel(count, *refs), "settle", first,
+            [a for group in arrivals for a in group]
+            + [zero, *zero_faces, integral, speed, coarse_grads, end_two],
+            [coarse] + coarse_faces + [coarse] + coarse_faces, [coarse_ext], 2_000_000,
+        )
         d0, d2 = list(results[:4]), [results[4], *swap_faces(results[5:])]
 
         if sweep_index == 0:
@@ -538,21 +588,22 @@
         results = call(
             lambda *refs, final=final: finish_kernel(final, *refs),
             "finish", first, [velocity, *layers, *u1, *rest],
-            [fine] if final else [fine] + fine_faces + [coarse] + coarse_faces,
+            [fine] if final else [fine] + layers_of(4) + [coarse],
             [ext, ext] if final else [ext, ext, summed, rows], 40_000_000,
         )
         if final:
             return results[0][None]
         value, *faces = results[:4]
+        end_two = results[4]
         u0 = hand_on(range(slabs - 1), value, faces)
         u2 = [value, *swap_faces(faces)]
-        zero_faces = hand_on(range(slabs - 1), None, results[5:])
-        end_two = results[4]
-        integral, zero, end, *sent = call(
+        integral, zero, *results = call(
             offset_later_kernel, "offset_later", first,
             [velocity, start_field, *layers, *u0, *u1, *u2],
-            [coarse, coarse, coarse] + coarse_faces, [ext, ext, summed, rows], 40_000_000,
+            [coarse, coarse] + coarse_faces + [coarse] + coarse_faces,
+            [ext, ext, summed, rows], 40_000_000,
         )
+        zero_faces, end, sent = results[:3], results[3], results[4:]
 
 
 def solution(mesh):

time: 222 us -> 204 us (0.919)
  starting transfers between devices: 61.7 us -> 51.7 us
  local copies, waits for them, and re-layouts: 17.3 us -> 11.3 us
    ppermute x31 -> x28, starting transfers between devices: 39.5 us -> 33.6 us  [permute(): return lax.ppermute(array, ('tm', 'gx', 'gy'), pairs)]
    slice x9 -> x0, local copies, waits for them, and re-layouts: 4.96 us -> none  [the longest x5 2.38 us: shards(): f[:, nx - 1:]]
    ppermute x31 -> x28, waiting for transfers between devices: 37.1 us -> 32.7 us  [permute(): return lax.ppermute(array, ('tm', 'gx', 'gy'), pairs)]
    ppermute x7 -> x6, waiting for transfers between devices: 12.1 us -> 14.8 us  [swap_faces(): behind = lax.ppermute(y_last, 'gy', ring(gy, 1))]
    ppermute x7 -> x6, starting transfers between devices: 8.62 us -> 6.01 us  [swap_faces(): lax.ppermute(a, 'gx', ring(gx, by))]
    ppermute x7 -> x6, starting transfers between devices: 7.89 us -> 5.83 us  [swap_faces(): ahead = lax.ppermute(y_first, 'gy', ring(gy, -1))]
    ppermute x7 -> x6, waiting for transfers between devices: 4.32 us -> 5.79 us  [swap_faces(): lax.ppermute(a, 'gx', ring(gx, by))]
    pallas_call x13 -> x14, Pallas kernels: 73.3 us -> 72.3 us  [call(): pl.pallas_call(kernel, name=name, out_shape=[jax.ShapeDtypeStruct(dims, F...]
  transfers between devices with their start and end apart: 52 -> 46, of which waited for: 27 -> 23; matrix products, arithmetic and copies ran while one was open for 2% -> 0% of each run, Pallas kernels for 2% -> 2%
where the time goes in v2:
time: 204 us; the launch traced here: 203 us
  Pallas kernels  72.3 us (35%)
  waiting for transfers between devices  67 us (33%)
  starting transfers between devices  51.7 us (25%)
  local copies, waits for them, and re-layouts  11.3 us (6%)
    pallas_call x14, Pallas kernels, call(): pl.pallas_call(kernel, name=name, out_shape=[jax.ShapeDtypeStruct(dims, F...  72.3 us
    ppermute x28, starting transfers between devices, permute(): return lax.ppermute(array, ('tm', 'gx', 'gy'), pairs)  33.6 us
    ppermute x28, waiting for transfers between devices, permute(): return lax.ppermute(array, ('tm', 'gx', 'gy'), pairs)  32.7 us
    ppermute x6, waiting for transfers between devices, swap_faces(): behind = lax.ppermute(y_last, 'gy', ring(gy, 1))  14.8 us
    ppermute x6, waiting for transfers between devices, swap_faces(): ahead = lax.ppermute(y_first, 'gy', ring(gy, -1))  13.7 us
    unnamed x92, local copies, waits for them, and re-layouts  11.3 us
    ppermute x6, starting transfers between devices, swap_faces(): behind = lax.ppermute(y_last, 'gy', ring(gy, 1))  6.31 us
    ppermute x6, starting transfers between devices, swap_faces(): lax.ppermute(a, 'gx', ring(gx, by))  6.01 us
  transfers between devices with their start and end apart: 46, of which 23 were waited for; matrix products, arithmetic and copies ran while one was open for 0% of the time, Pallas kernels for 2%

profile of v2, /device:TPU:26, one launch (start us, length us, event | category | flops | bytes accessed | tf_op | source)
XLA Modules:
  0.0 203.4 jit_solution(6189857843730341679)
XLA Ops:
  0.6 4.1 %pack.1 = (f32[3,8,16,128]{3,2,1,0:T(8,128)}, f32[10,2,32,256]{3,2,1,0:T(8,128)}, f32[10,16,256]{2,1,0:T(8,128)}, f32[10,16,256]{2,1,0:T(8,128)}) custom-call(f32[2]{0:T(128)} %add_convert_fusion.first.refs_0_, f32[3,16,32,256]{3,2,1,0:T(8,128)} %refs_1_.7, f32[3,16,32,256]{3,2,1,0:T(8,128)} %refs_5_.3, f32[3,16,32,256]{3,2,1,0:T(8,128)} %bitcast.4), custom_call_target="tpu_custom_call" | custom-call | flops 5000000 | bytes 4718592 | tf_op jit(solution)/shard_map/pack/pallas_call | solution.py:503
  8.3 3.7 %coarsen.1 = (f32[3,8,16,128]{3,2,1,0:T(8,128)}, f32[3,8,16,128]{3,2,1,0:T(8,128)}) custom-call(f32[2]{0:T(128)} %add_convert_fusion.first.refs_0_, f32[3,16,32,256]{3,2,1,0:T(8,128)} %refs_1_.7, f32[3,16,32,256]{3,2,1,0:T(8,128)} %refs_5_.3, f32[3,8,16,128]{3,2,1,0:T(8,128)} %get-tuple-element.85.end.refs_20_), custom_call_target="tpu_custom_call" | custom-call | flops 10000000 | bytes 3342336 | tf_op jit(solution)/shard_map/coarsen/pallas_call | solution.py:503
  11.9 3.7 %collective-permute-done.1.behind.refs_3_ = f32[10,16,256]{2,1,0:T(8,128)S(1)} collective-permute-done((f32[10,16,256]{2,1,0:T(8,128)}, f32[10,16,256]{2,1,0:T(8,128)S(1)}, u32[]{:S(2)}, u32[]{:S(2)}) %collective-permute-start.1) | collective-permute-done | bytes 163872 | tf_op jit(solution)/shard_map/ppermute | solution.py:33
  15.6 5.8 %collective-permute-done.x_faces.refs_2_ = f32[10,2,32,256]{3,2,1,0:T(8,128)S(1)} collective-permute-done((f32[10,2,32,256]{3,2,1,0:T(8,128)}, f32[10,2,32,256]{3,2,1,0:T(8,128)S(1)}, u32[]{:S(2)}, u32[]{:S(2)}) %collective-permute-start) | collective-permute-done | bytes 655392 | tf_op jit(solution)/shard_map/ppermute | solution.py:32
  22.3 7.7 %offset_start.1 = (f32[3,8,16,128]{3,2,1,0:T(8,128)}, f32[9,8,16,128]{3,2,1,0:T(8,128)}, f32[3,2,16,128]{3,2,1,0:T(8,128)}, f32[3,8,128]{2,1,0:T(8,128)}, f32[3,...) custom-call(f32[2]{0:T(128)} %add_convert_fusion.first.refs_0_, ...), custom_call_target="tpu_custom_call" | custom-call | flops 40000000 | bytes 5898240 | tf_op jit(solution)/shard_map/offset_start/pallas_call | solution.py:503
  40.9 7.1 %collective-permute-done.9.refs_3_.refs_7_ = f32[3,8,128]{2,1,0:T(8,128)S(1)} collective-permute-done((f32[3,8,128]{2,1,0:T(8,128)}, f32[3,8,128]{2,1,0:T(8,128)S(1)}, u32[]{:S(2)}, u32[]{:S(2)}) %collective-permute-start.9) | collective-permute-done | bytes 12320 | tf_op jit(solution)/shard_map/ppermute | solution.py:49
  51.0 2.5 %chain.5 = (f32[3,8,16,128]{3,2,1,0:T(8,128)}, f32[3,2,16,128]{3,2,1,0:T(8,128)}, f32[3,8,128]{2,1,0:T(8,128)}, f32[3,8,128]{2,1,0:T(8,128)}) custom-call(f32[2]{0:T(128)} %add_convert_fusion.first.refs_0_, f32[3,8,16,128]{3,2,1,0:T(8,128)} %copy-done.10, f32[3,2,16,128]{3,2,1,0:T(8,128)} %copy-done.22, f32[3,8,128]{2,1,0:T(8,128)} %copy-done.33, ...), custom_call_target="tpu_custom_call" | custom-call | flops 2000000 | bytes 1523712 | tf_op jit(solution)/shard_map/chain/pallas_call | solution.py:503
  61.5 2.7 %settle.2 = (f32[3,8,16,128]{3,2,1,0:T(8,128)}, f32[3,2,16,128]{3,2,1,0:T(8,128)}, f32[3,8,128]{2,1,0:T(8,128)}, f32[3,8,128]{2,1,0:T(8,128)}, f32[3,8,16,128]{3...) custom-call(f32[2]{0:T(128)} %add_convert_fusion.first.refs_0_, ...), custom_call_target="tpu_custom_call" | custom-call | flops 2000000 | bytes 2260992 | tf_op jit(solution)/shard_map/settle/pallas_call | solution.py:503
  65.3 2.9 %collective-permute-start.16 = (f32[3,8,128]{2,1,0:T(8,128)}, f32[3,8,128]{2,1,0:T(8,128)S(1)}, u32[]{:S(2)}, u32[]{:S(2)}) collective-permute-start(f32[3,8,128]{2,1,0:T(8,128)} %get-tuple-element.111), channel_id=1, source_target_pairs={{0,1},{1,2},{2,3},{3,0},{4,5},{5,6},{6,7},{7,4},{8,9},{9,10},{10,1... | collective-permute-start | bytes 36872 | tf_op jit(solution)/shard_map/ppermute | solution.py:33
  69.8 4.1 %collective-permute-done.17.refs_14_ = f32[3,8,128]{2,1,0:T(8,128)S(1)} collective-permute-done((f32[3,8,128]{2,1,0:T(8,128)}, f32[3,8,128]{2,1,0:T(8,128)S(1)}, u32[]{:S(2)}, u32[]{:S(2)}) %collective-permute-start.17) | collective-permute-done | bytes 12320 | tf_op jit(solution)/shard_map/ppermute | solution.py:34
  74.5 8.6 %middle.2 = (f32[3,16,32,256]{3,2,1,0:T(8,128)}, f32[3,2,32,256]{3,2,1,0:T(8,128)}, f32[3,16,256]{2,1,0:T(8,128)}, f32[3,16,256]{2,1,0:T(8,128)}, f32[3,16,32,25...) custom-call(f32[2]{0:T(128)} %add_convert_fusion.first.refs_0_, ...), custom_call_target="tpu_custom_call" | custom-call | flops 60000000 | bytes 6242304 | tf_op jit(solution)/shard_map/middle/pallas_call | solution.py:503
  90.5 7.1 %finish.2 = (f32[3,16,32,256]{3,2,1,0:T(8,128)}, f32[4,2,32,256]{3,2,1,0:T(8,128)}, f32[4,16,256]{2,1,0:T(8,128)}, f32[4,16,256]{2,1,0:T(8,128)}, f32[3,8,16,128]{3,2,1,0:T(8,128)}) custom-call(f32[2]{0:T(128)} %add_convert_fusion.first.refs_0_, f32[3,16,32,256]{3,2,1,0:T(8,128)} %refs_1_.7, f32[10,2,32,256]{3,2,1,0:T(8,128)} %copy-done, ...), custom_call_target="tpu_custom_call" | custom-call | flops 40000000 | bytes 6291456 | tf_op jit(solution)/shard_map/finish/pallas_call | solution.py:503
  105.0 3.0 %collective-permute-done.26.u2_b.refs_16_ = f32[4,16,256]{2,1,0:T(8,128)S(1)} collective-permute-done((f32[4,16,256]{2,1,0:T(8,128)}, f32[4,16,256]{2,1,0:T(8,128)S(1)}, u32[]{:S(2)}, u32[]{:S(2)}) %collective-permute-start.26) | collective-permute-done | bytes 65568 | tf_op jit(solution)/shard_map/ppermute | solution.py:33
  114.3 4.7 %collective-permute-done.24.u0_a.refs_9_ = f32[4,16,256]{2,1,0:T(8,128)S(1)} collective-permute-done((f32[4,16,256]{2,1,0:T(8,128)}, f32[4,16,256]{2,1,0:T(8,128)S(1)}, u32[]{:S(2)}, u32[]{:S(2)}) %collective-permute-start.24) | collective-permute-done | bytes 65568 | tf_op jit(solution)/shard_map/ppermute | solution.py:49
  119.0 5.7 %collective-permute-done.22.u0_x.refs_7_ = f32[4,2,32,256]{3,2,1,0:T(8,128)S(1)} collective-permute-done((f32[4,2,32,256]{3,2,1,0:T(8,128)}, f32[4,2,32,256]{3,2,1,0:T(8,128)S(1)}, u32[]{:S(2)}, u32[]{:S(2)}) %collective-permute-start.22) | collective-permute-done | bytes 262176 | tf_op jit(solution)/shard_map/ppermute | solution.py:49
  126.6 8.8 %offset_later.1 = (f32[3,8,16,128]{3,2,1,0:T(8,128)}, f32[3,8,16,128]{3,2,1,0:T(8,128)}, f32[3,2,16,128]{3,2,1,0:T(8,128)}, f32[3,8,128]{2,1,0:T(8,128)}, f32[3,...) custom-call(f32[2]{0:T(128)} %add_convert_fusion.first.refs_0_, ...), custom_call_target="tpu_custom_call" | custom-call | flops 40000000 | bytes 9928704 | tf_op jit(solution)/shard_map/offset_later/pallas_call | solution.py:503
  146.2 6.4 %collective-permute-done.34.refs_3_.refs_7_ = f32[3,8,128]{2,1,0:T(8,128)S(1)} collective-permute-done((f32[3,8,128]{2,1,0:T(8,128)}, f32[3,8,128]{2,1,0:T(8,128)S(1)}, u32[]{:S(2)}, u32[]{:S(2)}) %collective-permute-start.34) | collective-permute-done | bytes 12320 | tf_op jit(solution)/shard_map/ppermute | solution.py:49
  155.7 2.5 %chain.7 = (f32[3,8,16,128]{3,2,1,0:T(8,128)}, f32[3,2,16,128]{3,2,1,0:T(8,128)}, f32[3,8,128]{2,1,0:T(8,128)}, f32[3,8,128]{2,1,0:T(8,128)}) custom-call(f32[2]{0:T(128)} %add_convert_fusion.first.refs_0_, f32[3,8,16,128]{3,2,1,0:T(8,128)} %copy-done.9, f32[3,2,16,128]{3,2,1,0:T(8,128)} %copy-done.21, f32[3,8,128]{2,1,0:T(8,128)} %copy-done.32, ...), custom_call_target="tpu_custom_call" | custom-call | flops 2000000 | bytes 1523712 | tf_op jit(solution)/shard_map/chain/pallas_call | solution.py:503
  165.6 2.7 %settle.3 = (f32[3,8,16,128]{3,2,1,0:T(8,128)}, f32[3,2,16,128]{3,2,1,0:T(8,128)}, f32[3,8,128]{2,1,0:T(8,128)}, f32[3,8,128]{2,1,0:T(8,128)}, f32[3,8,16,128]{3...) custom-call(f32[2]{0:T(128)} %add_convert_fusion.first.refs_0_, ...), custom_call_target="tpu_custom_call" | custom-call | flops 2000000 | bytes 2260992 | tf_op jit(solution)/shard_map/settle/pallas_call | solution.py:503
  169.1 3.1 %collective-permute-start.41 = (f32[3,8,128]{2,1,0:T(8,128)}, f32[3,8,128]{2,1,0:T(8,128)S(1)}, u32[]{:S(2)}, u32[]{:S(2)}) collective-permute-start(f32[3,8,128]{2,1,0:T(8,128)} %get-tuple-element.149), channel_id=1, source_target_pairs={{0,1},{1,2},{2,3},{3,0},{4,5},{5,6},{6,7},{7,4},{8,9},{9,10},{10,1... | collective-permute-start | bytes 36872 | tf_op jit(solution)/shard_map/ppermute | solution.py:33
  173.9 4.1 %collective-permute-done.42.refs_25_ = f32[3,8,128]{2,1,0:T(8,128)S(1)} collective-permute-done((f32[3,8,128]{2,1,0:T(8,128)}, f32[3,8,128]{2,1,0:T(8,128)S(1)}, u32[]{:S(2)}, u32[]{:S(2)}) %collective-permute-start.42) | collective-permute-done | bytes 12320 | tf_op jit(solution)/shard_map/ppermute | solution.py:34
  178.6 10.6 %middle.3 = (f32[3,16,32,256]{3,2,1,0:T(8,128)}, f32[3,2,32,256]{3,2,1,0:T(8,128)}, f32[3,16,256]{2,1,0:T(8,128)}, f32[3,16,256]{2,1,0:T(8,128)}, f32[3,16,32,25...) custom-call(f32[2]{0:T(128)} %add_convert_fusion.first.refs_0_, ...), custom_call_target="tpu_custom_call" | custom-call | flops 60000000 | bytes 10469376 | tf_op jit(solution)/shard_map/middle/pallas_call | solution.py:503
  191.8 2.4 %collective-permute-done.44.refs_7_ = f32[3,16,256]{2,1,0:T(8,128)S(1)} collective-permute-done((f32[3,16,256]{2,1,0:T(8,128)}, f32[3,16,256]{2,1,0:T(8,128)S(1)}, u32[]{:S(2)}, u32[]{:S(2)}) %collective-permute-start.44) | collective-permute-done | bytes 49184 | tf_op jit(solution)/shard_map/ppermute | solution.py:33
  196.6 6.8 %finish.3 = f32[3,16,32,256]{3,2,1,0:T(8,128)} custom-call(f32[2]{0:T(128)} %add_convert_fusion.first.refs_0_, f32[3,16,32,256]{3,2,1,0:T(8,128)} %refs_1_.7, f32[10,2,32,256]{3,2,1,0:T(8,128)} %copy-done, f32[10,16,256]{2,1,0:T(8,128)} %copy-done.2, f32[10,16,256]{2,1,0:T(8,128)} %copy-done.3, f32[3,16,32,256]{3,2,1,0:T(8,128)} %get-tuple-element.151.refs_5_, ...), custom_call_target="tpu_custom_call" | custom-call | flops 40000000 | bytes 6291456 | tf_op jit(solution)/shard_map/finish/pallas_call | solution.py:503
  (175 shorter events, 82.0 us)
Async XLA Ops:
  4.7 16.7 %collective-permute-start = (f32[10,2,32,256]{3,2,1,0:T(8,128)}, f32[10,2,32,256]{3,2,1,0:T(8,128)S(1)}, u32[]{:S(2)}, u32[]{:S(2)}) collective-permute-start(f32[10,2,32,256]{3,2,1,0:T(8,128)} %get-tuple-element.82), channel_id=1, source_target_pairs={{0,4},{4,0},{1,5},{5,1},{2,6},{6,2},{3,7},{7,3},{8,12},{12,8},{9,1... | collective-permute-start | bytes 1966088 | tf_op jit(solution)/shard_map/ppermute | solution.py:32
  6.2 9.4 %collective-permute-start.1 = (f32[10,16,256]{2,1,0:T(8,128)}, f32[10,16,256]{2,1,0:T(8,128)S(1)}, u32[]{:S(2)}, u32[]{:S(2)}) collective-permute-start(f32[10,16,256]{2,1,0:T(8,128)} %get-tuple-element.83), channel_id=1, source_target_pairs={{0,1},{1,2},{2,3},{3,0},{4,5},{5,6},{6,7},{7,4},{8,9},{9,10},{10,1... | collective-permute-start | bytes 491528 | tf_op jit(solution)/shard_map/ppermute | solution.py:33
  6.4 9.2 %collective-permute-start.2 = (f32[10,16,256]{2,1,0:T(8,128)}, f32[10,16,256]{2,1,0:T(8,128)S(1)}, u32[]{:S(2)}, u32[]{:S(2)}) collective-permute-start(f32[10,16,256]{2,1,0:T(8,128)} %get-tuple-element.84), channel_id=1, source_target_pairs={{0,3},{1,0},{2,1},{3,2},{4,7},{5,4},{6,5},{7,6},{8,11},{9,8},{10,9... | collective-permute-start | bytes 491528 | tf_op jit(solution)/shard_map/ppermute | solution.py:34
  35.7 14.0 %collective-permute-start.7 = (f32[3,8,16,128]{3,2,1,0:T(8,128)}, f32[3,8,16,128]{3,2,1,0:T(8,128)S(1)}, u32[]{:S(2)}, u32[]{:S(2)}) collective-permute-start(f32[3,8,16,128]{3,2,1,0:T(8,128)} %get-tuple-element.97), channel_id=1, source_target_pairs={{8,16},{9,17},{10,18},{11,19},{12,20},{13,21},{14,22},{15,23}} | collective-permute-start | bytes 589832 | tf_op jit(solution)/shard_map/ppermute | solution.py:49
  37.0 12.7 %collective-permute-start.8 = (f32[3,2,16,128]{3,2,1,0:T(8,128)}, f32[3,2,16,128]{3,2,1,0:T(8,128)S(1)}, u32[]{:S(2)}, u32[]{:S(2)}) collective-permute-start(f32[3,2,16,128]{3,2,1,0:T(8,128)} %get-tuple-element.98), channel_id=1, source_target_pairs={{8,20},{9,21},{10,22},{11,23},{12,16},{13,17},{14,18},{15,19}} | collective-permute-start | bytes 147464 | tf_op jit(solution)/shard_map/ppermute | solution.py:49
  38.3 9.7 %collective-permute-start.9 = (f32[3,8,128]{2,1,0:T(8,128)}, f32[3,8,128]{2,1,0:T(8,128)S(1)}, u32[]{:S(2)}, u32[]{:S(2)}) collective-permute-start(f32[3,8,128]{2,1,0:T(8,128)} %get-tuple-element.99), channel_id=1, source_target_pairs={{8,17},{9,18},{10,19},{11,16},{12,21},{13,22},{14,23},{15,20}} | collective-permute-start | bytes 36872 | tf_op jit(solution)/shard_map/ppermute | solution.py:49
  39.6 10.1 %collective-permute-start.10 = (f32[3,8,128]{2,1,0:T(8,128)}, f32[3,8,128]{2,1,0:T(8,128)S(1)}, u32[]{:S(2)}, u32[]{:S(2)}) collective-permute-start(f32[3,8,128]{2,1,0:T(8,128)} %get-tuple-element.100), channel_id=1, source_target_pairs={{8,19},{9,16},{10,17},{11,18},{12,23},{13,20},{14,21},{15,22}} | collective-permute-start | bytes 36872 | tf_op jit(solution)/shard_map/ppermute | solution.py:49
  53.4 6.8 %collective-permute-start.11 = (f32[3,8,16,128]{3,2,1,0:T(8,128)}, f32[3,8,16,128]{3,2,1,0:T(8,128)S(1)}, u32[]{:S(2)}, u32[]{:S(2)}) collective-permute-start(f32[3,8,16,128]{3,2,1,0:T(8,128)} %get-tuple-element.101), channel_id=1, source_target_pairs={{16,24},{17,25},{18,26},{19,27},{20,28},{21,29},{22,30},{23,31}} | collective-permute-start | bytes 589832 | tf_op jit(solution)/shard_map/ppermute | solution.py:49
  64.3 9.6 %collective-permute-start.15 = (f32[3,2,16,128]{3,2,1,0:T(8,128)}, f32[3,2,16,128]{3,2,1,0:T(8,128)S(1)}, u32[]{:S(2)}, u32[]{:S(2)}) collective-permute-start(f32[3,2,16,128]{3,2,1,0:T(8,128)} %get-tuple-element.110), channel_id=1, source_target_pairs={{0,4},{4,0},{1,5},{5,1},{2,6},{6,2},{3,7},{7,3},{8,12},{12,8},{9,1... | collective-permute-start | bytes 147464 | tf_op jit(solution)/shard_map/ppermute | solution.py:32
  83.1 6.7 %collective-permute-start.18 = (f32[3,2,32,256]{3,2,1,0:T(8,128)}, f32[3,2,32,256]{3,2,1,0:T(8,128)S(1)}, u32[]{:S(2)}, u32[]{:S(2)}) collective-permute-start(f32[3,2,32,256]{3,2,1,0:T(8,128)} %get-tuple-element.114), channel_id=1, source_target_pairs={{0,4},{4,0},{1,5},{5,1},{2,6},{6,2},{3,7},{7,3},{8,12},{12,8},{9,1... | collective-permute-start | bytes 589832 | tf_op jit(solution)/shard_map/ppermute | solution.py:32
  83.7 6.1 %collective-permute-start.20 = (f32[3,16,256]{2,1,0:T(8,128)}, f32[3,16,256]{2,1,0:T(8,128)S(1)}, u32[]{:S(2)}, u32[]{:S(2)}) collective-permute-start(f32[3,16,256]{2,1,0:T(8,128)} %get-tuple-element.116), channel_id=1, source_target_pairs={{0,3},{1,0},{2,1},{3,2},{4,7},{5,4},{6,5},{7,6},{8,11},{9,8},{10,9... | collective-permute-start | bytes 147464 | tf_op jit(solution)/shard_map/ppermute | solution.py:34
  97.6 27.1 %collective-permute-start.21 = (f32[3,16,32,256]{3,2,1,0:T(8,128)}, f32[3,16,32,256]{3,2,1,0:T(8,128)S(1)}, u32[]{:S(2)}, u32[]{:S(2)}) collective-permute-start(f32[3,16,32,256]{3,2,1,0:T(8,128)} %get-tuple-element.121.u2.refs_14_), channel_id=1, source_target_pairs={{0,8},{1,9},{2,10},{3,11},{4,12},{5,13},{6,14},{7,15},{8,16},{9,17... | collective-permute-start | bytes 4718600 | tf_op jit(solution)/shard_map/ppermute | solution.py:49
  99.5 19.5 %collective-permute-start.25 = (f32[4,2,32,256]{3,2,1,0:T(8,128)}, f32[4,2,32,256]{3,2,1,0:T(8,128)S(1)}, u32[]{:S(2)}, u32[]{:S(2)}) collective-permute-start(f32[4,2,32,256]{3,2,1,0:T(8,128)} %get-tuple-element.122), channel_id=1, source_target_pairs={{0,4},{4,0},{1,5},{5,1},{2,6},{6,2},{3,7},{7,3},{8,12},{12,8},{9,1... | collective-permute-start | bytes 786440 | tf_op jit(solution)/shard_map/ppermute | solution.py:32
  101.1 23.6 %collective-permute-start.22 = (f32[4,2,32,256]{3,2,1,0:T(8,128)}, f32[4,2,32,256]{3,2,1,0:T(8,128)S(1)}, u32[]{:S(2)}, u32[]{:S(2)}) collective-permute-start(f32[4,2,32,256]{3,2,1,0:T(8,128)} %get-tuple-element.122), channel_id=1, source_target_pairs={{0,12},{1,13},{2,14},{3,15},{4,8},{5,9},{6,10},{7,11},{8,20},{9,21... | collective-permute-start | bytes 786440 | tf_op jit(solution)/shard_map/ppermute | solution.py:49
  103.1 7.1 %collective-permute-start.23 = (f32[4,16,256]{2,1,0:T(8,128)}, f32[4,16,256]{2,1,0:T(8,128)S(1)}, u32[]{:S(2)}, u32[]{:S(2)}) collective-permute-start(f32[4,16,256]{2,1,0:T(8,128)} %get-tuple-element.123), channel_id=1, source_target_pairs={{0,9},{1,10},{2,11},{3,8},{4,13},{5,14},{6,15},{7,12},{8,17},{9,18... | collective-permute-start | bytes 196616 | tf_op jit(solution)/shard_map/ppermute | solution.py:49
  108.0 6.3 %collective-permute-start.27 = (f32[4,16,256]{2,1,0:T(8,128)}, f32[4,16,256]{2,1,0:T(8,128)S(1)}, u32[]{:S(2)}, u32[]{:S(2)}) collective-permute-start(f32[4,16,256]{2,1,0:T(8,128)} %get-tuple-element.124), channel_id=1, source_target_pairs={{0,3},{1,0},{2,1},{3,2},{4,7},{5,4},{6,5},{7,6},{8,11},{9,8},{10,9... | collective-permute-start | bytes 196616 | tf_op jit(solution)/shard_map/ppermute | solution.py:34
  110.1 8.8 %collective-permute-start.24 = (f32[4,16,256]{2,1,0:T(8,128)}, f32[4,16,256]{2,1,0:T(8,128)S(1)}, u32[]{:S(2)}, u32[]{:S(2)}) collective-permute-start(f32[4,16,256]{2,1,0:T(8,128)} %get-tuple-element.124), channel_id=1, source_target_pairs={{0,11},{1,8},{2,9},{3,10},{4,15},{5,12},{6,13},{7,14},{8,19},{9,16... | collective-permute-start | bytes 196616 | tf_op jit(solution)/shard_map/ppermute | solution.py:49
  141.1 13.3 %collective-permute-start.32 = (f32[3,8,16,128]{3,2,1,0:T(8,128)}, f32[3,8,16,128]{3,2,1,0:T(8,128)S(1)}, u32[]{:S(2)}, u32[]{:S(2)}) collective-permute-start(f32[3,8,16,128]{3,2,1,0:T(8,128)} %get-tuple-element.134), channel_id=1, source_target_pairs={{8,16},{9,17},{10,18},{11,19},{12,20},{13,21},{14,22},{15,23}} | collective-permute-start | bytes 589832 | tf_op jit(solution)/shard_map/ppermute | solution.py:49
  142.3 12.0 %collective-permute-start.33 = (f32[3,2,16,128]{3,2,1,0:T(8,128)}, f32[3,2,16,128]{3,2,1,0:T(8,128)S(1)}, u32[]{:S(2)}, u32[]{:S(2)}) collective-permute-start(f32[3,2,16,128]{3,2,1,0:T(8,128)} %get-tuple-element.135), channel_id=1, source_target_pairs={{8,20},{9,21},{10,22},{11,23},{12,16},{13,17},{14,18},{15,19}} | collective-permute-start | bytes 147464 | tf_op jit(solution)/shard_map/ppermute | solution.py:49
  143.6 9.0 %collective-permute-start.34 = (f32[3,8,128]{2,1,0:T(8,128)}, f32[3,8,128]{2,1,0:T(8,128)S(1)}, u32[]{:S(2)}, u32[]{:S(2)}) collective-permute-start(f32[3,8,128]{2,1,0:T(8,128)} %get-tuple-element.136), channel_id=1, source_target_pairs={{8,17},{9,18},{10,19},{11,16},{12,21},{13,22},{14,23},{15,20}} | collective-permute-start | bytes 36872 | tf_op jit(solution)/shard_map/ppermute | solution.py:49
  144.9 9.4 %collective-permute-start.35 = (f32[3,8,128]{2,1,0:T(8,128)}, f32[3,8,128]{2,1,0:T(8,128)S(1)}, u32[]{:S(2)}, u32[]{:S(2)}) collective-permute-start(f32[3,8,128]{2,1,0:T(8,128)} %get-tuple-element.137), channel_id=1, source_target_pairs={{8,19},{9,16},{10,17},{11,18},{12,23},{13,20},{14,21},{15,22}} | collective-permute-start | bytes 36872 | tf_op jit(solution)/shard_map/ppermute | solution.py:49
  158.1 6.8 %collective-permute-start.36 = (f32[3,8,16,128]{3,2,1,0:T(8,128)}, f32[3,8,16,128]{3,2,1,0:T(8,128)S(1)}, u32[]{:S(2)}, u32[]{:S(2)}) collective-permute-start(f32[3,8,16,128]{3,2,1,0:T(8,128)} %get-tuple-element.138), channel_id=1, source_target_pairs={{16,24},{17,25},{18,26},{19,27},{20,28},{21,29},{22,30},{23,31}} | collective-permute-start | bytes 589832 | tf_op jit(solution)/shard_map/ppermute | solution.py:49
  168.4 9.6 %collective-permute-start.40 = (f32[3,2,16,128]{3,2,1,0:T(8,128)}, f32[3,2,16,128]{3,2,1,0:T(8,128)S(1)}, u32[]{:S(2)}, u32[]{:S(2)}) collective-permute-start(f32[3,2,16,128]{3,2,1,0:T(8,128)} %get-tuple-element.148), channel_id=1, source_target_pairs={{0,4},{4,0},{1,5},{5,1},{2,6},{6,2},{3,7},{7,3},{8,12},{12,8},{9,1... | collective-permute-start | bytes 147464 | tf_op jit(solution)/shard_map/ppermute | solution.py:32
  189.2 6.7 %collective-permute-start.43 = (f32[3,2,32,256]{3,2,1,0:T(8,128)}, f32[3,2,32,256]{3,2,1,0:T(8,128)S(1)}, u32[]{:S(2)}, u32[]{:S(2)}) collective-permute-start(f32[3,2,32,256]{3,2,1,0:T(8,128)} %get-tuple-element.152), channel_id=1, source_target_pairs={{0,4},{4,0},{1,5},{5,1},{2,6},{6,2},{3,7},{7,3},{8,12},{12,8},{9,1... | collective-permute-start | bytes 589832 | tf_op jit(solution)/shard_map/ppermute | solution.py:32
  (68 other events, 179.7 us)

commit v3 on v2

--- a/solution.py
+++ b/solution.py
@@ -245,19 +245,21 @@
     squeeze(summed, rows, store, 3)
 
 
-def pack_kernel(first, v, s, g, end, x_faces, y_last, y_first, summed, rows):
+def pack_kernel(feed, first, g, v, s, end, x_faces, y_last, y_first, summed, rows):
     outs = (x_faces, y_last, y_first)
-    for k, field in enumerate((v, g, s)):
-        emit_faces(field, outs, 3 * k)
 
     def store(c, value):
         end[c] = value
 
+    feed.need(g)
     coarsen(g, summed, rows, store)
     emit_coarse_faces(end, outs, 9)
-
-
-def coarsen_kernel(first, v, s, end, speed, zero, summed, rows):
+    for k, field in enumerate((v, g, s)):
+        feed.need(field)
+        emit_faces(field, outs, 3 * k)
+
+
+def coarsen_kernel(feed, first, v, s, end, speed, zero, summed, rows):
     f = first[0]
 
     def store_zero(c, value):
@@ -266,7 +268,9 @@
     def store_speed(c, value):
         speed[c] = value * 0.25
 
+    feed.need(s, end)
     coarsen(s, summed, rows, store_zero)
+    feed.need(v)
     coarsen(v, summed, rows, store_speed)
 
 
@@ -287,18 +291,22 @@
 
 
 def offset_start_kernel(
-    first, v, s, g, x_faces, behind, ahead, zero,
+    feed, first, v, s, g, x_faces, behind, ahead, zero,
     integral, coarse_grads, zero_x, zero_b, zero_a, end, end_x, end_l, end_f,
     ext, half, summed, grads_summed, rows,
 ):
     f = first[0]
+    feed.need(v, x_faces, behind, ahead)
     fill(half, [(0.5, Node(v, x_faces, behind, ahead))])
+    feed.need(s, g)
     start = Node(s, x_faces, behind, ahead, 6)
     guess = Node(g, x_faces, behind, ahead, 3)
     share = f * (TIME_STEP / 6.0)
     fill(ext, [(share, start), (TIME_STEP - share, guess)])
     integral_loop(ext, half, summed, grads_summed)
 
+    feed.need(zero)
+
     def store(c, value):
         integral[c] = value
         end[c] = zero[c] + value
@@ -306,6 +314,7 @@
     squeeze(summed, rows, store, 3)
     emit_faces(end, (end_x, end_l, end_f))
     take_coarse_faces(x_faces, behind, ahead, 9, (zero_x, zero_b, zero_a))
+    feed.send(integral, end, end_x, end_l, end_f, zero_x, zero_b, zero_a)
 
     def store_grads(c, value):
         coarse_grads[c] = value
@@ -314,13 +323,15 @@
 
 
 def offset_later_kernel(
-    first, v, s, x_faces, behind, ahead,
+    feed, first, v, s, x_faces, behind, ahead,
     u0, u0_x, u0_b, u0_a, u1, u1_x, u1_b, u1_a, u2, u2_x, u2_b, u2_a,
     integral, zero, zero_x, zero_b, zero_a, end, end_x, end_l, end_f,
     ext, half, summed, rows,
 ):
     f = first[0]
+    feed.need(v, x_faces, behind, ahead)
     fill(half, [(0.5, Node(v, x_faces, behind, ahead))])
+    feed.need(s, u1, u1_x, u1_b, u1_a, u2, u2_x, u2_b, u2_a, u0, u0_x, u0_b, u0_a)
     sixth = TIME_STEP / 6.0
     fill(
         ext,
@@ -368,21 +379,20 @@
             store(a, x, zero[0][a, x] + d0[0][a, x] + integral[a, x] + changes[a])
 
 
-def pass_kernel(turn, first, *refs):
+def pass_kernel(feed, first, *refs):
     arrived, zero = refs[:4], refs[4:8]
     integral, speed, coarse_grads, end, end_x, end_l, end_f = refs[8:15]
     d0, ext = refs[15:19], refs[19]
 
-    @pl.when(first[1] == float(turn))
-    def _():
-        def store(a, x, value):
-            end[a, x] = value
-
-        chain_step(1.0, [arrived], zero, integral, speed, coarse_grads, d0, ext, store)
-        emit_faces(end, (end_x, end_l, end_f))
-
-
-def settle_kernel(count, first, *refs):
+    def store(a, x, value):
+        end[a, x] = value
+
+    feed.need(*arrived, *zero, integral, speed, coarse_grads)
+    chain_step(1.0, [arrived], zero, integral, speed, coarse_grads, d0, ext, store)
+    emit_faces(end, (end_x, end_l, end_f))
+
+
+def settle_kernel(count, feed, first, *refs):
     arrived = [refs[4 * k : 4 * k + 4] for k in range(count)]
     refs = refs[4 * count :]
     zero, (integral, speed, coarse_grads, end_two) = refs[:4], refs[4:8]
@@ -391,13 +401,15 @@
     def store(a, x, value):
         d2[a, x] = value - end_two[a, x]
 
+    feed.need(*[a for group in arrived for a in group], *zero, integral, speed, coarse_grads, end_two)
     chain_step(1.0 - first[0], arrived, zero, integral, speed, coarse_grads, d0, ext, store)
     emit_faces(d2, (d2_x, d2_l, d2_f))
 
 
-def middle_kernel(nodes, *refs):
-    first, v, vx, vb, va = refs[:5]
-    at = 5
+def middle_kernel(nodes, feed, *refs):
+    first, (v, vx, vb, va) = refs[0], refs[9:13]
+    d0, d2 = Node(*refs[1:5]), Node(*refs[5:9])
+    at = 13
     parts = []
     for _, _, _, own, off in nodes:
         main = refs[at]
@@ -408,17 +420,18 @@
         else:
             x_faces, behind, ahead = vx, vb, va
         parts.append(Node(main, x_faces, behind, ahead, off))
-    d0 = Node(*refs[at : at + 4])
-    d2 = Node(*refs[at + 4 : at + 8])
-    a1, a1_x, a1_l, a1_f, rest, rest_x, rest_b, rest_a = refs[at + 8 : at + 16]
-    ext, half, wide0, edge0, wide2, edge2, rows = refs[at + 16 :]
+    a1, a1_x, a1_l, a1_f, rest, rest_x, rest_b, rest_a = refs[at : at + 8]
+    ext, half, wide0, edge0, wide2, edge2, rows = refs[at + 8 :]
     f = first[0]
     begin, first_stage, second_stage = [
         [(spec[k][0] * f + spec[k][1], node) for spec, node in zip(nodes, parts)] for k in range(3)
     ]
-    fill(half, [(0.5, Node(v, vx, vb, va))])
+    feed.need_nodes(d0, d2)
     prolong(d0, wide0, edge0, rows)
     prolong(d2, wide2, edge2, rows)
+    feed.need(v, vx, vb, va)
+    fill(half, [(0.5, Node(v, vx, vb, va))])
+    feed.need_nodes(*parts)
     fill(
         ext,
         [(TIME_STEP * w, node) for w, node in first_stage],
@@ -458,12 +471,14 @@
     emit_faces(a1, (a1_x, a1_l, a1_f))
 
 
-def finish_kernel(last, first, v, vx, vb, va, a1, a1_x, a1_b, a1_a, rest, rest_x, rest_b, rest_a, *refs):
+def finish_kernel(last, feed, first, v, vx, vb, va, a1, a1_x, a1_b, a1_a, rest, rest_x, rest_b, rest_a, *refs):
     if last:
         a2, ext, half = refs
     else:
         a2, a2_x, a2_l, a2_f, end, ext, half, summed, rows = refs
+    feed.need(v, vx, vb, va)
     fill(half, [(0.5, Node(v, vx, vb, va))])
+    feed.need(a1, a1_x, a1_b, a1_a, rest, rest_x, rest_b, rest_a)
     fill(
         ext,
         [
@@ -498,15 +513,73 @@
         emit_coarse_faces(end, (a2_x, a2_l, a2_f), 3)
 
 
-def call(kernel, name, first, args, outs, scratch, flops=0):
+class Feed:
+    def __init__(self, inward, outward):
+        self.inward = {id(buffer): copy for buffer, copy in inward}
+        self.outward = {id(buffer): copy for buffer, copy in outward}
+        self.going = []
+        for copy in self.inward.values():
+            copy.start()
+
+    def need(self, *buffers):
+        for buffer in buffers:
+            copy = self.inward.pop(id(buffer), None)
+            if copy is not None:
+                copy.wait()
+
+    def need_nodes(self, *nodes):
+        for node in nodes:
+            self.need(node.main, node.x_faces, node.behind, node.ahead)
+
+    def send(self, *buffers):
+        for buffer in buffers:
+            copy = self.outward.pop(id(buffer), None)
+            if copy is not None:
+                copy.start()
+                self.going.append(copy)
+
+    def finish(self):
+        for copy in self.inward.values():
+            copy.wait()
+        for copy in self.outward.values():
+            copy.start()
+        for copy in self.going + list(self.outward.values()):
+            copy.wait()
+
+
+def call(kernel, name, first, args, outs, scratch, flops=0, turn=None):
+    n_in, n_out = len(args), len(outs)
     moved = sum(4 * a.size for a in args)
+
+    def body(first_ref, *refs):
+        sources, refs = refs[:n_in], refs[n_in:]
+        targets, refs = refs[:n_out], refs[n_out:]
+        held, refs = refs[:n_in], refs[n_in:]
+        made, refs = refs[:n_out], refs[n_out:]
+        in_sem, out_sem = refs[-2:]
+
+        def work():
+            feed = Feed(
+                [(h, pltpu.make_async_copy(s, h, in_sem.at[k])) for k, (s, h) in enumerate(zip(sources, held))],
+                [(m, pltpu.make_async_copy(m, t, out_sem.at[k])) for k, (m, t) in enumerate(zip(made, targets))],
+            )
+            kernel(feed, first_ref, *held, *made, *refs[:-2])
+            feed.finish()
+
+        if turn is None:
+            work()
+        else:
+            pl.when(first_ref[1] == float(turn))(work)
+
     return pl.pallas_call(
-        kernel,
+        body,
         name=name,
         out_shape=[jax.ShapeDtypeStruct(dims, F32) for dims in outs],
-        in_specs=[pl.BlockSpec(memory_space=pltpu.SMEM)] + [pl.BlockSpec(memory_space=pltpu.VMEM)] * len(args),
-        out_specs=[pl.BlockSpec(memory_space=pltpu.VMEM)] * len(outs),
-        scratch_shapes=[pltpu.VMEM(dims, F32) for dims in scratch],
+        in_specs=[pl.BlockSpec(memory_space=pltpu.SMEM)] + [pl.BlockSpec(memory_space=pltpu.HBM)] * n_in,
+        out_specs=[pl.BlockSpec(memory_space=pltpu.HBM)] * n_out,
+        scratch_shapes=[pltpu.VMEM(a.shape, F32) for a in args]
+        + [pltpu.VMEM(dims, F32) for dims in outs + scratch]
+        + [pltpu.SemaphoreType.DMA((n_in,)), pltpu.SemaphoreType.DMA((n_out,))],
         compiler_params=pltpu.CompilerParams(vmem_limit_bytes=56 << 20),
         cost_estimate=pl.CostEstimate(flops=flops, bytes_accessed=moved, transcendentals=0),
     )(first, *args)
@@ -531,7 +604,7 @@
     wide, edge, wide_rows = (3, cx + 2, ny, nz), (2, 3, cx, nz), ((cx + 2) * ny, cz)
 
     end_two, *packed = call(
-        pack_kernel, "pack", first, [velocity, start_field, own],
+        pack_kernel, "pack", first, [own, velocity, start_field],
         [coarse] + layers_of(10), [summed, rows], 5_000_000,
     )
     layers = swap_faces(packed)
@@ -552,9 +625,9 @@
             arrivals.append(hand_on([turn - 1], end, sent))
             if turn + 1 < slabs:
                 end, *sent = call(
-                    lambda *refs, turn=turn: pass_kernel(turn, *refs), "chain", first,
+                    pass_kernel, "chain", first,
                     [*arrivals[-1], zero, *zero_faces, integral, speed, coarse_grads],
-                    [coarse] + coarse_faces, [coarse, *coarse_faces, coarse_ext], 2_000_000,
+                    [coarse] + coarse_faces, [coarse, *coarse_faces, coarse_ext], 2_000_000, turn,
                 )
         results = call(
             lambda *refs, count=len(arrivals): settle_kernel(count, *refs), "settle", first,
@@ -580,7 +653,7 @@
             args = [start_field, *u0, *u1, *u2]
         middle, m_x, m_l, m_f, *rest = call(
             lambda *refs, nodes=nodes: middle_kernel(nodes, *refs),
-            "middle", first, [velocity, *layers, *args, *d0, *d2],
+            "middle", first, [*d0, *d2, velocity, *layers, *args],
             [fine] + fine_faces + [fine] + fine_faces,
             [ext, ext, wide, edge, wide, edge, wide_rows], 60_000_000,
         )

time: 204 us -> 213 us (1.044)
  Pallas kernels: 72.3 us -> 77.1 us
  waiting for transfers between devices: 67 us -> 70.6 us
    pallas_call x14, Pallas kernels: 72.3 us -> 77.1 us  [call(): pl.pallas_call(body, name=name, out_shape=[jax.ShapeDtypeStruct(dims, F32...]
    ppermute x28, waiting for transfers between devices: 32.7 us -> 37.1 us  [permute(): return lax.ppermute(array, ('tm', 'gx', 'gy'), pairs)]
where the time goes in v3:
time: 213 us; the launch traced here: 212 us
  Pallas kernels  77.1 us (36%)
  waiting for transfers between devices  70.6 us (33%)
  starting transfers between devices  51.9 us (24%)
  local copies, waits for them, and re-layouts  11.3 us (5%)
    pallas_call x14, Pallas kernels, call(): pl.pallas_call(body, name=name, out_shape=[jax.ShapeDtypeStruct(dims, F32...  77.1 us
    ppermute x28, waiting for transfers between devices, permute(): return lax.ppermute(array, ('tm', 'gx', 'gy'), pairs)  37.1 us
    ppermute x28, starting transfers between devices, permute(): return lax.ppermute(array, ('tm', 'gx', 'gy'), pairs)  33.7 us
    ppermute x6, waiting for transfers between devices, swap_faces(): behind = lax.ppermute(y_last, 'gy', ring(gy, 1))  14 us
    ppermute x6, waiting for transfers between devices, swap_faces(): ahead = lax.ppermute(y_first, 'gy', ring(gy, -1))  13.7 us
    unnamed x92, local copies, waits for them, and re-layouts  11.3 us
    ppermute x6, starting transfers between devices, swap_faces(): behind = lax.ppermute(y_last, 'gy', ring(gy, 1))  6.32 us
    ppermute x6, starting transfers between devices, swap_faces(): lax.ppermute(a, 'gx', ring(gx, by))  6.07 us
  transfers between devices with their start and end apart: 46, of which 23 were waited for; matrix products, arithmetic and copies ran while one was open for 0% of the time, Pallas kernels for 2%

profile of v3, /device:TPU:26, one launch (start us, length us, event | category | flops | bytes accessed | tf_op | source)
XLA Modules:
  0.0 212.0 jit_solution(4935920685725122915)
XLA Ops:
  0.6 4.1 %pack.1 = (f32[3,8,16,128]{3,2,1,0:T(8,128)}, f32[10,2,32,256]{3,2,1,0:T(8,128)}, f32[10,16,256]{2,1,0:T(8,128)}, f32[10,16,256]{2,1,0:T(8,128)}) custom-call(f32[2]{0:T(128)} %add_convert_fusion.first_ref, f32[3,16,32,256]{3,2,1,0:T(8,128)} %bitcast.4, f32[3,16,32,256]{3,2,1,0:T(8,128)} %refs_0_.9, f32[3,16,32,256]{3,2,1,0:T(8,128)} %refs_12_.3), custom_call_target="tpu_custom_call" | custom-call | flops 5000000 | bytes 4718592 | tf_op jit(solution)/shard_map/pack/pallas_call | solution.py:574
  8.3 4.4 %coarsen.1 = (f32[3,8,16,128]{3,2,1,0:T(8,128)}, f32[3,8,16,128]{3,2,1,0:T(8,128)}) custom-call(f32[2]{0:T(128)} %add_convert_fusion.first_ref, f32[3,16,32,256]{3,2,1,0:T(8,128)} %refs_0_.9, f32[3,16,32,256]{3,2,1,0:T(8,128)} %refs_12_.3, f32[3,8,16,128]{3,2,1,0:T(8,128)} %get-tuple-element.85.refs_2_.refs_19_), custom_call_target="tpu_custom_call" | custom-call | flops 10000000 | bytes 3342336 | tf_op jit(solution)/shard_map/coarsen/pallas_call | solution.py:574
  12.7 2.9 %collective-permute-done.1.refs_4_.refs_10_.refs_2_.refs_3_ = f32[10,16,256]{2,1,0:T(8,128)S(1)} collective-permute-done((f32[10,16,256]{2,1,0:T(8,128)}, f32[10,16,256]{2,1,0:T(8,128)S(1)}, u32[]{:S(2)}, u32[]{:S(2)}) %collective-permute-start.1) | collective-permute-done | bytes 163872 | tf_op jit(solution)/shard_map/ppermute | solution.py:33
  15.7 5.8 %collective-permute-done.refs_3_.refs_9_.refs_1_.refs_2_ = f32[10,2,32,256]{3,2,1,0:T(8,128)S(1)} collective-permute-done((f32[10,2,32,256]{3,2,1,0:T(8,128)}, f32[10,2,32,256]{3,2,1,0:T(8,128)S(1)}, u32[]{:S(2)}, u32[]{:S(2)}) %collective-permute-start) | collective-permute-done | bytes 655392 | tf_op jit(solution)/shard_map/ppermute | solution.py:32
  22.3 8.4 %offset_start.1 = (f32[3,8,16,128]{3,2,1,0:T(8,128)}, f32[9,8,16,128]{3,2,1,0:T(8,128)}, f32[3,2,16,128]{3,2,1,0:T(8,128)}, f32[3,8,128]{2,1,0:T(8,128)}, f32[3,...) custom-call(f32[2]{0:T(128)} %add_convert_fusion.first_ref, ...), custom_call_target="tpu_custom_call" | custom-call | flops 40000000 | bytes 5898240 | tf_op jit(solution)/shard_map/offset_start/pallas_call | solution.py:574
  40.3 9.3 %collective-permute-done.9.refs_2_.refs_6_ = f32[3,8,128]{2,1,0:T(8,128)S(1)} collective-permute-done((f32[3,8,128]{2,1,0:T(8,128)}, f32[3,8,128]{2,1,0:T(8,128)S(1)}, u32[]{:S(2)}, u32[]{:S(2)}) %collective-permute-start.9) | collective-permute-done | bytes 12320 | tf_op jit(solution)/shard_map/ppermute | solution.py:49
  52.6 3.3 %chain.5 = (f32[3,8,16,128]{3,2,1,0:T(8,128)}, f32[3,2,16,128]{3,2,1,0:T(8,128)}, f32[3,8,128]{2,1,0:T(8,128)}, f32[3,8,128]{2,1,0:T(8,128)}) custom-call(f32[2]{0:T(128)} %add_convert_fusion.first_ref, f32[3,8,16,128]{3,2,1,0:T(8,128)} %copy-done.10, f32[3,2,16,128]{3,2,1,0:T(8,128)} %copy-done.22, f32[3,8,128]{2,1,0:T(8,128)} %copy-done.33, ...), custom_call_target="tpu_custom_call" | custom-call | flops 2000000 | bytes 1523712 | tf_op jit(solution)/shard_map/chain/pallas_call | solution.py:574
  63.9 3.6 %settle.2 = (f32[3,8,16,128]{3,2,1,0:T(8,128)}, f32[3,2,16,128]{3,2,1,0:T(8,128)}, f32[3,8,128]{2,1,0:T(8,128)}, f32[3,8,128]{2,1,0:T(8,128)}, f32[3,8,16,128]{3...) custom-call(f32[2]{0:T(128)} %add_convert_fusion.first_ref, ...), custom_call_target="tpu_custom_call" | custom-call | flops 2000000 | bytes 2260992 | tf_op jit(solution)/shard_map/settle/pallas_call | solution.py:574
  68.5 2.9 %collective-permute-start.16 = (f32[3,8,128]{2,1,0:T(8,128)}, f32[3,8,128]{2,1,0:T(8,128)S(1)}, u32[]{:S(2)}, u32[]{:S(2)}) collective-permute-start(f32[3,8,128]{2,1,0:T(8,128)} %get-tuple-element.111), channel_id=1, source_target_pairs={{0,1},{1,2},{2,3},{3,0},{4,5},{5,6},{6,7},{7,4},{8,9},{9,10},{10,1... | collective-permute-start | bytes 36872 | tf_op jit(solution)/shard_map/ppermute | solution.py:33
  73.0 4.1 %collective-permute-done.17.refs_7_ = f32[3,8,128]{2,1,0:T(8,128)S(1)} collective-permute-done((f32[3,8,128]{2,1,0:T(8,128)}, f32[3,8,128]{2,1,0:T(8,128)S(1)}, u32[]{:S(2)}, u32[]{:S(2)}) %collective-permute-start.17) | collective-permute-done | bytes 12320 | tf_op jit(solution)/shard_map/ppermute | solution.py:34
  77.8 9.1 %middle.2 = (f32[3,16,32,256]{3,2,1,0:T(8,128)}, f32[3,2,32,256]{3,2,1,0:T(8,128)}, f32[3,16,256]{2,1,0:T(8,128)}, f32[3,16,256]{2,1,0:T(8,128)}, f32[3,16,32,25...) custom-call(f32[2]{0:T(128)} %add_convert_fusion.first_ref, ...), custom_call_target="tpu_custom_call" | custom-call | flops 60000000 | bytes 6242304 | tf_op jit(solution)/shard_map/middle/pallas_call | solution.py:574
  89.4 2.4 %collective-permute-done.19.refs_6_.refs_11_.refs_19_ = f32[3,16,256]{2,1,0:T(8,128)S(1)} collective-permute-done((f32[3,16,256]{2,1,0:T(8,128)}, f32[3,16,256]{2,1,0:T(8,128)S(1)}, u32[]{:S(2)}, u32[]{:S(2)}) %collective-permute-start.19) | collective-permute-done | bytes 49184 | tf_op jit(solution)/shard_map/ppermute | solution.py:33
  94.2 7.6 %finish.2 = (f32[3,16,32,256]{3,2,1,0:T(8,128)}, f32[4,2,32,256]{3,2,1,0:T(8,128)}, f32[4,16,256]{2,1,0:T(8,128)}, f32[4,16,256]{2,1,0:T(8,128)}, f32[3,8,16,128]{3,2,1,0:T(8,128)}) custom-call(f32[2]{0:T(128)} %add_convert_fusion.first_ref, f32[3,16,32,256]{3,2,1,0:T(8,128)} %refs_0_.9, f32[10,2,32,256]{3,2,1,0:T(8,128)} %copy-done, ...), custom_call_target="tpu_custom_call" | custom-call | flops 40000000 | bytes 6291456 | tf_op jit(solution)/shard_map/finish/pallas_call | solution.py:574
  109.2 3.0 %collective-permute-done.26.refs_15_.refs_23_ = f32[4,16,256]{2,1,0:T(8,128)S(1)} collective-permute-done((f32[4,16,256]{2,1,0:T(8,128)}, f32[4,16,256]{2,1,0:T(8,128)S(1)}, u32[]{:S(2)}, u32[]{:S(2)}) %collective-permute-start.26) | collective-permute-done | bytes 65568 | tf_op jit(solution)/shard_map/ppermute | solution.py:33
  118.5 4.7 %collective-permute-done.24.refs_8_.refs_16_ = f32[4,16,256]{2,1,0:T(8,128)S(1)} collective-permute-done((f32[4,16,256]{2,1,0:T(8,128)}, f32[4,16,256]{2,1,0:T(8,128)S(1)}, u32[]{:S(2)}, u32[]{:S(2)}) %collective-permute-start.24) | collective-permute-done | bytes 65568 | tf_op jit(solution)/shard_map/ppermute | solution.py:49
  123.2 5.7 %collective-permute-done.22.refs_6_.refs_14_ = f32[4,2,32,256]{3,2,1,0:T(8,128)S(1)} collective-permute-done((f32[4,2,32,256]{3,2,1,0:T(8,128)}, f32[4,2,32,256]{3,2,1,0:T(8,128)S(1)}, u32[]{:S(2)}, u32[]{:S(2)}) %collective-permute-start.22) | collective-permute-done | bytes 262176 | tf_op jit(solution)/shard_map/ppermute | solution.py:49
  130.8 9.6 %offset_later.1 = (f32[3,8,16,128]{3,2,1,0:T(8,128)}, f32[3,8,16,128]{3,2,1,0:T(8,128)}, f32[3,2,16,128]{3,2,1,0:T(8,128)}, f32[3,8,128]{2,1,0:T(8,128)}, f32[3,...) custom-call(f32[2]{0:T(128)} %add_convert_fusion.first_ref, ...), custom_call_target="tpu_custom_call" | custom-call | flops 40000000 | bytes 9928704 | tf_op jit(solution)/shard_map/offset_later/pallas_call | solution.py:574
  149.9 8.6 %collective-permute-done.34.refs_2_.refs_6_ = f32[3,8,128]{2,1,0:T(8,128)S(1)} collective-permute-done((f32[3,8,128]{2,1,0:T(8,128)}, f32[3,8,128]{2,1,0:T(8,128)S(1)}, u32[]{:S(2)}, u32[]{:S(2)}) %collective-permute-start.34) | collective-permute-done | bytes 12320 | tf_op jit(solution)/shard_map/ppermute | solution.py:49
  161.5 3.3 %chain.7 = (f32[3,8,16,128]{3,2,1,0:T(8,128)}, f32[3,2,16,128]{3,2,1,0:T(8,128)}, f32[3,8,128]{2,1,0:T(8,128)}, f32[3,8,128]{2,1,0:T(8,128)}) custom-call(f32[2]{0:T(128)} %add_convert_fusion.first_ref, f32[3,8,16,128]{3,2,1,0:T(8,128)} %copy-done.9, f32[3,2,16,128]{3,2,1,0:T(8,128)} %copy-done.21, f32[3,8,128]{2,1,0:T(8,128)} %copy-done.32, ...), custom_call_target="tpu_custom_call" | custom-call | flops 2000000 | bytes 1523712 | tf_op jit(solution)/shard_map/chain/pallas_call | solution.py:574
  172.3 3.6 %settle.3 = (f32[3,8,16,128]{3,2,1,0:T(8,128)}, f32[3,2,16,128]{3,2,1,0:T(8,128)}, f32[3,8,128]{2,1,0:T(8,128)}, f32[3,8,128]{2,1,0:T(8,128)}, f32[3,8,16,128]{3...) custom-call(f32[2]{0:T(128)} %add_convert_fusion.first_ref, ...), custom_call_target="tpu_custom_call" | custom-call | flops 2000000 | bytes 2260992 | tf_op jit(solution)/shard_map/settle/pallas_call | solution.py:574
  176.7 3.1 %collective-permute-start.41 = (f32[3,8,128]{2,1,0:T(8,128)}, f32[3,8,128]{2,1,0:T(8,128)S(1)}, u32[]{:S(2)}, u32[]{:S(2)}) collective-permute-start(f32[3,8,128]{2,1,0:T(8,128)} %get-tuple-element.149), channel_id=1, source_target_pairs={{0,1},{1,2},{2,3},{3,0},{4,5},{5,6},{6,7},{7,4},{8,9},{9,10},{10,1... | collective-permute-start | bytes 36872 | tf_op jit(solution)/shard_map/ppermute | solution.py:33
  181.4 4.1 %collective-permute-done.42.refs_7_ = f32[3,8,128]{2,1,0:T(8,128)S(1)} collective-permute-done((f32[3,8,128]{2,1,0:T(8,128)}, f32[3,8,128]{2,1,0:T(8,128)S(1)}, u32[]{:S(2)}, u32[]{:S(2)}) %collective-permute-start.42) | collective-permute-done | bytes 12320 | tf_op jit(solution)/shard_map/ppermute | solution.py:34
  186.1 11.2 %middle.3 = (f32[3,16,32,256]{3,2,1,0:T(8,128)}, f32[3,2,32,256]{3,2,1,0:T(8,128)}, f32[3,16,256]{2,1,0:T(8,128)}, f32[3,16,256]{2,1,0:T(8,128)}, f32[3,16,32,25...) custom-call(f32[2]{0:T(128)} %add_convert_fusion.first_ref, ...), custom_call_target="tpu_custom_call" | custom-call | flops 60000000 | bytes 10469376 | tf_op jit(solution)/shard_map/middle/pallas_call | solution.py:574
  204.7 7.3 %finish.3 = f32[3,16,32,256]{3,2,1,0:T(8,128)} custom-call(f32[2]{0:T(128)} %add_convert_fusion.first_ref, f32[3,16,32,256]{3,2,1,0:T(8,128)} %refs_0_.9, f32[10,2,32,256]{3,2,1,0:T(8,128)} %copy-done, f32[10,16,256]{2,1,0:T(8,128)} %copy-done.2, f32[10,16,256]{2,1,0:T(8,128)} %copy-done.3, f32[3,16,32,256]{3,2,1,0:T(8,128)} %get-tuple-element.151.refs_4_, ...), custom_call_target="tpu_custom_call" | custom-call | flops 40000000 | bytes 6291456 | tf_op jit(solution)/shard_map/finish/pallas_call | solution.py:574
  (175 shorter events, 79.4 us)
Async XLA Ops:
  4.7 16.7 %collective-permute-start = (f32[10,2,32,256]{3,2,1,0:T(8,128)}, f32[10,2,32,256]{3,2,1,0:T(8,128)S(1)}, u32[]{:S(2)}, u32[]{:S(2)}) collective-permute-start(f32[10,2,32,256]{3,2,1,0:T(8,128)} %get-tuple-element.82), channel_id=1, source_target_pairs={{0,4},{4,0},{1,5},{5,1},{2,6},{6,2},{3,7},{7,3},{8,12},{12,8},{9,1... | collective-permute-start | bytes 1966088 | tf_op jit(solution)/shard_map/ppermute | solution.py:32
  6.3 9.4 %collective-permute-start.1 = (f32[10,16,256]{2,1,0:T(8,128)}, f32[10,16,256]{2,1,0:T(8,128)S(1)}, u32[]{:S(2)}, u32[]{:S(2)}) collective-permute-start(f32[10,16,256]{2,1,0:T(8,128)} %get-tuple-element.83), channel_id=1, source_target_pairs={{0,1},{1,2},{2,3},{3,0},{4,5},{5,6},{6,7},{7,4},{8,9},{9,10},{10,1... | collective-permute-start | bytes 491528 | tf_op jit(solution)/shard_map/ppermute | solution.py:33
  6.5 9.2 %collective-permute-start.2 = (f32[10,16,256]{2,1,0:T(8,128)}, f32[10,16,256]{2,1,0:T(8,128)S(1)}, u32[]{:S(2)}, u32[]{:S(2)}) collective-permute-start(f32[10,16,256]{2,1,0:T(8,128)} %get-tuple-element.84), channel_id=1, source_target_pairs={{0,3},{1,0},{2,1},{3,2},{4,7},{5,4},{6,5},{7,6},{8,11},{9,8},{10,9... | collective-permute-start | bytes 491528 | tf_op jit(solution)/shard_map/ppermute | solution.py:34
  35.1 16.2 %collective-permute-start.7 = (f32[3,8,16,128]{3,2,1,0:T(8,128)}, f32[3,8,16,128]{3,2,1,0:T(8,128)S(1)}, u32[]{:S(2)}, u32[]{:S(2)}) collective-permute-start(f32[3,8,16,128]{3,2,1,0:T(8,128)} %get-tuple-element.97), channel_id=1, source_target_pairs={{8,16},{9,17},{10,18},{11,19},{12,20},{13,21},{14,22},{15,23}} | collective-permute-start | bytes 589832 | tf_op jit(solution)/shard_map/ppermute | solution.py:49
  36.4 14.9 %collective-permute-start.8 = (f32[3,2,16,128]{3,2,1,0:T(8,128)}, f32[3,2,16,128]{3,2,1,0:T(8,128)S(1)}, u32[]{:S(2)}, u32[]{:S(2)}) collective-permute-start(f32[3,2,16,128]{3,2,1,0:T(8,128)} %get-tuple-element.98), channel_id=1, source_target_pairs={{8,20},{9,21},{10,22},{11,23},{12,16},{13,17},{14,18},{15,19}} | collective-permute-start | bytes 147464 | tf_op jit(solution)/shard_map/ppermute | solution.py:49
  37.7 11.9 %collective-permute-start.9 = (f32[3,8,128]{2,1,0:T(8,128)}, f32[3,8,128]{2,1,0:T(8,128)S(1)}, u32[]{:S(2)}, u32[]{:S(2)}) collective-permute-start(f32[3,8,128]{2,1,0:T(8,128)} %get-tuple-element.99), channel_id=1, source_target_pairs={{8,17},{9,18},{10,19},{11,16},{12,21},{13,22},{14,23},{15,20}} | collective-permute-start | bytes 36872 | tf_op jit(solution)/shard_map/ppermute | solution.py:49
  39.0 12.3 %collective-permute-start.10 = (f32[3,8,128]{2,1,0:T(8,128)}, f32[3,8,128]{2,1,0:T(8,128)S(1)}, u32[]{:S(2)}, u32[]{:S(2)}) collective-permute-start(f32[3,8,128]{2,1,0:T(8,128)} %get-tuple-element.100), channel_id=1, source_target_pairs={{8,19},{9,16},{10,17},{11,18},{12,23},{13,20},{14,21},{15,22}} | collective-permute-start | bytes 36872 | tf_op jit(solution)/shard_map/ppermute | solution.py:49
  55.8 6.8 %collective-permute-start.11 = (f32[3,8,16,128]{3,2,1,0:T(8,128)}, f32[3,8,16,128]{3,2,1,0:T(8,128)S(1)}, u32[]{:S(2)}, u32[]{:S(2)}) collective-permute-start(f32[3,8,16,128]{3,2,1,0:T(8,128)} %get-tuple-element.101), channel_id=1, source_target_pairs={{16,24},{17,25},{18,26},{19,27},{20,28},{21,29},{22,30},{23,31}} | collective-permute-start | bytes 589832 | tf_op jit(solution)/shard_map/ppermute | solution.py:49
  67.5 9.6 %collective-permute-start.15 = (f32[3,2,16,128]{3,2,1,0:T(8,128)}, f32[3,2,16,128]{3,2,1,0:T(8,128)S(1)}, u32[]{:S(2)}, u32[]{:S(2)}) collective-permute-start(f32[3,2,16,128]{3,2,1,0:T(8,128)} %get-tuple-element.110), channel_id=1, source_target_pairs={{0,4},{4,0},{1,5},{5,1},{2,6},{6,2},{3,7},{7,3},{8,12},{12,8},{9,1... | collective-permute-start | bytes 147464 | tf_op jit(solution)/shard_map/ppermute | solution.py:32
  86.8 6.7 %collective-permute-start.18 = (f32[3,2,32,256]{3,2,1,0:T(8,128)}, f32[3,2,32,256]{3,2,1,0:T(8,128)S(1)}, u32[]{:S(2)}, u32[]{:S(2)}) collective-permute-start(f32[3,2,32,256]{3,2,1,0:T(8,128)} %get-tuple-element.114), channel_id=1, source_target_pairs={{0,4},{4,0},{1,5},{5,1},{2,6},{6,2},{3,7},{7,3},{8,12},{12,8},{9,1... | collective-permute-start | bytes 589832 | tf_op jit(solution)/shard_map/ppermute | solution.py:32
  87.4 6.1 %collective-permute-start.20 = (f32[3,16,256]{2,1,0:T(8,128)}, f32[3,16,256]{2,1,0:T(8,128)S(1)}, u32[]{:S(2)}, u32[]{:S(2)}) collective-permute-start(f32[3,16,256]{2,1,0:T(8,128)} %get-tuple-element.116), channel_id=1, source_target_pairs={{0,3},{1,0},{2,1},{3,2},{4,7},{5,4},{6,5},{7,6},{8,11},{9,8},{10,9... | collective-permute-start | bytes 147464 | tf_op jit(solution)/shard_map/ppermute | solution.py:34
  101.8 27.1 %collective-permute-start.21 = (f32[3,16,32,256]{3,2,1,0:T(8,128)}, f32[3,16,32,256]{3,2,1,0:T(8,128)S(1)}, u32[]{:S(2)}, u32[]{:S(2)}) collective-permute-start(f32[3,16,32,256]{3,2,1,0:T(8,128)} %get-tuple-element.121.refs_13_.refs_21_), channel_id=1, source_target_pairs={{0,8},{1,9},{2,10},{3,11},{4,12},{5,13},{6,14},{7,15},{8,16},{9,17... | collective-permute-start | bytes 4718600 | tf_op jit(solution)/shard_map/ppermute | solution.py:49
  103.8 19.5 %collective-permute-start.25 = (f32[4,2,32,256]{3,2,1,0:T(8,128)}, f32[4,2,32,256]{3,2,1,0:T(8,128)S(1)}, u32[]{:S(2)}, u32[]{:S(2)}) collective-permute-start(f32[4,2,32,256]{3,2,1,0:T(8,128)} %get-tuple-element.122), channel_id=1, source_target_pairs={{0,4},{4,0},{1,5},{5,1},{2,6},{6,2},{3,7},{7,3},{8,12},{12,8},{9,1... | collective-permute-start | bytes 786440 | tf_op jit(solution)/shard_map/ppermute | solution.py:32
  105.3 23.6 %collective-permute-start.22 = (f32[4,2,32,256]{3,2,1,0:T(8,128)}, f32[4,2,32,256]{3,2,1,0:T(8,128)S(1)}, u32[]{:S(2)}, u32[]{:S(2)}) collective-permute-start(f32[4,2,32,256]{3,2,1,0:T(8,128)} %get-tuple-element.122), channel_id=1, source_target_pairs={{0,12},{1,13},{2,14},{3,15},{4,8},{5,9},{6,10},{7,11},{8,20},{9,21... | collective-permute-start | bytes 786440 | tf_op jit(solution)/shard_map/ppermute | solution.py:49
  107.3 7.1 %collective-permute-start.23 = (f32[4,16,256]{2,1,0:T(8,128)}, f32[4,16,256]{2,1,0:T(8,128)S(1)}, u32[]{:S(2)}, u32[]{:S(2)}) collective-permute-start(f32[4,16,256]{2,1,0:T(8,128)} %get-tuple-element.123), channel_id=1, source_target_pairs={{0,9},{1,10},{2,11},{3,8},{4,13},{5,14},{6,15},{7,12},{8,17},{9,18... | collective-permute-start | bytes 196616 | tf_op jit(solution)/shard_map/ppermute | solution.py:49
  112.2 6.3 %collective-permute-start.27 = (f32[4,16,256]{2,1,0:T(8,128)}, f32[4,16,256]{2,1,0:T(8,128)S(1)}, u32[]{:S(2)}, u32[]{:S(2)}) collective-permute-start(f32[4,16,256]{2,1,0:T(8,128)} %get-tuple-element.124), channel_id=1, source_target_pairs={{0,3},{1,0},{2,1},{3,2},{4,7},{5,4},{6,5},{7,6},{8,11},{9,8},{10,9... | collective-permute-start | bytes 196616 | tf_op jit(solution)/shard_map/ppermute | solution.py:34
  114.4 8.8 %collective-permute-start.24 = (f32[4,16,256]{2,1,0:T(8,128)}, f32[4,16,256]{2,1,0:T(8,128)S(1)}, u32[]{:S(2)}, u32[]{:S(2)}) collective-permute-start(f32[4,16,256]{2,1,0:T(8,128)} %get-tuple-element.124), channel_id=1, source_target_pairs={{0,11},{1,8},{2,9},{3,10},{4,15},{5,12},{6,13},{7,14},{8,19},{9,16... | collective-permute-start | bytes 196616 | tf_op jit(solution)/shard_map/ppermute | solution.py:49
  144.7 15.5 %collective-permute-start.32 = (f32[3,8,16,128]{3,2,1,0:T(8,128)}, f32[3,8,16,128]{3,2,1,0:T(8,128)S(1)}, u32[]{:S(2)}, u32[]{:S(2)}) collective-permute-start(f32[3,8,16,128]{3,2,1,0:T(8,128)} %get-tuple-element.134), channel_id=1, source_target_pairs={{8,16},{9,17},{10,18},{11,19},{12,20},{13,21},{14,22},{15,23}} | collective-permute-start | bytes 589832 | tf_op jit(solution)/shard_map/ppermute | solution.py:49
  146.0 14.2 %collective-permute-start.33 = (f32[3,2,16,128]{3,2,1,0:T(8,128)}, f32[3,2,16,128]{3,2,1,0:T(8,128)S(1)}, u32[]{:S(2)}, u32[]{:S(2)}) collective-permute-start(f32[3,2,16,128]{3,2,1,0:T(8,128)} %get-tuple-element.135), channel_id=1, source_target_pairs={{8,20},{9,21},{10,22},{11,23},{12,16},{13,17},{14,18},{15,19}} | collective-permute-start | bytes 147464 | tf_op jit(solution)/shard_map/ppermute | solution.py:49
  147.3 11.2 %collective-permute-start.34 = (f32[3,8,128]{2,1,0:T(8,128)}, f32[3,8,128]{2,1,0:T(8,128)S(1)}, u32[]{:S(2)}, u32[]{:S(2)}) collective-permute-start(f32[3,8,128]{2,1,0:T(8,128)} %get-tuple-element.136), channel_id=1, source_target_pairs={{8,17},{9,18},{10,19},{11,16},{12,21},{13,22},{14,23},{15,20}} | collective-permute-start | bytes 36872 | tf_op jit(solution)/shard_map/ppermute | solution.py:49
  148.6 11.6 %collective-permute-start.35 = (f32[3,8,128]{2,1,0:T(8,128)}, f32[3,8,128]{2,1,0:T(8,128)S(1)}, u32[]{:S(2)}, u32[]{:S(2)}) collective-permute-start(f32[3,8,128]{2,1,0:T(8,128)} %get-tuple-element.137), channel_id=1, source_target_pairs={{8,19},{9,16},{10,17},{11,18},{12,23},{13,20},{14,21},{15,22}} | collective-permute-start | bytes 36872 | tf_op jit(solution)/shard_map/ppermute | solution.py:49
  164.8 6.8 %collective-permute-start.36 = (f32[3,8,16,128]{3,2,1,0:T(8,128)}, f32[3,8,16,128]{3,2,1,0:T(8,128)S(1)}, u32[]{:S(2)}, u32[]{:S(2)}) collective-permute-start(f32[3,8,16,128]{3,2,1,0:T(8,128)} %get-tuple-element.138), channel_id=1, source_target_pairs={{16,24},{17,25},{18,26},{19,27},{20,28},{21,29},{22,30},{23,31}} | collective-permute-start | bytes 589832 | tf_op jit(solution)/shard_map/ppermute | solution.py:49
  175.9 9.6 %collective-permute-start.40 = (f32[3,2,16,128]{3,2,1,0:T(8,128)}, f32[3,2,16,128]{3,2,1,0:T(8,128)S(1)}, u32[]{:S(2)}, u32[]{:S(2)}) collective-permute-start(f32[3,2,16,128]{3,2,1,0:T(8,128)} %get-tuple-element.148), channel_id=1, source_target_pairs={{0,4},{4,0},{1,5},{5,1},{2,6},{6,2},{3,7},{7,3},{8,12},{12,8},{9,1... | collective-permute-start | bytes 147464 | tf_op jit(solution)/shard_map/ppermute | solution.py:32
  197.4 6.7 %collective-permute-start.43 = (f32[3,2,32,256]{3,2,1,0:T(8,128)}, f32[3,2,32,256]{3,2,1,0:T(8,128)S(1)}, u32[]{:S(2)}, u32[]{:S(2)}) collective-permute-start(f32[3,2,32,256]{3,2,1,0:T(8,128)} %get-tuple-element.152), channel_id=1, source_target_pairs={{0,4},{4,0},{1,5},{5,1},{2,6},{6,2},{3,7},{7,3},{8,12},{12,8},{9,1... | collective-permute-start | bytes 589832 | tf_op jit(solution)/shard_map/ppermute | solution.py:32
  (68 other events, 179.7 us)

commit v4 on v2

--- a/solution.py
+++ b/solution.py
@@ -1,3 +1,5 @@
+import math
+
 import jax
 import jax.numpy as jnp
 from jax import lax
@@ -10,6 +12,7 @@
 TIME_STEP = 0.5
 PAD = 8
 CHUNK = 8
+ROOM = 4 << 20
 F32 = jnp.float32
 BF16 = jnp.bfloat16
 
@@ -500,6 +503,7 @@
 
 def call(kernel, name, first, args, outs, scratch, flops=0):
     moved = sum(4 * a.size for a in args)
+    room = moved + sum(4 * math.prod(dims) for dims in outs + scratch)
     return pl.pallas_call(
         kernel,
         name=name,
@@ -507,7 +511,7 @@
         in_specs=[pl.BlockSpec(memory_space=pltpu.SMEM)] + [pl.BlockSpec(memory_space=pltpu.VMEM)] * len(args),
         out_specs=[pl.BlockSpec(memory_space=pltpu.VMEM)] * len(outs),
         scratch_shapes=[pltpu.VMEM(dims, F32) for dims in scratch],
-        compiler_params=pltpu.CompilerParams(vmem_limit_bytes=56 << 20),
+        compiler_params=pltpu.CompilerParams(vmem_limit_bytes=min(room + ROOM, 56 << 20)),
         cost_estimate=pl.CostEstimate(flops=flops, bytes_accessed=moved, transcendentals=0),
     )(first, *args)
 

time: 204 us -> 160 us (0.78)
  Pallas kernels: 72.3 us -> 36.3 us
  local copies, waits for them, and re-layouts: 11.3 us -> 4.23 us
    pallas_call x14, Pallas kernels: 72.3 us -> 36.3 us  [call(): pl.pallas_call(kernel, name=name, out_shape=[jax.ShapeDtypeStruct(dims, F...]
    unnamed x92 -> x12, local copies, waits for them, and re-layouts: 11.3 us -> 4.23 us
  transfers between devices with their start and end apart: 46 -> 46, of which waited for: 23 -> 23; matrix products, arithmetic and copies ran while one was open for 0% -> 0% of each run, Pallas kernels for 2% -> 1%
where the time goes in v4:
time: 160 us; the launch traced here: 159 us
  waiting for transfers between devices  66.4 us (42%)
  starting transfers between devices  51.9 us (32%)
  Pallas kernels  36.3 us (23%)
  local copies, waits for them, and re-layouts  4.23 us (3%)
    pallas_call x14, Pallas kernels, call(): pl.pallas_call(kernel, name=name, out_shape=[jax.ShapeDtypeStruct(dims, F...  36.3 us
    ppermute x28, starting transfers between devices, permute(): return lax.ppermute(array, ('tm', 'gx', 'gy'), pairs)  33.7 us
    ppermute x28, waiting for transfers between devices, permute(): return lax.ppermute(array, ('tm', 'gx', 'gy'), pairs)  31.1 us
    ppermute x6, waiting for transfers between devices, swap_faces(): behind = lax.ppermute(y_last, 'gy', ring(gy, 1))  15.8 us
    ppermute x6, waiting for transfers between devices, swap_faces(): ahead = lax.ppermute(y_first, 'gy', ring(gy, -1))  13.7 us
    ppermute x6, starting transfers between devices, swap_faces(): behind = lax.ppermute(y_last, 'gy', ring(gy, 1))  6.28 us
    ppermute x6, starting transfers between devices, swap_faces(): lax.ppermute(a, 'gx', ring(gx, by))  6.08 us
    ppermute x6, starting transfers between devices, swap_faces(): ahead = lax.ppermute(y_first, 'gy', ring(gy, -1))  5.85 us
  transfers between devices with their start and end apart: 46, of which 23 were waited for; matrix products, arithmetic and copies ran while one was open for 0% of the time, Pallas kernels for 1%

profile of v4, /device:TPU:26, one launch (start us, length us, event | category | flops | bytes accessed | tf_op | source)
XLA Modules:
  0.0 159.3 jit_solution(5890093618321575935)
XLA Ops:
  10.8 5.5 %collective-permute-done.1.behind.refs_3_ = f32[10,16,256]{2,1,0:T(8,128)S(1)} collective-permute-done((f32[10,16,256]{2,1,0:T(8,128)S(1)}, f32[10,16,256]{2,1,0:T(8,128)S(1)}, u32[]{:S(2)}, u32[]{:S(2)}) %collective-permute-start.1) | collective-permute-done | bytes 163872 | tf_op jit(solution)/shard_map/ppermute | solution.py:36
  16.3 5.8 %collective-permute-done.x_faces.refs_2_ = f32[10,2,32,256]{3,2,1,0:T(8,128)S(1)} collective-permute-done((f32[10,2,32,256]{3,2,1,0:T(8,128)S(1)}, f32[10,2,32,256]{3,2,1,0:T(8,128)S(1)}, u32[]{:S(2)}, u32[]{:S(2)}) %collective-permute-start) | collective-permute-done | bytes 655392 | tf_op jit(solution)/shard_map/ppermute | solution.py:35
  22.1 4.8 %offset_start.1 = (f32[3,8,16,128]{3,2,1,0:T(8,128)S(1)}, f32[9,8,16,128]{3,2,1,0:T(8,128)S(1)}, f32[3,2,16,128]{3,2,1,0:T(8,128)S(1)}, f32[3,8,128]{2,1,0:T(8,1...) custom-call(f32[2]{0:T(128)S(1)} %add_convert_fusion.first.refs_0_, ...), custom_call_target="tpu_custom_call" | custom-call | flops 40000000 | bytes 5898240 | tf_op jit(solution)/shard_map/offset_start/pallas_call | solution.py:507
  35.4 6.7 %collective-permute-done.9.refs_3_.refs_7_ = f32[3,8,128]{2,1,0:T(8,128)S(1)} collective-permute-done((f32[3,8,128]{2,1,0:T(8,128)S(1)}, f32[3,8,128]{2,1,0:T(8,128)S(1)}, u32[]{:S(2)}, u32[]{:S(2)}) %collective-permute-start.9) | collective-permute-done | bytes 12320 | tf_op jit(solution)/shard_map/ppermute | solution.py:52
  53.1 2.9 %collective-permute-start.16 = (f32[3,8,128]{2,1,0:T(8,128)S(1)}, f32[3,8,128]{2,1,0:T(8,128)S(1)}, u32[]{:S(2)}, u32[]{:S(2)}) collective-permute-start(f32[3,8,128]{2,1,0:T(8,128)S(1)} %get-tuple-element.111), channel_id=1, source_target_pairs={{0,1},{1,2},{2,3},{3,0},{4,5},{5,6},{6,7},{7,4},{8,9},{9,10},{10,1... | collective-permute-start | bytes 36872 | tf_op jit(solution)/shard_map/ppermute | solution.py:36
  57.4 4.1 %collective-permute-done.17.refs_14_ = f32[3,8,128]{2,1,0:T(8,128)S(1)} collective-permute-done((f32[3,8,128]{2,1,0:T(8,128)S(1)}, f32[3,8,128]{2,1,0:T(8,128)S(1)}, u32[]{:S(2)}, u32[]{:S(2)}) %collective-permute-start.17) | collective-permute-done | bytes 12320 | tf_op jit(solution)/shard_map/ppermute | solution.py:37
  61.5 4.9 %middle.2 = (f32[3,16,32,256]{3,2,1,0:T(8,128)S(1)}, f32[3,2,32,256]{3,2,1,0:T(8,128)S(1)}, f32[3,16,256]{2,1,0:T(8,128)S(1)}, f32[3,16,256]{2,1,0:T(8,128)S(1)}...) custom-call(f32[2]{0:T(128)S(1)} %add_convert_fusion.first.refs_0_, ...), custom_call_target="tpu_custom_call" | custom-call | flops 60000000 | bytes 6242304 | tf_op jit(solution)/shard_map/middle/pallas_call | solution.py:507
  67.0 2.0 %collective-permute-start.20 = (f32[3,16,256]{2,1,0:T(8,128)S(1)}, f32[3,16,256]{2,1,0:T(8,128)S(1)}, u32[]{:S(2)}, u32[]{:S(2)}) collective-permute-start(f32[3,16,256]{2,1,0:T(8,128)S(1)} %get-tuple-element.116), channel_id=1, source_target_pairs={{0,3},{1,0},{2,1},{3,2},{4,7},{5,4},{6,5},{7,6},{8,11},{9,8},{10,9... | collective-permute-start | bytes 147464 | tf_op jit(solution)/shard_map/ppermute | solution.py:37
  69.0 2.2 %collective-permute-done.19.refs_7_.u1_b.refs_12_ = f32[3,16,256]{2,1,0:T(8,128)S(1)} collective-permute-done((f32[3,16,256]{2,1,0:T(8,128)S(1)}, f32[3,16,256]{2,1,0:T(8,128)S(1)}, u32[]{:S(2)}, u32[]{:S(2)}) %collective-permute-start.19) | collective-permute-done | bytes 49184 | tf_op jit(solution)/shard_map/ppermute | solution.py:36
  72.9 4.0 %finish.2 = (f32[3,16,32,256]{3,2,1,0:T(8,128)S(1)}, f32[4,2,32,256]{3,2,1,0:T(8,128)S(1)}, f32[4,16,256]{2,1,0:T(8,128)S(1)}, f32[4,16,256]{2,1,0:T(8,128)S(1)}, f32[3,8,16,128]{3,2,1,0:T(8,128)S(1)}) custom-call(f32[2]{0:T(128)S(1)} %add_convert_fusion.first.refs_0_, f32[3,16,32,256]{3,2,1,0:T(8,128)S(1)} %copy-done.1, ...), custom_call_target="tpu_custom_call" | custom-call | flops 40000000 | bytes 6291456 | tf_op jit(solution)/shard_map/finish/pallas_call | solution.py:507
  76.8 1.9 %collective-permute-start.21 = (f32[3,16,32,256]{3,2,1,0:T(8,128)S(1)}, f32[3,16,32,256]{3,2,1,0:T(8,128)S(1)}, u32[]{:S(2)}, u32[]{:S(2)}) collective-permute-start(f32[3,16,32,256]{3,2,1,0:T(8,128)S(1)} %get-tuple-element.121.u2.refs_14_), channel_id=1, source_target_pairs={{0,8},{1,9},{2,10},{3,11},{4,12},{5,13},{6,14},{7,15},{8,16},{9,17... | collective-permute-start | bytes 4718600 | tf_op jit(solution)/shard_map/ppermute | solution.py:52
  82.3 1.9 %collective-permute-start.23 = (f32[4,16,256]{2,1,0:T(8,128)S(1)}, f32[4,16,256]{2,1,0:T(8,128)S(1)}, u32[]{:S(2)}, u32[]{:S(2)}) collective-permute-start(f32[4,16,256]{2,1,0:T(8,128)S(1)} %get-tuple-element.123), channel_id=1, source_target_pairs={{0,9},{1,10},{2,11},{3,8},{4,13},{5,14},{6,15},{7,12},{8,17},{9,18... | collective-permute-start | bytes 196616 | tf_op jit(solution)/shard_map/ppermute | solution.py:52
  84.3 3.0 %collective-permute-done.26.u2_b.refs_16_ = f32[4,16,256]{2,1,0:T(8,128)S(1)} collective-permute-done((f32[4,16,256]{2,1,0:T(8,128)S(1)}, f32[4,16,256]{2,1,0:T(8,128)S(1)}, u32[]{:S(2)}, u32[]{:S(2)}) %collective-permute-start.26) | collective-permute-done | bytes 65568 | tf_op jit(solution)/shard_map/ppermute | solution.py:36
  91.1 2.2 %collective-permute-done.27.u2_a.refs_17_ = f32[4,16,256]{2,1,0:T(8,128)S(1)} collective-permute-done((f32[4,16,256]{2,1,0:T(8,128)S(1)}, f32[4,16,256]{2,1,0:T(8,128)S(1)}, u32[]{:S(2)}, u32[]{:S(2)}) %collective-permute-start.27) | collective-permute-done | bytes 65568 | tf_op jit(solution)/shard_map/ppermute | solution.py:37
  93.4 4.5 %collective-permute-done.24.u0_a.refs_9_ = f32[4,16,256]{2,1,0:T(8,128)S(1)} collective-permute-done((f32[4,16,256]{2,1,0:T(8,128)S(1)}, f32[4,16,256]{2,1,0:T(8,128)S(1)}, u32[]{:S(2)}, u32[]{:S(2)}) %collective-permute-start.24) | collective-permute-done | bytes 65568 | tf_op jit(solution)/shard_map/ppermute | solution.py:52
  97.8 5.9 %collective-permute-done.22.u0_x.refs_7_ = f32[4,2,32,256]{3,2,1,0:T(8,128)S(1)} collective-permute-done((f32[4,2,32,256]{3,2,1,0:T(8,128)S(1)}, f32[4,2,32,256]{3,2,1,0:T(8,128)S(1)}, u32[]{:S(2)}, u32[]{:S(2)}) %collective-permute-start.22) | collective-permute-done | bytes 262176 | tf_op jit(solution)/shard_map/ppermute | solution.py:52
  103.8 4.9 %offset_later.1 = (f32[3,8,16,128]{3,2,1,0:T(8,128)S(1)}, f32[3,8,16,128]{3,2,1,0:T(8,128)S(1)}, f32[3,2,16,128]{3,2,1,0:T(8,128)S(1)}, f32[3,8,128]{2,1,0:T(8,1...) custom-call(f32[2]{0:T(128)S(1)} %add_convert_fusion.first.refs_0_, ...), custom_call_target="tpu_custom_call" | custom-call | flops 40000000 | bytes 9928704 | tf_op jit(solution)/shard_map/offset_later/pallas_call | solution.py:507
  117.1 5.9 %collective-permute-done.34.refs_3_.refs_7_ = f32[3,8,128]{2,1,0:T(8,128)S(1)} collective-permute-done((f32[3,8,128]{2,1,0:T(8,128)S(1)}, f32[3,8,128]{2,1,0:T(8,128)S(1)}, u32[]{:S(2)}, u32[]{:S(2)}) %collective-permute-start.34) | collective-permute-done | bytes 12320 | tf_op jit(solution)/shard_map/ppermute | solution.py:52
  133.8 3.1 %collective-permute-start.41 = (f32[3,8,128]{2,1,0:T(8,128)S(1)}, f32[3,8,128]{2,1,0:T(8,128)S(1)}, u32[]{:S(2)}, u32[]{:S(2)}) collective-permute-start(f32[3,8,128]{2,1,0:T(8,128)S(1)} %get-tuple-element.149), channel_id=1, source_target_pairs={{0,1},{1,2},{2,3},{3,0},{4,5},{5,6},{6,7},{7,4},{8,9},{9,10},{10,1... | collective-permute-start | bytes 36872 | tf_op jit(solution)/shard_map/ppermute | solution.py:36
  138.3 4.1 %collective-permute-done.42.refs_25_ = f32[3,8,128]{2,1,0:T(8,128)S(1)} collective-permute-done((f32[3,8,128]{2,1,0:T(8,128)S(1)}, f32[3,8,128]{2,1,0:T(8,128)S(1)}, u32[]{:S(2)}, u32[]{:S(2)}) %collective-permute-start.42) | collective-permute-done | bytes 12320 | tf_op jit(solution)/shard_map/ppermute | solution.py:37
  142.4 5.8 %middle.3 = (f32[3,16,32,256]{3,2,1,0:T(8,128)S(1)}, f32[3,2,32,256]{3,2,1,0:T(8,128)S(1)}, f32[3,16,256]{2,1,0:T(8,128)S(1)}, f32[3,16,256]{2,1,0:T(8,128)S(1)}...) custom-call(f32[2]{0:T(128)S(1)} %add_convert_fusion.first.refs_0_, ...), custom_call_target="tpu_custom_call" | custom-call | flops 60000000 | bytes 10469376 | tf_op jit(solution)/shard_map/middle/pallas_call | solution.py:507
  148.9 2.0 %collective-permute-start.45 = (f32[3,16,256]{2,1,0:T(8,128)S(1)}, f32[3,16,256]{2,1,0:T(8,128)S(1)}, u32[]{:S(2)}, u32[]{:S(2)}) collective-permute-start(f32[3,16,256]{2,1,0:T(8,128)S(1)} %get-tuple-element.154), channel_id=1, source_target_pairs={{0,3},{1,0},{2,1},{3,2},{4,7},{5,4},{6,5},{7,6},{8,11},{9,8},{10,9... | collective-permute-start | bytes 147464 | tf_op jit(solution)/shard_map/ppermute | solution.py:37
  150.9 2.2 %collective-permute-done.44.refs_7_ = f32[3,16,256]{2,1,0:T(8,128)S(1)} collective-permute-done((f32[3,16,256]{2,1,0:T(8,128)S(1)}, f32[3,16,256]{2,1,0:T(8,128)S(1)}, u32[]{:S(2)}, u32[]{:S(2)}) %collective-permute-start.44) | collective-permute-done | bytes 49184 | tf_op jit(solution)/shard_map/ppermute | solution.py:36
  154.7 4.6 %finish.3 = f32[3,16,32,256]{3,2,1,0:T(8,128)} custom-call(f32[2]{0:T(128)S(1)} %add_convert_fusion.first.refs_0_, f32[3,16,32,256]{3,2,1,0:T(8,128)S(1)} %copy-done.1, f32[10,2,32,256]{3,2,1,0:T(8,128)S(1)} %collective-permute-done.x_faces.refs_2_, f32[10,16,256]{2,1,0:T(8,128)S(1)} %collective-permute-done.1.behind.refs_3_, ...), custom_call_target="tpu_custom_call" | custom-call | flops 40000000 | bytes 6291456 | tf_op jit(solution)/shard_map/finish/pallas_call | solution.py:507
  (95 shorter events, 64.0 us)
Async XLA Ops:
  5.6 16.5 %collective-permute-start = (f32[10,2,32,256]{3,2,1,0:T(8,128)S(1)}, f32[10,2,32,256]{3,2,1,0:T(8,128)S(1)}, u32[]{:S(2)}, u32[]{:S(2)}) collective-permute-start(f32[10,2,32,256]{3,2,1,0:T(8,128)S(1)} %get-tuple-element.82), channel_id=1, source_target_pairs={{0,4},{4,0},{1,5},{5,1},{2,6},{6,2},{3,7},{7,3},{8,12},{12,8},{9,1... | collective-permute-start | bytes 1966088 | tf_op jit(solution)/shard_map/ppermute | solution.py:35
  7.2 9.2 %collective-permute-start.1 = (f32[10,16,256]{2,1,0:T(8,128)S(1)}, f32[10,16,256]{2,1,0:T(8,128)S(1)}, u32[]{:S(2)}, u32[]{:S(2)}) collective-permute-start(f32[10,16,256]{2,1,0:T(8,128)S(1)} %get-tuple-element.83), channel_id=1, source_target_pairs={{0,1},{1,2},{2,3},{3,0},{4,5},{5,6},{6,7},{7,4},{8,9},{9,10},{10,1... | collective-permute-start | bytes 491528 | tf_op jit(solution)/shard_map/ppermute | solution.py:36
  7.4 9.0 %collective-permute-start.2 = (f32[10,16,256]{2,1,0:T(8,128)S(1)}, f32[10,16,256]{2,1,0:T(8,128)S(1)}, u32[]{:S(2)}, u32[]{:S(2)}) collective-permute-start(f32[10,16,256]{2,1,0:T(8,128)S(1)} %get-tuple-element.84), channel_id=1, source_target_pairs={{0,3},{1,0},{2,1},{3,2},{4,7},{5,4},{6,5},{7,6},{8,11},{9,8},{10,9... | collective-permute-start | bytes 491528 | tf_op jit(solution)/shard_map/ppermute | solution.py:37
  30.2 13.6 %collective-permute-start.7 = (f32[3,8,16,128]{3,2,1,0:T(8,128)S(1)}, f32[3,8,16,128]{3,2,1,0:T(8,128)S(1)}, u32[]{:S(2)}, u32[]{:S(2)}) collective-permute-start(f32[3,8,16,128]{3,2,1,0:T(8,128)S(1)} %get-tuple-element.97), channel_id=1, source_target_pairs={{8,16},{9,17},{10,18},{11,19},{12,20},{13,21},{14,22},{15,23}} | collective-permute-start | bytes 589832 | tf_op jit(solution)/shard_map/ppermute | solution.py:52
  31.5 12.3 %collective-permute-start.8 = (f32[3,2,16,128]{3,2,1,0:T(8,128)S(1)}, f32[3,2,16,128]{3,2,1,0:T(8,128)S(1)}, u32[]{:S(2)}, u32[]{:S(2)}) collective-permute-start(f32[3,2,16,128]{3,2,1,0:T(8,128)S(1)} %get-tuple-element.98), channel_id=1, source_target_pairs={{8,20},{9,21},{10,22},{11,23},{12,16},{13,17},{14,18},{15,19}} | collective-permute-start | bytes 147464 | tf_op jit(solution)/shard_map/ppermute | solution.py:52
  32.8 9.3 %collective-permute-start.9 = (f32[3,8,128]{2,1,0:T(8,128)S(1)}, f32[3,8,128]{2,1,0:T(8,128)S(1)}, u32[]{:S(2)}, u32[]{:S(2)}) collective-permute-start(f32[3,8,128]{2,1,0:T(8,128)S(1)} %get-tuple-element.99), channel_id=1, source_target_pairs={{8,17},{9,18},{10,19},{11,16},{12,21},{13,22},{14,23},{15,20}} | collective-permute-start | bytes 36872 | tf_op jit(solution)/shard_map/ppermute | solution.py:52
  34.1 9.7 %collective-permute-start.10 = (f32[3,8,128]{2,1,0:T(8,128)S(1)}, f32[3,8,128]{2,1,0:T(8,128)S(1)}, u32[]{:S(2)}, u32[]{:S(2)}) collective-permute-start(f32[3,8,128]{2,1,0:T(8,128)S(1)} %get-tuple-element.100), channel_id=1, source_target_pairs={{8,19},{9,16},{10,17},{11,18},{12,23},{13,20},{14,21},{15,22}} | collective-permute-start | bytes 36872 | tf_op jit(solution)/shard_map/ppermute | solution.py:52
  44.6 6.6 %collective-permute-start.11 = (f32[3,8,16,128]{3,2,1,0:T(8,128)S(1)}, f32[3,8,16,128]{3,2,1,0:T(8,128)S(1)}, u32[]{:S(2)}, u32[]{:S(2)}) collective-permute-start(f32[3,8,16,128]{3,2,1,0:T(8,128)S(1)} %get-tuple-element.101), channel_id=1, source_target_pairs={{16,24},{17,25},{18,26},{19,27},{20,28},{21,29},{22,30},{23,31}} | collective-permute-start | bytes 589832 | tf_op jit(solution)/shard_map/ppermute | solution.py:52
  52.1 9.4 %collective-permute-start.15 = (f32[3,2,16,128]{3,2,1,0:T(8,128)S(1)}, f32[3,2,16,128]{3,2,1,0:T(8,128)S(1)}, u32[]{:S(2)}, u32[]{:S(2)}) collective-permute-start(f32[3,2,16,128]{3,2,1,0:T(8,128)S(1)} %get-tuple-element.110), channel_id=1, source_target_pairs={{0,4},{4,0},{1,5},{5,1},{2,6},{6,2},{3,7},{7,3},{8,12},{12,8},{9,1... | collective-permute-start | bytes 147464 | tf_op jit(solution)/shard_map/ppermute | solution.py:35
  66.4 6.5 %collective-permute-start.18 = (f32[3,2,32,256]{3,2,1,0:T(8,128)S(1)}, f32[3,2,32,256]{3,2,1,0:T(8,128)S(1)}, u32[]{:S(2)}, u32[]{:S(2)}) collective-permute-start(f32[3,2,32,256]{3,2,1,0:T(8,128)S(1)} %get-tuple-element.114), channel_id=1, source_target_pairs={{0,4},{4,0},{1,5},{5,1},{2,6},{6,2},{3,7},{7,3},{8,12},{12,8},{9,1... | collective-permute-start | bytes 589832 | tf_op jit(solution)/shard_map/ppermute | solution.py:35
  67.0 5.9 %collective-permute-start.20 = (f32[3,16,256]{2,1,0:T(8,128)S(1)}, f32[3,16,256]{2,1,0:T(8,128)S(1)}, u32[]{:S(2)}, u32[]{:S(2)}) collective-permute-start(f32[3,16,256]{2,1,0:T(8,128)S(1)} %get-tuple-element.116), channel_id=1, source_target_pairs={{0,3},{1,0},{2,1},{3,2},{4,7},{5,4},{6,5},{7,6},{8,11},{9,8},{10,9... | collective-permute-start | bytes 147464 | tf_op jit(solution)/shard_map/ppermute | solution.py:37
  76.8 26.9 %collective-permute-start.21 = (f32[3,16,32,256]{3,2,1,0:T(8,128)S(1)}, f32[3,16,32,256]{3,2,1,0:T(8,128)S(1)}, u32[]{:S(2)}, u32[]{:S(2)}) collective-permute-start(f32[3,16,32,256]{3,2,1,0:T(8,128)S(1)} %get-tuple-element.121.u2.refs_14_), channel_id=1, source_target_pairs={{0,8},{1,9},{2,10},{3,11},{4,12},{5,13},{6,14},{7,15},{8,16},{9,17... | collective-permute-start | bytes 4718600 | tf_op jit(solution)/shard_map/ppermute | solution.py:52
  78.8 19.1 %collective-permute-start.25 = (f32[4,2,32,256]{3,2,1,0:T(8,128)S(1)}, f32[4,2,32,256]{3,2,1,0:T(8,128)S(1)}, u32[]{:S(2)}, u32[]{:S(2)}) collective-permute-start(f32[4,2,32,256]{3,2,1,0:T(8,128)S(1)} %get-tuple-element.122), channel_id=1, source_target_pairs={{0,4},{4,0},{1,5},{5,1},{2,6},{6,2},{3,7},{7,3},{8,12},{12,8},{9,1... | collective-permute-start | bytes 786440 | tf_op jit(solution)/shard_map/ppermute | solution.py:35
  80.4 23.4 %collective-permute-start.22 = (f32[4,2,32,256]{3,2,1,0:T(8,128)S(1)}, f32[4,2,32,256]{3,2,1,0:T(8,128)S(1)}, u32[]{:S(2)}, u32[]{:S(2)}) collective-permute-start(f32[4,2,32,256]{3,2,1,0:T(8,128)S(1)} %get-tuple-element.122), channel_id=1, source_target_pairs={{0,12},{1,13},{2,14},{3,15},{4,8},{5,9},{6,10},{7,11},{8,20},{9,21... | collective-permute-start | bytes 786440 | tf_op jit(solution)/shard_map/ppermute | solution.py:52
  82.3 6.9 %collective-permute-start.23 = (f32[4,16,256]{2,1,0:T(8,128)S(1)}, f32[4,16,256]{2,1,0:T(8,128)S(1)}, u32[]{:S(2)}, u32[]{:S(2)}) collective-permute-start(f32[4,16,256]{2,1,0:T(8,128)S(1)} %get-tuple-element.123), channel_id=1, source_target_pairs={{0,9},{1,10},{2,11},{3,8},{4,13},{5,14},{6,15},{7,12},{8,17},{9,18... | collective-permute-start | bytes 196616 | tf_op jit(solution)/shard_map/ppermute | solution.py:52
  87.3 6.1 %collective-permute-start.27 = (f32[4,16,256]{2,1,0:T(8,128)S(1)}, f32[4,16,256]{2,1,0:T(8,128)S(1)}, u32[]{:S(2)}, u32[]{:S(2)}) collective-permute-start(f32[4,16,256]{2,1,0:T(8,128)S(1)} %get-tuple-element.124), channel_id=1, source_target_pairs={{0,3},{1,0},{2,1},{3,2},{4,7},{5,4},{6,5},{7,6},{8,11},{9,8},{10,9... | collective-permute-start | bytes 196616 | tf_op jit(solution)/shard_map/ppermute | solution.py:37
  89.2 8.6 %collective-permute-start.24 = (f32[4,16,256]{2,1,0:T(8,128)S(1)}, f32[4,16,256]{2,1,0:T(8,128)S(1)}, u32[]{:S(2)}, u32[]{:S(2)}) collective-permute-start(f32[4,16,256]{2,1,0:T(8,128)S(1)} %get-tuple-element.124), channel_id=1, source_target_pairs={{0,11},{1,8},{2,9},{3,10},{4,15},{5,12},{6,13},{7,14},{8,19},{9,16... | collective-permute-start | bytes 196616 | tf_op jit(solution)/shard_map/ppermute | solution.py:52
  111.9 12.8 %collective-permute-start.32 = (f32[3,8,16,128]{3,2,1,0:T(8,128)S(1)}, f32[3,8,16,128]{3,2,1,0:T(8,128)S(1)}, u32[]{:S(2)}, u32[]{:S(2)}) collective-permute-start(f32[3,8,16,128]{3,2,1,0:T(8,128)S(1)} %get-tuple-element.134), channel_id=1, source_target_pairs={{8,16},{9,17},{10,18},{11,19},{12,20},{13,21},{14,22},{15,23}} | collective-permute-start | bytes 589832 | tf_op jit(solution)/shard_map/ppermute | solution.py:52
  113.2 11.5 %collective-permute-start.33 = (f32[3,2,16,128]{3,2,1,0:T(8,128)S(1)}, f32[3,2,16,128]{3,2,1,0:T(8,128)S(1)}, u32[]{:S(2)}, u32[]{:S(2)}) collective-permute-start(f32[3,2,16,128]{3,2,1,0:T(8,128)S(1)} %get-tuple-element.135), channel_id=1, source_target_pairs={{8,20},{9,21},{10,22},{11,23},{12,16},{13,17},{14,18},{15,19}} | collective-permute-start | bytes 147464 | tf_op jit(solution)/shard_map/ppermute | solution.py:52
  114.5 8.5 %collective-permute-start.34 = (f32[3,8,128]{2,1,0:T(8,128)S(1)}, f32[3,8,128]{2,1,0:T(8,128)S(1)}, u32[]{:S(2)}, u32[]{:S(2)}) collective-permute-start(f32[3,8,128]{2,1,0:T(8,128)S(1)} %get-tuple-element.136), channel_id=1, source_target_pairs={{8,17},{9,18},{10,19},{11,16},{12,21},{13,22},{14,23},{15,20}} | collective-permute-start | bytes 36872 | tf_op jit(solution)/shard_map/ppermute | solution.py:52
  115.8 8.9 %collective-permute-start.35 = (f32[3,8,128]{2,1,0:T(8,128)S(1)}, f32[3,8,128]{2,1,0:T(8,128)S(1)}, u32[]{:S(2)}, u32[]{:S(2)}) collective-permute-start(f32[3,8,128]{2,1,0:T(8,128)S(1)} %get-tuple-element.137), channel_id=1, source_target_pairs={{8,19},{9,16},{10,17},{11,18},{12,23},{13,20},{14,21},{15,22}} | collective-permute-start | bytes 36872 | tf_op jit(solution)/shard_map/ppermute | solution.py:52
  125.6 6.6 %collective-permute-start.36 = (f32[3,8,16,128]{3,2,1,0:T(8,128)S(1)}, f32[3,8,16,128]{3,2,1,0:T(8,128)S(1)}, u32[]{:S(2)}, u32[]{:S(2)}) collective-permute-start(f32[3,8,16,128]{3,2,1,0:T(8,128)S(1)} %get-tuple-element.138), channel_id=1, source_target_pairs={{16,24},{17,25},{18,26},{19,27},{20,28},{21,29},{22,30},{23,31}} | collective-permute-start | bytes 589832 | tf_op jit(solution)/shard_map/ppermute | solution.py:52
  133.1 9.4 %collective-permute-start.40 = (f32[3,2,16,128]{3,2,1,0:T(8,128)S(1)}, f32[3,2,16,128]{3,2,1,0:T(8,128)S(1)}, u32[]{:S(2)}, u32[]{:S(2)}) collective-permute-start(f32[3,2,16,128]{3,2,1,0:T(8,128)S(1)} %get-tuple-element.148), channel_id=1, source_target_pairs={{0,4},{4,0},{1,5},{5,1},{2,6},{6,2},{3,7},{7,3},{8,12},{12,8},{9,1... | collective-permute-start | bytes 147464 | tf_op jit(solution)/shard_map/ppermute | solution.py:35
  148.3 6.5 %collective-permute-start.43 = (f32[3,2,32,256]{3,2,1,0:T(8,128)S(1)}, f32[3,2,32,256]{3,2,1,0:T(8,128)S(1)}, u32[]{:S(2)}, u32[]{:S(2)}) collective-permute-start(f32[3,2,32,256]{3,2,1,0:T(8,128)S(1)} %get-tuple-element.152), channel_id=1, source_target_pairs={{0,4},{4,0},{1,5},{5,1},{2,6},{6,2},{3,7},{7,3},{8,12},{12,8},{9,1... | collective-permute-start | bytes 589832 | tf_op jit(solution)/shard_map/ppermute | solution.py:35
  (28 other events, 109.1 us)

commit v5 on v4

--- a/solution.py
+++ b/solution.py
@@ -136,16 +136,18 @@
     return outputs
 
 
-def fine_rates(ext, half, x, r, n):
-    rows = []
+def slopes(half, a, x, r, n):
+    _, ahead, behind = sides(half, a, x, r, n)
+    return [ahead[b] - behind[b] for b in range(3)]
+
+
+def fine_rates(ext, v, grads, x, r, n):
+    speeds = [0.5 * v[b, x, r : r + n] for b in range(3)]
 
     def grads_of(a):
-        _, ahead, behind = sides(half, a, x, r, n)
-        rows.append([ahead[b] - behind[b] for b in range(3)])
-        return rows[a]
-
-    speeds = [half[b, x, r : r + n] for b in range(3)]
-    return rates(ext, x, r, n, speeds, grads_of, VISCOSITY), rows
+        return [grads[3 * a + b, x, r : r + n] for b in range(3)]
+
+    return rates(ext, x + 1, PAD + r, n, speeds, grads_of, VISCOSITY)
 
 
 def split(value):
@@ -273,25 +275,9 @@
     coarsen(v, summed, rows, store_speed)
 
 
-def integral_loop(ext, half, summed, grads_summed):
-    width, length = ext.shape[1] - 2, ext.shape[2] - 2 * PAD
-    n = min(CHUNK, length)
-
-    @pl.loop(0, width // 2)
-    def _(i):
-        for r in range(0, length, n):
-            pair = [fine_rates(ext, half, 2 * i + 1 + q, PAD + r, n) for q in range(2)]
-            for a in range(3):
-                summed[a, i, r : r + n] = pair[0][0][a] + pair[1][0][a]
-                if grads_summed is not None:
-                    for b in range(3):
-                        value = pair[0][1][a][b] + pair[1][1][a][b]
-                        grads_summed[3 * a + b, i, r : r + n] = value
-
-
 def offset_start_kernel(
     first, v, s, g, x_faces, behind, ahead, zero,
-    integral, coarse_grads, zero_x, zero_b, zero_a, end, end_x, end_l, end_f,
+    grads, integral, coarse_grads, zero_x, zero_b, zero_a, end, end_x, end_l, end_f,
     ext, half, summed, grads_summed, rows,
 ):
     f = first[0]
@@ -300,7 +286,25 @@
     guess = Node(g, x_faces, behind, ahead, 3)
     share = f * (TIME_STEP / 6.0)
     fill(ext, [(share, start), (TIME_STEP - share, guess)])
-    integral_loop(ext, half, summed, grads_summed)
+    width, length = v.shape[1:3]
+    n = min(CHUNK, length)
+
+    @pl.loop(0, width // 2)
+    def _(i):
+        for r in range(0, length, n):
+            at = slice(r, r + n)
+            for q in range(2):
+                x = 2 * i + q
+                for a in range(3):
+                    row = slopes(half, a, x + 1, PAD + r, n)
+                    for b in range(3):
+                        grads[3 * a + b, x, at] = row[b]
+                        if q:
+                            row[b] = row[b] + grads_summed[3 * a + b, i, at]
+                        grads_summed[3 * a + b, i, at] = row[b]
+            pair = [fine_rates(ext, v, grads, 2 * i + q, r, n) for q in range(2)]
+            for a in range(3):
+                summed[a, i, at] = pair[0][a] + pair[1][a]
 
     def store(c, value):
         integral[c] = value
@@ -317,49 +321,54 @@
 
 
 def offset_later_kernel(
-    first, v, s, x_faces, behind, ahead,
-    u0, u0_x, u0_b, u0_a, u1, u1_x, u1_b, u1_a, u2, u2_x, u2_b, u2_a,
-    integral, zero, zero_x, zero_b, zero_a, end, end_x, end_l, end_f,
-    ext, half, summed, rows,
+    first, v, grads, s, x_faces, behind, ahead,
+    u1, u1_x, u1_b, u1_a, u2, u2_x, u2_b, u2_a, zero, end_two,
+    own, following, sent, sent_x, sent_l, sent_f,
+    ext, ext_two, summed, summed_two, rows,
 ):
     f = first[0]
-    fill(half, [(0.5, Node(v, x_faces, behind, ahead))])
     sixth = TIME_STEP / 6.0
+    last = Node(u2, u2_x, u2_b, u2_a)
+    fill(ext_two, [(sixth, last)])
     fill(
         ext,
         [
             (f * sixth, Node(s, x_faces, behind, ahead, 6)),
-            (sixth, Node(u0, u0_x, u0_b, u0_a)),
             (TIME_STEP * 2.0 / 3.0, Node(u1, u1_x, u1_b, u1_a)),
-            (sixth, Node(u2, u2_x, u2_b, u2_a)),
+            (sixth, last),
         ],
     )
-
-    @pl.loop(0, s.shape[1] // 2)
+    width, length = v.shape[1:3]
+    n = min(CHUNK, length)
+
+    @pl.loop(0, width // 2)
     def _(i):
-        for c in range(3):
-            summed[c, i] = f * (s[c, 2 * i] + s[c, 2 * i + 1]) + (u0[c, 2 * i] + u0[c, 2 * i + 1])
-
-    def store_zero(c, value):
-        zero[c] = value
-
-    squeeze(summed, rows, store_zero, 3)
-    integral_loop(ext, half, summed, None)
+        for r in range(0, length, n):
+            at = slice(r, r + n)
+            pair = [fine_rates(ext, v, grads, 2 * i + q, r, n) for q in range(2)]
+            for a in range(3):
+                summed[a, i, at] = pair[0][a] + pair[1][a]
+            pair = [fine_rates(ext_two, v, grads, 2 * i + q, r, n) for q in range(2)]
+            for a in range(3):
+                summed_two[a, i, at] = (pair[0][a] + u2[a, 2 * i, at]) + (pair[1][a] + u2[a, 2 * i + 1, at])
 
     def store(c, value):
-        integral[c] = value
-        end[c] = zero[c] + value
+        own[c] = value + (f * zero[c] - end_two[c])
+        sent[c] = own[c]
 
     squeeze(summed, rows, store, 3)
-    emit_faces(end, (end_x, end_l, end_f))
-    take_coarse_faces(u0_x, u0_b, u0_a, 3, (zero_x, zero_b, zero_a))
-
-
-def chain_step(rest, arrived, zero, integral, speed, coarse_grads, d0, ext, store):
-    for k in range(4):
-        d0[k][...] = rest * (total([group[k][...] for group in arrived]) - zero[k][...])
+    emit_faces(own, (sent_x, sent_l, sent_f))
+
+    def store_following(c, value):
+        following[c] = value
+        sent[3 + c] = value
+
+    squeeze(summed_two, rows, store_following, 3)
+
+
+def chain_step(base, speed, coarse_grads, d0, ext, store):
     fill(ext, [(TIME_STEP, Node(*d0))], unrolled=True)
-    width, length = zero[0].shape[1:3]
+    width, length = speed.shape[1:3]
     for x in range(width):
         speeds = [speed[b, x] for b in range(3)]
 
@@ -368,39 +377,86 @@
 
         changes = rates(ext, x + 1, PAD, length, speeds, grads_of, VISCOSITY / 4.0)
         for a in range(3):
-            store(a, x, zero[0][a, x] + d0[0][a, x] + integral[a, x] + changes[a])
-
-
-def pass_kernel(turn, first, *refs):
+            store(a, x, base(a, x) + d0[0][a, x] + changes[a])
+
+
+def pass_start_kernel(turn, first, *refs):
     arrived, zero = refs[:4], refs[4:8]
     integral, speed, coarse_grads, end, end_x, end_l, end_f = refs[8:15]
     d0, ext = refs[15:19], refs[19]
 
     @pl.when(first[1] == float(turn))
     def _():
+        def base(a, x):
+            return zero[0][a, x] + integral[a, x]
+
         def store(a, x, value):
             end[a, x] = value
 
-        chain_step(1.0, [arrived], zero, integral, speed, coarse_grads, d0, ext, store)
+        for k in range(4):
+            d0[k][...] = arrived[k][...] - zero[k][...]
+        chain_step(base, speed, coarse_grads, d0, ext, store)
         emit_faces(end, (end_x, end_l, end_f))
 
 
-def settle_kernel(count, first, *refs):
+def settle_start_kernel(count, first, *refs):
     arrived = [refs[4 * k : 4 * k + 4] for k in range(count)]
     refs = refs[4 * count :]
     zero, (integral, speed, coarse_grads, end_two) = refs[:4], refs[4:8]
     d0, (d2, d2_x, d2_l, d2_f, ext) = refs[8:12], refs[12:17]
+    rest = 1.0 - first[0]
+
+    def base(a, x):
+        return zero[0][a, x] + integral[a, x] - end_two[a, x]
 
     def store(a, x, value):
-        d2[a, x] = value - end_two[a, x]
-
-    chain_step(1.0 - first[0], arrived, zero, integral, speed, coarse_grads, d0, ext, store)
+        d2[a, x] = value
+
+    for k in range(4):
+        d0[k][...] = rest * (total([group[k][...] for group in arrived]) - zero[k][...])
+    chain_step(base, speed, coarse_grads, d0, ext, store)
     emit_faces(d2, (d2_x, d2_l, d2_f))
 
 
+def pass_later_kernel(turn, first, *refs):
+    arrived, (own, following, speed, coarse_grads) = refs[:4], refs[4:8]
+    sent, sent_x, sent_l, sent_f, ext = refs[8:13]
+
+    @pl.when(first[1] == float(turn))
+    def _():
+        def base(a, x):
+            return own[a, x] + arrived[0][3 + a, x]
+
+        def store(a, x, value):
+            sent[a, x] = value
+            sent[3 + a, x] = following[a, x]
+
+        chain_step(base, speed, coarse_grads, arrived, ext, store)
+        emit_faces(sent, (sent_x, sent_l, sent_f))
+
+
+def settle_later_kernel(count, first, *refs):
+    arrived = [refs[4 * k : 4 * k + 4] for k in range(count)]
+    own, speed, coarse_grads = refs[4 * count : 4 * count + 3]
+    refs = refs[4 * count + 3 :]
+    d0, (d2, d2_x, d2_l, d2_f, ext) = refs[:4], refs[4:9]
+
+    def base(a, x):
+        return own[a, x] + total([group[0][3 + a, x] for group in arrived])
+
+    def store(a, x, value):
+        d2[a, x] = value
+
+    d0[0][...] = total([group[0][0:3] for group in arrived])
+    for k in range(1, 4):
+        d0[k][...] = total([group[k][...] for group in arrived])
+    chain_step(base, speed, coarse_grads, d0, ext, store)
+    emit_faces(d2, (d2_x, d2_l, d2_f))
+
+
 def middle_kernel(nodes, *refs):
-    first, v, vx, vb, va = refs[:5]
-    at = 5
+    first, v, grads, vx, vb, va = refs[:6]
+    at = 6
     parts = []
     for _, _, _, own, off in nodes:
         main = refs[at]
@@ -414,12 +470,11 @@
     d0 = Node(*refs[at : at + 4])
     d2 = Node(*refs[at + 4 : at + 8])
     a1, a1_x, a1_l, a1_f, rest, rest_x, rest_b, rest_a = refs[at + 8 : at + 16]
-    ext, half, wide0, edge0, wide2, edge2, rows = refs[at + 16 :]
+    ext, wide0, edge0, wide2, edge2, rows = refs[at + 16 :]
     f = first[0]
     begin, first_stage, second_stage = [
         [(spec[k][0] * f + spec[k][1], node) for spec, node in zip(nodes, parts)] for k in range(3)
     ]
-    fill(half, [(0.5, Node(v, vx, vb, va))])
     prolong(d0, wide0, edge0, rows)
     prolong(d2, wide2, edge2, rows)
     fill(
@@ -446,7 +501,7 @@
             x = 2 * i + q
             row = pl.ds(x, 1)
             for r in range(0, length, n):
-                changes, _ = fine_rates(ext, half, x + 1, PAD + r, n)
+                changes = fine_rates(ext, v, grads, x, r, n)
                 for a in range(3):
                     p0, p2 = wide0[a, i + 1, r : r + n], wide2[a, i + 1, r : r + n]
                     start = total([w * nd.main[a, x, r : r + n] for w, nd in begin])
@@ -461,12 +516,11 @@
     emit_faces(a1, (a1_x, a1_l, a1_f))
 
 
-def finish_kernel(last, first, v, vx, vb, va, a1, a1_x, a1_b, a1_a, rest, rest_x, rest_b, rest_a, *refs):
+def finish_kernel(last, first, v, grads, a1, a1_x, a1_b, a1_a, rest, rest_x, rest_b, rest_a, *refs):
     if last:
-        a2, ext, half = refs
+        a2, ext = refs
     else:
-        a2, a2_x, a2_l, a2_f, end, ext, half, summed, rows = refs
-    fill(half, [(0.5, Node(v, vx, vb, va))])
+        a2, a2_x, a2_l, a2_f, end, ext, summed, rows = refs
     fill(
         ext,
         [
@@ -483,7 +537,7 @@
             pair = []
             for q in range(2):
                 x = 2 * i + q
-                changes, _ = fine_rates(ext, half, x + 1, PAD + r, n)
+                changes = fine_rates(ext, v, grads, x, r, n)
                 pair.append([a1[a, x, r : r + n] + changes[a] for a in range(3)])
                 for a in range(3):
                     a2[a, x, r : r + n] = pair[q][a]
@@ -498,7 +552,6 @@
             end[c] = value
 
         squeeze(summed, rows, store, 3)
-        emit_coarse_faces(end, (a2_x, a2_l, a2_f), 3)
 
 
 def call(kernel, name, first, args, outs, scratch, flops=0):
@@ -543,27 +596,34 @@
         coarsen_kernel, "coarsen", first, [velocity, start_field, end_two],
         [coarse, coarse], [summed, rows], 10_000_000,
     )
-    integral, coarse_grads, *results = call(
+    grads, integral, coarse_grads, *results = call(
         offset_start_kernel, "offset_start", first, [velocity, start_field, own, *layers, zero],
-        [coarse, (9, cx, cy, cz)] + coarse_faces + [coarse] + coarse_faces,
+        [(9, nx, ny, nz), coarse, (9, cx, cy, cz)] + coarse_faces + [coarse] + coarse_faces,
         [ext, ext, summed, (9, cx, ny, nz), rows], 40_000_000,
     )
-    zero_faces, end, sent = results[:3], results[3], results[4:]
+    zero_faces, sent = results[:3], results[3:]
     for sweep_index in range(ITERS):
         final = sweep_index + 1 == ITERS
+        if sweep_index == 0:
+            step, settle, outs, scratch = pass_start_kernel, settle_start_kernel, coarse, [coarse, *coarse_faces]
+            own_terms, end_terms = [zero, *zero_faces, integral], [end_two]
+            held = own_terms
+        else:
+            step, settle, outs, scratch = pass_later_kernel, settle_later_kernel, (6, cx, cy, cz), []
+            own_terms, end_terms = [own_part, following], []
+            held = [own_part]
         arrivals = []
         for turn in range(1, slabs):
-            arrivals.append(hand_on([turn - 1], end, sent))
+            arrivals.append(hand_on([turn - 1], sent[0], sent[1:]))
             if turn + 1 < slabs:
-                end, *sent = call(
-                    lambda *refs, turn=turn: pass_kernel(turn, *refs), "chain", first,
-                    [*arrivals[-1], zero, *zero_faces, integral, speed, coarse_grads],
-                    [coarse] + coarse_faces, [coarse, *coarse_faces, coarse_ext], 2_000_000,
+                sent = call(
+                    lambda *refs, step=step, turn=turn: step(turn, *refs), "chain", first,
+                    [*arrivals[-1], *own_terms, speed, coarse_grads],
+                    [outs] + coarse_faces, scratch + [coarse_ext], 2_000_000,
                 )
         results = call(
-            lambda *refs, count=len(arrivals): settle_kernel(count, *refs), "settle", first,
-            [a for group in arrivals for a in group]
-            + [zero, *zero_faces, integral, speed, coarse_grads, end_two],
+            lambda *refs, settle=settle, count=len(arrivals): settle(count, *refs), "settle", first,
+            [a for group in arrivals for a in group] + held + [speed, coarse_grads] + end_terms,
             [coarse] + coarse_faces + [coarse] + coarse_faces, [coarse_ext], 2_000_000,
         )
         d0, d2 = list(results[:4]), [results[4], *swap_faces(results[5:])]
@@ -584,16 +644,16 @@
             args = [start_field, *u0, *u1, *u2]
         middle, m_x, m_l, m_f, *rest = call(
             lambda *refs, nodes=nodes: middle_kernel(nodes, *refs),
-            "middle", first, [velocity, *layers, *args, *d0, *d2],
+            "middle", first, [velocity, grads, *layers, *args, *d0, *d2],
             [fine] + fine_faces + [fine] + fine_faces,
-            [ext, ext, wide, edge, wide, edge, wide_rows], 60_000_000,
+            [ext, wide, edge, wide, edge, wide_rows], 60_000_000,
         )
         u1 = [middle, *swap_faces((m_x, m_l, m_f))]
         results = call(
             lambda *refs, final=final: finish_kernel(final, *refs),
-            "finish", first, [velocity, *layers, *u1, *rest],
-            [fine] if final else [fine] + layers_of(4) + [coarse],
-            [ext, ext] if final else [ext, ext, summed, rows], 40_000_000,
+            "finish", first, [velocity, grads, *u1, *rest],
+            [fine] if final else [fine] + fine_faces + [coarse],
+            [ext] if final else [ext, summed, rows], 40_000_000,
         )
         if final:
             return results[0][None]
@@ -601,13 +661,12 @@
         end_two = results[4]
         u0 = hand_on(range(slabs - 1), value, faces)
         u2 = [value, *swap_faces(faces)]
-        integral, zero, *results = call(
+        own_part, following, *sent = call(
             offset_later_kernel, "offset_later", first,
-            [velocity, start_field, *layers, *u0, *u1, *u2],
-            [coarse, coarse] + coarse_faces + [coarse] + coarse_faces,
-            [ext, ext, summed, rows], 40_000_000,
+            [velocity, grads, start_field, *layers, *u1, *u2, zero, end_two],
+            [coarse, coarse, (6, cx, cy, cz)] + coarse_faces,
+            [ext, ext, summed, summed, rows], 60_000_000,
         )
-        zero_faces, end, sent = results[:3], results[3], results[4:]
 
 
 def solution(mesh):

time: 160 us -> 160 us (level)
  starting transfers between devices: 51.9 us -> 59.6 us
  waiting for transfers between devices: 66.4 us -> 59.9 us
  Pallas kernels: 36.3 us -> 34.3 us
    ppermute x28, starting transfers between devices: 33.7 us -> 39.5 us  [permute(): return lax.ppermute(array, ('tm', 'gx', 'gy'), pairs)]
    ppermute x28, waiting for transfers between devices: 31.1 us -> 26 us  [permute(): return lax.ppermute(array, ('tm', 'gx', 'gy'), pairs)]
    ppermute x6, waiting for transfers between devices: 15.8 us -> 13.3 us  [swap_faces(): behind = lax.ppermute(y_last, 'gy', ring(gy, 1))]
    ppermute x6, starting transfers between devices: 5.85 us -> 7.87 us  [swap_faces(): ahead = lax.ppermute(y_first, 'gy', ring(gy, -1))]
    ppermute x6, starting transfers between devices: 6.28 us -> 4.3 us  [swap_faces(): behind = lax.ppermute(y_last, 'gy', ring(gy, 1))]
    pallas_call x14, Pallas kernels: 36.3 us -> 34.3 us  [call(): pl.pallas_call(kernel, name=name, out_shape=[jax.ShapeDtypeStruct(dims, F...]
    ppermute x6, starting transfers between devices: 6.08 us -> 7.92 us  [swap_faces(): lax.ppermute(a, 'gx', ring(gx, by))]
  transfers between devices with their start and end apart: 46 -> 46, of which waited for: 23 -> 21; matrix products, arithmetic and copies ran while one was open for 0% -> 0% of each run, Pallas kernels for 1% -> 6%
where the time goes in v5:
time: 160 us; the launch traced here: 159 us
  waiting for transfers between devices  59.9 us (37%)
  starting transfers between devices  59.6 us (37%)
  Pallas kernels  34.3 us (21%)
  local copies, waits for them, and re-layouts  4.23 us (3%)
    ppermute x28, starting transfers between devices, permute(): return lax.ppermute(array, ('tm', 'gx', 'gy'), pairs)  39.5 us
    pallas_call x14, Pallas kernels, call(): pl.pallas_call(kernel, name=name, out_shape=[jax.ShapeDtypeStruct(dims, F...  34.3 us
    ppermute x28, waiting for transfers between devices, permute(): return lax.ppermute(array, ('tm', 'gx', 'gy'), pairs)  26 us
    ppermute x6, waiting for transfers between devices, swap_faces(): ahead = lax.ppermute(y_first, 'gy', ring(gy, -1))  14.8 us
    ppermute x6, waiting for transfers between devices, swap_faces(): behind = lax.ppermute(y_last, 'gy', ring(gy, 1))  13.3 us
    ppermute x6, starting transfers between devices, swap_faces(): lax.ppermute(a, 'gx', ring(gx, by))  7.92 us
    ppermute x6, starting transfers between devices, swap_faces(): ahead = lax.ppermute(y_first, 'gy', ring(gy, -1))  7.87 us
    ppermute x6, waiting for transfers between devices, swap_faces(): lax.ppermute(a, 'gx', ring(gx, by))  5.79 us
  transfers between devices with their start and end apart: 46, of which 21 were waited for; matrix products, arithmetic and copies ran while one was open for 0% of the time, Pallas kernels for 6%

profile of v5, /device:TPU:26, one launch (start us, length us, event | category | flops | bytes accessed | tf_op | source)
XLA Modules:
  0.0 158.5 jit_solution(3512495282538385925)
XLA Ops:
  10.8 5.5 %collective-permute-done.1.behind.refs_4_ = f32[10,16,256]{2,1,0:T(8,128)S(1)} collective-permute-done((f32[10,16,256]{2,1,0:T(8,128)S(1)}, f32[10,16,256]{2,1,0:T(8,128)S(1)}, u32[]{:S(2)}, u32[]{:S(2)}) %collective-permute-start.1) | collective-permute-done | bytes 163872 | tf_op jit(solution)/shard_map/ppermute | solution.py:36
  16.3 5.8 %collective-permute-done.x_faces.refs_3_ = f32[10,2,32,256]{3,2,1,0:T(8,128)S(1)} collective-permute-done((f32[10,2,32,256]{3,2,1,0:T(8,128)S(1)}, f32[10,2,32,256]{3,2,1,0:T(8,128)S(1)}, u32[]{:S(2)}, u32[]{:S(2)}) %collective-permute-start) | collective-permute-done | bytes 655392 | tf_op jit(solution)/shard_map/ppermute | solution.py:35
  22.1 5.0 %offset_start.1 = (f32[9,16,32,256]{3,2,1,0:T(8,128)S(1)}, f32[3,8,16,128]{3,2,1,0:T(8,128)S(1)}, f32[9,8,16,128]{3,2,1,0:T(8,128)S(1)}, f32[3,2,16,128]{3,2,1,0...) custom-call(f32[2]{0:T(128)S(1)} %add_convert_fusion.first.refs_0_, ...), custom_call_target="tpu_custom_call" | custom-call | flops 40000000 | bytes 5898240 | tf_op jit(solution)/shard_map/offset_start/pallas_call | solution.py:560
  35.6 6.7 %collective-permute-done.9.refs_3_.refs_7_ = f32[3,8,128]{2,1,0:T(8,128)S(1)} collective-permute-done((f32[3,8,128]{2,1,0:T(8,128)S(1)}, f32[3,8,128]{2,1,0:T(8,128)S(1)}, u32[]{:S(2)}, u32[]{:S(2)}) %collective-permute-start.9) | collective-permute-done | bytes 12320 | tf_op jit(solution)/shard_map/ppermute | solution.py:52
  53.3 2.9 %collective-permute-start.16 = (f32[3,8,128]{2,1,0:T(8,128)S(1)}, f32[3,8,128]{2,1,0:T(8,128)S(1)}, u32[]{:S(2)}, u32[]{:S(2)}) collective-permute-start(f32[3,8,128]{2,1,0:T(8,128)S(1)} %get-tuple-element.110), channel_id=1, source_target_pairs={{0,1},{1,2},{2,3},{3,0},{4,5},{5,6},{6,7},{7,4},{8,9},{9,10},{10,1... | collective-permute-start | bytes 36872 | tf_op jit(solution)/shard_map/ppermute | solution.py:36
  57.6 4.1 %collective-permute-done.17.refs_15_ = f32[3,8,128]{2,1,0:T(8,128)S(1)} collective-permute-done((f32[3,8,128]{2,1,0:T(8,128)S(1)}, f32[3,8,128]{2,1,0:T(8,128)S(1)}, u32[]{:S(2)}, u32[]{:S(2)}) %collective-permute-start.17) | collective-permute-done | bytes 12320 | tf_op jit(solution)/shard_map/ppermute | solution.py:37
  61.7 4.2 %middle.2 = (f32[3,16,32,256]{3,2,1,0:T(8,128)S(1)}, f32[3,2,32,256]{3,2,1,0:T(8,128)S(1)}, f32[3,16,256]{2,1,0:T(8,128)S(1)}, f32[3,16,256]{2,1,0:T(8,128)S(1)}...) custom-call(f32[2]{0:T(128)S(1)} %add_convert_fusion.first.refs_0_, ...), custom_call_target="tpu_custom_call" | custom-call | flops 60000000 | bytes 10960896 | tf_op jit(solution)/shard_map/middle/pallas_call | solution.py:560
  66.5 2.0 %collective-permute-start.20 = (f32[3,16,256]{2,1,0:T(8,128)S(1)}, f32[3,16,256]{2,1,0:T(8,128)S(1)}, u32[]{:S(2)}, u32[]{:S(2)}) collective-permute-start(f32[3,16,256]{2,1,0:T(8,128)S(1)} %get-tuple-element.115), channel_id=1, source_target_pairs={{0,3},{1,0},{2,1},{3,2},{4,7},{5,4},{6,5},{7,6},{8,11},{9,8},{10,9... | collective-permute-start | bytes 147464 | tf_op jit(solution)/shard_map/ppermute | solution.py:37
  68.6 2.2 %collective-permute-done.19.refs_5_.u1_b.refs_13_ = f32[3,16,256]{2,1,0:T(8,128)S(1)} collective-permute-done((f32[3,16,256]{2,1,0:T(8,128)S(1)}, f32[3,16,256]{2,1,0:T(8,128)S(1)}, u32[]{:S(2)}, u32[]{:S(2)}) %collective-permute-start.19) | collective-permute-done | bytes 49184 | tf_op jit(solution)/shard_map/ppermute | solution.py:36
  72.4 3.2 %finish.2 = (f32[3,16,32,256]{3,2,1,0:T(8,128)S(1)}, f32[3,2,32,256]{3,2,1,0:T(8,128)S(1)}, f32[3,16,256]{2,1,0:T(8,128)S(1)}, f32[3,16,256]{2,1,0:T(8,128)S(1)}, f32[3,8,16,128]{3,2,1,0:T(8,128)S(1)}) custom-call(f32[2]{0:T(128)S(1)} %add_convert_fusion.first.refs_0_, f32[3,16,32,256]{3,2,1,0:T(8,128)S(1)} %copy-done.1, ...), custom_call_target="tpu_custom_call" | custom-call | flops 40000000 | bytes 10027008 | tf_op jit(solution)/shard_map/finish/pallas_call | solution.py:560
  75.7 1.9 %collective-permute-start.21 = (f32[3,16,32,256]{3,2,1,0:T(8,128)S(1)}, f32[3,16,32,256]{3,2,1,0:T(8,128)S(1)}, u32[]{:S(2)}, u32[]{:S(2)}) collective-permute-start(f32[3,16,32,256]{3,2,1,0:T(8,128)S(1)} %get-tuple-element.120.u2.refs_15_), channel_id=1, source_target_pairs={{0,8},{1,9},{2,10},{3,11},{4,12},{5,13},{6,14},{7,15},{8,16},{9,17... | collective-permute-start | bytes 4718600 | tf_op jit(solution)/shard_map/ppermute | solution.py:52
  79.2 2.0 %collective-permute-start.27 = (f32[3,16,256]{2,1,0:T(8,128)S(1)}, f32[3,16,256]{2,1,0:T(8,128)S(1)}, u32[]{:S(2)}, u32[]{:S(2)}) collective-permute-start(f32[3,16,256]{2,1,0:T(8,128)S(1)} %get-tuple-element.123), channel_id=1, source_target_pairs={{0,3},{1,0},{2,1},{3,2},{4,7},{5,4},{6,5},{7,6},{8,11},{9,8},{10,9... | collective-permute-start | bytes 147464 | tf_op jit(solution)/shard_map/ppermute | solution.py:37
  81.2 2.1 %collective-permute-done.26.u2_b.refs_17_ = f32[3,16,256]{2,1,0:T(8,128)S(1)} collective-permute-done((f32[3,16,256]{2,1,0:T(8,128)S(1)}, f32[3,16,256]{2,1,0:T(8,128)S(1)}, u32[]{:S(2)}, u32[]{:S(2)}) %collective-permute-start.26) | collective-permute-done | bytes 49184 | tf_op jit(solution)/shard_map/ppermute | solution.py:36
  85.1 5.4 %offset_later.1 = (f32[3,8,16,128]{3,2,1,0:T(8,128)S(1)}, f32[3,8,16,128]{3,2,1,0:T(8,128)S(1)}, f32[6,8,16,128]{3,2,1,0:T(8,128)S(1)}, f32[3,2,16,128]{3,2,1,0:...) custom-call(f32[2]{0:T(128)S(1)} %add_convert_fusion.first.refs_0_, f32[3,16,32,256]{3,2,1,0:T(8,128)S(1)} %copy-done.1, ...), custom_call_target="tpu_custom_call" | custom-call | flops 60000000 | bytes 12976128 | tf_op jit(solution)/shard_map/offset_later/pallas_call | solution.py:560
  99.0 6.9 %collective-permute-done.34.refs_3_.refs_7_ = f32[3,8,128]{2,1,0:T(8,128)S(1)} collective-permute-done((f32[3,8,128]{2,1,0:T(8,128)S(1)}, f32[3,8,128]{2,1,0:T(8,128)S(1)}, u32[]{:S(2)}, u32[]{:S(2)}) %collective-permute-start.34) | collective-permute-done | bytes 12320 | tf_op jit(solution)/shard_map/ppermute | solution.py:52
  107.7 2.1 %collective-permute-done.33.refs_2_.refs_6_ = f32[3,2,16,128]{3,2,1,0:T(8,128)S(1)} collective-permute-done((f32[3,2,16,128]{3,2,1,0:T(8,128)S(1)}, f32[3,2,16,128]{3,2,1,0:T(8,128)S(1)}, u32[]{:S(2)}, u32[]{:S(2)}) %collective-permute-start.33) | collective-permute-done | bytes 49184 | tf_op jit(solution)/shard_map/ppermute | solution.py:52
  112.0 1.9 %collective-permute-start.22 = (f32[3,2,32,256]{3,2,1,0:T(8,128)S(1)}, f32[3,2,32,256]{3,2,1,0:T(8,128)S(1)}, u32[]{:S(2)}, u32[]{:S(2)}) collective-permute-start(f32[3,2,32,256]{3,2,1,0:T(8,128)S(1)} %get-tuple-element.121), channel_id=1, source_target_pairs={{0,12},{1,13},{2,14},{3,15},{4,8},{5,9},{6,10},{7,11},{8,20},{9,21... | collective-permute-start | bytes 589832 | tf_op jit(solution)/shard_map/ppermute | solution.py:52
  121.0 7.3 %collective-permute-start.23 = (f32[3,16,256]{2,1,0:T(8,128)S(1)}, f32[3,16,256]{2,1,0:T(8,128)S(1)}, u32[]{:S(2)}, u32[]{:S(2)}) collective-permute-start(f32[3,16,256]{2,1,0:T(8,128)S(1)} %get-tuple-element.122), channel_id=1, source_target_pairs={{0,9},{1,10},{2,11},{3,8},{4,13},{5,14},{6,15},{7,12},{8,17},{9,18... | collective-permute-start | bytes 147464 | tf_op jit(solution)/shard_map/ppermute | solution.py:52
  134.0 2.5 %collective-permute-done.24.refs_10_ = f32[3,16,256]{2,1,0:T(8,128)S(1)} collective-permute-done((f32[3,16,256]{2,1,0:T(8,128)S(1)}, f32[3,16,256]{2,1,0:T(8,128)S(1)}, u32[]{:S(2)}, u32[]{:S(2)}) %collective-permute-start.24) | collective-permute-done | bytes 49184 | tf_op jit(solution)/shard_map/ppermute | solution.py:52
  136.5 5.5 %collective-permute-done.42.refs_26_ = f32[3,8,128]{2,1,0:T(8,128)S(1)} collective-permute-done((f32[3,8,128]{2,1,0:T(8,128)S(1)}, f32[3,8,128]{2,1,0:T(8,128)S(1)}, u32[]{:S(2)}, u32[]{:S(2)}) %collective-permute-start.42) | collective-permute-done | bytes 12320 | tf_op jit(solution)/shard_map/ppermute | solution.py:37
  142.0 5.2 %middle.3 = (f32[3,16,32,256]{3,2,1,0:T(8,128)S(1)}, f32[3,2,32,256]{3,2,1,0:T(8,128)S(1)}, f32[3,16,256]{2,1,0:T(8,128)S(1)}, f32[3,16,256]{2,1,0:T(8,128)S(1)}...) custom-call(f32[2]{0:T(128)S(1)} %add_convert_fusion.first.refs_0_, ...), custom_call_target="tpu_custom_call" | custom-call | flops 60000000 | bytes 14991360 | tf_op jit(solution)/shard_map/middle/pallas_call | solution.py:560
  148.8 2.0 %collective-permute-start.45 = (f32[3,16,256]{2,1,0:T(8,128)S(1)}, f32[3,16,256]{2,1,0:T(8,128)S(1)}, u32[]{:S(2)}, u32[]{:S(2)}) collective-permute-start(f32[3,16,256]{2,1,0:T(8,128)S(1)} %get-tuple-element.150), channel_id=1, source_target_pairs={{0,3},{1,0},{2,1},{3,2},{4,7},{5,4},{6,5},{7,6},{8,11},{9,8},{10,9... | collective-permute-start | bytes 147464 | tf_op jit(solution)/shard_map/ppermute | solution.py:37
  150.8 2.1 %collective-permute-done.44.refs_5_ = f32[3,16,256]{2,1,0:T(8,128)S(1)} collective-permute-done((f32[3,16,256]{2,1,0:T(8,128)S(1)}, f32[3,16,256]{2,1,0:T(8,128)S(1)}, u32[]{:S(2)}, u32[]{:S(2)}) %collective-permute-start.44) | collective-permute-done | bytes 49184 | tf_op jit(solution)/shard_map/ppermute | solution.py:36
  154.7 3.9 %finish.3 = f32[3,16,32,256]{3,2,1,0:T(8,128)} custom-call(f32[2]{0:T(128)S(1)} %add_convert_fusion.first.refs_0_, f32[3,16,32,256]{3,2,1,0:T(8,128)S(1)} %copy-done.1, f32[9,16,32,256]{3,2,1,0:T(8,128)S(1)} %get-tuple-element.85.refs_2_.grads, f32[3,16,32,256]{3,2,1,0:T(8,128)S(1)} %get-tuple-element.147.refs_3_, ...), custom_call_target="tpu_custom_call" | custom-call | flops 40000000 | bytes 10027008 | tf_op jit(solution)/shard_map/finish/pallas_call | solution.py:560
  (95 shorter events, 65.7 us)
Async XLA Ops:
  5.6 16.5 %collective-permute-start = (f32[10,2,32,256]{3,2,1,0:T(8,128)S(1)}, f32[10,2,32,256]{3,2,1,0:T(8,128)S(1)}, u32[]{:S(2)}, u32[]{:S(2)}) collective-permute-start(f32[10,2,32,256]{3,2,1,0:T(8,128)S(1)} %get-tuple-element.80), channel_id=1, source_target_pairs={{0,4},{4,0},{1,5},{5,1},{2,6},{6,2},{3,7},{7,3},{8,12},{12,8},{9,1... | collective-permute-start | bytes 1966088 | tf_op jit(solution)/shard_map/ppermute | solution.py:35
  7.2 9.2 %collective-permute-start.1 = (f32[10,16,256]{2,1,0:T(8,128)S(1)}, f32[10,16,256]{2,1,0:T(8,128)S(1)}, u32[]{:S(2)}, u32[]{:S(2)}) collective-permute-start(f32[10,16,256]{2,1,0:T(8,128)S(1)} %get-tuple-element.81), channel_id=1, source_target_pairs={{0,1},{1,2},{2,3},{3,0},{4,5},{5,6},{6,7},{7,4},{8,9},{9,10},{10,1... | collective-permute-start | bytes 491528 | tf_op jit(solution)/shard_map/ppermute | solution.py:36
  7.4 9.0 %collective-permute-start.2 = (f32[10,16,256]{2,1,0:T(8,128)S(1)}, f32[10,16,256]{2,1,0:T(8,128)S(1)}, u32[]{:S(2)}, u32[]{:S(2)}) collective-permute-start(f32[10,16,256]{2,1,0:T(8,128)S(1)} %get-tuple-element.82), channel_id=1, source_target_pairs={{0,3},{1,0},{2,1},{3,2},{4,7},{5,4},{6,5},{7,6},{8,11},{9,8},{10,9... | collective-permute-start | bytes 491528 | tf_op jit(solution)/shard_map/ppermute | solution.py:37
  30.4 13.6 %collective-permute-start.7 = (f32[3,8,16,128]{3,2,1,0:T(8,128)S(1)}, f32[3,8,16,128]{3,2,1,0:T(8,128)S(1)}, u32[]{:S(2)}, u32[]{:S(2)}) collective-permute-start(f32[3,8,16,128]{3,2,1,0:T(8,128)S(1)} %get-tuple-element.96), channel_id=1, source_target_pairs={{8,16},{9,17},{10,18},{11,19},{12,20},{13,21},{14,22},{15,23}} | collective-permute-start | bytes 589832 | tf_op jit(solution)/shard_map/ppermute | solution.py:52
  31.7 12.3 %collective-permute-start.8 = (f32[3,2,16,128]{3,2,1,0:T(8,128)S(1)}, f32[3,2,16,128]{3,2,1,0:T(8,128)S(1)}, u32[]{:S(2)}, u32[]{:S(2)}) collective-permute-start(f32[3,2,16,128]{3,2,1,0:T(8,128)S(1)} %get-tuple-element.97), channel_id=1, source_target_pairs={{8,20},{9,21},{10,22},{11,23},{12,16},{13,17},{14,18},{15,19}} | collective-permute-start | bytes 147464 | tf_op jit(solution)/shard_map/ppermute | solution.py:52
  33.0 9.3 %collective-permute-start.9 = (f32[3,8,128]{2,1,0:T(8,128)S(1)}, f32[3,8,128]{2,1,0:T(8,128)S(1)}, u32[]{:S(2)}, u32[]{:S(2)}) collective-permute-start(f32[3,8,128]{2,1,0:T(8,128)S(1)} %get-tuple-element.98), channel_id=1, source_target_pairs={{8,17},{9,18},{10,19},{11,16},{12,21},{13,22},{14,23},{15,20}} | collective-permute-start | bytes 36872 | tf_op jit(solution)/shard_map/ppermute | solution.py:52
  34.3 9.7 %collective-permute-start.10 = (f32[3,8,128]{2,1,0:T(8,128)S(1)}, f32[3,8,128]{2,1,0:T(8,128)S(1)}, u32[]{:S(2)}, u32[]{:S(2)}) collective-permute-start(f32[3,8,128]{2,1,0:T(8,128)S(1)} %get-tuple-element.99), channel_id=1, source_target_pairs={{8,19},{9,16},{10,17},{11,18},{12,23},{13,20},{14,21},{15,22}} | collective-permute-start | bytes 36872 | tf_op jit(solution)/shard_map/ppermute | solution.py:52
  44.8 6.6 %collective-permute-start.11 = (f32[3,8,16,128]{3,2,1,0:T(8,128)S(1)}, f32[3,8,16,128]{3,2,1,0:T(8,128)S(1)}, u32[]{:S(2)}, u32[]{:S(2)}) collective-permute-start(f32[3,8,16,128]{3,2,1,0:T(8,128)S(1)} %get-tuple-element.100), channel_id=1, source_target_pairs={{16,24},{17,25},{18,26},{19,27},{20,28},{21,29},{22,30},{23,31}} | collective-permute-start | bytes 589832 | tf_op jit(solution)/shard_map/ppermute | solution.py:52
  52.3 9.4 %collective-permute-start.15 = (f32[3,2,16,128]{3,2,1,0:T(8,128)S(1)}, f32[3,2,16,128]{3,2,1,0:T(8,128)S(1)}, u32[]{:S(2)}, u32[]{:S(2)}) collective-permute-start(f32[3,2,16,128]{3,2,1,0:T(8,128)S(1)} %get-tuple-element.109), channel_id=1, source_target_pairs={{0,4},{4,0},{1,5},{5,1},{2,6},{6,2},{3,7},{7,3},{8,12},{12,8},{9,1... | collective-permute-start | bytes 147464 | tf_op jit(solution)/shard_map/ppermute | solution.py:35
  66.0 6.5 %collective-permute-start.18 = (f32[3,2,32,256]{3,2,1,0:T(8,128)S(1)}, f32[3,2,32,256]{3,2,1,0:T(8,128)S(1)}, u32[]{:S(2)}, u32[]{:S(2)}) collective-permute-start(f32[3,2,32,256]{3,2,1,0:T(8,128)S(1)} %get-tuple-element.113), channel_id=1, source_target_pairs={{0,4},{4,0},{1,5},{5,1},{2,6},{6,2},{3,7},{7,3},{8,12},{12,8},{9,1... | collective-permute-start | bytes 589832 | tf_op jit(solution)/shard_map/ppermute | solution.py:35
  66.5 5.9 %collective-permute-start.20 = (f32[3,16,256]{2,1,0:T(8,128)S(1)}, f32[3,16,256]{2,1,0:T(8,128)S(1)}, u32[]{:S(2)}, u32[]{:S(2)}) collective-permute-start(f32[3,16,256]{2,1,0:T(8,128)S(1)} %get-tuple-element.115), channel_id=1, source_target_pairs={{0,3},{1,0},{2,1},{3,2},{4,7},{5,4},{6,5},{7,6},{8,11},{9,8},{10,9... | collective-permute-start | bytes 147464 | tf_op jit(solution)/shard_map/ppermute | solution.py:37
  75.7 66.4 %collective-permute-start.21 = (f32[3,16,32,256]{3,2,1,0:T(8,128)S(1)}, f32[3,16,32,256]{3,2,1,0:T(8,128)S(1)}, u32[]{:S(2)}, u32[]{:S(2)}) collective-permute-start(f32[3,16,32,256]{3,2,1,0:T(8,128)S(1)} %get-tuple-element.120.u2.refs_15_), channel_id=1, source_target_pairs={{0,8},{1,9},{2,10},{3,11},{4,12},{5,13},{6,14},{7,15},{8,16},{9,17... | collective-permute-start | bytes 4718600 | tf_op jit(solution)/shard_map/ppermute | solution.py:52
  77.6 7.5 %collective-permute-start.25 = (f32[3,2,32,256]{3,2,1,0:T(8,128)S(1)}, f32[3,2,32,256]{3,2,1,0:T(8,128)S(1)}, u32[]{:S(2)}, u32[]{:S(2)}) collective-permute-start(f32[3,2,32,256]{3,2,1,0:T(8,128)S(1)} %get-tuple-element.121), channel_id=1, source_target_pairs={{0,4},{4,0},{1,5},{5,1},{2,6},{6,2},{3,7},{7,3},{8,12},{12,8},{9,1... | collective-permute-start | bytes 589832 | tf_op jit(solution)/shard_map/ppermute | solution.py:35
  93.8 16.0 %collective-permute-start.32 = (f32[6,8,16,128]{3,2,1,0:T(8,128)S(1)}, f32[6,8,16,128]{3,2,1,0:T(8,128)S(1)}, u32[]{:S(2)}, u32[]{:S(2)}) collective-permute-start(f32[6,8,16,128]{3,2,1,0:T(8,128)S(1)} %get-tuple-element.131), channel_id=1, source_target_pairs={{8,16},{9,17},{10,18},{11,19},{12,20},{13,21},{14,22},{15,23}} | collective-permute-start | bytes 1179656 | tf_op jit(solution)/shard_map/ppermute | solution.py:52
  95.1 14.7 %collective-permute-start.33 = (f32[3,2,16,128]{3,2,1,0:T(8,128)S(1)}, f32[3,2,16,128]{3,2,1,0:T(8,128)S(1)}, u32[]{:S(2)}, u32[]{:S(2)}) collective-permute-start(f32[3,2,16,128]{3,2,1,0:T(8,128)S(1)} %get-tuple-element.132), channel_id=1, source_target_pairs={{8,20},{9,21},{10,22},{11,23},{12,16},{13,17},{14,18},{15,19}} | collective-permute-start | bytes 147464 | tf_op jit(solution)/shard_map/ppermute | solution.py:52
  96.4 9.5 %collective-permute-start.34 = (f32[3,8,128]{2,1,0:T(8,128)S(1)}, f32[3,8,128]{2,1,0:T(8,128)S(1)}, u32[]{:S(2)}, u32[]{:S(2)}) collective-permute-start(f32[3,8,128]{2,1,0:T(8,128)S(1)} %get-tuple-element.133), channel_id=1, source_target_pairs={{8,17},{9,18},{10,19},{11,16},{12,21},{13,22},{14,23},{15,20}} | collective-permute-start | bytes 36872 | tf_op jit(solution)/shard_map/ppermute | solution.py:52
  97.7 10.0 %collective-permute-start.35 = (f32[3,8,128]{2,1,0:T(8,128)S(1)}, f32[3,8,128]{2,1,0:T(8,128)S(1)}, u32[]{:S(2)}, u32[]{:S(2)}) collective-permute-start(f32[3,8,128]{2,1,0:T(8,128)S(1)} %get-tuple-element.134), channel_id=1, source_target_pairs={{8,19},{9,16},{10,17},{11,18},{12,23},{13,20},{14,21},{15,22}} | collective-permute-start | bytes 36872 | tf_op jit(solution)/shard_map/ppermute | solution.py:52
  110.7 19.6 %collective-permute-start.36 = (f32[6,8,16,128]{3,2,1,0:T(8,128)S(1)}, f32[6,8,16,128]{3,2,1,0:T(8,128)S(1)}, u32[]{:S(2)}, u32[]{:S(2)}) collective-permute-start(f32[6,8,16,128]{3,2,1,0:T(8,128)S(1)} %get-tuple-element.135), channel_id=1, source_target_pairs={{16,24},{17,25},{18,26},{19,27},{20,28},{21,29},{22,30},{23,31}} | collective-permute-start | bytes 1179656 | tf_op jit(solution)/shard_map/ppermute | solution.py:52
  112.0 24.5 %collective-permute-start.22 = (f32[3,2,32,256]{3,2,1,0:T(8,128)S(1)}, f32[3,2,32,256]{3,2,1,0:T(8,128)S(1)}, u32[]{:S(2)}, u32[]{:S(2)}) collective-permute-start(f32[3,2,32,256]{3,2,1,0:T(8,128)S(1)} %get-tuple-element.121), channel_id=1, source_target_pairs={{0,12},{1,13},{2,14},{3,15},{4,8},{5,9},{6,10},{7,11},{8,20},{9,21... | collective-permute-start | bytes 589832 | tf_op jit(solution)/shard_map/ppermute | solution.py:52
  114.0 14.4 %collective-permute-start.37 = (f32[3,2,16,128]{3,2,1,0:T(8,128)S(1)}, f32[3,2,16,128]{3,2,1,0:T(8,128)S(1)}, u32[]{:S(2)}, u32[]{:S(2)}) collective-permute-start(f32[3,2,16,128]{3,2,1,0:T(8,128)S(1)} %get-tuple-element.136), channel_id=1, source_target_pairs={{16,28},{17,29},{18,30},{19,31},{20,24},{21,25},{22,26},{23,27}} | collective-permute-start | bytes 147464 | tf_op jit(solution)/shard_map/ppermute | solution.py:52
  121.0 11.8 %collective-permute-start.23 = (f32[3,16,256]{2,1,0:T(8,128)S(1)}, f32[3,16,256]{2,1,0:T(8,128)S(1)}, u32[]{:S(2)}, u32[]{:S(2)}) collective-permute-start(f32[3,16,256]{2,1,0:T(8,128)S(1)} %get-tuple-element.122), channel_id=1, source_target_pairs={{0,9},{1,10},{2,11},{3,8},{4,13},{5,14},{6,15},{7,12},{8,17},{9,18... | collective-permute-start | bytes 147464 | tf_op jit(solution)/shard_map/ppermute | solution.py:52
  128.4 8.2 %collective-permute-start.24 = (f32[3,16,256]{2,1,0:T(8,128)S(1)}, f32[3,16,256]{2,1,0:T(8,128)S(1)}, u32[]{:S(2)}, u32[]{:S(2)}) collective-permute-start(f32[3,16,256]{2,1,0:T(8,128)S(1)} %get-tuple-element.123), channel_id=1, source_target_pairs={{0,11},{1,8},{2,9},{3,10},{4,15},{5,12},{6,13},{7,14},{8,19},{9,16... | collective-permute-start | bytes 147464 | tf_op jit(solution)/shard_map/ppermute | solution.py:52
  131.2 10.8 %collective-permute-start.40 = (f32[3,2,16,128]{3,2,1,0:T(8,128)S(1)}, f32[3,2,16,128]{3,2,1,0:T(8,128)S(1)}, u32[]{:S(2)}, u32[]{:S(2)}) collective-permute-start(f32[3,2,16,128]{3,2,1,0:T(8,128)S(1)} %get-tuple-element.144), channel_id=1, source_target_pairs={{0,4},{4,0},{1,5},{5,1},{2,6},{6,2},{3,7},{7,3},{8,12},{12,8},{9,1... | collective-permute-start | bytes 147464 | tf_op jit(solution)/shard_map/ppermute | solution.py:35
  147.2 7.5 %collective-permute-start.43 = (f32[3,2,32,256]{3,2,1,0:T(8,128)S(1)}, f32[3,2,32,256]{3,2,1,0:T(8,128)S(1)}, u32[]{:S(2)}, u32[]{:S(2)}) collective-permute-start(f32[3,2,32,256]{3,2,1,0:T(8,128)S(1)} %get-tuple-element.148), channel_id=1, source_target_pairs={{0,4},{4,0},{1,5},{5,1},{2,6},{6,2},{3,7},{7,3},{8,12},{12,8},{9,1... | collective-permute-start | bytes 589832 | tf_op jit(solution)/shard_map/ppermute | solution.py:35
  (28 other events, 108.2 us)

commit v6 on v5

--- a/solution.py
+++ b/solution.py
@@ -7,7 +7,6 @@
 from jax.experimental.pallas import tpu as pltpu
 from jax.sharding import PartitionSpec as P
 
-ITERS = 2
 VISCOSITY = 0.25
 TIME_STEP = 0.5
 PAD = 8
@@ -38,30 +37,35 @@
     return before_after, behind, ahead
 
 
+def pass_on(slabs, array, dx=0, dy=0):
+    gx, gy = lax.axis_size("gx"), lax.axis_size("gy")
+    pairs = []
+    for t in slabs:
+        for x in range(gx):
+            for y in range(gy):
+                source = (t * gx + x) * gy + y
+                target = ((t + 1) * gx + (x + dx) % gx) * gy + (y + dy) % gy
+                pairs.append((source, target))
+    return lax.ppermute(array, ("tm", "gx", "gy"), pairs)
+
+
 def hand_on(slabs, value, faces):
-    gx, gy = lax.axis_size("gx"), lax.axis_size("gy")
-
-    def permute(array, dx, dy):
-        pairs = []
-        for t in slabs:
-            for x in range(gx):
-                for y in range(gy):
-                    source = (t * gx + x) * gy + y
-                    target = ((t + 1) * gx + (x + dx) % gx) * gy + (y + dy) % gy
-                    pairs.append((source, target))
-        return lax.ppermute(array, ("tm", "gx", "gy"), pairs)
-
-    moved = [] if value is None else [permute(value, 0, 0)]
     x_faces, y_last, y_first = faces
-    moved.append(both_faces(x_faces, lambda a, by: permute(a, by, 0), gx))
-    moved.append(permute(y_last, 0, 1))
-    moved.append(permute(y_first, 0, -1))
-    return moved
+    return [
+        pass_on(slabs, value),
+        both_faces(x_faces, lambda a, by: pass_on(slabs, a, by, 0), lax.axis_size("gx")),
+        pass_on(slabs, y_last, 0, 1),
+        pass_on(slabs, y_first, 0, -1),
+    ]
 
 
 class Node:
     def __init__(self, main, x_faces, behind, ahead, off=0):
         self.main, self.x_faces, self.behind, self.ahead, self.off = main, x_faces, behind, ahead, off
+
+
+def scaled(weight, value):
+    return value if isinstance(weight, float) and weight == 1.0 else weight * value
 
 
 def total(terms):
@@ -87,7 +91,7 @@
     inner = slice(PAD, PAD + length)
     for c in range(3):
         for k, at in ((0, 0), (1, width + 1)):
-            terms = [w * n.x_faces[n.off + c, k] for w, n in parts]
+            terms = [scaled(w, n.x_faces[n.off + c, k]) for w, n in parts]
             terms += [w * p[c, k * (width // 2 + 1)] for w, p, _ in spread]
             ext[c, at, inner] = total(terms)
 
@@ -96,12 +100,12 @@
         for q in range(2):
             x = 2 * i + q
             for c in range(3):
-                terms = [w * n.main[c, x] for w, n in parts]
+                terms = [scaled(w, n.main[c, x]) for w, n in parts]
                 terms += [w * p[c, i + 1] for w, p, _ in spread]
                 ext[c, x + 1, inner] = total(terms)
                 row = pl.ds(x, 1)
                 for k, at in ((0, PAD - 1), (1, PAD + length)):
-                    terms = [w * (n.ahead if k else n.behind)[n.off + c, row] for w, n in parts]
+                    terms = [scaled(w, (n.ahead if k else n.behind)[n.off + c, row]) for w, n in parts]
                     terms += [w * e[k, c, pl.ds(i, 1)] for w, _, e in spread]
                     ext[c, x + 1, at : at + 1] = total(terms)
 
@@ -176,25 +180,37 @@
         store(c, value.reshape(cx, y // 2, z // 2))
 
 
+def spread_along(value):
+    cz = value.shape[1]
+    single = pair_table(cz, 2 * cz, False, 1.0)
+    table = jnp.concatenate([single, single], axis=0)
+    high, low = split(value)
+    return jnp.dot(jnp.concatenate([high, low], axis=1), table, preferred_element_type=F32)
+
+
+def doubled(value, rows):
+    count = value.shape[0]
+    rows[pl.ds(0, count, stride=2)] = value
+    rows[pl.ds(1, count, stride=2)] = value
+    return rows[...]
+
+
+def prolong_own(main, wide, rows):
+    cx, cy, cz = main.shape[1:]
+    for c in range(3):
+        value = doubled(main[c].reshape(cx * cy, cz), rows)
+        wide[c] = spread_along(value).reshape(cx, 2 * cy, 2 * cz)
+
+
 def prolong(field, wide, edge, rows):
     cx, cy, cz = field.main.shape[1:]
-    single = pair_table(cz, 2 * cz, False, 1.0)
-    table = jnp.concatenate([single, single], axis=0)
-
-    def along_z(value):
-        high, low = split(value)
-        return jnp.dot(jnp.concatenate([high, low], axis=1), table, preferred_element_type=F32)
-
-    count = (cx + 2) * cy
     edges = []
     for c in range(3):
         layers = [field.x_faces[c, 0:1], field.main[c], field.x_faces[c, 1:2]]
-        value = jnp.concatenate(layers, axis=0).reshape(count, cz)
-        rows[pl.ds(0, count, stride=2)] = value
-        rows[pl.ds(1, count, stride=2)] = value
-        wide[c] = along_z(rows[...]).reshape(cx + 2, 2 * cy, 2 * cz)
+        value = doubled(jnp.concatenate(layers, axis=0).reshape((cx + 2) * cy, cz), rows)
+        wide[c] = spread_along(value).reshape(cx + 2, 2 * cy, 2 * cz)
         edges += [field.behind[c], field.ahead[c]]
-    value = along_z(jnp.concatenate(edges, axis=0))
+    value = spread_along(jnp.concatenate(edges, axis=0))
     for c in range(3):
         for k in range(2):
             at = (2 * c + k) * cx
@@ -437,9 +453,9 @@
 
 def settle_later_kernel(count, first, *refs):
     arrived = [refs[4 * k : 4 * k + 4] for k in range(count)]
-    own, speed, coarse_grads = refs[4 * count : 4 * count + 3]
-    refs = refs[4 * count + 3 :]
-    d0, (d2, d2_x, d2_l, d2_f, ext) = refs[:4], refs[4:9]
+    own, speed, coarse_grads, s, u0, u1, u2, stage, stage_x, stage_l, stage_f, begin, rest = refs[4 * count : 4 * count + 13]
+    d0, (d2, ext, wide0, wide2, rows) = refs[4 * count + 13 : 4 * count + 17], refs[4 * count + 17 :]
+    f = first[0]
 
     def base(a, x):
         return own[a, x] + total([group[0][3 + a, x] for group in arrived])
@@ -451,7 +467,47 @@
     for k in range(1, 4):
         d0[k][...] = total([group[k][...] for group in arrived])
     chain_step(base, speed, coarse_grads, d0, ext, store)
-    emit_faces(d2, (d2_x, d2_l, d2_f))
+    prolong_own(d0[0], wide0, rows)
+    prolong_own(d2, wide2, rows)
+
+    @pl.loop(0, u0.shape[1] // 2)
+    def _(i):
+        for c in range(3):
+            p0, p2 = wide0[c, i], wide2[c, i]
+            toward_stage = TIME_STEP * (0.375 * p0 + 0.125 * p2)
+            toward_rest = 0.125 * (p2 - p0)
+            for q in range(2):
+                x = 2 * i + q
+                start, one, two = f * s[c, x] + u0[c, x], u1[c, x], u2[c, x]
+                stage[c, x] = toward_stage + TIME_STEP * (start * (5.0 / 24.0) + one / 3.0 - two / 24.0)
+                begin[c, x] = start + p0
+                rest[c, x] = toward_rest + (two * (5.0 / 24.0) - one / 6.0 - start / 24.0)
+
+    emit_faces(stage, (stage_x, stage_l, stage_f))
+
+
+def stage_kernel(first, v, grads, y, y_x, y_b, y_a, begin, *refs):
+    if len(refs) == 2:
+        out, ext = refs
+    else:
+        rest, out, following, following_x, following_l, following_f, ext = refs
+    fill(ext, [(1.0, Node(y, y_x, y_b, y_a))])
+    width, length = v.shape[1:3]
+    n = min(CHUNK, length)
+
+    @pl.loop(0, width)
+    def _(x):
+        for r in range(0, length, n):
+            at = slice(r, r + n)
+            changes = fine_rates(ext, v, grads, x, r, n)
+            for a in range(3):
+                value = begin[a, x, at] + changes[a]
+                out[a, x, at] = value
+                if len(refs) > 2:
+                    following[a, x, at] = TIME_STEP * (0.5 * value + rest[a, x, at])
+
+    if len(refs) > 2:
+        emit_faces(following, (following_x, following_l, following_f))
 
 
 def middle_kernel(nodes, *refs):
@@ -516,11 +572,10 @@
     emit_faces(a1, (a1_x, a1_l, a1_f))
 
 
-def finish_kernel(last, first, v, grads, a1, a1_x, a1_b, a1_a, rest, rest_x, rest_b, rest_a, *refs):
-    if last:
-        a2, ext = refs
-    else:
-        a2, a2_x, a2_l, a2_f, end, ext, summed, rows = refs
+def finish_kernel(
+    first, v, grads, a1, a1_x, a1_b, a1_a, rest, rest_x, rest_b, rest_a,
+    a2, a2_x, a2_l, a2_f, end, ext, summed, rows,
+):
     fill(
         ext,
         [
@@ -541,17 +596,15 @@
                 pair.append([a1[a, x, r : r + n] + changes[a] for a in range(3)])
                 for a in range(3):
                     a2[a, x, r : r + n] = pair[q][a]
-            if not last:
-                for a in range(3):
-                    summed[a, i, r : r + n] = pair[0][a] + pair[1][a]
-
-    if not last:
-        emit_faces(a2, (a2_x, a2_l, a2_f))
-
-        def store(c, value):
-            end[c] = value
-
-        squeeze(summed, rows, store, 3)
+            for a in range(3):
+                summed[a, i, r : r + n] = pair[0][a] + pair[1][a]
+
+    emit_faces(a2, (a2_x, a2_l, a2_f))
+
+    def store(c, value):
+        end[c] = value
+
+    squeeze(summed, rows, store, 3)
 
 
 def call(kernel, name, first, args, outs, scratch, flops=0):
@@ -602,71 +655,68 @@
         [ext, ext, summed, (9, cx, ny, nz), rows], 40_000_000,
     )
     zero_faces, sent = results[:3], results[3:]
-    for sweep_index in range(ITERS):
-        final = sweep_index + 1 == ITERS
-        if sweep_index == 0:
-            step, settle, outs, scratch = pass_start_kernel, settle_start_kernel, coarse, [coarse, *coarse_faces]
-            own_terms, end_terms = [zero, *zero_faces, integral], [end_two]
-            held = own_terms
-        else:
-            step, settle, outs, scratch = pass_later_kernel, settle_later_kernel, (6, cx, cy, cz), []
-            own_terms, end_terms = [own_part, following], []
-            held = [own_part]
+
+    def chain(step, sent, outs, scratch, own_terms):
         arrivals = []
         for turn in range(1, slabs):
-            arrivals.append(hand_on([turn - 1], sent[0], sent[1:]))
+            arrivals += hand_on([turn - 1], sent[0], sent[1:])
             if turn + 1 < slabs:
                 sent = call(
-                    lambda *refs, step=step, turn=turn: step(turn, *refs), "chain", first,
-                    [*arrivals[-1], *own_terms, speed, coarse_grads],
+                    lambda *refs, turn=turn: step(turn, *refs), "chain", first,
+                    [*arrivals[-4:], *own_terms, speed, coarse_grads],
                     [outs] + coarse_faces, scratch + [coarse_ext], 2_000_000,
                 )
-        results = call(
-            lambda *refs, settle=settle, count=len(arrivals): settle(count, *refs), "settle", first,
-            [a for group in arrivals for a in group] + held + [speed, coarse_grads] + end_terms,
-            [coarse] + coarse_faces + [coarse] + coarse_faces, [coarse_ext], 2_000_000,
-        )
-        d0, d2 = list(results[:4]), [results[4], *swap_faces(results[5:])]
-
-        if sweep_index == 0:
-            nodes = (
-                ((1.0, 0.0), (5.0 / 24.0, 0.0), (-1.0 / 24.0, 0.0), False, 6),
-                ((-1.0, 1.0), (-5.0 / 24.0, 0.5), (1.0 / 24.0, 0.0), False, 3),
-            )
-            args = [start_field, own]
-        else:
-            nodes = (
-                ((1.0, 0.0), (5.0 / 24.0, 0.0), (-1.0 / 24.0, 0.0), False, 6),
-                ((0.0, 1.0), (0.0, 5.0 / 24.0), (0.0, -1.0 / 24.0), True, 0),
-                ((0.0, 0.0), (0.0, 1.0 / 3.0), (0.0, -1.0 / 6.0), True, 0),
-                ((0.0, 0.0), (0.0, -1.0 / 24.0), (0.0, 5.0 / 24.0), True, 0),
-            )
-            args = [start_field, *u0, *u1, *u2]
-        middle, m_x, m_l, m_f, *rest = call(
-            lambda *refs, nodes=nodes: middle_kernel(nodes, *refs),
-            "middle", first, [velocity, grads, *layers, *args, *d0, *d2],
-            [fine] + fine_faces + [fine] + fine_faces,
-            [ext, wide, edge, wide, edge, wide_rows], 60_000_000,
-        )
-        u1 = [middle, *swap_faces((m_x, m_l, m_f))]
-        results = call(
-            lambda *refs, final=final: finish_kernel(final, *refs),
-            "finish", first, [velocity, grads, *u1, *rest],
-            [fine] if final else [fine] + fine_faces + [coarse],
-            [ext] if final else [ext, summed, rows], 40_000_000,
-        )
-        if final:
-            return results[0][None]
-        value, *faces = results[:4]
-        end_two = results[4]
-        u0 = hand_on(range(slabs - 1), value, faces)
-        u2 = [value, *swap_faces(faces)]
-        own_part, following, *sent = call(
-            offset_later_kernel, "offset_later", first,
-            [velocity, grads, start_field, *layers, *u1, *u2, zero, end_two],
-            [coarse, coarse, (6, cx, cy, cz)] + coarse_faces,
-            [ext, ext, summed, summed, rows], 60_000_000,
-        )
+        return arrivals
+
+    terms = [zero, *zero_faces, integral]
+    arrivals = chain(pass_start_kernel, sent, coarse, [coarse] + coarse_faces, terms)
+    results = call(
+        lambda *refs: settle_start_kernel(slabs - 1, *refs), "settle", first,
+        [*arrivals, *terms, speed, coarse_grads, end_two],
+        [coarse] + coarse_faces + [coarse] + coarse_faces, [coarse_ext], 2_000_000,
+    )
+    d0, d2 = list(results[:4]), [results[4], *swap_faces(results[5:])]
+    nodes = (
+        ((1.0, 0.0), (5.0 / 24.0, 0.0), (-1.0 / 24.0, 0.0), False, 6),
+        ((-1.0, 1.0), (-5.0 / 24.0, 0.5), (1.0 / 24.0, 0.0), False, 3),
+    )
+    middle, m_x, m_l, m_f, *rest = call(
+        lambda *refs: middle_kernel(nodes, *refs), "middle", first,
+        [velocity, grads, *layers, start_field, own, *d0, *d2],
+        [fine] + fine_faces + [fine] + fine_faces,
+        [ext, wide, edge, wide, edge, wide_rows], 60_000_000,
+    )
+    u1 = [middle, *swap_faces((m_x, m_l, m_f))]
+    value, *results = call(
+        finish_kernel, "finish", first, [velocity, grads, *u1, *rest],
+        [fine] + fine_faces + [coarse], [ext, summed, rows], 40_000_000,
+    )
+    faces, end_two = results[:3], results[3]
+    u0 = pass_on(range(slabs - 1), value)
+    u2 = [value, *swap_faces(faces)]
+
+    own_part, following, *sent = call(
+        offset_later_kernel, "offset_later", first,
+        [velocity, grads, start_field, *layers, *u1, *u2, zero, end_two],
+        [coarse, coarse, (6, cx, cy, cz)] + coarse_faces,
+        [ext, ext, summed, summed, rows], 60_000_000,
+    )
+    arrivals = chain(pass_later_kernel, sent, (6, cx, cy, cz), [], [own_part, following])
+    stage, *faces, begin, rest = call(
+        lambda *refs: settle_later_kernel(slabs - 1, *refs), "settle", first,
+        [*arrivals, own_part, speed, coarse_grads, start_field, u0, middle, value],
+        [fine] + fine_faces + [fine, fine],
+        [coarse, *coarse_faces, coarse, coarse_ext, summed, summed, rows], 10_000_000,
+    )
+    middle, stage, *faces = call(
+        stage_kernel, "stage", first, [velocity, grads, stage, *swap_faces(faces), begin, rest],
+        [fine, fine] + fine_faces, [ext], 40_000_000,
+    )
+    result, = call(
+        stage_kernel, "stage", first, [velocity, grads, stage, *swap_faces(faces), middle],
+        [fine], [ext], 40_000_000,
+    )
+    return result[None]
 
 
 def solution(mesh):

time: 160 us -> 143 us (0.89)
  starting transfers between devices: 59.6 us -> 49.3 us
  waiting for transfers between devices: 59.9 us -> 54.5 us
    ppermute x28 -> x25, starting transfers between devices: 39.5 us -> 28 us  [pass_on(): return lax.ppermute(array, ('tm', 'gx', 'gy'), pairs)]
    ppermute x28 -> x25, waiting for transfers between devices: 26 us -> 22.1 us  [pass_on(): return lax.ppermute(array, ('tm', 'gx', 'gy'), pairs)]
    ppermute x6, waiting for transfers between devices: 14.8 us -> 11.2 us  [swap_faces(): ahead = lax.ppermute(y_first, 'gy', ring(gy, -1))]
    ppermute x6, waiting for transfers between devices: 13.3 us -> 15.3 us  [swap_faces(): behind = lax.ppermute(y_last, 'gy', ring(gy, 1))]
    ppermute x6, starting transfers between devices: 7.87 us -> 9.82 us  [swap_faces(): ahead = lax.ppermute(y_first, 'gy', ring(gy, -1))]
  transfers between devices with their start and end apart: 46 -> 43, of which waited for: 21 -> 22; matrix products, arithmetic and copies ran while one was open for 0% -> 0% of each run, Pallas kernels for 6% -> 6%
where the time goes in v6:
time: 143 us; the launch traced here: 142 us
  waiting for transfers between devices  54.5 us (38%)
  starting transfers between devices  49.3 us (34%)
  Pallas kernels  33.7 us (24%)
  local copies, waits for them, and re-layouts  4.23 us (3%)
    pallas_call x14, Pallas kernels, call(): pl.pallas_call(kernel, name=name, out_shape=[jax.ShapeDtypeStruct(dims, F...  33.7 us
    ppermute x25, starting transfers between devices, pass_on(): return lax.ppermute(array, ('tm', 'gx', 'gy'), pairs)  28 us
    ppermute x25, waiting for transfers between devices, pass_on(): return lax.ppermute(array, ('tm', 'gx', 'gy'), pairs)  22.1 us
    ppermute x6, waiting for transfers between devices, swap_faces(): behind = lax.ppermute(y_last, 'gy', ring(gy, 1))  15.3 us
    ppermute x6, waiting for transfers between devices, swap_faces(): ahead = lax.ppermute(y_first, 'gy', ring(gy, -1))  11.2 us
    ppermute x6, starting transfers between devices, swap_faces(): ahead = lax.ppermute(y_first, 'gy', ring(gy, -1))  9.82 us
    ppermute x6, starting transfers between devices, swap_faces(): lax.ppermute(a, 'gx', ring(gx, by))  8.32 us
    ppermute x6, waiting for transfers between devices, swap_faces(): lax.ppermute(a, 'gx', ring(gx, by))  5.9 us
  transfers between devices with their start and end apart: 43, of which 22 were waited for; matrix products, arithmetic and copies ran while one was open for 0% of the time, Pallas kernels for 6%

profile of v6, /device:TPU:26, one launch (start us, length us, event | category | flops | bytes accessed | tf_op | source)
XLA Modules:
  0.0 142.1 jit_solution(9133891571826154378)
XLA Ops:
  10.8 5.5 %collective-permute-done.1.behind.refs_4_ = f32[10,16,256]{2,1,0:T(8,128)S(1)} collective-permute-done((f32[10,16,256]{2,1,0:T(8,128)S(1)}, f32[10,16,256]{2,1,0:T(8,128)S(1)}, u32[]{:S(2)}, u32[]{:S(2)}) %collective-permute-start.1) | collective-permute-done | bytes 163872 | tf_op jit(solution)/shard_map/ppermute | solution.py:35
  16.3 5.8 %collective-permute-done.x_faces.refs_3_ = f32[10,2,32,256]{3,2,1,0:T(8,128)S(1)} collective-permute-done((f32[10,2,32,256]{3,2,1,0:T(8,128)S(1)}, f32[10,2,32,256]{3,2,1,0:T(8,128)S(1)}, u32[]{:S(2)}, u32[]{:S(2)}) %collective-permute-start) | collective-permute-done | bytes 655392 | tf_op jit(solution)/shard_map/ppermute | solution.py:34
  22.1 5.0 %offset_start.1 = (f32[9,16,32,256]{3,2,1,0:T(8,128)S(1)}, f32[3,8,16,128]{3,2,1,0:T(8,128)S(1)}, f32[9,8,16,128]{3,2,1,0:T(8,128)S(1)}, f32[3,2,16,128]{3,2,1,0...) custom-call(f32[2]{0:T(128)S(1)} %add_convert_fusion.first.refs_0_, ...), custom_call_target="tpu_custom_call" | custom-call | flops 40000000 | bytes 5898240 | tf_op jit(solution)/shard_map/offset_start/pallas_call | solution.py:613
  35.6 6.7 %collective-permute-done.9.refs_3_.refs_7_ = f32[3,8,128]{2,1,0:T(8,128)S(1)} collective-permute-done((f32[3,8,128]{2,1,0:T(8,128)S(1)}, f32[3,8,128]{2,1,0:T(8,128)S(1)}, u32[]{:S(2)}, u32[]{:S(2)}) %collective-permute-start.9) | collective-permute-done | bytes 12320 | tf_op jit(solution)/shard_map/ppermute | solution.py:49
  53.3 2.9 %collective-permute-start.16 = (f32[3,8,128]{2,1,0:T(8,128)S(1)}, f32[3,8,128]{2,1,0:T(8,128)S(1)}, u32[]{:S(2)}, u32[]{:S(2)}) collective-permute-start(f32[3,8,128]{2,1,0:T(8,128)S(1)} %get-tuple-element.105), channel_id=1, source_target_pairs={{0,1},{1,2},{2,3},{3,0},{4,5},{5,6},{6,7},{7,4},{8,9},{9,10},{10,1... | collective-permute-start | bytes 36872 | tf_op jit(solution)/shard_map/ppermute | solution.py:35
  57.6 4.1 %collective-permute-done.17.refs_15_ = f32[3,8,128]{2,1,0:T(8,128)S(1)} collective-permute-done((f32[3,8,128]{2,1,0:T(8,128)S(1)}, f32[3,8,128]{2,1,0:T(8,128)S(1)}, u32[]{:S(2)}, u32[]{:S(2)}) %collective-permute-start.17) | collective-permute-done | bytes 12320 | tf_op jit(solution)/shard_map/ppermute | solution.py:36
  61.7 4.2 %middle.1 = (f32[3,16,32,256]{3,2,1,0:T(8,128)S(1)}, f32[3,2,32,256]{3,2,1,0:T(8,128)S(1)}, f32[3,16,256]{2,1,0:T(8,128)S(1)}, f32[3,16,256]{2,1,0:T(8,128)S(1)}...) custom-call(f32[2]{0:T(128)S(1)} %add_convert_fusion.first.refs_0_, ...), custom_call_target="tpu_custom_call" | custom-call | flops 60000000 | bytes 10960896 | tf_op jit(solution)/shard_map/middle/pallas_call | solution.py:613
  66.5 2.0 %collective-permute-start.20 = (f32[3,16,256]{2,1,0:T(8,128)S(1)}, f32[3,16,256]{2,1,0:T(8,128)S(1)}, u32[]{:S(2)}, u32[]{:S(2)}) collective-permute-start(f32[3,16,256]{2,1,0:T(8,128)S(1)} %get-tuple-element.110), channel_id=1, source_target_pairs={{0,3},{1,0},{2,1},{3,2},{4,7},{5,4},{6,5},{7,6},{8,11},{9,8},{10,9... | collective-permute-start | bytes 147464 | tf_op jit(solution)/shard_map/ppermute | solution.py:36
  68.6 2.2 %collective-permute-done.19.a1_b.u1_b = f32[3,16,256]{2,1,0:T(8,128)S(1)} collective-permute-done((f32[3,16,256]{2,1,0:T(8,128)S(1)}, f32[3,16,256]{2,1,0:T(8,128)S(1)}, u32[]{:S(2)}, u32[]{:S(2)}) %collective-permute-start.19) | collective-permute-done | bytes 49184 | tf_op jit(solution)/shard_map/ppermute | solution.py:35
  72.4 3.3 %finish.1 = (f32[3,16,32,256]{3,2,1,0:T(8,128)S(1)}, f32[3,2,32,256]{3,2,1,0:T(8,128)S(1)}, f32[3,16,256]{2,1,0:T(8,128)S(1)}, f32[3,16,256]{2,1,0:T(8,128)S(1)}, f32[3,8,16,128]{3,2,1,0:T(8,128)S(1)}) custom-call(f32[2]{0:T(128)S(1)} %add_convert_fusion.first.refs_0_, f32[3,16,32,256]{3,2,1,0:T(8,128)S(1)} %copy-done.1, ...), custom_call_target="tpu_custom_call" | custom-call | flops 40000000 | bytes 10027008 | tf_op jit(solution)/shard_map/finish/pallas_call | solution.py:613
  75.7 1.9 %collective-permute-start.36 = (f32[3,16,32,256]{3,2,1,0:T(8,128)S(1)}, f32[3,16,32,256]{3,2,1,0:T(8,128)S(1)}, u32[]{:S(2)}, u32[]{:S(2)}) collective-permute-start(f32[3,16,32,256]{3,2,1,0:T(8,128)S(1)} %get-tuple-element.115.u2.refs_19_), channel_id=1, source_target_pairs={{0,8},{1,9},{2,10},{3,11},{4,12},{5,13},{6,14},{7,15},{8,16},{9,17... | collective-permute-start | bytes 4718600 | tf_op jit(solution)/shard_map/ppermute | solution.py:49
  79.2 2.0 %collective-permute-start.23 = (f32[3,16,256]{2,1,0:T(8,128)S(1)}, f32[3,16,256]{2,1,0:T(8,128)S(1)}, u32[]{:S(2)}, u32[]{:S(2)}) collective-permute-start(f32[3,16,256]{2,1,0:T(8,128)S(1)} %get-tuple-element.118), channel_id=1, source_target_pairs={{0,3},{1,0},{2,1},{3,2},{4,7},{5,4},{6,5},{7,6},{8,11},{9,8},{10,9... | collective-permute-start | bytes 147464 | tf_op jit(solution)/shard_map/ppermute | solution.py:36
  81.2 2.1 %collective-permute-done.22.u2_b = f32[3,16,256]{2,1,0:T(8,128)S(1)} collective-permute-done((f32[3,16,256]{2,1,0:T(8,128)S(1)}, f32[3,16,256]{2,1,0:T(8,128)S(1)}, u32[]{:S(2)}, u32[]{:S(2)}) %collective-permute-start.22) | collective-permute-done | bytes 49184 | tf_op jit(solution)/shard_map/ppermute | solution.py:35
  85.1 5.4 %offset_later.1 = (f32[3,8,16,128]{3,2,1,0:T(8,128)S(1)}, f32[3,8,16,128]{3,2,1,0:T(8,128)S(1)}, f32[6,8,16,128]{3,2,1,0:T(8,128)S(1)}, f32[3,2,16,128]{3,2,1,0:...) custom-call(f32[2]{0:T(128)S(1)} %add_convert_fusion.first.refs_0_, f32[3,16,32,256]{3,2,1,0:T(8,128)S(1)} %copy-done.1, ...), custom_call_target="tpu_custom_call" | custom-call | flops 60000000 | bytes 12976128 | tf_op jit(solution)/shard_map/offset_later/pallas_call | solution.py:613
  99.0 6.9 %collective-permute-done.30.refs_3_.refs_7_ = f32[3,8,128]{2,1,0:T(8,128)S(1)} collective-permute-done((f32[3,8,128]{2,1,0:T(8,128)S(1)}, f32[3,8,128]{2,1,0:T(8,128)S(1)}, u32[]{:S(2)}, u32[]{:S(2)}) %collective-permute-start.30) | collective-permute-done | bytes 12320 | tf_op jit(solution)/shard_map/ppermute | solution.py:49
  107.7 2.1 %collective-permute-done.29.refs_2_.refs_6_ = f32[3,2,16,128]{3,2,1,0:T(8,128)S(1)} collective-permute-done((f32[3,2,16,128]{3,2,1,0:T(8,128)S(1)}, f32[3,2,16,128]{3,2,1,0:T(8,128)S(1)}, u32[]{:S(2)}, u32[]{:S(2)}) %collective-permute-start.29) | collective-permute-done | bytes 49184 | tf_op jit(solution)/shard_map/ppermute | solution.py:49
  117.3 2.3 %settle.3 = (f32[3,16,32,256]{3,2,1,0:T(8,128)S(1)}, f32[3,2,32,256]{3,2,1,0:T(8,128)S(1)}, f32[3,16,256]{2,1,0:T(8,128)S(1)}, f32[3,16,256]{2,1,0:T(8,128)S(1)}...) custom-call(f32[2]{0:T(128)S(1)} %add_convert_fusion.first.refs_0_, ...), custom_call_target="tpu_custom_call" | custom-call | flops 10000000 | bytes 8675328 | tf_op jit(solution)/shard_map/settle/pallas_call | solution.py:613
  121.3 2.0 %collective-permute-start.39 = (f32[3,16,256]{2,1,0:T(8,128)S(1)}, f32[3,16,256]{2,1,0:T(8,128)S(1)}, u32[]{:S(2)}, u32[]{:S(2)}) collective-permute-start(f32[3,16,256]{2,1,0:T(8,128)S(1)} %get-tuple-element.137), channel_id=1, source_target_pairs={{0,3},{1,0},{2,1},{3,2},{4,7},{5,4},{6,5},{7,6},{8,11},{9,8},{10,9... | collective-permute-start | bytes 147464 | tf_op jit(solution)/shard_map/ppermute | solution.py:36
  123.3 2.1 %collective-permute-done.38.y_b = f32[3,16,256]{2,1,0:T(8,128)S(1)} collective-permute-done((f32[3,16,256]{2,1,0:T(8,128)S(1)}, f32[3,16,256]{2,1,0:T(8,128)S(1)}, u32[]{:S(2)}, u32[]{:S(2)}) %collective-permute-start.38) | collective-permute-done | bytes 49184 | tf_op jit(solution)/shard_map/ppermute | solution.py:35
  127.3 3.0 %stage.2 = (f32[3,16,32,256]{3,2,1,0:T(8,128)S(1)}, f32[3,16,32,256]{3,2,1,0:T(8,128)S(1)}, f32[3,2,32,256]{3,2,1,0:T(8,128)S(1)}, f32[3,16,256]{2,1,0:T(8,128)S(1)}, f32[3,16,256]{2,1,0:T(8,128)S(1)}) custom-call(f32[2]{0:T(128)S(1)} %add_convert_fusion.first.refs_0_, f32[3,16,32,256]{3,2,1,0:T(8,128)S(1)} %copy-done.1, ...), custom_call_target="tpu_custom_call" | custom-call | flops 40000000 | bytes 11304960 | tf_op jit(solution)/shard_map/stage/pallas_call | solution.py:613
  130.3 2.0 %collective-permute-start.40 = (f32[3,2,32,256]{3,2,1,0:T(8,128)S(1)}, f32[3,2,32,256]{3,2,1,0:T(8,128)S(1)}, u32[]{:S(2)}, u32[]{:S(2)}) collective-permute-start(f32[3,2,32,256]{3,2,1,0:T(8,128)S(1)} %get-tuple-element.141), channel_id=1, source_target_pairs={{0,4},{4,0},{1,5},{5,1},{2,6},{6,2},{3,7},{7,3},{8,12},{12,8},{9,1... | collective-permute-start | bytes 589832 | tf_op jit(solution)/shard_map/ppermute | solution.py:34
  132.3 2.0 %collective-permute-start.42 = (f32[3,16,256]{2,1,0:T(8,128)S(1)}, f32[3,16,256]{2,1,0:T(8,128)S(1)}, u32[]{:S(2)}, u32[]{:S(2)}) collective-permute-start(f32[3,16,256]{2,1,0:T(8,128)S(1)} %get-tuple-element.143), channel_id=1, source_target_pairs={{0,3},{1,0},{2,1},{3,2},{4,7},{5,4},{6,5},{7,6},{8,11},{9,8},{10,9... | collective-permute-start | bytes 147464 | tf_op jit(solution)/shard_map/ppermute | solution.py:36
  134.3 2.1 %collective-permute-done.41.y_b = f32[3,16,256]{2,1,0:T(8,128)S(1)} collective-permute-done((f32[3,16,256]{2,1,0:T(8,128)S(1)}, f32[3,16,256]{2,1,0:T(8,128)S(1)}, u32[]{:S(2)}, u32[]{:S(2)}) %collective-permute-start.41) | collective-permute-done | bytes 49184 | tf_op jit(solution)/shard_map/ppermute | solution.py:35
  138.2 3.9 %stage.3 = f32[3,16,32,256]{3,2,1,0:T(8,128)} custom-call(f32[2]{0:T(128)S(1)} %add_convert_fusion.first.refs_0_, f32[3,16,32,256]{3,2,1,0:T(8,128)S(1)} %copy-done.1, f32[9,16,32,256]{3,2,1,0:T(8,128)S(1)} %get-tuple-element.80.refs_2_.grads, f32[3,16,32,256]{3,2,1,0:T(8,128)S(1)} %get-tuple-element.140.y, ...), custom_call_target="tpu_custom_call" | custom-call | flops 40000000 | bytes 9732096 | tf_op jit(solution)/shard_map/stage/pallas_call | solution.py:613
  (89 shorter events, 60.3 us)
Async XLA Ops:
  5.6 16.5 %collective-permute-start = (f32[10,2,32,256]{3,2,1,0:T(8,128)S(1)}, f32[10,2,32,256]{3,2,1,0:T(8,128)S(1)}, u32[]{:S(2)}, u32[]{:S(2)}) collective-permute-start(f32[10,2,32,256]{3,2,1,0:T(8,128)S(1)} %get-tuple-element.75), channel_id=1, source_target_pairs={{0,4},{4,0},{1,5},{5,1},{2,6},{6,2},{3,7},{7,3},{8,12},{12,8},{9,1... | collective-permute-start | bytes 1966088 | tf_op jit(solution)/shard_map/ppermute | solution.py:34
  7.2 9.2 %collective-permute-start.1 = (f32[10,16,256]{2,1,0:T(8,128)S(1)}, f32[10,16,256]{2,1,0:T(8,128)S(1)}, u32[]{:S(2)}, u32[]{:S(2)}) collective-permute-start(f32[10,16,256]{2,1,0:T(8,128)S(1)} %get-tuple-element.76), channel_id=1, source_target_pairs={{0,1},{1,2},{2,3},{3,0},{4,5},{5,6},{6,7},{7,4},{8,9},{9,10},{10,1... | collective-permute-start | bytes 491528 | tf_op jit(solution)/shard_map/ppermute | solution.py:35
  7.4 9.0 %collective-permute-start.2 = (f32[10,16,256]{2,1,0:T(8,128)S(1)}, f32[10,16,256]{2,1,0:T(8,128)S(1)}, u32[]{:S(2)}, u32[]{:S(2)}) collective-permute-start(f32[10,16,256]{2,1,0:T(8,128)S(1)} %get-tuple-element.77), channel_id=1, source_target_pairs={{0,3},{1,0},{2,1},{3,2},{4,7},{5,4},{6,5},{7,6},{8,11},{9,8},{10,9... | collective-permute-start | bytes 491528 | tf_op jit(solution)/shard_map/ppermute | solution.py:36
  30.4 13.6 %collective-permute-start.7 = (f32[3,8,16,128]{3,2,1,0:T(8,128)S(1)}, f32[3,8,16,128]{3,2,1,0:T(8,128)S(1)}, u32[]{:S(2)}, u32[]{:S(2)}) collective-permute-start(f32[3,8,16,128]{3,2,1,0:T(8,128)S(1)} %get-tuple-element.91), channel_id=1, source_target_pairs={{8,16},{9,17},{10,18},{11,19},{12,20},{13,21},{14,22},{15,23}} | collective-permute-start | bytes 589832 | tf_op jit(solution)/shard_map/ppermute | solution.py:49
  31.7 12.3 %collective-permute-start.8 = (f32[3,2,16,128]{3,2,1,0:T(8,128)S(1)}, f32[3,2,16,128]{3,2,1,0:T(8,128)S(1)}, u32[]{:S(2)}, u32[]{:S(2)}) collective-permute-start(f32[3,2,16,128]{3,2,1,0:T(8,128)S(1)} %get-tuple-element.92), channel_id=1, source_target_pairs={{8,20},{9,21},{10,22},{11,23},{12,16},{13,17},{14,18},{15,19}} | collective-permute-start | bytes 147464 | tf_op jit(solution)/shard_map/ppermute | solution.py:49
  33.0 9.3 %collective-permute-start.9 = (f32[3,8,128]{2,1,0:T(8,128)S(1)}, f32[3,8,128]{2,1,0:T(8,128)S(1)}, u32[]{:S(2)}, u32[]{:S(2)}) collective-permute-start(f32[3,8,128]{2,1,0:T(8,128)S(1)} %get-tuple-element.93), channel_id=1, source_target_pairs={{8,17},{9,18},{10,19},{11,16},{12,21},{13,22},{14,23},{15,20}} | collective-permute-start | bytes 36872 | tf_op jit(solution)/shard_map/ppermute | solution.py:49
  34.3 9.7 %collective-permute-start.10 = (f32[3,8,128]{2,1,0:T(8,128)S(1)}, f32[3,8,128]{2,1,0:T(8,128)S(1)}, u32[]{:S(2)}, u32[]{:S(2)}) collective-permute-start(f32[3,8,128]{2,1,0:T(8,128)S(1)} %get-tuple-element.94), channel_id=1, source_target_pairs={{8,19},{9,16},{10,17},{11,18},{12,23},{13,20},{14,21},{15,22}} | collective-permute-start | bytes 36872 | tf_op jit(solution)/shard_map/ppermute | solution.py:49
  44.8 6.6 %collective-permute-start.11 = (f32[3,8,16,128]{3,2,1,0:T(8,128)S(1)}, f32[3,8,16,128]{3,2,1,0:T(8,128)S(1)}, u32[]{:S(2)}, u32[]{:S(2)}) collective-permute-start(f32[3,8,16,128]{3,2,1,0:T(8,128)S(1)} %get-tuple-element.95), channel_id=1, source_target_pairs={{16,24},{17,25},{18,26},{19,27},{20,28},{21,29},{22,30},{23,31}} | collective-permute-start | bytes 589832 | tf_op jit(solution)/shard_map/ppermute | solution.py:49
  52.3 9.4 %collective-permute-start.15 = (f32[3,2,16,128]{3,2,1,0:T(8,128)S(1)}, f32[3,2,16,128]{3,2,1,0:T(8,128)S(1)}, u32[]{:S(2)}, u32[]{:S(2)}) collective-permute-start(f32[3,2,16,128]{3,2,1,0:T(8,128)S(1)} %get-tuple-element.104), channel_id=1, source_target_pairs={{0,4},{4,0},{1,5},{5,1},{2,6},{6,2},{3,7},{7,3},{8,12},{12,8},{9,1... | collective-permute-start | bytes 147464 | tf_op jit(solution)/shard_map/ppermute | solution.py:34
  56.2 5.5 %collective-permute-start.17 = (f32[3,8,128]{2,1,0:T(8,128)S(1)}, f32[3,8,128]{2,1,0:T(8,128)S(1)}, u32[]{:S(2)}, u32[]{:S(2)}) collective-permute-start(f32[3,8,128]{2,1,0:T(8,128)S(1)} %get-tuple-element.106), channel_id=1, source_target_pairs={{0,3},{1,0},{2,1},{3,2},{4,7},{5,4},{6,5},{7,6},{8,11},{9,8},{10,9... | collective-permute-start | bytes 36872 | tf_op jit(solution)/shard_map/ppermute | solution.py:36
  65.9 6.5 %collective-permute-start.18 = (f32[3,2,32,256]{3,2,1,0:T(8,128)S(1)}, f32[3,2,32,256]{3,2,1,0:T(8,128)S(1)}, u32[]{:S(2)}, u32[]{:S(2)}) collective-permute-start(f32[3,2,32,256]{3,2,1,0:T(8,128)S(1)} %get-tuple-element.108), channel_id=1, source_target_pairs={{0,4},{4,0},{1,5},{5,1},{2,6},{6,2},{3,7},{7,3},{8,12},{12,8},{9,1... | collective-permute-start | bytes 589832 | tf_op jit(solution)/shard_map/ppermute | solution.py:34
  66.5 5.9 %collective-permute-start.20 = (f32[3,16,256]{2,1,0:T(8,128)S(1)}, f32[3,16,256]{2,1,0:T(8,128)S(1)}, u32[]{:S(2)}, u32[]{:S(2)}) collective-permute-start(f32[3,16,256]{2,1,0:T(8,128)S(1)} %get-tuple-element.110), channel_id=1, source_target_pairs={{0,3},{1,0},{2,1},{3,2},{4,7},{5,4},{6,5},{7,6},{8,11},{9,8},{10,9... | collective-permute-start | bytes 147464 | tf_op jit(solution)/shard_map/ppermute | solution.py:36
  75.7 41.7 %collective-permute-start.36 = (f32[3,16,32,256]{3,2,1,0:T(8,128)S(1)}, f32[3,16,32,256]{3,2,1,0:T(8,128)S(1)}, u32[]{:S(2)}, u32[]{:S(2)}) collective-permute-start(f32[3,16,32,256]{3,2,1,0:T(8,128)S(1)} %get-tuple-element.115.u2.refs_19_), channel_id=1, source_target_pairs={{0,8},{1,9},{2,10},{3,11},{4,12},{5,13},{6,14},{7,15},{8,16},{9,17... | collective-permute-start | bytes 4718600 | tf_op jit(solution)/shard_map/ppermute | solution.py:49
  77.6 7.5 %collective-permute-start.21 = (f32[3,2,32,256]{3,2,1,0:T(8,128)S(1)}, f32[3,2,32,256]{3,2,1,0:T(8,128)S(1)}, u32[]{:S(2)}, u32[]{:S(2)}) collective-permute-start(f32[3,2,32,256]{3,2,1,0:T(8,128)S(1)} %get-tuple-element.116), channel_id=1, source_target_pairs={{0,4},{4,0},{1,5},{5,1},{2,6},{6,2},{3,7},{7,3},{8,12},{12,8},{9,1... | collective-permute-start | bytes 589832 | tf_op jit(solution)/shard_map/ppermute | solution.py:34
  79.2 5.9 %collective-permute-start.23 = (f32[3,16,256]{2,1,0:T(8,128)S(1)}, f32[3,16,256]{2,1,0:T(8,128)S(1)}, u32[]{:S(2)}, u32[]{:S(2)}) collective-permute-start(f32[3,16,256]{2,1,0:T(8,128)S(1)} %get-tuple-element.118), channel_id=1, source_target_pairs={{0,3},{1,0},{2,1},{3,2},{4,7},{5,4},{6,5},{7,6},{8,11},{9,8},{10,9... | collective-permute-start | bytes 147464 | tf_op jit(solution)/shard_map/ppermute | solution.py:36
  93.8 16.0 %collective-permute-start.28 = (f32[6,8,16,128]{3,2,1,0:T(8,128)S(1)}, f32[6,8,16,128]{3,2,1,0:T(8,128)S(1)}, u32[]{:S(2)}, u32[]{:S(2)}) collective-permute-start(f32[6,8,16,128]{3,2,1,0:T(8,128)S(1)} %get-tuple-element.126), channel_id=1, source_target_pairs={{8,16},{9,17},{10,18},{11,19},{12,20},{13,21},{14,22},{15,23}} | collective-permute-start | bytes 1179656 | tf_op jit(solution)/shard_map/ppermute | solution.py:49
  95.1 14.7 %collective-permute-start.29 = (f32[3,2,16,128]{3,2,1,0:T(8,128)S(1)}, f32[3,2,16,128]{3,2,1,0:T(8,128)S(1)}, u32[]{:S(2)}, u32[]{:S(2)}) collective-permute-start(f32[3,2,16,128]{3,2,1,0:T(8,128)S(1)} %get-tuple-element.127), channel_id=1, source_target_pairs={{8,20},{9,21},{10,22},{11,23},{12,16},{13,17},{14,18},{15,19}} | collective-permute-start | bytes 147464 | tf_op jit(solution)/shard_map/ppermute | solution.py:49
  96.4 9.5 %collective-permute-start.30 = (f32[3,8,128]{2,1,0:T(8,128)S(1)}, f32[3,8,128]{2,1,0:T(8,128)S(1)}, u32[]{:S(2)}, u32[]{:S(2)}) collective-permute-start(f32[3,8,128]{2,1,0:T(8,128)S(1)} %get-tuple-element.128), channel_id=1, source_target_pairs={{8,17},{9,18},{10,19},{11,16},{12,21},{13,22},{14,23},{15,20}} | collective-permute-start | bytes 36872 | tf_op jit(solution)/shard_map/ppermute | solution.py:49
  97.7 10.0 %collective-permute-start.31 = (f32[3,8,128]{2,1,0:T(8,128)S(1)}, f32[3,8,128]{2,1,0:T(8,128)S(1)}, u32[]{:S(2)}, u32[]{:S(2)}) collective-permute-start(f32[3,8,128]{2,1,0:T(8,128)S(1)} %get-tuple-element.129), channel_id=1, source_target_pairs={{8,19},{9,16},{10,17},{11,18},{12,23},{13,20},{14,21},{15,22}} | collective-permute-start | bytes 36872 | tf_op jit(solution)/shard_map/ppermute | solution.py:49
  110.7 6.6 %collective-permute-start.32 = (f32[6,8,16,128]{3,2,1,0:T(8,128)S(1)}, f32[6,8,16,128]{3,2,1,0:T(8,128)S(1)}, u32[]{:S(2)}, u32[]{:S(2)}) collective-permute-start(f32[6,8,16,128]{3,2,1,0:T(8,128)S(1)} %get-tuple-element.130), channel_id=1, source_target_pairs={{16,24},{17,25},{18,26},{19,27},{20,28},{21,29},{22,30},{23,31}} | collective-permute-start | bytes 1179656 | tf_op jit(solution)/shard_map/ppermute | solution.py:49
  119.7 7.7 %collective-permute-start.37 = (f32[3,2,32,256]{3,2,1,0:T(8,128)S(1)}, f32[3,2,32,256]{3,2,1,0:T(8,128)S(1)}, u32[]{:S(2)}, u32[]{:S(2)}) collective-permute-start(f32[3,2,32,256]{3,2,1,0:T(8,128)S(1)} %get-tuple-element.135), channel_id=1, source_target_pairs={{0,4},{4,0},{1,5},{5,1},{2,6},{6,2},{3,7},{7,3},{8,12},{12,8},{9,1... | collective-permute-start | bytes 589832 | tf_op jit(solution)/shard_map/ppermute | solution.py:34
  121.3 5.9 %collective-permute-start.39 = (f32[3,16,256]{2,1,0:T(8,128)S(1)}, f32[3,16,256]{2,1,0:T(8,128)S(1)}, u32[]{:S(2)}, u32[]{:S(2)}) collective-permute-start(f32[3,16,256]{2,1,0:T(8,128)S(1)} %get-tuple-element.137), channel_id=1, source_target_pairs={{0,3},{1,0},{2,1},{3,2},{4,7},{5,4},{6,5},{7,6},{8,11},{9,8},{10,9... | collective-permute-start | bytes 147464 | tf_op jit(solution)/shard_map/ppermute | solution.py:36
  130.3 7.9 %collective-permute-start.40 = (f32[3,2,32,256]{3,2,1,0:T(8,128)S(1)}, f32[3,2,32,256]{3,2,1,0:T(8,128)S(1)}, u32[]{:S(2)}, u32[]{:S(2)}) collective-permute-start(f32[3,2,32,256]{3,2,1,0:T(8,128)S(1)} %get-tuple-element.141), channel_id=1, source_target_pairs={{0,4},{4,0},{1,5},{5,1},{2,6},{6,2},{3,7},{7,3},{8,12},{12,8},{9,1... | collective-permute-start | bytes 589832 | tf_op jit(solution)/shard_map/ppermute | solution.py:34
  132.3 5.9 %collective-permute-start.42 = (f32[3,16,256]{2,1,0:T(8,128)S(1)}, f32[3,16,256]{2,1,0:T(8,128)S(1)}, u32[]{:S(2)}, u32[]{:S(2)}) collective-permute-start(f32[3,16,256]{2,1,0:T(8,128)S(1)} %get-tuple-element.143), channel_id=1, source_target_pairs={{0,3},{1,0},{2,1},{3,2},{4,7},{5,4},{6,5},{7,6},{8,11},{9,8},{10,9... | collective-permute-start | bytes 147464 | tf_op jit(solution)/shard_map/ppermute | solution.py:36
  (25 other events, 90.7 us)

commit v7 on v6

--- a/solution.py
+++ b/solution.py
@@ -51,17 +51,24 @@
 
 def hand_on(slabs, value, faces):
     x_faces, y_last, y_first = faces
-    return [
-        pass_on(slabs, value),
-        both_faces(x_faces, lambda a, by: pass_on(slabs, a, by, 0), lax.axis_size("gx")),
-        pass_on(slabs, y_last, 0, 1),
-        pass_on(slabs, y_first, 0, -1),
-    ]
+    main = pass_on(slabs, value)
+    behind = pass_on(slabs, y_last, 0, 1)
+    ahead = pass_on(slabs, y_first, 0, -1)
+    before_after = both_faces(x_faces, lambda a, by: pass_on(slabs, a, by, 0), lax.axis_size("gx"))
+    return [main, behind, ahead, before_after]
 
 
 class Node:
     def __init__(self, main, x_faces, behind, ahead, off=0):
         self.main, self.x_faces, self.behind, self.ahead, self.off = main, x_faces, behind, ahead, off
+
+
+class Mix:
+    def __init__(self, *parts):
+        self.parts, self.shape = parts, parts[0][1].shape
+
+    def __getitem__(self, key):
+        return total([w * field[key] for w, field in self.parts])
 
 
 def scaled(weight, value):
@@ -266,16 +273,20 @@
     squeeze(summed, rows, store, 3)
 
 
+def offset_mix(f, s, g):
+    return Mix((f / 6.0, s), (1.0 - f / 6.0, g))
+
+
 def pack_kernel(first, v, s, g, end, x_faces, y_last, y_first, summed, rows):
     outs = (x_faces, y_last, y_first)
-    for k, field in enumerate((v, g, s)):
-        emit_faces(field, outs, 3 * k)
+    emit_faces(v, outs, 0)
+    emit_faces(offset_mix(first[0], s, g), outs, 3)
 
     def store(c, value):
         end[c] = value
 
     coarsen(g, summed, rows, store)
-    emit_coarse_faces(end, outs, 9)
+    emit_coarse_faces(end, outs, 6)
 
 
 def coarsen_kernel(first, v, s, end, speed, zero, summed, rows):
@@ -298,10 +309,7 @@
 ):
     f = first[0]
     fill(half, [(0.5, Node(v, x_faces, behind, ahead))])
-    start = Node(s, x_faces, behind, ahead, 6)
-    guess = Node(g, x_faces, behind, ahead, 3)
-    share = f * (TIME_STEP / 6.0)
-    fill(ext, [(share, start), (TIME_STEP - share, guess)])
+    fill(ext, [(TIME_STEP, Node(offset_mix(f, s, g), x_faces, behind, ahead, 3))])
     width, length = v.shape[1:3]
     n = min(CHUNK, length)
 
@@ -328,7 +336,7 @@
 
     squeeze(summed, rows, store, 3)
     emit_faces(end, (end_x, end_l, end_f))
-    take_coarse_faces(x_faces, behind, ahead, 9, (zero_x, zero_b, zero_a))
+    take_coarse_faces(x_faces, behind, ahead, 6, (zero_x, zero_b, zero_a))
 
     def store_grads(c, value):
         coarse_grads[c] = value
@@ -349,7 +357,7 @@
     fill(
         ext,
         [
-            (f * sixth, Node(s, x_faces, behind, ahead, 6)),
+            (f * sixth, Node(s, x_faces, behind, ahead)),
             (TIME_STEP * 2.0 / 3.0, Node(u1, u1_x, u1_b, u1_a)),
             (sixth, last),
         ],
@@ -396,8 +404,13 @@
             store(a, x, base(a, x) + d0[0][a, x] + changes[a])
 
 
+def arrival(refs):
+    main, behind, ahead, x_faces = refs
+    return main, x_faces, behind, ahead
+
+
 def pass_start_kernel(turn, first, *refs):
-    arrived, zero = refs[:4], refs[4:8]
+    arrived, zero = arrival(refs[:4]), refs[4:8]
     integral, speed, coarse_grads, end, end_x, end_l, end_f = refs[8:15]
     d0, ext = refs[15:19], refs[19]
 
@@ -416,10 +429,10 @@
 
 
 def settle_start_kernel(count, first, *refs):
-    arrived = [refs[4 * k : 4 * k + 4] for k in range(count)]
+    arrived = [arrival(refs[4 * k : 4 * k + 4]) for k in range(count)]
     refs = refs[4 * count :]
-    zero, (integral, speed, coarse_grads, end_two) = refs[:4], refs[4:8]
-    d0, (d2, d2_x, d2_l, d2_f, ext) = refs[8:12], refs[12:17]
+    zero, (integral, speed, coarse_grads, end_two, s) = refs[:4], refs[4:9]
+    d0, d2, outs, ext = refs[9:13], refs[13], refs[14:17], refs[17]
     rest = 1.0 - first[0]
 
     def base(a, x):
@@ -431,11 +444,12 @@
     for k in range(4):
         d0[k][...] = rest * (total([group[k][...] for group in arrived]) - zero[k][...])
     chain_step(base, speed, coarse_grads, d0, ext, store)
-    emit_faces(d2, (d2_x, d2_l, d2_f))
+    emit_faces(s, outs, 0)
+    emit_coarse_faces(d2, outs, 3)
 
 
 def pass_later_kernel(turn, first, *refs):
-    arrived, (own, following, speed, coarse_grads) = refs[:4], refs[4:8]
+    arrived, (own, following, speed, coarse_grads) = arrival(refs[:4]), refs[4:8]
     sent, sent_x, sent_l, sent_f, ext = refs[8:13]
 
     @pl.when(first[1] == float(turn))
@@ -452,7 +466,7 @@
 
 
 def settle_later_kernel(count, first, *refs):
-    arrived = [refs[4 * k : 4 * k + 4] for k in range(count)]
+    arrived = [arrival(refs[4 * k : 4 * k + 4]) for k in range(count)]
     own, speed, coarse_grads, s, u0, u1, u2, stage, stage_x, stage_l, stage_f, begin, rest = refs[4 * count : 4 * count + 13]
     d0, (d2, ext, wide0, wide2, rows) = refs[4 * count + 13 : 4 * count + 17], refs[4 * count + 17 :]
     f = first[0]
@@ -510,29 +524,22 @@
         emit_faces(following, (following_x, following_l, following_f))
 
 
-def middle_kernel(nodes, *refs):
-    first, v, grads, vx, vb, va = refs[:6]
-    at = 6
-    parts = []
-    for _, _, _, own, off in nodes:
-        main = refs[at]
-        at += 1
-        if own:
-            x_faces, behind, ahead = refs[at : at + 3]
-            at += 3
-        else:
-            x_faces, behind, ahead = vx, vb, va
-        parts.append(Node(main, x_faces, behind, ahead, off))
-    d0 = Node(*refs[at : at + 4])
-    d2 = Node(*refs[at + 4 : at + 8])
-    a1, a1_x, a1_l, a1_f, rest, rest_x, rest_b, rest_a = refs[at + 8 : at + 16]
-    ext, wide0, edge0, wide2, edge2, rows = refs[at + 16 :]
+def middle_kernel(
+    first, v, grads, s, g, w_x, w_b, w_a, d0, d0_x, d0_b, d0_a, d2, m_x, m_b, m_a,
+    a1, a1_x, a1_l, a1_f, rest, rest_x, rest_b, rest_a,
+    ext, wide0, edge0, wide2, edge2, rows, d2_x, d2_b, d2_a, g_x, g_b, g_a,
+):
     f = first[0]
-    begin, first_stage, second_stage = [
-        [(spec[k][0] * f + spec[k][1], node) for spec, node in zip(nodes, parts)] for k in range(3)
-    ]
-    prolong(d0, wide0, edge0, rows)
-    prolong(d2, wide2, edge2, rows)
+    take_coarse_faces(m_x, m_b, m_a, 3, (d2_x, d2_b, d2_a))
+    for out, mixed, start, off in ((g_x, w_x, m_x, 3), (g_b, w_b, m_b, 3), (g_a, w_a, m_a, 3)):
+        for c in range(3):
+            out[c] = (1.0 + 0.2 * f) * mixed[off + c] - (0.2 * f) * start[c]
+    parts = [Node(s, m_x, m_b, m_a), Node(g, g_x, g_b, g_a)]
+    begin = list(zip((f, 1.0 - f), parts))
+    first_stage = list(zip((5.0 / 24.0 * f, 0.5 - 5.0 / 24.0 * f), parts))
+    second_stage = list(zip((f / -24.0, f / 24.0), parts))
+    prolong(Node(d0, d0_x, d0_b, d0_a), wide0, edge0, rows)
+    prolong(Node(d2, d2_x, d2_b, d2_a), wide2, edge2, rows)
     fill(
         ext,
         [(TIME_STEP * w, node) for w, node in first_stage],
@@ -607,7 +614,7 @@
     squeeze(summed, rows, store, 3)
 
 
-def call(kernel, name, first, args, outs, scratch, flops=0):
+def call(kernel, name, first, args, outs, scratch, flops=0, least=0):
     moved = sum(4 * a.size for a in args)
     room = moved + sum(4 * math.prod(dims) for dims in outs + scratch)
     return pl.pallas_call(
@@ -617,7 +624,7 @@
         in_specs=[pl.BlockSpec(memory_space=pltpu.SMEM)] + [pl.BlockSpec(memory_space=pltpu.VMEM)] * len(args),
         out_specs=[pl.BlockSpec(memory_space=pltpu.VMEM)] * len(outs),
         scratch_shapes=[pltpu.VMEM(dims, F32) for dims in scratch],
-        compiler_params=pltpu.CompilerParams(vmem_limit_bytes=min(room + ROOM, 56 << 20)),
+        compiler_params=pltpu.CompilerParams(vmem_limit_bytes=min(max(room + ROOM, least), 56 << 20)),
         cost_estimate=pl.CostEstimate(flops=flops, bytes_accessed=moved, transcendentals=0),
     )(first, *args)
 
@@ -642,7 +649,7 @@
 
     end_two, *packed = call(
         pack_kernel, "pack", first, [velocity, start_field, own],
-        [coarse] + layers_of(10), [summed, rows], 5_000_000,
+        [coarse] + layers_of(7), [summed, rows], 5_000_000, 56 << 20,
     )
     layers = swap_faces(packed)
     speed, zero = call(
@@ -672,19 +679,15 @@
     arrivals = chain(pass_start_kernel, sent, coarse, [coarse] + coarse_faces, terms)
     results = call(
         lambda *refs: settle_start_kernel(slabs - 1, *refs), "settle", first,
-        [*arrivals, *terms, speed, coarse_grads, end_two],
-        [coarse] + coarse_faces + [coarse] + coarse_faces, [coarse_ext], 2_000_000,
-    )
-    d0, d2 = list(results[:4]), [results[4], *swap_faces(results[5:])]
-    nodes = (
-        ((1.0, 0.0), (5.0 / 24.0, 0.0), (-1.0 / 24.0, 0.0), False, 6),
-        ((-1.0, 1.0), (-5.0 / 24.0, 0.5), (1.0 / 24.0, 0.0), False, 3),
-    )
+        [*arrivals, *terms, speed, coarse_grads, end_two, start_field],
+        [coarse] + coarse_faces + [coarse] + layers_of(4), [coarse_ext], 2_000_000,
+    )
+    start_layers = swap_faces(results[5:])
     middle, m_x, m_l, m_f, *rest = call(
-        lambda *refs: middle_kernel(nodes, *refs), "middle", first,
-        [velocity, grads, *layers, start_field, own, *d0, *d2],
+        middle_kernel, "middle", first,
+        [velocity, grads, start_field, own, *layers, *results[:5], *start_layers],
         [fine] + fine_faces + [fine] + fine_faces,
-        [ext, wide, edge, wide, edge, wide_rows], 60_000_000,
+        [ext, wide, edge, wide, edge, wide_rows] + coarse_faces + fine_faces, 60_000_000,
     )
     u1 = [middle, *swap_faces((m_x, m_l, m_f))]
     value, *results = call(
@@ -697,7 +700,7 @@
 
     own_part, following, *sent = call(
         offset_later_kernel, "offset_later", first,
-        [velocity, grads, start_field, *layers, *u1, *u2, zero, end_two],
+        [velocity, grads, start_field, *start_layers, *u1, *u2, zero, end_two],
         [coarse, coarse, (6, cx, cy, cz)] + coarse_faces,
         [ext, ext, summed, summed, rows], 60_000_000,
     )

time: 143 us -> 139 us (0.972)
  local copies, waits for them, and re-layouts: 4.23 us -> 0.94 us
  Pallas kernels: 33.7 us -> 36.7 us
  waiting for transfers between devices: 54.5 us -> 52.6 us
  starting transfers between devices: 49.3 us -> 47.5 us
    unnamed x12 -> x10, local copies, waits for them, and re-layouts: 4.23 us -> 0.94 us
    pallas_call x14, Pallas kernels: 33.7 us -> 36.7 us  [call(): pl.pallas_call(kernel, name=name, out_shape=[jax.ShapeDtypeStruct(dims, F...]
    ppermute x6, waiting for transfers between devices: 15.3 us -> 13.1 us  [swap_faces(): behind = lax.ppermute(y_last, 'gy', ring(gy, 1))]
    ppermute x6, waiting for transfers between devices: 5.9 us -> 3.75 us  [swap_faces(): lax.ppermute(a, 'gx', ring(gx, by))]
    ppermute x6, waiting for transfers between devices: 11.2 us -> 13.3 us  [swap_faces(): ahead = lax.ppermute(y_first, 'gy', ring(gy, -1))]
    ppermute x6, starting transfers between devices: 3.18 us -> 5.09 us  [swap_faces(): behind = lax.ppermute(y_last, 'gy', ring(gy, 1))]
    ppermute x6, starting transfers between devices: 9.82 us -> 7.92 us  [swap_faces(): ahead = lax.ppermute(y_first, 'gy', ring(gy, -1))]
    ppermute x6, starting transfers between devices: 8.32 us -> 6.55 us  [swap_faces(): lax.ppermute(a, 'gx', ring(gx, by))]
  transfers between devices with their start and end apart: 43 -> 43, of which waited for: 22 -> 23; matrix products, arithmetic and copies ran while one was open for 0% -> 0% of each run, Pallas kernels for 6% -> 6%
where the time goes in v7:
time: 139 us
  waiting for transfers between devices  52.6 us (38%)
  starting transfers between devices  47.5 us (34%)
  Pallas kernels  36.7 us (26%)
    pallas_call x14, Pallas kernels, call(): pl.pallas_call(kernel, name=name, out_shape=[jax.ShapeDtypeStruct(dims, F...  36.7 us
    ppermute x25, starting transfers between devices, pass_on(): return lax.ppermute(array, ('tm', 'gx', 'gy'), pairs)  28 us
    ppermute x25, waiting for transfers between devices, pass_on(): return lax.ppermute(array, ('tm', 'gx', 'gy'), pairs)  22.4 us
    ppermute x6, waiting for transfers between devices, swap_faces(): ahead = lax.ppermute(y_first, 'gy', ring(gy, -1))  13.3 us
    ppermute x6, waiting for transfers between devices, swap_faces(): behind = lax.ppermute(y_last, 'gy', ring(gy, 1))  13.1 us
    ppermute x6, starting transfers between devices, swap_faces(): ahead = lax.ppermute(y_first, 'gy', ring(gy, -1))  7.92 us
    ppermute x6, starting transfers between devices, swap_faces(): lax.ppermute(a, 'gx', ring(gx, by))  6.55 us
    ppermute x6, starting transfers between devices, swap_faces(): behind = lax.ppermute(y_last, 'gy', ring(gy, 1))  5.09 us
  transfers between devices with their start and end apart: 43, of which 23 were waited for; matrix products, arithmetic and copies ran while one was open for 0% of the time, Pallas kernels for 6%

profile of v7, /device:TPU:26, one launch (start us, length us, event | category | flops | bytes accessed | tf_op | source)
XLA Modules:
  0.0 138.7 jit_solution(2999711843160269176)
XLA Ops:
  0.7 4.1 %pack.1 = (f32[3,8,16,128]{3,2,1,0:T(8,128)}, f32[7,2,32,256]{3,2,1,0:T(8,128)}, f32[7,16,256]{2,1,0:T(8,128)}, f32[7,16,256]{2,1,0:T(8,128)}) custom-call(f32[2]{0:T(128)} %add_convert_fusion.first.refs_0_, f32[3,16,32,256]{3,2,1,0:T(8,128)} %v.15, f32[3,16,32,256]{3,2,1,0:T(8,128)} %refs_16_.1, f32[3,16,32,256]{3,2,1,0:T(8,128)} %bitcast.4), custom_call_target="tpu_custom_call" | custom-call | flops 5000000 | bytes 4718592 | tf_op jit(solution)/shard_map/pack/pallas_call | solution.py:620
  10.9 2.9 %collective-permute-done.1.behind.w_b = f32[7,16,256]{2,1,0:T(8,128)S(1)} collective-permute-done((f32[7,16,256]{2,1,0:T(8,128)}, f32[7,16,256]{2,1,0:T(8,128)S(1)}, u32[]{:S(2)}, u32[]{:S(2)}) %collective-permute-start.1) | collective-permute-done | bytes 114720 | tf_op jit(solution)/shard_map/ppermute | solution.py:35
  13.8 3.5 %collective-permute-done.x_faces.w_x = f32[7,2,32,256]{3,2,1,0:T(8,128)S(1)} collective-permute-done((f32[7,2,32,256]{3,2,1,0:T(8,128)}, f32[7,2,32,256]{3,2,1,0:T(8,128)S(1)}, u32[]{:S(2)}, u32[]{:S(2)}) %collective-permute-start) | collective-permute-done | bytes 458784 | tf_op jit(solution)/shard_map/ppermute | solution.py:34
  17.2 4.9 %offset_start.1 = (f32[9,16,32,256]{3,2,1,0:T(8,128)S(1)}, f32[3,8,16,128]{3,2,1,0:T(8,128)S(1)}, f32[9,8,16,128]{3,2,1,0:T(8,128)S(1)}, f32[3,2,16,128]{3,2,1,0...) custom-call(f32[2]{0:T(128)S(1)} %copy-done.4, ...), custom_call_target="tpu_custom_call" | custom-call | flops 40000000 | bytes 5603328 | tf_op jit(solution)/shard_map/offset_start/pallas_call | solution.py:620
  30.7 6.7 %collective-permute-done.8.refs_2_.refs_6_ = f32[3,8,128]{2,1,0:T(8,128)S(1)} collective-permute-done((f32[3,8,128]{2,1,0:T(8,128)S(1)}, f32[3,8,128]{2,1,0:T(8,128)S(1)}, u32[]{:S(2)}, u32[]{:S(2)}) %collective-permute-start.8) | collective-permute-done | bytes 12320 | tf_op jit(solution)/shard_map/ppermute | solution.py:49
  48.5 2.9 %collective-permute-start.16 = (f32[4,16,256]{2,1,0:T(8,128)S(1)}, f32[4,16,256]{2,1,0:T(8,128)S(1)}, u32[]{:S(2)}, u32[]{:S(2)}) collective-permute-start(f32[4,16,256]{2,1,0:T(8,128)S(1)} %get-tuple-element.100), channel_id=1, source_target_pairs={{0,1},{1,2},{2,3},{3,0},{4,5},{5,6},{6,7},{7,4},{8,9},{9,10},{10,1... | collective-permute-start | bytes 196616 | tf_op jit(solution)/shard_map/ppermute | solution.py:35
  51.4 2.0 %collective-permute-done.16.m_b.behind = f32[4,16,256]{2,1,0:T(8,128)S(1)} collective-permute-done((f32[4,16,256]{2,1,0:T(8,128)S(1)}, f32[4,16,256]{2,1,0:T(8,128)S(1)}, u32[]{:S(2)}, u32[]{:S(2)}) %collective-permute-start.16) | collective-permute-done | bytes 65568 | tf_op jit(solution)/shard_map/ppermute | solution.py:35
  53.4 4.1 %collective-permute-done.17.m_a.ahead = f32[4,16,256]{2,1,0:T(8,128)S(1)} collective-permute-done((f32[4,16,256]{2,1,0:T(8,128)S(1)}, f32[4,16,256]{2,1,0:T(8,128)S(1)}, u32[]{:S(2)}, u32[]{:S(2)}) %collective-permute-start.17) | collective-permute-done | bytes 65568 | tf_op jit(solution)/shard_map/ppermute | solution.py:36
  57.5 4.3 %middle.1 = (f32[3,16,32,256]{3,2,1,0:T(8,128)S(1)}, f32[3,2,32,256]{3,2,1,0:T(8,128)S(1)}, f32[3,16,256]{2,1,0:T(8,128)S(1)}, f32[3,16,256]{2,1,0:T(8,128)S(1)}...) custom-call(f32[2]{0:T(128)S(1)} %copy-done.4, ...), custom_call_target="tpu_custom_call" | custom-call | flops 60000000 | bytes 10985472 | tf_op jit(solution)/shard_map/middle/pallas_call | solution.py:620
  64.3 2.1 %collective-permute-done.19.a1_b.u1_b = f32[3,16,256]{2,1,0:T(8,128)S(1)} collective-permute-done((f32[3,16,256]{2,1,0:T(8,128)S(1)}, f32[3,16,256]{2,1,0:T(8,128)S(1)}, u32[]{:S(2)}, u32[]{:S(2)}) %collective-permute-start.19) | collective-permute-done | bytes 49184 | tf_op jit(solution)/shard_map/ppermute | solution.py:35
  66.4 3.2 %collective-permute-done.20.a1_a.u1_a = f32[3,16,256]{2,1,0:T(8,128)S(1)} collective-permute-done((f32[3,16,256]{2,1,0:T(8,128)S(1)}, f32[3,16,256]{2,1,0:T(8,128)S(1)}, u32[]{:S(2)}, u32[]{:S(2)}) %collective-permute-start.20) | collective-permute-done | bytes 49184 | tf_op jit(solution)/shard_map/ppermute | solution.py:36
  69.6 3.2 %finish.1 = (f32[3,16,32,256]{3,2,1,0:T(8,128)S(1)}, f32[3,2,32,256]{3,2,1,0:T(8,128)S(1)}, f32[3,16,256]{2,1,0:T(8,128)S(1)}, f32[3,16,256]{2,1,0:T(8,128)S(1)}, f32[3,8,16,128]{3,2,1,0:T(8,128)S(1)}) custom-call(f32[2]{0:T(128)S(1)} %copy-done.4, f32[3,16,32,256]{3,2,1,0:T(8,128)S(1)} %copy-done, f32[9,16,32,256]{3,2,1,0:T(8,128)S(1)} %get-tuple-element.80.grads, ...), custom_call_target="tpu_custom_call" | custom-call | flops 40000000 | bytes 10027008 | tf_op jit(solution)/shard_map/finish/pallas_call | solution.py:620
  76.0 2.0 %collective-permute-start.23 = (f32[3,16,256]{2,1,0:T(8,128)S(1)}, f32[3,16,256]{2,1,0:T(8,128)S(1)}, u32[]{:S(2)}, u32[]{:S(2)}) collective-permute-start(f32[3,16,256]{2,1,0:T(8,128)S(1)} %get-tuple-element.118), channel_id=1, source_target_pairs={{0,3},{1,0},{2,1},{3,2},{4,7},{5,4},{6,5},{7,6},{8,11},{9,8},{10,9... | collective-permute-start | bytes 147464 | tf_op jit(solution)/shard_map/ppermute | solution.py:36
  78.0 2.1 %collective-permute-done.22.u2_b = f32[3,16,256]{2,1,0:T(8,128)S(1)} collective-permute-done((f32[3,16,256]{2,1,0:T(8,128)S(1)}, f32[3,16,256]{2,1,0:T(8,128)S(1)}, u32[]{:S(2)}, u32[]{:S(2)}) %collective-permute-start.22) | collective-permute-done | bytes 49184 | tf_op jit(solution)/shard_map/ppermute | solution.py:35
  81.9 5.4 %offset_later.1 = (f32[3,8,16,128]{3,2,1,0:T(8,128)S(1)}, f32[3,8,16,128]{3,2,1,0:T(8,128)S(1)}, f32[6,8,16,128]{3,2,1,0:T(8,128)S(1)}, f32[3,2,16,128]{3,2,1,0:...) custom-call(f32[2]{0:T(128)S(1)} %copy-done.4, f32[3,16,32,256]{3,2,1,0:T(8,128)S(1)} %copy-done, ...), custom_call_target="tpu_custom_call" | custom-call | flops 60000000 | bytes 12386304 | tf_op jit(solution)/shard_map/offset_later/pallas_call | solution.py:620
  95.8 7.2 %collective-permute-done.29.refs_2_.refs_6_ = f32[3,8,128]{2,1,0:T(8,128)S(1)} collective-permute-done((f32[3,8,128]{2,1,0:T(8,128)S(1)}, f32[3,8,128]{2,1,0:T(8,128)S(1)}, u32[]{:S(2)}, u32[]{:S(2)}) %collective-permute-start.29) | collective-permute-done | bytes 12320 | tf_op jit(solution)/shard_map/ppermute | solution.py:49
  104.9 2.1 %collective-permute-done.31.refs_4_.refs_8_ = f32[3,2,16,128]{3,2,1,0:T(8,128)S(1)} collective-permute-done((f32[3,2,16,128]{3,2,1,0:T(8,128)S(1)}, f32[3,2,16,128]{3,2,1,0:T(8,128)S(1)}, u32[]{:S(2)}, u32[]{:S(2)}) %collective-permute-start.31) | collective-permute-done | bytes 49184 | tf_op jit(solution)/shard_map/ppermute | solution.py:49
  114.5 2.4 %settle.3 = (f32[3,16,32,256]{3,2,1,0:T(8,128)S(1)}, f32[3,2,32,256]{3,2,1,0:T(8,128)S(1)}, f32[3,16,256]{2,1,0:T(8,128)S(1)}, f32[3,16,256]{2,1,0:T(8,128)S(1)}...) custom-call(f32[2]{0:T(128)S(1)} %copy-done.4, f32[6,8,16,128]{3,2,1,0:T(8,128)S(1)} %collective-permute-done.24.refs_1_, ...), custom_call_target="tpu_custom_call" | custom-call | flops 10000000 | bytes 8675328 | tf_op jit(solution)/shard_map/settle/pallas_call | solution.py:620
  120.1 2.1 %collective-permute-done.38.y_b = f32[3,16,256]{2,1,0:T(8,128)S(1)} collective-permute-done((f32[3,16,256]{2,1,0:T(8,128)S(1)}, f32[3,16,256]{2,1,0:T(8,128)S(1)}, u32[]{:S(2)}, u32[]{:S(2)}) %collective-permute-start.38) | collective-permute-done | bytes 49184 | tf_op jit(solution)/shard_map/ppermute | solution.py:35
  122.1 2.3 %collective-permute-done.39.y_a = f32[3,16,256]{2,1,0:T(8,128)S(1)} collective-permute-done((f32[3,16,256]{2,1,0:T(8,128)S(1)}, f32[3,16,256]{2,1,0:T(8,128)S(1)}, u32[]{:S(2)}, u32[]{:S(2)}) %collective-permute-start.39) | collective-permute-done | bytes 49184 | tf_op jit(solution)/shard_map/ppermute | solution.py:36
  124.5 3.0 %stage.2 = (f32[3,16,32,256]{3,2,1,0:T(8,128)S(1)}, f32[3,16,32,256]{3,2,1,0:T(8,128)S(1)}, f32[3,2,32,256]{3,2,1,0:T(8,128)S(1)}, f32[3,16,256]{2,1,0:T(8,128)S(1)}, f32[3,16,256]{2,1,0:T(8,128)S(1)}) custom-call(f32[2]{0:T(128)S(1)} %copy-done.4, f32[3,16,32,256]{3,2,1,0:T(8,128)S(1)} %copy-done, f32[9,16,32,256]{3,2,1,0:T(8,128)S(1)} %get-tuple-element.80.grads, ...), custom_call_target="tpu_custom_call" | custom-call | flops 40000000 | bytes 11304960 | tf_op jit(solution)/shard_map/stage/pallas_call | solution.py:620
  128.7 2.0 %collective-permute-start.42 = (f32[3,16,256]{2,1,0:T(8,128)S(1)}, f32[3,16,256]{2,1,0:T(8,128)S(1)}, u32[]{:S(2)}, u32[]{:S(2)}) collective-permute-start(f32[3,16,256]{2,1,0:T(8,128)S(1)} %get-tuple-element.143), channel_id=1, source_target_pairs={{0,3},{1,0},{2,1},{3,2},{4,7},{5,4},{6,5},{7,6},{8,11},{9,8},{10,9... | collective-permute-start | bytes 147464 | tf_op jit(solution)/shard_map/ppermute | solution.py:36
  130.6 2.1 %collective-permute-done.41.y_b = f32[3,16,256]{2,1,0:T(8,128)S(1)} collective-permute-done((f32[3,16,256]{2,1,0:T(8,128)S(1)}, f32[3,16,256]{2,1,0:T(8,128)S(1)}, u32[]{:S(2)}, u32[]{:S(2)}) %collective-permute-start.41) | collective-permute-done | bytes 49184 | tf_op jit(solution)/shard_map/ppermute | solution.py:35
  134.7 4.0 %stage.3 = f32[3,16,32,256]{3,2,1,0:T(8,128)} custom-call(f32[2]{0:T(128)S(1)} %copy-done.4, f32[3,16,32,256]{3,2,1,0:T(8,128)S(1)} %copy-done, f32[9,16,32,256]{3,2,1,0:T(8,128)S(1)} %get-tuple-element.80.grads, f32[3,16,32,256]{3,2,1,0:T(8,128)S(1)} %get-tuple-element.140.y, f32[3,2,32,256]{3,2,1,0:T(8,128)S(1)} %collective-permute-done.40.y_x, ...), custom_call_target="tpu_custom_call" | custom-call | flops 40000000 | bytes 9732096 | tf_op jit(solution)/shard_map/stage/pallas_call | solution.py:620
  (87 shorter events, 58.0 us)
Async XLA Ops:
  4.8 12.5 %collective-permute-start = (f32[7,2,32,256]{3,2,1,0:T(8,128)}, f32[7,2,32,256]{3,2,1,0:T(8,128)S(1)}, u32[]{:S(2)}, u32[]{:S(2)}) collective-permute-start(f32[7,2,32,256]{3,2,1,0:T(8,128)} %get-tuple-element.75), channel_id=1, source_target_pairs={{0,4},{4,0},{1,5},{5,1},{2,6},{6,2},{3,7},{7,3},{8,12},{12,8},{9,1... | collective-permute-start | bytes 1376264 | tf_op jit(solution)/shard_map/ppermute | solution.py:34
  6.3 7.5 %collective-permute-start.1 = (f32[7,16,256]{2,1,0:T(8,128)}, f32[7,16,256]{2,1,0:T(8,128)S(1)}, u32[]{:S(2)}, u32[]{:S(2)}) collective-permute-start(f32[7,16,256]{2,1,0:T(8,128)} %get-tuple-element.76), channel_id=1, source_target_pairs={{0,1},{1,2},{2,3},{3,0},{4,5},{5,6},{6,7},{7,4},{8,9},{9,10},{10,1... | collective-permute-start | bytes 344072 | tf_op jit(solution)/shard_map/ppermute | solution.py:35
  6.5 7.2 %collective-permute-start.2 = (f32[7,16,256]{2,1,0:T(8,128)}, f32[7,16,256]{2,1,0:T(8,128)S(1)}, u32[]{:S(2)}, u32[]{:S(2)}) collective-permute-start(f32[7,16,256]{2,1,0:T(8,128)} %get-tuple-element.77), channel_id=1, source_target_pairs={{0,3},{1,0},{2,1},{3,2},{4,7},{5,4},{6,5},{7,6},{8,11},{9,8},{10,9... | collective-permute-start | bytes 344072 | tf_op jit(solution)/shard_map/ppermute | solution.py:36
  25.5 13.6 %collective-permute-start.7 = (f32[3,8,16,128]{3,2,1,0:T(8,128)S(1)}, f32[3,8,16,128]{3,2,1,0:T(8,128)S(1)}, u32[]{:S(2)}, u32[]{:S(2)}) collective-permute-start(f32[3,8,16,128]{3,2,1,0:T(8,128)S(1)} %get-tuple-element.91), channel_id=1, source_target_pairs={{8,16},{9,17},{10,18},{11,19},{12,20},{13,21},{14,22},{15,23}} | collective-permute-start | bytes 589832 | tf_op jit(solution)/shard_map/ppermute | solution.py:49
  26.8 12.3 %collective-permute-start.10 = (f32[3,2,16,128]{3,2,1,0:T(8,128)S(1)}, f32[3,2,16,128]{3,2,1,0:T(8,128)S(1)}, u32[]{:S(2)}, u32[]{:S(2)}) collective-permute-start(f32[3,2,16,128]{3,2,1,0:T(8,128)S(1)} %get-tuple-element.94), channel_id=1, source_target_pairs={{8,20},{9,21},{10,22},{11,23},{12,16},{13,17},{14,18},{15,19}} | collective-permute-start | bytes 147464 | tf_op jit(solution)/shard_map/ppermute | solution.py:49
  28.1 9.3 %collective-permute-start.8 = (f32[3,8,128]{2,1,0:T(8,128)S(1)}, f32[3,8,128]{2,1,0:T(8,128)S(1)}, u32[]{:S(2)}, u32[]{:S(2)}) collective-permute-start(f32[3,8,128]{2,1,0:T(8,128)S(1)} %get-tuple-element.92), channel_id=1, source_target_pairs={{8,17},{9,18},{10,19},{11,16},{12,21},{13,22},{14,23},{15,20}} | collective-permute-start | bytes 36872 | tf_op jit(solution)/shard_map/ppermute | solution.py:49
  29.4 9.7 %collective-permute-start.9 = (f32[3,8,128]{2,1,0:T(8,128)S(1)}, f32[3,8,128]{2,1,0:T(8,128)S(1)}, u32[]{:S(2)}, u32[]{:S(2)}) collective-permute-start(f32[3,8,128]{2,1,0:T(8,128)S(1)} %get-tuple-element.93), channel_id=1, source_target_pairs={{8,19},{9,16},{10,17},{11,18},{12,23},{13,20},{14,21},{15,22}} | collective-permute-start | bytes 36872 | tf_op jit(solution)/shard_map/ppermute | solution.py:49
  40.0 6.6 %collective-permute-start.11 = (f32[3,8,16,128]{3,2,1,0:T(8,128)S(1)}, f32[3,8,16,128]{3,2,1,0:T(8,128)S(1)}, u32[]{:S(2)}, u32[]{:S(2)}) collective-permute-start(f32[3,8,16,128]{3,2,1,0:T(8,128)S(1)} %get-tuple-element.95), channel_id=1, source_target_pairs={{16,24},{17,25},{18,26},{19,27},{20,28},{21,29},{22,30},{23,31}} | collective-permute-start | bytes 589832 | tf_op jit(solution)/shard_map/ppermute | solution.py:49
  47.5 9.9 %collective-permute-start.15 = (f32[4,2,32,256]{3,2,1,0:T(8,128)S(1)}, f32[4,2,32,256]{3,2,1,0:T(8,128)S(1)}, u32[]{:S(2)}, u32[]{:S(2)}) collective-permute-start(f32[4,2,32,256]{3,2,1,0:T(8,128)S(1)} %get-tuple-element.99), channel_id=1, source_target_pairs={{0,4},{4,0},{1,5},{5,1},{2,6},{6,2},{3,7},{7,3},{8,12},{12,8},{9,1... | collective-permute-start | bytes 786440 | tf_op jit(solution)/shard_map/ppermute | solution.py:34
  51.4 6.1 %collective-permute-start.17 = (f32[4,16,256]{2,1,0:T(8,128)S(1)}, f32[4,16,256]{2,1,0:T(8,128)S(1)}, u32[]{:S(2)}, u32[]{:S(2)}) collective-permute-start(f32[4,16,256]{2,1,0:T(8,128)S(1)} %get-tuple-element.101), channel_id=1, source_target_pairs={{0,3},{1,0},{2,1},{3,2},{4,7},{5,4},{6,5},{7,6},{8,11},{9,8},{10,9... | collective-permute-start | bytes 196616 | tf_op jit(solution)/shard_map/ppermute | solution.py:36
  61.7 7.9 %collective-permute-start.18 = (f32[3,2,32,256]{3,2,1,0:T(8,128)S(1)}, f32[3,2,32,256]{3,2,1,0:T(8,128)S(1)}, u32[]{:S(2)}, u32[]{:S(2)}) collective-permute-start(f32[3,2,32,256]{3,2,1,0:T(8,128)S(1)} %get-tuple-element.108), channel_id=1, source_target_pairs={{0,4},{4,0},{1,5},{5,1},{2,6},{6,2},{3,7},{7,3},{8,12},{12,8},{9,1... | collective-permute-start | bytes 589832 | tf_op jit(solution)/shard_map/ppermute | solution.py:34
  63.7 5.9 %collective-permute-start.20 = (f32[3,16,256]{2,1,0:T(8,128)S(1)}, f32[3,16,256]{2,1,0:T(8,128)S(1)}, u32[]{:S(2)}, u32[]{:S(2)}) collective-permute-start(f32[3,16,256]{2,1,0:T(8,128)S(1)} %get-tuple-element.110), channel_id=1, source_target_pairs={{0,3},{1,0},{2,1},{3,2},{4,7},{5,4},{6,5},{7,6},{8,11},{9,8},{10,9... | collective-permute-start | bytes 147464 | tf_op jit(solution)/shard_map/ppermute | solution.py:36
  72.8 41.6 %collective-permute-start.36 = (f32[3,16,32,256]{3,2,1,0:T(8,128)S(1)}, f32[3,16,32,256]{3,2,1,0:T(8,128)S(1)}, u32[]{:S(2)}, u32[]{:S(2)}) collective-permute-start(f32[3,16,32,256]{3,2,1,0:T(8,128)S(1)} %get-tuple-element.115.u2.refs_19_), channel_id=1, source_target_pairs={{0,8},{1,9},{2,10},{3,11},{4,12},{5,13},{6,14},{7,15},{8,16},{9,17... | collective-permute-start | bytes 4718600 | tf_op jit(solution)/shard_map/ppermute | solution.py:49
  74.8 7.1 %collective-permute-start.21 = (f32[3,2,32,256]{3,2,1,0:T(8,128)S(1)}, f32[3,2,32,256]{3,2,1,0:T(8,128)S(1)}, u32[]{:S(2)}, u32[]{:S(2)}) collective-permute-start(f32[3,2,32,256]{3,2,1,0:T(8,128)S(1)} %get-tuple-element.116), channel_id=1, source_target_pairs={{0,4},{4,0},{1,5},{5,1},{2,6},{6,2},{3,7},{7,3},{8,12},{12,8},{9,1... | collective-permute-start | bytes 589832 | tf_op jit(solution)/shard_map/ppermute | solution.py:34
  76.0 5.9 %collective-permute-start.23 = (f32[3,16,256]{2,1,0:T(8,128)S(1)}, f32[3,16,256]{2,1,0:T(8,128)S(1)}, u32[]{:S(2)}, u32[]{:S(2)}) collective-permute-start(f32[3,16,256]{2,1,0:T(8,128)S(1)} %get-tuple-element.118), channel_id=1, source_target_pairs={{0,3},{1,0},{2,1},{3,2},{4,7},{5,4},{6,5},{7,6},{8,11},{9,8},{10,9... | collective-permute-start | bytes 147464 | tf_op jit(solution)/shard_map/ppermute | solution.py:36
  90.6 16.4 %collective-permute-start.28 = (f32[6,8,16,128]{3,2,1,0:T(8,128)S(1)}, f32[6,8,16,128]{3,2,1,0:T(8,128)S(1)}, u32[]{:S(2)}, u32[]{:S(2)}) collective-permute-start(f32[6,8,16,128]{3,2,1,0:T(8,128)S(1)} %get-tuple-element.126), channel_id=1, source_target_pairs={{8,16},{9,17},{10,18},{11,19},{12,20},{13,21},{14,22},{15,23}} | collective-permute-start | bytes 1179656 | tf_op jit(solution)/shard_map/ppermute | solution.py:49
  91.9 15.1 %collective-permute-start.31 = (f32[3,2,16,128]{3,2,1,0:T(8,128)S(1)}, f32[3,2,16,128]{3,2,1,0:T(8,128)S(1)}, u32[]{:S(2)}, u32[]{:S(2)}) collective-permute-start(f32[3,2,16,128]{3,2,1,0:T(8,128)S(1)} %get-tuple-element.129), channel_id=1, source_target_pairs={{8,20},{9,21},{10,22},{11,23},{12,16},{13,17},{14,18},{15,19}} | collective-permute-start | bytes 147464 | tf_op jit(solution)/shard_map/ppermute | solution.py:49
  93.2 9.8 %collective-permute-start.29 = (f32[3,8,128]{2,1,0:T(8,128)S(1)}, f32[3,8,128]{2,1,0:T(8,128)S(1)}, u32[]{:S(2)}, u32[]{:S(2)}) collective-permute-start(f32[3,8,128]{2,1,0:T(8,128)S(1)} %get-tuple-element.127), channel_id=1, source_target_pairs={{8,17},{9,18},{10,19},{11,16},{12,21},{13,22},{14,23},{15,20}} | collective-permute-start | bytes 36872 | tf_op jit(solution)/shard_map/ppermute | solution.py:49
  94.5 10.3 %collective-permute-start.30 = (f32[3,8,128]{2,1,0:T(8,128)S(1)}, f32[3,8,128]{2,1,0:T(8,128)S(1)}, u32[]{:S(2)}, u32[]{:S(2)}) collective-permute-start(f32[3,8,128]{2,1,0:T(8,128)S(1)} %get-tuple-element.128), channel_id=1, source_target_pairs={{8,19},{9,16},{10,17},{11,18},{12,23},{13,20},{14,21},{15,22}} | collective-permute-start | bytes 36872 | tf_op jit(solution)/shard_map/ppermute | solution.py:49
  107.9 6.6 %collective-permute-start.32 = (f32[6,8,16,128]{3,2,1,0:T(8,128)S(1)}, f32[6,8,16,128]{3,2,1,0:T(8,128)S(1)}, u32[]{:S(2)}, u32[]{:S(2)}) collective-permute-start(f32[6,8,16,128]{3,2,1,0:T(8,128)S(1)} %get-tuple-element.130), channel_id=1, source_target_pairs={{16,24},{17,25},{18,26},{19,27},{20,28},{21,29},{22,30},{23,31}} | collective-permute-start | bytes 1179656 | tf_op jit(solution)/shard_map/ppermute | solution.py:49
  116.9 7.6 %collective-permute-start.37 = (f32[3,2,32,256]{3,2,1,0:T(8,128)S(1)}, f32[3,2,32,256]{3,2,1,0:T(8,128)S(1)}, u32[]{:S(2)}, u32[]{:S(2)}) collective-permute-start(f32[3,2,32,256]{3,2,1,0:T(8,128)S(1)} %get-tuple-element.135), channel_id=1, source_target_pairs={{0,4},{4,0},{1,5},{5,1},{2,6},{6,2},{3,7},{7,3},{8,12},{12,8},{9,1... | collective-permute-start | bytes 589832 | tf_op jit(solution)/shard_map/ppermute | solution.py:34
  118.5 5.9 %collective-permute-start.39 = (f32[3,16,256]{2,1,0:T(8,128)S(1)}, f32[3,16,256]{2,1,0:T(8,128)S(1)}, u32[]{:S(2)}, u32[]{:S(2)}) collective-permute-start(f32[3,16,256]{2,1,0:T(8,128)S(1)} %get-tuple-element.137), channel_id=1, source_target_pairs={{0,3},{1,0},{2,1},{3,2},{4,7},{5,4},{6,5},{7,6},{8,11},{9,8},{10,9... | collective-permute-start | bytes 147464 | tf_op jit(solution)/shard_map/ppermute | solution.py:36
  127.5 7.2 %collective-permute-start.40 = (f32[3,2,32,256]{3,2,1,0:T(8,128)S(1)}, f32[3,2,32,256]{3,2,1,0:T(8,128)S(1)}, u32[]{:S(2)}, u32[]{:S(2)}) collective-permute-start(f32[3,2,32,256]{3,2,1,0:T(8,128)S(1)} %get-tuple-element.141), channel_id=1, source_target_pairs={{0,4},{4,0},{1,5},{5,1},{2,6},{6,2},{3,7},{7,3},{8,12},{12,8},{9,1... | collective-permute-start | bytes 589832 | tf_op jit(solution)/shard_map/ppermute | solution.py:34
  128.7 5.9 %collective-permute-start.42 = (f32[3,16,256]{2,1,0:T(8,128)S(1)}, f32[3,16,256]{2,1,0:T(8,128)S(1)}, u32[]{:S(2)}, u32[]{:S(2)}) collective-permute-start(f32[3,16,256]{2,1,0:T(8,128)S(1)} %get-tuple-element.143), channel_id=1, source_target_pairs={{0,3},{1,0},{2,1},{3,2},{4,7},{5,4},{6,5},{7,6},{8,11},{9,8},{10,9... | collective-permute-start | bytes 147464 | tf_op jit(solution)/shard_map/ppermute | solution.py:36
  (24 other events, 88.0 us)

commit v8 on v7

--- a/solution.py
+++ b/solution.py
@@ -61,6 +61,47 @@
 class Node:
     def __init__(self, main, x_faces, behind, ahead, off=0):
         self.main, self.x_faces, self.behind, self.ahead, self.off = main, x_faces, behind, ahead, off
+
+
+def packed_rows(width, length):
+    return width * length + 2 * length + 2 * width
+
+
+class Reader:
+    def __init__(self, read):
+        self.read = read
+
+    def __getitem__(self, key):
+        return self.read(*key)
+
+
+def packed_node(ref, width, length):
+    inner = width * length
+
+    def main(c, x, rows=slice(0, length)):
+        begin = pl.multiple_of(x * length + rows.start, 8)
+        return ref[c, pl.ds(begin, rows.stop - rows.start)]
+
+    def x_layer(c, k):
+        return ref[c, inner + k * length : inner + (k + 1) * length]
+
+    def y_layer(base):
+        return Reader(lambda c, row: ref[c, pl.ds(base + row.start, 1)])
+
+    base = inner + 2 * length
+    return Node(Reader(main), Reader(x_layer), y_layer(base), y_layer(base + width))
+
+
+def emit_packed(node, ref):
+    width, length = node.main.shape[1:3]
+    inner = width * length
+    base = inner + 2 * length
+    for c in range(3):
+        ref[c, 0:inner] = node.main[c].reshape(inner, ref.shape[2])
+        for k in range(2):
+            ref[c, inner + k * length : inner + (k + 1) * length] = node.x_faces[c, k]
+        ref[c, base : base + width] = node.behind[c]
+        ref[c, base + width : base + 2 * width] = node.ahead[c]
 
 
 class Mix:
@@ -347,12 +388,13 @@
 def offset_later_kernel(
     first, v, grads, s, x_faces, behind, ahead,
     u1, u1_x, u1_b, u1_a, u2, u2_x, u2_b, u2_a, zero, end_two,
-    own, following, sent, sent_x, sent_l, sent_f,
+    own, following, sent, sent_x, sent_l, sent_f, bulk,
     ext, ext_two, summed, summed_two, rows,
 ):
     f = first[0]
     sixth = TIME_STEP / 6.0
     last = Node(u2, u2_x, u2_b, u2_a)
+    emit_packed(last, bulk)
     fill(ext_two, [(sixth, last)])
     fill(
         ext,
@@ -467,8 +509,8 @@
 
 def settle_later_kernel(count, first, *refs):
     arrived = [arrival(refs[4 * k : 4 * k + 4]) for k in range(count)]
-    own, speed, coarse_grads, s, u0, u1, u2, stage, stage_x, stage_l, stage_f, begin, rest = refs[4 * count : 4 * count + 13]
-    d0, (d2, ext, wide0, wide2, rows) = refs[4 * count + 13 : 4 * count + 17], refs[4 * count + 17 :]
+    own, speed, coarse_grads, s, u1, u2, stage, stage_x, stage_l, stage_f, begin, rest = refs[4 * count : 4 * count + 12]
+    d0, (d2, ext, wide0, wide2, rows) = refs[4 * count + 12 : 4 * count + 16], refs[4 * count + 16 :]
     f = first[0]
 
     def base(a, x):
@@ -484,7 +526,7 @@
     prolong_own(d0[0], wide0, rows)
     prolong_own(d2, wide2, rows)
 
-    @pl.loop(0, u0.shape[1] // 2)
+    @pl.loop(0, u1.shape[1] // 2)
     def _(i):
         for c in range(3):
             p0, p2 = wide0[c, i], wide2[c, i]
@@ -492,7 +534,7 @@
             toward_rest = 0.125 * (p2 - p0)
             for q in range(2):
                 x = 2 * i + q
-                start, one, two = f * s[c, x] + u0[c, x], u1[c, x], u2[c, x]
+                start, one, two = f * s[c, x], u1[c, x], u2[c, x]
                 stage[c, x] = toward_stage + TIME_STEP * (start * (5.0 / 24.0) + one / 3.0 - two / 24.0)
                 begin[c, x] = start + p0
                 rest[c, x] = toward_rest + (two * (5.0 / 24.0) - one / 6.0 - start / 24.0)
@@ -500,13 +542,10 @@
     emit_faces(stage, (stage_x, stage_l, stage_f))
 
 
-def stage_kernel(first, v, grads, y, y_x, y_b, y_a, begin, *refs):
-    if len(refs) == 2:
-        out, ext = refs
-    else:
-        rest, out, following, following_x, following_l, following_f, ext = refs
-    fill(ext, [(1.0, Node(y, y_x, y_b, y_a))])
+def first_stage_kernel(first, v, grads, y, y_x, y_b, y_a, begin, rest, bulk, out, stage, stage_x, stage_l, stage_f, ext):
     width, length = v.shape[1:3]
+    arrived = packed_node(bulk, width, length)
+    fill(ext, [(1.0, Node(y, y_x, y_b, y_a)), (TIME_STEP * 5.0 / 24.0, arrived)])
     n = min(CHUNK, length)
 
     @pl.loop(0, width)
@@ -515,13 +554,25 @@
             at = slice(r, r + n)
             changes = fine_rates(ext, v, grads, x, r, n)
             for a in range(3):
-                value = begin[a, x, at] + changes[a]
+                start = arrived.main[a, x, at]
+                value = begin[a, x, at] + start + changes[a]
                 out[a, x, at] = value
-                if len(refs) > 2:
-                    following[a, x, at] = TIME_STEP * (0.5 * value + rest[a, x, at])
-
-    if len(refs) > 2:
-        emit_faces(following, (following_x, following_l, following_f))
+                stage[a, x, at] = TIME_STEP * (0.5 * value + (rest[a, x, at] - start / 24.0))
+
+    emit_faces(stage, (stage_x, stage_l, stage_f))
+
+
+def last_stage_kernel(first, v, grads, y, y_x, y_b, y_a, begin, out, ext):
+    fill(ext, [(1.0, Node(y, y_x, y_b, y_a))])
+    width, length = v.shape[1:3]
+    n = min(CHUNK, length)
+
+    @pl.loop(0, width)
+    def _(x):
+        for r in range(0, length, n):
+            changes = fine_rates(ext, v, grads, x, r, n)
+            for a in range(3):
+                out[a, x, r : r + n] = begin[a, x, r : r + n] + changes[a]
 
 
 def middle_kernel(
@@ -663,7 +714,7 @@
     )
     zero_faces, sent = results[:3], results[3:]
 
-    def chain(step, sent, outs, scratch, own_terms):
+    def chain(step, sent, outs, scratch, own_terms, bulk=None):
         arrivals = []
         for turn in range(1, slabs):
             arrivals += hand_on([turn - 1], sent[0], sent[1:])
@@ -673,10 +724,13 @@
                     [*arrivals[-4:], *own_terms, speed, coarse_grads],
                     [outs] + coarse_faces, scratch + [coarse_ext], 2_000_000,
                 )
-        return arrivals
+            if turn == 1 and bulk is not None:
+                *sent, bulk = lax.optimization_barrier([*sent, bulk])
+                bulk = pass_on(range(slabs - 1), bulk)
+        return arrivals, bulk
 
     terms = [zero, *zero_faces, integral]
-    arrivals = chain(pass_start_kernel, sent, coarse, [coarse] + coarse_faces, terms)
+    arrivals, _ = chain(pass_start_kernel, sent, coarse, [coarse] + coarse_faces, terms)
     results = call(
         lambda *refs: settle_start_kernel(slabs - 1, *refs), "settle", first,
         [*arrivals, *terms, speed, coarse_grads, end_two, start_field],
@@ -695,28 +749,27 @@
         [fine] + fine_faces + [coarse], [ext, summed, rows], 40_000_000,
     )
     faces, end_two = results[:3], results[3]
-    u0 = pass_on(range(slabs - 1), value)
     u2 = [value, *swap_faces(faces)]
 
-    own_part, following, *sent = call(
+    own_part, following, *sent, bulk = call(
         offset_later_kernel, "offset_later", first,
         [velocity, grads, start_field, *start_layers, *u1, *u2, zero, end_two],
-        [coarse, coarse, (6, cx, cy, cz)] + coarse_faces,
+        [coarse, coarse, (6, cx, cy, cz)] + coarse_faces + [(3, packed_rows(nx, ny), nz)],
         [ext, ext, summed, summed, rows], 60_000_000,
     )
-    arrivals = chain(pass_later_kernel, sent, (6, cx, cy, cz), [], [own_part, following])
+    arrivals, bulk = chain(pass_later_kernel, sent, (6, cx, cy, cz), [], [own_part, following], bulk)
     stage, *faces, begin, rest = call(
         lambda *refs: settle_later_kernel(slabs - 1, *refs), "settle", first,
-        [*arrivals, own_part, speed, coarse_grads, start_field, u0, middle, value],
+        [*arrivals, own_part, speed, coarse_grads, start_field, middle, value],
         [fine] + fine_faces + [fine, fine],
         [coarse, *coarse_faces, coarse, coarse_ext, summed, summed, rows], 10_000_000,
     )
     middle, stage, *faces = call(
-        stage_kernel, "stage", first, [velocity, grads, stage, *swap_faces(faces), begin, rest],
+        first_stage_kernel, "stage", first, [velocity, grads, stage, *swap_faces(faces), begin, rest, bulk],
         [fine, fine] + fine_faces, [ext], 40_000_000,
     )
     result, = call(
-        stage_kernel, "stage", first, [velocity, grads, stage, *swap_faces(faces), middle],
+        last_stage_kernel, "stage", first, [velocity, grads, stage, *swap_faces(faces), middle],
         [fine], [ext], 40_000_000,
     )
     return result[None]

time: 139 us -> 152 us (1.094)
  waiting for transfers between devices: 52.6 us -> 64.5 us
    ppermute x25, waiting for transfers between devices: 22.4 us -> 34.4 us  [pass_on(): return lax.ppermute(array, ('tm', 'gx', 'gy'), pairs)]
  transfers between devices with their start and end apart: 43 -> 43, of which waited for: 23 -> 22; matrix products, arithmetic and copies ran while one was open for 0% -> 0% of each run, Pallas kernels for 6% -> 3%
where the time goes in v8:
time: 152 us; the launch traced here: 151 us
  waiting for transfers between devices  64.5 us (42%)
  starting transfers between devices  47.6 us (31%)
  Pallas kernels  37.1 us (24%)
    pallas_call x14, Pallas kernels, call(): pl.pallas_call(kernel, name=name, out_shape=[jax.ShapeDtypeStruct(dims, F...  37.1 us
    ppermute x25, waiting for transfers between devices, pass_on(): return lax.ppermute(array, ('tm', 'gx', 'gy'), pairs)  34.4 us
    ppermute x25, starting transfers between devices, pass_on(): return lax.ppermute(array, ('tm', 'gx', 'gy'), pairs)  28.1 us
    ppermute x6, waiting for transfers between devices, swap_faces(): behind = lax.ppermute(y_last, 'gy', ring(gy, 1))  13.2 us
    ppermute x6, waiting for transfers between devices, swap_faces(): ahead = lax.ppermute(y_first, 'gy', ring(gy, -1))  12.9 us
    ppermute x6, starting transfers between devices, swap_faces(): ahead = lax.ppermute(y_first, 'gy', ring(gy, -1))  8.43 us
    ppermute x6, starting transfers between devices, swap_faces(): lax.ppermute(a, 'gx', ring(gx, by))  6.48 us
    ppermute x6, starting transfers between devices, swap_faces(): behind = lax.ppermute(y_last, 'gy', ring(gy, 1))  4.58 us
  transfers between devices with their start and end apart: 43, of which 22 were waited for; matrix products, arithmetic and copies ran while one was open for 0% of the time, Pallas kernels for 3%

profile of v8, /device:TPU:26, one launch (start us, length us, event | category | flops | bytes accessed | tf_op | source)
XLA Modules:
  0.0 151.1 jit_solution(16569541787669897219)
XLA Ops:
  0.6 4.1 %pack.1 = (f32[3,8,16,128]{3,2,1,0:T(8,128)}, f32[7,2,32,256]{3,2,1,0:T(8,128)}, f32[7,16,256]{2,1,0:T(8,128)}, f32[7,16,256]{2,1,0:T(8,128)}) custom-call(f32[2]{0:T(128)} %add_convert_fusion.first.refs_0_, f32[3,16,32,256]{3,2,1,0:T(8,128)} %v.15, f32[3,16,32,256]{3,2,1,0:T(8,128)} %refs_16_.1, f32[3,16,32,256]{3,2,1,0:T(8,128)} %bitcast.4), custom_call_target="tpu_custom_call" | custom-call | flops 5000000 | bytes 4718592 | tf_op jit(solution)/shard_map/pack/pallas_call | solution.py:671
  10.8 2.9 %collective-permute-done.1.behind.w_b = f32[7,16,256]{2,1,0:T(8,128)S(1)} collective-permute-done((f32[7,16,256]{2,1,0:T(8,128)}, f32[7,16,256]{2,1,0:T(8,128)S(1)}, u32[]{:S(2)}, u32[]{:S(2)}) %collective-permute-start.1) | collective-permute-done | bytes 114720 | tf_op jit(solution)/shard_map/ppermute | solution.py:35
  13.7 3.5 %collective-permute-done.x_faces.w_x = f32[7,2,32,256]{3,2,1,0:T(8,128)S(1)} collective-permute-done((f32[7,2,32,256]{3,2,1,0:T(8,128)}, f32[7,2,32,256]{3,2,1,0:T(8,128)S(1)}, u32[]{:S(2)}, u32[]{:S(2)}) %collective-permute-start) | collective-permute-done | bytes 458784 | tf_op jit(solution)/shard_map/ppermute | solution.py:34
  17.2 4.9 %offset_start.1 = (f32[9,16,32,256]{3,2,1,0:T(8,128)S(1)}, f32[3,8,16,128]{3,2,1,0:T(8,128)S(1)}, f32[9,8,16,128]{3,2,1,0:T(8,128)S(1)}, f32[3,2,16,128]{3,2,1,0...) custom-call(f32[2]{0:T(128)S(1)} %copy-done.5, ...), custom_call_target="tpu_custom_call" | custom-call | flops 40000000 | bytes 5603328 | tf_op jit(solution)/shard_map/offset_start/pallas_call | solution.py:671
  30.8 6.7 %collective-permute-done.8.refs_2_.refs_6_ = f32[3,8,128]{2,1,0:T(8,128)S(1)} collective-permute-done((f32[3,8,128]{2,1,0:T(8,128)S(1)}, f32[3,8,128]{2,1,0:T(8,128)S(1)}, u32[]{:S(2)}, u32[]{:S(2)}) %collective-permute-start.8) | collective-permute-done | bytes 12320 | tf_op jit(solution)/shard_map/ppermute | solution.py:49
  48.7 2.9 %collective-permute-start.16 = (f32[4,16,256]{2,1,0:T(8,128)S(1)}, f32[4,16,256]{2,1,0:T(8,128)S(1)}, u32[]{:S(2)}, u32[]{:S(2)}) collective-permute-start(f32[4,16,256]{2,1,0:T(8,128)S(1)} %get-tuple-element.106), channel_id=1, source_target_pairs={{0,1},{1,2},{2,3},{3,0},{4,5},{5,6},{6,7},{7,4},{8,9},{9,10},{10,1... | collective-permute-start | bytes 196616 | tf_op jit(solution)/shard_map/ppermute | solution.py:35
  53.5 4.1 %collective-permute-done.17.m_a.ahead = f32[4,16,256]{2,1,0:T(8,128)S(1)} collective-permute-done((f32[4,16,256]{2,1,0:T(8,128)S(1)}, f32[4,16,256]{2,1,0:T(8,128)S(1)}, u32[]{:S(2)}, u32[]{:S(2)}) %collective-permute-start.17) | collective-permute-done | bytes 65568 | tf_op jit(solution)/shard_map/ppermute | solution.py:36
  57.6 4.2 %middle.1 = (f32[3,16,32,256]{3,2,1,0:T(8,128)S(1)}, f32[3,2,32,256]{3,2,1,0:T(8,128)S(1)}, f32[3,16,256]{2,1,0:T(8,128)S(1)}, f32[3,16,256]{2,1,0:T(8,128)S(1)}...) custom-call(f32[2]{0:T(128)S(1)} %copy-done.5, ...), custom_call_target="tpu_custom_call" | custom-call | flops 60000000 | bytes 10985472 | tf_op jit(solution)/shard_map/middle/pallas_call | solution.py:671
  64.4 2.1 %collective-permute-done.19.a1_b.u1_b = f32[3,16,256]{2,1,0:T(8,128)S(1)} collective-permute-done((f32[3,16,256]{2,1,0:T(8,128)S(1)}, f32[3,16,256]{2,1,0:T(8,128)S(1)}, u32[]{:S(2)}, u32[]{:S(2)}) %collective-permute-start.19) | collective-permute-done | bytes 49184 | tf_op jit(solution)/shard_map/ppermute | solution.py:35
  66.5 3.2 %collective-permute-done.20.a1_a.u1_a = f32[3,16,256]{2,1,0:T(8,128)S(1)} collective-permute-done((f32[3,16,256]{2,1,0:T(8,128)S(1)}, f32[3,16,256]{2,1,0:T(8,128)S(1)}, u32[]{:S(2)}, u32[]{:S(2)}) %collective-permute-start.20) | collective-permute-done | bytes 49184 | tf_op jit(solution)/shard_map/ppermute | solution.py:36
  69.7 3.2 %finish.1 = (f32[3,16,32,256]{3,2,1,0:T(8,128)S(1)}, f32[3,2,32,256]{3,2,1,0:T(8,128)S(1)}, f32[3,16,256]{2,1,0:T(8,128)S(1)}, f32[3,16,256]{2,1,0:T(8,128)S(1)}, f32[3,8,16,128]{3,2,1,0:T(8,128)S(1)}) custom-call(f32[2]{0:T(128)S(1)} %copy-done.5, f32[3,16,32,256]{3,2,1,0:T(8,128)S(1)} %copy-done, f32[9,16,32,256]{3,2,1,0:T(8,128)S(1)} %get-tuple-element.86.grads, ...), custom_call_target="tpu_custom_call" | custom-call | flops 40000000 | bytes 10027008 | tf_op jit(solution)/shard_map/finish/pallas_call | solution.py:671
  74.1 2.0 %collective-permute-start.23 = (f32[3,16,256]{2,1,0:T(8,128)S(1)}, f32[3,16,256]{2,1,0:T(8,128)S(1)}, u32[]{:S(2)}, u32[]{:S(2)}) collective-permute-start(f32[3,16,256]{2,1,0:T(8,128)S(1)} %get-tuple-element.124), channel_id=1, source_target_pairs={{0,3},{1,0},{2,1},{3,2},{4,7},{5,4},{6,5},{7,6},{8,11},{9,8},{10,9... | collective-permute-start | bytes 147464 | tf_op jit(solution)/shard_map/ppermute | solution.py:36
  76.1 2.1 %collective-permute-done.22.u2_b = f32[3,16,256]{2,1,0:T(8,128)S(1)} collective-permute-done((f32[3,16,256]{2,1,0:T(8,128)S(1)}, f32[3,16,256]{2,1,0:T(8,128)S(1)}, u32[]{:S(2)}, u32[]{:S(2)}) %collective-permute-start.22) | collective-permute-done | bytes 49184 | tf_op jit(solution)/shard_map/ppermute | solution.py:35
  80.0 5.6 %offset_later.1 = (f32[3,8,16,128]{3,2,1,0:T(8,128)S(1)}, f32[3,8,16,128]{3,2,1,0:T(8,128)S(1)}, f32[6,8,16,128]{3,2,1,0:T(8,128)S(1)}, f32[3,2,16,128]{3,2,1,0:...) custom-call(f32[2]{0:T(128)S(1)} %copy-done.5, ...), custom_call_target="tpu_custom_call" | custom-call | flops 60000000 | bytes 12386304 | tf_op jit(solution)/shard_map/offset_later/pallas_call | solution.py:671
  96.1 3.4 %collective-permute-done.29.refs_2_.refs_6_ = f32[3,8,128]{2,1,0:T(8,128)S(1)} collective-permute-done((f32[3,8,128]{2,1,0:T(8,128)S(1)}, f32[3,8,128]{2,1,0:T(8,128)S(1)}, u32[]{:S(2)}, u32[]{:S(2)}) %collective-permute-start.29) | collective-permute-done | bytes 12320 | tf_op jit(solution)/shard_map/ppermute | solution.py:49
  99.5 3.1 %collective-permute-done.30.refs_3_.refs_7_ = f32[3,8,128]{2,1,0:T(8,128)S(1)} collective-permute-done((f32[3,8,128]{2,1,0:T(8,128)S(1)}, f32[3,8,128]{2,1,0:T(8,128)S(1)}, u32[]{:S(2)}, u32[]{:S(2)}) %collective-permute-start.30) | collective-permute-done | bytes 12320 | tf_op jit(solution)/shard_map/ppermute | solution.py:49
  102.6 16.6 %collective-permute-done.31.refs_4_.refs_8_ = f32[3,2,16,128]{3,2,1,0:T(8,128)S(1)} collective-permute-done((f32[3,2,16,128]{3,2,1,0:T(8,128)S(1)}, f32[3,2,16,128]{3,2,1,0:T(8,128)S(1)}, u32[]{:S(2)}, u32[]{:S(2)}) %collective-permute-start.31) | collective-permute-done | bytes 49184 | tf_op jit(solution)/shard_map/ppermute | solution.py:49
  126.7 2.3 %settle.3 = (f32[3,16,32,256]{3,2,1,0:T(8,128)S(1)}, f32[3,2,32,256]{3,2,1,0:T(8,128)S(1)}, f32[3,16,256]{2,1,0:T(8,128)S(1)}, f32[3,16,256]{2,1,0:T(8,128)S(1)}...) custom-call(f32[2]{0:T(128)S(1)} %copy-done.5, f32[6,8,16,128]{3,2,1,0:T(8,128)S(1)} %collective-permute-done.24.refs_1_, ...), custom_call_target="tpu_custom_call" | custom-call | flops 10000000 | bytes 7102464 | tf_op jit(solution)/shard_map/settle/pallas_call | solution.py:671
  130.2 2.0 %collective-permute-start.38 = (f32[3,16,256]{2,1,0:T(8,128)S(1)}, f32[3,16,256]{2,1,0:T(8,128)S(1)}, u32[]{:S(2)}, u32[]{:S(2)}) collective-permute-start(f32[3,16,256]{2,1,0:T(8,128)S(1)} %get-tuple-element.148), channel_id=1, source_target_pairs={{0,3},{1,0},{2,1},{3,2},{4,7},{5,4},{6,5},{7,6},{8,11},{9,8},{10,9... | collective-permute-start | bytes 147464 | tf_op jit(solution)/shard_map/ppermute | solution.py:36
  132.2 2.1 %collective-permute-done.37.y_b = f32[3,16,256]{2,1,0:T(8,128)S(1)} collective-permute-done((f32[3,16,256]{2,1,0:T(8,128)S(1)}, f32[3,16,256]{2,1,0:T(8,128)S(1)}, u32[]{:S(2)}, u32[]{:S(2)}) %collective-permute-start.37) | collective-permute-done | bytes 49184 | tf_op jit(solution)/shard_map/ppermute | solution.py:35
  136.0 3.3 %stage.2 = (f32[3,16,32,256]{3,2,1,0:T(8,128)S(1)}, f32[3,16,32,256]{3,2,1,0:T(8,128)S(1)}, f32[3,2,32,256]{3,2,1,0:T(8,128)S(1)}, f32[3,16,256]{2,1,0:T(8,128)S(1)}, f32[3,16,256]{2,1,0:T(8,128)S(1)}) custom-call(f32[2]{0:T(128)S(1)} %copy-done.5, f32[3,16,32,256]{3,2,1,0:T(8,128)S(1)} %copy-done, f32[9,16,32,256]{3,2,1,0:T(8,128)S(1)} %get-tuple-element.86.grads, ...), custom_call_target="tpu_custom_call" | custom-call | flops 40000000 | bytes 13172736 | tf_op jit(solution)/shard_map/stage/pallas_call | solution.py:671
  140.4 2.0 %collective-permute-start.42 = (f32[3,16,256]{2,1,0:T(8,128)S(1)}, f32[3,16,256]{2,1,0:T(8,128)S(1)}, u32[]{:S(2)}, u32[]{:S(2)}) collective-permute-start(f32[3,16,256]{2,1,0:T(8,128)S(1)} %get-tuple-element.155), channel_id=1, source_target_pairs={{0,3},{1,0},{2,1},{3,2},{4,7},{5,4},{6,5},{7,6},{8,11},{9,8},{10,9... | collective-permute-start | bytes 147464 | tf_op jit(solution)/shard_map/ppermute | solution.py:36
  142.4 2.2 %collective-permute-done.41.y_b = f32[3,16,256]{2,1,0:T(8,128)S(1)} collective-permute-done((f32[3,16,256]{2,1,0:T(8,128)S(1)}, f32[3,16,256]{2,1,0:T(8,128)S(1)}, u32[]{:S(2)}, u32[]{:S(2)}) %collective-permute-start.41) | collective-permute-done | bytes 49184 | tf_op jit(solution)/shard_map/ppermute | solution.py:35
  147.1 3.9 %stage.3 = f32[3,16,32,256]{3,2,1,0:T(8,128)} custom-call(f32[2]{0:T(128)S(1)} %copy-done.5, f32[3,16,32,256]{3,2,1,0:T(8,128)S(1)} %copy-done, f32[9,16,32,256]{3,2,1,0:T(8,128)S(1)} %get-tuple-element.86.grads, f32[3,16,32,256]{3,2,1,0:T(8,128)S(1)} %get-tuple-element.152.y, f32[3,2,32,256]{3,2,1,0:T(8,128)S(1)} %collective-permute-done.40.y_x, ...), custom_call_target="tpu_custom_call" | custom-call | flops 40000000 | bytes 9732096 | tf_op jit(solution)/shard_map/stage/pallas_call | solution.py:671
  (89 shorter events, 58.3 us)
Async XLA Ops:
  4.7 12.5 %collective-permute-start = (f32[7,2,32,256]{3,2,1,0:T(8,128)}, f32[7,2,32,256]{3,2,1,0:T(8,128)S(1)}, u32[]{:S(2)}, u32[]{:S(2)}) collective-permute-start(f32[7,2,32,256]{3,2,1,0:T(8,128)} %get-tuple-element.81), channel_id=1, source_target_pairs={{0,4},{4,0},{1,5},{5,1},{2,6},{6,2},{3,7},{7,3},{8,12},{12,8},{9,1... | collective-permute-start | bytes 1376264 | tf_op jit(solution)/shard_map/ppermute | solution.py:34
  6.3 7.5 %collective-permute-start.1 = (f32[7,16,256]{2,1,0:T(8,128)}, f32[7,16,256]{2,1,0:T(8,128)S(1)}, u32[]{:S(2)}, u32[]{:S(2)}) collective-permute-start(f32[7,16,256]{2,1,0:T(8,128)} %get-tuple-element.82), channel_id=1, source_target_pairs={{0,1},{1,2},{2,3},{3,0},{4,5},{5,6},{6,7},{7,4},{8,9},{9,10},{10,1... | collective-permute-start | bytes 344072 | tf_op jit(solution)/shard_map/ppermute | solution.py:35
  6.5 7.2 %collective-permute-start.2 = (f32[7,16,256]{2,1,0:T(8,128)}, f32[7,16,256]{2,1,0:T(8,128)S(1)}, u32[]{:S(2)}, u32[]{:S(2)}) collective-permute-start(f32[7,16,256]{2,1,0:T(8,128)} %get-tuple-element.83), channel_id=1, source_target_pairs={{0,3},{1,0},{2,1},{3,2},{4,7},{5,4},{6,5},{7,6},{8,11},{9,8},{10,9... | collective-permute-start | bytes 344072 | tf_op jit(solution)/shard_map/ppermute | solution.py:36
  25.6 13.6 %collective-permute-start.7 = (f32[3,8,16,128]{3,2,1,0:T(8,128)S(1)}, f32[3,8,16,128]{3,2,1,0:T(8,128)S(1)}, u32[]{:S(2)}, u32[]{:S(2)}) collective-permute-start(f32[3,8,16,128]{3,2,1,0:T(8,128)S(1)} %get-tuple-element.97), channel_id=1, source_target_pairs={{8,16},{9,17},{10,18},{11,19},{12,20},{13,21},{14,22},{15,23}} | collective-permute-start | bytes 589832 | tf_op jit(solution)/shard_map/ppermute | solution.py:49
  26.9 12.3 %collective-permute-start.10 = (f32[3,2,16,128]{3,2,1,0:T(8,128)S(1)}, f32[3,2,16,128]{3,2,1,0:T(8,128)S(1)}, u32[]{:S(2)}, u32[]{:S(2)}) collective-permute-start(f32[3,2,16,128]{3,2,1,0:T(8,128)S(1)} %get-tuple-element.100), channel_id=1, source_target_pairs={{8,20},{9,21},{10,22},{11,23},{12,16},{13,17},{14,18},{15,19}} | collective-permute-start | bytes 147464 | tf_op jit(solution)/shard_map/ppermute | solution.py:49
  28.2 9.3 %collective-permute-start.8 = (f32[3,8,128]{2,1,0:T(8,128)S(1)}, f32[3,8,128]{2,1,0:T(8,128)S(1)}, u32[]{:S(2)}, u32[]{:S(2)}) collective-permute-start(f32[3,8,128]{2,1,0:T(8,128)S(1)} %get-tuple-element.98), channel_id=1, source_target_pairs={{8,17},{9,18},{10,19},{11,16},{12,21},{13,22},{14,23},{15,20}} | collective-permute-start | bytes 36872 | tf_op jit(solution)/shard_map/ppermute | solution.py:49
  29.5 9.7 %collective-permute-start.9 = (f32[3,8,128]{2,1,0:T(8,128)S(1)}, f32[3,8,128]{2,1,0:T(8,128)S(1)}, u32[]{:S(2)}, u32[]{:S(2)}) collective-permute-start(f32[3,8,128]{2,1,0:T(8,128)S(1)} %get-tuple-element.99), channel_id=1, source_target_pairs={{8,19},{9,16},{10,17},{11,18},{12,23},{13,20},{14,21},{15,22}} | collective-permute-start | bytes 36872 | tf_op jit(solution)/shard_map/ppermute | solution.py:49
  40.1 6.6 %collective-permute-start.11 = (f32[3,8,16,128]{3,2,1,0:T(8,128)S(1)}, f32[3,8,16,128]{3,2,1,0:T(8,128)S(1)}, u32[]{:S(2)}, u32[]{:S(2)}) collective-permute-start(f32[3,8,16,128]{3,2,1,0:T(8,128)S(1)} %get-tuple-element.101), channel_id=1, source_target_pairs={{16,24},{17,25},{18,26},{19,27},{20,28},{21,29},{22,30},{23,31}} | collective-permute-start | bytes 589832 | tf_op jit(solution)/shard_map/ppermute | solution.py:49
  47.7 9.9 %collective-permute-start.15 = (f32[4,2,32,256]{3,2,1,0:T(8,128)S(1)}, f32[4,2,32,256]{3,2,1,0:T(8,128)S(1)}, u32[]{:S(2)}, u32[]{:S(2)}) collective-permute-start(f32[4,2,32,256]{3,2,1,0:T(8,128)S(1)} %get-tuple-element.105), channel_id=1, source_target_pairs={{0,4},{4,0},{1,5},{5,1},{2,6},{6,2},{3,7},{7,3},{8,12},{12,8},{9,1... | collective-permute-start | bytes 786440 | tf_op jit(solution)/shard_map/ppermute | solution.py:34
  51.5 6.1 %collective-permute-start.17 = (f32[4,16,256]{2,1,0:T(8,128)S(1)}, f32[4,16,256]{2,1,0:T(8,128)S(1)}, u32[]{:S(2)}, u32[]{:S(2)}) collective-permute-start(f32[4,16,256]{2,1,0:T(8,128)S(1)} %get-tuple-element.107), channel_id=1, source_target_pairs={{0,3},{1,0},{2,1},{3,2},{4,7},{5,4},{6,5},{7,6},{8,11},{9,8},{10,9... | collective-permute-start | bytes 196616 | tf_op jit(solution)/shard_map/ppermute | solution.py:36
  61.8 7.8 %collective-permute-start.18 = (f32[3,2,32,256]{3,2,1,0:T(8,128)S(1)}, f32[3,2,32,256]{3,2,1,0:T(8,128)S(1)}, u32[]{:S(2)}, u32[]{:S(2)}) collective-permute-start(f32[3,2,32,256]{3,2,1,0:T(8,128)S(1)} %get-tuple-element.114), channel_id=1, source_target_pairs={{0,4},{4,0},{1,5},{5,1},{2,6},{6,2},{3,7},{7,3},{8,12},{12,8},{9,1... | collective-permute-start | bytes 589832 | tf_op jit(solution)/shard_map/ppermute | solution.py:34
  63.8 5.9 %collective-permute-start.20 = (f32[3,16,256]{2,1,0:T(8,128)S(1)}, f32[3,16,256]{2,1,0:T(8,128)S(1)}, u32[]{:S(2)}, u32[]{:S(2)}) collective-permute-start(f32[3,16,256]{2,1,0:T(8,128)S(1)} %get-tuple-element.116), channel_id=1, source_target_pairs={{0,3},{1,0},{2,1},{3,2},{4,7},{5,4},{6,5},{7,6},{8,11},{9,8},{10,9... | collective-permute-start | bytes 147464 | tf_op jit(solution)/shard_map/ppermute | solution.py:36
  72.9 7.1 %collective-permute-start.21 = (f32[3,2,32,256]{3,2,1,0:T(8,128)S(1)}, f32[3,2,32,256]{3,2,1,0:T(8,128)S(1)}, u32[]{:S(2)}, u32[]{:S(2)}) collective-permute-start(f32[3,2,32,256]{3,2,1,0:T(8,128)S(1)} %get-tuple-element.122), channel_id=1, source_target_pairs={{0,4},{4,0},{1,5},{5,1},{2,6},{6,2},{3,7},{7,3},{8,12},{12,8},{9,1... | collective-permute-start | bytes 589832 | tf_op jit(solution)/shard_map/ppermute | solution.py:34
  74.1 5.9 %collective-permute-start.23 = (f32[3,16,256]{2,1,0:T(8,128)S(1)}, f32[3,16,256]{2,1,0:T(8,128)S(1)}, u32[]{:S(2)}, u32[]{:S(2)}) collective-permute-start(f32[3,16,256]{2,1,0:T(8,128)S(1)} %get-tuple-element.124), channel_id=1, source_target_pairs={{0,3},{1,0},{2,1},{3,2},{4,7},{5,4},{6,5},{7,6},{8,11},{9,8},{10,9... | collective-permute-start | bytes 147464 | tf_op jit(solution)/shard_map/ppermute | solution.py:36
  89.0 47.1 %collective-permute-start.39 = (f32[3,608,256]{2,1,0:T(8,128)S(1)}, f32[3,608,256]{2,1,0:T(8,128)S(1)}, u32[]{:S(2)}, u32[]{:S(2)}) collective-permute-start(f32[3,608,256]{2,1,0:T(8,128)S(1)} %get-tuple-element.151), channel_id=1, source_target_pairs={{0,8},{1,9},{2,10},{3,11},{4,12},{5,13},{6,14},{7,15},{8,16},{9,17... | collective-permute-start | bytes 5603336 | tf_op jit(solution)/shard_map/ppermute | solution.py:49
  90.9 28.3 %collective-permute-start.28 = (f32[6,8,16,128]{3,2,1,0:T(8,128)S(1)}, f32[6,8,16,128]{3,2,1,0:T(8,128)S(1)}, u32[]{:S(2)}, u32[]{:S(2)}) collective-permute-start(f32[6,8,16,128]{3,2,1,0:T(8,128)S(1)} %get-tuple-element.137), channel_id=1, source_target_pairs={{8,16},{9,17},{10,18},{11,19},{12,20},{13,21},{14,22},{15,23}} | collective-permute-start | bytes 1179656 | tf_op jit(solution)/shard_map/ppermute | solution.py:49
  92.2 27.0 %collective-permute-start.31 = (f32[3,2,16,128]{3,2,1,0:T(8,128)S(1)}, f32[3,2,16,128]{3,2,1,0:T(8,128)S(1)}, u32[]{:S(2)}, u32[]{:S(2)}) collective-permute-start(f32[3,2,16,128]{3,2,1,0:T(8,128)S(1)} %get-tuple-element.140), channel_id=1, source_target_pairs={{8,20},{9,21},{10,22},{11,23},{12,16},{13,17},{14,18},{15,19}} | collective-permute-start | bytes 147464 | tf_op jit(solution)/shard_map/ppermute | solution.py:49
  93.5 6.0 %collective-permute-start.29 = (f32[3,8,128]{2,1,0:T(8,128)S(1)}, f32[3,8,128]{2,1,0:T(8,128)S(1)}, u32[]{:S(2)}, u32[]{:S(2)}) collective-permute-start(f32[3,8,128]{2,1,0:T(8,128)S(1)} %get-tuple-element.138), channel_id=1, source_target_pairs={{8,17},{9,18},{10,19},{11,16},{12,21},{13,22},{14,23},{15,20}} | collective-permute-start | bytes 36872 | tf_op jit(solution)/shard_map/ppermute | solution.py:49
  94.8 7.8 %collective-permute-start.30 = (f32[3,8,128]{2,1,0:T(8,128)S(1)}, f32[3,8,128]{2,1,0:T(8,128)S(1)}, u32[]{:S(2)}, u32[]{:S(2)}) collective-permute-start(f32[3,8,128]{2,1,0:T(8,128)S(1)} %get-tuple-element.139), channel_id=1, source_target_pairs={{8,19},{9,16},{10,17},{11,18},{12,23},{13,20},{14,21},{15,22}} | collective-permute-start | bytes 36872 | tf_op jit(solution)/shard_map/ppermute | solution.py:49
  120.1 6.6 %collective-permute-start.32 = (f32[6,8,16,128]{3,2,1,0:T(8,128)S(1)}, f32[6,8,16,128]{3,2,1,0:T(8,128)S(1)}, u32[]{:S(2)}, u32[]{:S(2)}) collective-permute-start(f32[6,8,16,128]{3,2,1,0:T(8,128)S(1)} %get-tuple-element.141), channel_id=1, source_target_pairs={{16,24},{17,25},{18,26},{19,27},{20,28},{21,29},{22,30},{23,31}} | collective-permute-start | bytes 1179656 | tf_op jit(solution)/shard_map/ppermute | solution.py:49
  129.0 7.1 %collective-permute-start.36 = (f32[3,2,32,256]{3,2,1,0:T(8,128)S(1)}, f32[3,2,32,256]{3,2,1,0:T(8,128)S(1)}, u32[]{:S(2)}, u32[]{:S(2)}) collective-permute-start(f32[3,2,32,256]{3,2,1,0:T(8,128)S(1)} %get-tuple-element.146), channel_id=1, source_target_pairs={{0,4},{4,0},{1,5},{5,1},{2,6},{6,2},{3,7},{7,3},{8,12},{12,8},{9,1... | collective-permute-start | bytes 589832 | tf_op jit(solution)/shard_map/ppermute | solution.py:34
  130.2 5.9 %collective-permute-start.38 = (f32[3,16,256]{2,1,0:T(8,128)S(1)}, f32[3,16,256]{2,1,0:T(8,128)S(1)}, u32[]{:S(2)}, u32[]{:S(2)}) collective-permute-start(f32[3,16,256]{2,1,0:T(8,128)S(1)} %get-tuple-element.148), channel_id=1, source_target_pairs={{0,3},{1,0},{2,1},{3,2},{4,7},{5,4},{6,5},{7,6},{8,11},{9,8},{10,9... | collective-permute-start | bytes 147464 | tf_op jit(solution)/shard_map/ppermute | solution.py:36
  139.3 7.8 %collective-permute-start.40 = (f32[3,2,32,256]{3,2,1,0:T(8,128)S(1)}, f32[3,2,32,256]{3,2,1,0:T(8,128)S(1)}, u32[]{:S(2)}, u32[]{:S(2)}) collective-permute-start(f32[3,2,32,256]{3,2,1,0:T(8,128)S(1)} %get-tuple-element.153), channel_id=1, source_target_pairs={{0,4},{4,0},{1,5},{5,1},{2,6},{6,2},{3,7},{7,3},{8,12},{12,8},{9,1... | collective-permute-start | bytes 589832 | tf_op jit(solution)/shard_map/ppermute | solution.py:34
  140.4 6.1 %collective-permute-start.42 = (f32[3,16,256]{2,1,0:T(8,128)S(1)}, f32[3,16,256]{2,1,0:T(8,128)S(1)}, u32[]{:S(2)}, u32[]{:S(2)}) collective-permute-start(f32[3,16,256]{2,1,0:T(8,128)S(1)} %get-tuple-element.155), channel_id=1, source_target_pairs={{0,3},{1,0},{2,1},{3,2},{4,7},{5,4},{6,5},{7,6},{8,11},{9,8},{10,9... | collective-permute-start | bytes 147464 | tf_op jit(solution)/shard_map/ppermute | solution.py:36
  (25 other events, 112.9 us)

commit v9 on v7

--- a/solution.py
+++ b/solution.py
@@ -10,7 +10,7 @@
 VISCOSITY = 0.25
 TIME_STEP = 0.5
 PAD = 8
-CHUNK = 8
+CHUNK = 16
 ROOM = 4 << 20
 F32 = jnp.float32
 BF16 = jnp.bfloat16
@@ -277,10 +277,11 @@
     return Mix((f / 6.0, s), (1.0 - f / 6.0, g))
 
 
-def pack_kernel(first, v, s, g, end, x_faces, y_last, y_first, summed, rows):
+def pack_kernel(v, s, g, end, x_faces, y_last, y_first, summed, rows):
     outs = (x_faces, y_last, y_first)
     emit_faces(v, outs, 0)
-    emit_faces(offset_mix(first[0], s, g), outs, 3)
+    f = jnp.where(lax.axis_index("tm") == 0, 1.0, 0.0)
+    emit_faces(offset_mix(f, s, g), outs, 3)
 
     def store(c, value):
         end[c] = value
@@ -500,11 +501,7 @@
     emit_faces(stage, (stage_x, stage_l, stage_f))
 
 
-def stage_kernel(first, v, grads, y, y_x, y_b, y_a, begin, *refs):
-    if len(refs) == 2:
-        out, ext = refs
-    else:
-        rest, out, following, following_x, following_l, following_f, ext = refs
+def first_stage_kernel(first, v, grads, y, y_x, y_b, y_a, begin, rest, out, stage, stage_x, stage_l, stage_f, ext):
     fill(ext, [(1.0, Node(y, y_x, y_b, y_a))])
     width, length = v.shape[1:3]
     n = min(CHUNK, length)
@@ -517,11 +514,26 @@
             for a in range(3):
                 value = begin[a, x, at] + changes[a]
                 out[a, x, at] = value
-                if len(refs) > 2:
-                    following[a, x, at] = TIME_STEP * (0.5 * value + rest[a, x, at])
-
-    if len(refs) > 2:
-        emit_faces(following, (following_x, following_l, following_f))
+                stage[a, x, at] = TIME_STEP * (0.5 * value + rest[a, x, at])
+
+    emit_faces(stage, (stage_x, stage_l, stage_f))
+
+
+def last_stage_kernel(v, grads, y, y_x, y_b, y_a, begin, out, ext, made, sent):
+    fill(ext, [(1.0, Node(y, y_x, y_b, y_a))])
+    width, length = v.shape[1:3]
+    n = min(CHUNK, length)
+
+    @pl.loop(0, width)
+    def _(x):
+        for r in range(0, length, n):
+            changes = fine_rates(ext, v, grads, x, r, n)
+            for a in range(3):
+                made[a, x, r : r + n] = begin[a, x, r : r + n] + changes[a]
+        plane = pl.ds(x, 1)
+        pltpu.make_async_copy(made.at[:, plane], out.at[:, plane], sent).start()
+
+    pltpu.make_async_copy(made, out, sent).wait()
 
 
 def middle_kernel(
@@ -614,19 +626,23 @@
     squeeze(summed, rows, store, 3)
 
 
-def call(kernel, name, first, args, outs, scratch, flops=0, least=0):
+def call(kernel, name, first, args, outs, scratch, flops=0, least=0, streamed=False):
     moved = sum(4 * a.size for a in args)
     room = moved + sum(4 * math.prod(dims) for dims in outs + scratch)
+    values = pl.BlockSpec(memory_space=pltpu.VMEM)
+    buffers = [pltpu.VMEM(dims, F32) for dims in scratch]
+    if streamed:
+        buffers += [pltpu.VMEM(dims, F32) for dims in outs] + [pltpu.SemaphoreType.DMA]
     return pl.pallas_call(
         kernel,
         name=name,
         out_shape=[jax.ShapeDtypeStruct(dims, F32) for dims in outs],
-        in_specs=[pl.BlockSpec(memory_space=pltpu.SMEM)] + [pl.BlockSpec(memory_space=pltpu.VMEM)] * len(args),
-        out_specs=[pl.BlockSpec(memory_space=pltpu.VMEM)] * len(outs),
-        scratch_shapes=[pltpu.VMEM(dims, F32) for dims in scratch],
+        in_specs=[pl.BlockSpec(memory_space=pltpu.SMEM)] * (first is not None) + [values] * len(args),
+        out_specs=[pl.BlockSpec(memory_space=pl.ANY) if streamed else values] * len(outs),
+        scratch_shapes=buffers,
         compiler_params=pltpu.CompilerParams(vmem_limit_bytes=min(max(room + ROOM, least), 56 << 20)),
         cost_estimate=pl.CostEstimate(flops=flops, bytes_accessed=moved, transcendentals=0),
-    )(first, *args)
+    )(*([] if first is None else [first]), *args)
 
 
 def shards(velocity, start_field, guess):
@@ -648,7 +664,7 @@
     wide, edge, wide_rows = (3, cx + 2, ny, nz), (2, 3, cx, nz), ((cx + 2) * ny, cz)
 
     end_two, *packed = call(
-        pack_kernel, "pack", first, [velocity, start_field, own],
+        pack_kernel, "pack", None, [velocity, start_field, own],
         [coarse] + layers_of(7), [summed, rows], 5_000_000, 56 << 20,
     )
     layers = swap_faces(packed)
@@ -712,12 +728,12 @@
         [coarse, *coarse_faces, coarse, coarse_ext, summed, summed, rows], 10_000_000,
     )
     middle, stage, *faces = call(
-        stage_kernel, "stage", first, [velocity, grads, stage, *swap_faces(faces), begin, rest],
+        first_stage_kernel, "stage", first, [velocity, grads, stage, *swap_faces(faces), begin, rest],
         [fine, fine] + fine_faces, [ext], 40_000_000,
     )
     result, = call(
-        stage_kernel, "stage", first, [velocity, grads, stage, *swap_faces(faces), middle],
-        [fine], [ext], 40_000_000,
+        last_stage_kernel, "last_stage", None, [velocity, grads, stage, *swap_faces(faces), middle],
+        [fine], [ext], 40_000_000, streamed=True,
     )
     return result[None]
 

time: 139 us -> 139 us (level)
  no operation moved by 1% of the time
where the time goes in v9:
time: 139 us; the launch traced here: 138 us
  waiting for transfers between devices  52.6 us (38%)
  starting transfers between devices  47.6 us (34%)
  Pallas kernels  36.2 us (26%)
    pallas_call x14, Pallas kernels, call(): pl.pallas_call(kernel, name=name, out_shape=[jax.ShapeDtypeStruct(dims, F...  36.2 us
    ppermute x25, starting transfers between devices, pass_on(): return lax.ppermute(array, ('tm', 'gx', 'gy'), pairs)  28.1 us
    ppermute x25, waiting for transfers between devices, pass_on(): return lax.ppermute(array, ('tm', 'gx', 'gy'), pairs)  22.4 us
    ppermute x6, waiting for transfers between devices, swap_faces(): ahead = lax.ppermute(y_first, 'gy', ring(gy, -1))  13.3 us
    ppermute x6, waiting for transfers between devices, swap_faces(): behind = lax.ppermute(y_last, 'gy', ring(gy, 1))  13 us
    ppermute x6, starting transfers between devices, swap_faces(): ahead = lax.ppermute(y_first, 'gy', ring(gy, -1))  7.92 us
    ppermute x6, starting transfers between devices, swap_faces(): lax.ppermute(a, 'gx', ring(gx, by))  6.52 us
    ppermute x6, starting transfers between devices, swap_faces(): behind = lax.ppermute(y_last, 'gy', ring(gy, 1))  5.09 us
  transfers between devices with their start and end apart: 43, of which 23 were waited for; matrix products, arithmetic and copies ran while one was open for 0% of the time, Pallas kernels for 6%

profile of v9, /device:TPU:26, one launch (start us, length us, event | category | flops | bytes accessed | tf_op | source)
XLA Modules:
  0.0 137.8 jit_solution(10190907684502465140)
XLA Ops:
  0.0 4.1 %pack.1 = (f32[3,8,16,128]{3,2,1,0:T(8,128)}, f32[7,2,32,256]{3,2,1,0:T(8,128)}, f32[7,16,256]{2,1,0:T(8,128)}, f32[7,16,256]{2,1,0:T(8,128)}) custom-call(f32[3,16,32,256]{3,2,1,0:T(8,128)} %v.15, f32[3,16,32,256]{3,2,1,0:T(8,128)} %refs_16_.1, f32[3,16,32,256]{3,2,1,0:T(8,128)} %bitcast.4), custom_call_target="tpu_custom_call" | custom-call | flops 5000000 | bytes 4718592 | tf_op jit(solution)/shard_map/pack/pallas_call | solution.py:636
  10.3 2.8 %collective-permute-done.1.behind.w_b = f32[7,16,256]{2,1,0:T(8,128)S(1)} collective-permute-done((f32[7,16,256]{2,1,0:T(8,128)}, f32[7,16,256]{2,1,0:T(8,128)S(1)}, u32[]{:S(2)}, u32[]{:S(2)}) %collective-permute-start.1) | collective-permute-done | bytes 114720 | tf_op jit(solution)/shard_map/ppermute | solution.py:35
  13.1 3.6 %collective-permute-done.x_faces.w_x = f32[7,2,32,256]{3,2,1,0:T(8,128)} collective-permute-done((f32[7,2,32,256]{3,2,1,0:T(8,128)}, f32[7,2,32,256]{3,2,1,0:T(8,128)}, u32[]{:S(2)}, u32[]{:S(2)}) %collective-permute-start) | collective-permute-done | bytes 458784 | tf_op jit(solution)/shard_map/ppermute | solution.py:34
  16.7 5.3 %offset_start.1 = (f32[9,16,32,256]{3,2,1,0:T(8,128)S(1)}, f32[3,8,16,128]{3,2,1,0:T(8,128)S(1)}, f32[9,8,16,128]{3,2,1,0:T(8,128)S(1)}, f32[3,2,16,128]{3,2,1,0...) custom-call(f32[2]{0:T(128)S(1)} %add_convert_fusion.first.refs_0_, ...), custom_call_target="tpu_custom_call" | custom-call | flops 40000000 | bytes 5603328 | tf_op jit(solution)/shard_map/offset_start/pallas_call | solution.py:636
  30.6 6.7 %collective-permute-done.8.refs_2_.refs_6_ = f32[3,8,128]{2,1,0:T(8,128)S(1)} collective-permute-done((f32[3,8,128]{2,1,0:T(8,128)S(1)}, f32[3,8,128]{2,1,0:T(8,128)S(1)}, u32[]{:S(2)}, u32[]{:S(2)}) %collective-permute-start.8) | collective-permute-done | bytes 12320 | tf_op jit(solution)/shard_map/ppermute | solution.py:49
  48.5 2.9 %collective-permute-start.16 = (f32[4,16,256]{2,1,0:T(8,128)S(1)}, f32[4,16,256]{2,1,0:T(8,128)S(1)}, u32[]{:S(2)}, u32[]{:S(2)}) collective-permute-start(f32[4,16,256]{2,1,0:T(8,128)S(1)} %get-tuple-element.100), channel_id=1, source_target_pairs={{0,1},{1,2},{2,3},{3,0},{4,5},{5,6},{6,7},{7,4},{8,9},{9,10},{10,1... | collective-permute-start | bytes 196616 | tf_op jit(solution)/shard_map/ppermute | solution.py:35
  51.4 2.0 %collective-permute-done.16.m_b.behind = f32[4,16,256]{2,1,0:T(8,128)S(1)} collective-permute-done((f32[4,16,256]{2,1,0:T(8,128)S(1)}, f32[4,16,256]{2,1,0:T(8,128)S(1)}, u32[]{:S(2)}, u32[]{:S(2)}) %collective-permute-start.16) | collective-permute-done | bytes 65568 | tf_op jit(solution)/shard_map/ppermute | solution.py:35
  53.3 4.1 %collective-permute-done.17.m_a.ahead = f32[4,16,256]{2,1,0:T(8,128)S(1)} collective-permute-done((f32[4,16,256]{2,1,0:T(8,128)S(1)}, f32[4,16,256]{2,1,0:T(8,128)S(1)}, u32[]{:S(2)}, u32[]{:S(2)}) %collective-permute-start.17) | collective-permute-done | bytes 65568 | tf_op jit(solution)/shard_map/ppermute | solution.py:36
  57.4 4.5 %middle.1 = (f32[3,16,32,256]{3,2,1,0:T(8,128)S(1)}, f32[3,2,32,256]{3,2,1,0:T(8,128)S(1)}, f32[3,16,256]{2,1,0:T(8,128)S(1)}, f32[3,16,256]{2,1,0:T(8,128)S(1)}...) custom-call(f32[2]{0:T(128)S(1)} %add_convert_fusion.first.refs_0_, ...), custom_call_target="tpu_custom_call" | custom-call | flops 60000000 | bytes 10985472 | tf_op jit(solution)/shard_map/middle/pallas_call | solution.py:636
  64.6 2.1 %collective-permute-done.19.a1_b.u1_b = f32[3,16,256]{2,1,0:T(8,128)S(1)} collective-permute-done((f32[3,16,256]{2,1,0:T(8,128)S(1)}, f32[3,16,256]{2,1,0:T(8,128)S(1)}, u32[]{:S(2)}, u32[]{:S(2)}) %collective-permute-start.19) | collective-permute-done | bytes 49184 | tf_op jit(solution)/shard_map/ppermute | solution.py:35
  66.6 3.2 %collective-permute-done.20.a1_a.u1_a = f32[3,16,256]{2,1,0:T(8,128)S(1)} collective-permute-done((f32[3,16,256]{2,1,0:T(8,128)S(1)}, f32[3,16,256]{2,1,0:T(8,128)S(1)}, u32[]{:S(2)}, u32[]{:S(2)}) %collective-permute-start.20) | collective-permute-done | bytes 49184 | tf_op jit(solution)/shard_map/ppermute | solution.py:36
  69.8 3.2 %finish.1 = (f32[3,16,32,256]{3,2,1,0:T(8,128)S(1)}, f32[3,2,32,256]{3,2,1,0:T(8,128)S(1)}, f32[3,16,256]{2,1,0:T(8,128)S(1)}, f32[3,16,256]{2,1,0:T(8,128)S(1)}, f32[3,8,16,128]{3,2,1,0:T(8,128)S(1)}) custom-call(f32[2]{0:T(128)S(1)} %add_convert_fusion.first.refs_0_, f32[3,16,32,256]{3,2,1,0:T(8,128)S(1)} %copy-done, ...), custom_call_target="tpu_custom_call" | custom-call | flops 40000000 | bytes 10027008 | tf_op jit(solution)/shard_map/finish/pallas_call | solution.py:636
  76.2 2.0 %collective-permute-start.23 = (f32[3,16,256]{2,1,0:T(8,128)S(1)}, f32[3,16,256]{2,1,0:T(8,128)S(1)}, u32[]{:S(2)}, u32[]{:S(2)}) collective-permute-start(f32[3,16,256]{2,1,0:T(8,128)S(1)} %get-tuple-element.118), channel_id=1, source_target_pairs={{0,3},{1,0},{2,1},{3,2},{4,7},{5,4},{6,5},{7,6},{8,11},{9,8},{10,9... | collective-permute-start | bytes 147464 | tf_op jit(solution)/shard_map/ppermute | solution.py:36
  78.2 2.1 %collective-permute-done.22.u2_b = f32[3,16,256]{2,1,0:T(8,128)S(1)} collective-permute-done((f32[3,16,256]{2,1,0:T(8,128)S(1)}, f32[3,16,256]{2,1,0:T(8,128)S(1)}, u32[]{:S(2)}, u32[]{:S(2)}) %collective-permute-start.22) | collective-permute-done | bytes 49184 | tf_op jit(solution)/shard_map/ppermute | solution.py:35
  82.1 5.4 %offset_later.1 = (f32[3,8,16,128]{3,2,1,0:T(8,128)S(1)}, f32[3,8,16,128]{3,2,1,0:T(8,128)S(1)}, f32[6,8,16,128]{3,2,1,0:T(8,128)S(1)}, f32[3,2,16,128]{3,2,1,0:...) custom-call(f32[2]{0:T(128)S(1)} %add_convert_fusion.first.refs_0_, f32[3,16,32,256]{3,2,1,0:T(8,128)S(1)} %copy-done, ...), custom_call_target="tpu_custom_call" | custom-call | flops 60000000 | bytes 12386304 | tf_op jit(solution)/shard_map/offset_later/pallas_call | solution.py:636
  96.0 7.2 %collective-permute-done.29.refs_2_.refs_6_ = f32[3,8,128]{2,1,0:T(8,128)S(1)} collective-permute-done((f32[3,8,128]{2,1,0:T(8,128)S(1)}, f32[3,8,128]{2,1,0:T(8,128)S(1)}, u32[]{:S(2)}, u32[]{:S(2)}) %collective-permute-start.29) | collective-permute-done | bytes 12320 | tf_op jit(solution)/shard_map/ppermute | solution.py:49
  105.1 2.1 %collective-permute-done.31.refs_4_.refs_8_ = f32[3,2,16,128]{3,2,1,0:T(8,128)S(1)} collective-permute-done((f32[3,2,16,128]{3,2,1,0:T(8,128)S(1)}, f32[3,2,16,128]{3,2,1,0:T(8,128)S(1)}, u32[]{:S(2)}, u32[]{:S(2)}) %collective-permute-start.31) | collective-permute-done | bytes 49184 | tf_op jit(solution)/shard_map/ppermute | solution.py:49
  114.7 2.4 %settle.3 = (f32[3,16,32,256]{3,2,1,0:T(8,128)S(1)}, f32[3,2,32,256]{3,2,1,0:T(8,128)S(1)}, f32[3,16,256]{2,1,0:T(8,128)S(1)}, f32[3,16,256]{2,1,0:T(8,128)S(1)}...) custom-call(f32[2]{0:T(128)S(1)} %add_convert_fusion.first.refs_0_, ...), custom_call_target="tpu_custom_call" | custom-call | flops 10000000 | bytes 8675328 | tf_op jit(solution)/shard_map/settle/pallas_call | solution.py:636
  120.3 2.1 %collective-permute-done.38.y_b = f32[3,16,256]{2,1,0:T(8,128)S(1)} collective-permute-done((f32[3,16,256]{2,1,0:T(8,128)S(1)}, f32[3,16,256]{2,1,0:T(8,128)S(1)}, u32[]{:S(2)}, u32[]{:S(2)}) %collective-permute-start.38) | collective-permute-done | bytes 49184 | tf_op jit(solution)/shard_map/ppermute | solution.py:35
  122.3 2.3 %collective-permute-done.39.y_a = f32[3,16,256]{2,1,0:T(8,128)S(1)} collective-permute-done((f32[3,16,256]{2,1,0:T(8,128)S(1)}, f32[3,16,256]{2,1,0:T(8,128)S(1)}, u32[]{:S(2)}, u32[]{:S(2)}) %collective-permute-start.39) | collective-permute-done | bytes 49184 | tf_op jit(solution)/shard_map/ppermute | solution.py:36
  124.7 2.9 %stage.1 = (f32[3,16,32,256]{3,2,1,0:T(8,128)S(1)}, f32[3,16,32,256]{3,2,1,0:T(8,128)S(1)}, f32[3,2,32,256]{3,2,1,0:T(8,128)S(1)}, f32[3,16,256]{2,1,0:T(8,128)S(1)}, f32[3,16,256]{2,1,0:T(8,128)S(1)}) custom-call(f32[2]{0:T(128)S(1)} %add_convert_fusion.first.refs_0_, f32[3,16,32,256]{3,2,1,0:T(8,128)S(1)} %copy-done, ...), custom_call_target="tpu_custom_call" | custom-call | flops 40000000 | bytes 11304960 | tf_op jit(solution)/shard_map/stage/pallas_call | solution.py:636
  128.8 2.0 %collective-permute-start.42 = (f32[3,16,256]{2,1,0:T(8,128)S(1)}, f32[3,16,256]{2,1,0:T(8,128)S(1)}, u32[]{:S(2)}, u32[]{:S(2)}) collective-permute-start(f32[3,16,256]{2,1,0:T(8,128)S(1)} %get-tuple-element.143), channel_id=1, source_target_pairs={{0,3},{1,0},{2,1},{3,2},{4,7},{5,4},{6,5},{7,6},{8,11},{9,8},{10,9... | collective-permute-start | bytes 147464 | tf_op jit(solution)/shard_map/ppermute | solution.py:36
  130.8 2.1 %collective-permute-done.41.y_b = f32[3,16,256]{2,1,0:T(8,128)S(1)} collective-permute-done((f32[3,16,256]{2,1,0:T(8,128)S(1)}, f32[3,16,256]{2,1,0:T(8,128)S(1)}, u32[]{:S(2)}, u32[]{:S(2)}) %collective-permute-start.41) | collective-permute-done | bytes 49184 | tf_op jit(solution)/shard_map/ppermute | solution.py:35
  134.8 2.9 %last_stage.1 = f32[3,16,32,256]{3,2,1,0:T(8,128)} custom-call(f32[3,16,32,256]{3,2,1,0:T(8,128)S(1)} %copy-done, f32[9,16,32,256]{3,2,1,0:T(8,128)S(1)} %get-tuple-element.80.grads, f32[3,16,32,256]{3,2,1,0:T(8,128)S(1)} %get-tuple-element.140.y, f32[3,2,32,256]{3,2,1,0:T(8,128)S(1)} %collective-permute-done.40.y_x, ...), custom_call_target="tpu_custom_call" | custom-call | flops 40000000 | bytes 9732096 | tf_op jit(solution)/shard_map/last_stage/pallas_call | solution.py:636
  (87 shorter events, 57.5 us)
Async XLA Ops:
  4.1 12.6 %collective-permute-start = (f32[7,2,32,256]{3,2,1,0:T(8,128)}, f32[7,2,32,256]{3,2,1,0:T(8,128)}, u32[]{:S(2)}, u32[]{:S(2)}) collective-permute-start(f32[7,2,32,256]{3,2,1,0:T(8,128)} %get-tuple-element.75), channel_id=1, source_target_pairs={{0,4},{4,0},{1,5},{5,1},{2,6},{6,2},{3,7},{7,3},{8,12},{12,8},{9,1... | collective-permute-start | bytes 1376264 | tf_op jit(solution)/shard_map/ppermute | solution.py:34
  5.6 7.5 %collective-permute-start.1 = (f32[7,16,256]{2,1,0:T(8,128)}, f32[7,16,256]{2,1,0:T(8,128)S(1)}, u32[]{:S(2)}, u32[]{:S(2)}) collective-permute-start(f32[7,16,256]{2,1,0:T(8,128)} %get-tuple-element.76), channel_id=1, source_target_pairs={{0,1},{1,2},{2,3},{3,0},{4,5},{5,6},{6,7},{7,4},{8,9},{9,10},{10,1... | collective-permute-start | bytes 344072 | tf_op jit(solution)/shard_map/ppermute | solution.py:35
  5.8 7.2 %collective-permute-start.2 = (f32[7,16,256]{2,1,0:T(8,128)}, f32[7,16,256]{2,1,0:T(8,128)S(1)}, u32[]{:S(2)}, u32[]{:S(2)}) collective-permute-start(f32[7,16,256]{2,1,0:T(8,128)} %get-tuple-element.77), channel_id=1, source_target_pairs={{0,3},{1,0},{2,1},{3,2},{4,7},{5,4},{6,5},{7,6},{8,11},{9,8},{10,9... | collective-permute-start | bytes 344072 | tf_op jit(solution)/shard_map/ppermute | solution.py:36
  25.4 13.6 %collective-permute-start.7 = (f32[3,8,16,128]{3,2,1,0:T(8,128)S(1)}, f32[3,8,16,128]{3,2,1,0:T(8,128)S(1)}, u32[]{:S(2)}, u32[]{:S(2)}) collective-permute-start(f32[3,8,16,128]{3,2,1,0:T(8,128)S(1)} %get-tuple-element.91), channel_id=1, source_target_pairs={{8,16},{9,17},{10,18},{11,19},{12,20},{13,21},{14,22},{15,23}} | collective-permute-start | bytes 589832 | tf_op jit(solution)/shard_map/ppermute | solution.py:49
  26.7 12.3 %collective-permute-start.10 = (f32[3,2,16,128]{3,2,1,0:T(8,128)S(1)}, f32[3,2,16,128]{3,2,1,0:T(8,128)S(1)}, u32[]{:S(2)}, u32[]{:S(2)}) collective-permute-start(f32[3,2,16,128]{3,2,1,0:T(8,128)S(1)} %get-tuple-element.94), channel_id=1, source_target_pairs={{8,20},{9,21},{10,22},{11,23},{12,16},{13,17},{14,18},{15,19}} | collective-permute-start | bytes 147464 | tf_op jit(solution)/shard_map/ppermute | solution.py:49
  28.0 9.3 %collective-permute-start.8 = (f32[3,8,128]{2,1,0:T(8,128)S(1)}, f32[3,8,128]{2,1,0:T(8,128)S(1)}, u32[]{:S(2)}, u32[]{:S(2)}) collective-permute-start(f32[3,8,128]{2,1,0:T(8,128)S(1)} %get-tuple-element.92), channel_id=1, source_target_pairs={{8,17},{9,18},{10,19},{11,16},{12,21},{13,22},{14,23},{15,20}} | collective-permute-start | bytes 36872 | tf_op jit(solution)/shard_map/ppermute | solution.py:49
  29.3 9.7 %collective-permute-start.9 = (f32[3,8,128]{2,1,0:T(8,128)S(1)}, f32[3,8,128]{2,1,0:T(8,128)S(1)}, u32[]{:S(2)}, u32[]{:S(2)}) collective-permute-start(f32[3,8,128]{2,1,0:T(8,128)S(1)} %get-tuple-element.93), channel_id=1, source_target_pairs={{8,19},{9,16},{10,17},{11,18},{12,23},{13,20},{14,21},{15,22}} | collective-permute-start | bytes 36872 | tf_op jit(solution)/shard_map/ppermute | solution.py:49
  39.9 6.6 %collective-permute-start.11 = (f32[3,8,16,128]{3,2,1,0:T(8,128)S(1)}, f32[3,8,16,128]{3,2,1,0:T(8,128)S(1)}, u32[]{:S(2)}, u32[]{:S(2)}) collective-permute-start(f32[3,8,16,128]{3,2,1,0:T(8,128)S(1)} %get-tuple-element.95), channel_id=1, source_target_pairs={{16,24},{17,25},{18,26},{19,27},{20,28},{21,29},{22,30},{23,31}} | collective-permute-start | bytes 589832 | tf_op jit(solution)/shard_map/ppermute | solution.py:49
  47.5 9.9 %collective-permute-start.15 = (f32[4,2,32,256]{3,2,1,0:T(8,128)S(1)}, f32[4,2,32,256]{3,2,1,0:T(8,128)S(1)}, u32[]{:S(2)}, u32[]{:S(2)}) collective-permute-start(f32[4,2,32,256]{3,2,1,0:T(8,128)S(1)} %get-tuple-element.99), channel_id=1, source_target_pairs={{0,4},{4,0},{1,5},{5,1},{2,6},{6,2},{3,7},{7,3},{8,12},{12,8},{9,1... | collective-permute-start | bytes 786440 | tf_op jit(solution)/shard_map/ppermute | solution.py:34
  51.4 6.1 %collective-permute-start.17 = (f32[4,16,256]{2,1,0:T(8,128)S(1)}, f32[4,16,256]{2,1,0:T(8,128)S(1)}, u32[]{:S(2)}, u32[]{:S(2)}) collective-permute-start(f32[4,16,256]{2,1,0:T(8,128)S(1)} %get-tuple-element.101), channel_id=1, source_target_pairs={{0,3},{1,0},{2,1},{3,2},{4,7},{5,4},{6,5},{7,6},{8,11},{9,8},{10,9... | collective-permute-start | bytes 196616 | tf_op jit(solution)/shard_map/ppermute | solution.py:36
  62.0 7.8 %collective-permute-start.18 = (f32[3,2,32,256]{3,2,1,0:T(8,128)S(1)}, f32[3,2,32,256]{3,2,1,0:T(8,128)S(1)}, u32[]{:S(2)}, u32[]{:S(2)}) collective-permute-start(f32[3,2,32,256]{3,2,1,0:T(8,128)S(1)} %get-tuple-element.108), channel_id=1, source_target_pairs={{0,4},{4,0},{1,5},{5,1},{2,6},{6,2},{3,7},{7,3},{8,12},{12,8},{9,1... | collective-permute-start | bytes 589832 | tf_op jit(solution)/shard_map/ppermute | solution.py:34
  63.9 5.9 %collective-permute-start.20 = (f32[3,16,256]{2,1,0:T(8,128)S(1)}, f32[3,16,256]{2,1,0:T(8,128)S(1)}, u32[]{:S(2)}, u32[]{:S(2)}) collective-permute-start(f32[3,16,256]{2,1,0:T(8,128)S(1)} %get-tuple-element.110), channel_id=1, source_target_pairs={{0,3},{1,0},{2,1},{3,2},{4,7},{5,4},{6,5},{7,6},{8,11},{9,8},{10,9... | collective-permute-start | bytes 147464 | tf_op jit(solution)/shard_map/ppermute | solution.py:36
  73.0 41.6 %collective-permute-start.36 = (f32[3,16,32,256]{3,2,1,0:T(8,128)S(1)}, f32[3,16,32,256]{3,2,1,0:T(8,128)S(1)}, u32[]{:S(2)}, u32[]{:S(2)}) collective-permute-start(f32[3,16,32,256]{3,2,1,0:T(8,128)S(1)} %get-tuple-element.115.u2.refs_19_), channel_id=1, source_target_pairs={{0,8},{1,9},{2,10},{3,11},{4,12},{5,13},{6,14},{7,15},{8,16},{9,17... | collective-permute-start | bytes 4718600 | tf_op jit(solution)/shard_map/ppermute | solution.py:49
  75.0 7.1 %collective-permute-start.21 = (f32[3,2,32,256]{3,2,1,0:T(8,128)S(1)}, f32[3,2,32,256]{3,2,1,0:T(8,128)S(1)}, u32[]{:S(2)}, u32[]{:S(2)}) collective-permute-start(f32[3,2,32,256]{3,2,1,0:T(8,128)S(1)} %get-tuple-element.116), channel_id=1, source_target_pairs={{0,4},{4,0},{1,5},{5,1},{2,6},{6,2},{3,7},{7,3},{8,12},{12,8},{9,1... | collective-permute-start | bytes 589832 | tf_op jit(solution)/shard_map/ppermute | solution.py:34
  76.2 5.9 %collective-permute-start.23 = (f32[3,16,256]{2,1,0:T(8,128)S(1)}, f32[3,16,256]{2,1,0:T(8,128)S(1)}, u32[]{:S(2)}, u32[]{:S(2)}) collective-permute-start(f32[3,16,256]{2,1,0:T(8,128)S(1)} %get-tuple-element.118), channel_id=1, source_target_pairs={{0,3},{1,0},{2,1},{3,2},{4,7},{5,4},{6,5},{7,6},{8,11},{9,8},{10,9... | collective-permute-start | bytes 147464 | tf_op jit(solution)/shard_map/ppermute | solution.py:36
  90.8 16.4 %collective-permute-start.28 = (f32[6,8,16,128]{3,2,1,0:T(8,128)S(1)}, f32[6,8,16,128]{3,2,1,0:T(8,128)S(1)}, u32[]{:S(2)}, u32[]{:S(2)}) collective-permute-start(f32[6,8,16,128]{3,2,1,0:T(8,128)S(1)} %get-tuple-element.126), channel_id=1, source_target_pairs={{8,16},{9,17},{10,18},{11,19},{12,20},{13,21},{14,22},{15,23}} | collective-permute-start | bytes 1179656 | tf_op jit(solution)/shard_map/ppermute | solution.py:49
  92.1 15.1 %collective-permute-start.31 = (f32[3,2,16,128]{3,2,1,0:T(8,128)S(1)}, f32[3,2,16,128]{3,2,1,0:T(8,128)S(1)}, u32[]{:S(2)}, u32[]{:S(2)}) collective-permute-start(f32[3,2,16,128]{3,2,1,0:T(8,128)S(1)} %get-tuple-element.129), channel_id=1, source_target_pairs={{8,20},{9,21},{10,22},{11,23},{12,16},{13,17},{14,18},{15,19}} | collective-permute-start | bytes 147464 | tf_op jit(solution)/shard_map/ppermute | solution.py:49
  93.4 9.8 %collective-permute-start.29 = (f32[3,8,128]{2,1,0:T(8,128)S(1)}, f32[3,8,128]{2,1,0:T(8,128)S(1)}, u32[]{:S(2)}, u32[]{:S(2)}) collective-permute-start(f32[3,8,128]{2,1,0:T(8,128)S(1)} %get-tuple-element.127), channel_id=1, source_target_pairs={{8,17},{9,18},{10,19},{11,16},{12,21},{13,22},{14,23},{15,20}} | collective-permute-start | bytes 36872 | tf_op jit(solution)/shard_map/ppermute | solution.py:49
  94.7 10.4 %collective-permute-start.30 = (f32[3,8,128]{2,1,0:T(8,128)S(1)}, f32[3,8,128]{2,1,0:T(8,128)S(1)}, u32[]{:S(2)}, u32[]{:S(2)}) collective-permute-start(f32[3,8,128]{2,1,0:T(8,128)S(1)} %get-tuple-element.128), channel_id=1, source_target_pairs={{8,19},{9,16},{10,17},{11,18},{12,23},{13,20},{14,21},{15,22}} | collective-permute-start | bytes 36872 | tf_op jit(solution)/shard_map/ppermute | solution.py:49
  108.1 6.6 %collective-permute-start.32 = (f32[6,8,16,128]{3,2,1,0:T(8,128)S(1)}, f32[6,8,16,128]{3,2,1,0:T(8,128)S(1)}, u32[]{:S(2)}, u32[]{:S(2)}) collective-permute-start(f32[6,8,16,128]{3,2,1,0:T(8,128)S(1)} %get-tuple-element.130), channel_id=1, source_target_pairs={{16,24},{17,25},{18,26},{19,27},{20,28},{21,29},{22,30},{23,31}} | collective-permute-start | bytes 1179656 | tf_op jit(solution)/shard_map/ppermute | solution.py:49
  117.1 7.6 %collective-permute-start.37 = (f32[3,2,32,256]{3,2,1,0:T(8,128)S(1)}, f32[3,2,32,256]{3,2,1,0:T(8,128)S(1)}, u32[]{:S(2)}, u32[]{:S(2)}) collective-permute-start(f32[3,2,32,256]{3,2,1,0:T(8,128)S(1)} %get-tuple-element.135), channel_id=1, source_target_pairs={{0,4},{4,0},{1,5},{5,1},{2,6},{6,2},{3,7},{7,3},{8,12},{12,8},{9,1... | collective-permute-start | bytes 589832 | tf_op jit(solution)/shard_map/ppermute | solution.py:34
  118.7 5.9 %collective-permute-start.39 = (f32[3,16,256]{2,1,0:T(8,128)S(1)}, f32[3,16,256]{2,1,0:T(8,128)S(1)}, u32[]{:S(2)}, u32[]{:S(2)}) collective-permute-start(f32[3,16,256]{2,1,0:T(8,128)S(1)} %get-tuple-element.137), channel_id=1, source_target_pairs={{0,3},{1,0},{2,1},{3,2},{4,7},{5,4},{6,5},{7,6},{8,11},{9,8},{10,9... | collective-permute-start | bytes 147464 | tf_op jit(solution)/shard_map/ppermute | solution.py:36
  127.6 7.2 %collective-permute-start.40 = (f32[3,2,32,256]{3,2,1,0:T(8,128)S(1)}, f32[3,2,32,256]{3,2,1,0:T(8,128)S(1)}, u32[]{:S(2)}, u32[]{:S(2)}) collective-permute-start(f32[3,2,32,256]{3,2,1,0:T(8,128)S(1)} %get-tuple-element.141), channel_id=1, source_target_pairs={{0,4},{4,0},{1,5},{5,1},{2,6},{6,2},{3,7},{7,3},{8,12},{12,8},{9,1... | collective-permute-start | bytes 589832 | tf_op jit(solution)/shard_map/ppermute | solution.py:34
  128.8 5.9 %collective-permute-start.42 = (f32[3,16,256]{2,1,0:T(8,128)S(1)}, f32[3,16,256]{2,1,0:T(8,128)S(1)}, u32[]{:S(2)}, u32[]{:S(2)}) collective-permute-start(f32[3,16,256]{2,1,0:T(8,128)S(1)} %get-tuple-element.143), channel_id=1, source_target_pairs={{0,3},{1,0},{2,1},{3,2},{4,7},{5,4},{6,5},{7,6},{8,11},{9,8},{10,9... | collective-permute-start | bytes 147464 | tf_op jit(solution)/shard_map/ppermute | solution.py:36
  (24 other events, 105.1 us)

commit v10 on v9

--- a/solution.py
+++ b/solution.py
@@ -10,7 +10,7 @@
 VISCOSITY = 0.25
 TIME_STEP = 0.5
 PAD = 8
-CHUNK = 16
+CHUNK = 8
 ROOM = 4 << 20
 F32 = jnp.float32
 BF16 = jnp.bfloat16
@@ -37,16 +37,22 @@
     return before_after, behind, ahead
 
 
-def pass_on(slabs, array, dx=0, dy=0):
+def pass_on(slabs, array, dx=0, dy=0, dt=1):
     gx, gy = lax.axis_size("gx"), lax.axis_size("gy")
     pairs = []
     for t in slabs:
         for x in range(gx):
             for y in range(gy):
                 source = (t * gx + x) * gy + y
-                target = ((t + 1) * gx + (x + dx) % gx) * gy + (y + dy) % gy
+                target = ((t + dt) * gx + (x + dx) % gx) * gy + (y + dy) % gy
                 pairs.append((source, target))
     return lax.ppermute(array, ("tm", "gx", "gy"), pairs)
+
+
+def swap_within(slabs, faces):
+    x_faces, y_last, y_first = faces
+    before_after = both_faces(x_faces, lambda a, by: pass_on(slabs, a, by, 0, 0), lax.axis_size("gx"))
+    return before_after, pass_on(slabs, y_last, 0, 1, 0), pass_on(slabs, y_first, 0, -1, 0)
 
 
 def hand_on(slabs, value, faces):
@@ -389,6 +395,25 @@
         sent[3 + c] = value
 
     squeeze(summed_two, rows, store_following, 3)
+
+
+def offset_early_kernel(count, first, *refs):
+    @pl.when(first[1] < float(count))
+    def _():
+        offset_later_kernel(first, *refs)
+
+
+def offset_late_kernel(count, first, *refs):
+    args, early, outs, scratch = refs[:16], refs[16:22], refs[22:28], refs[28:]
+
+    @pl.when(first[1] >= float(count))
+    def _():
+        offset_later_kernel(first, *args, *outs, *scratch)
+
+    @pl.when(first[1] < float(count))
+    def _():
+        for out, made in zip(outs, early):
+            out[...] = made[...]
 
 
 def chain_step(base, speed, coarse_grads, d0, ext, store):
@@ -711,14 +736,20 @@
         [fine] + fine_faces + [coarse], [ext, summed, rows], 40_000_000,
     )
     faces, end_two = results[:3], results[3]
-    u0 = pass_on(range(slabs - 1), value)
-    u2 = [value, *swap_faces(faces)]
-
+    half = (slabs + 1) // 2
+    shared = [velocity, grads, start_field, *start_layers, *u1]
+    outs = [coarse, coarse, (6, cx, cy, cz)] + coarse_faces
+    scratch = [ext, ext, summed, summed, rows]
+    early = call(
+        lambda *refs: offset_early_kernel(half, *refs), "offset_early", first,
+        [*shared, value, *swap_within(range(half), faces), zero, end_two], outs, scratch, 60_000_000,
+    )
+    tied, moving, *faces = lax.optimization_barrier([early[0], value, *faces])
+    early = [tied, *early[1:]]
+    u0 = pass_on(range(slabs - 1), moving)
     own_part, following, *sent = call(
-        offset_later_kernel, "offset_later", first,
-        [velocity, grads, start_field, *start_layers, *u1, *u2, zero, end_two],
-        [coarse, coarse, (6, cx, cy, cz)] + coarse_faces,
-        [ext, ext, summed, summed, rows], 60_000_000,
+        lambda *refs: offset_late_kernel(half, *refs), "offset_late", first,
+        [*shared, value, *swap_within(range(half, slabs), faces), zero, end_two, *early], outs, scratch, 60_000_000,
     )
     arrivals = chain(pass_later_kernel, sent, (6, cx, cy, cz), [], [own_part, following])
     stage, *faces, begin, rest = call(

time: 139 us -> 142 us (1.022)
  starting transfers between devices: 47.6 us -> 55.2 us
  waiting for transfers between devices: 52.6 us -> 47.8 us
    ppermute x25 -> x31, starting transfers between devices: 28.1 us -> 38.9 us  [pass_on(): return lax.ppermute(array, ('tm', 'gx', 'gy'), pairs)]
    ppermute x6 -> x5, waiting for transfers between devices: 13.3 us -> 11 us  [swap_faces(): ahead = lax.ppermute(y_first, 'gy', ring(gy, -1))]
    ppermute x6 -> x5, waiting for transfers between devices: 13 us -> 11.2 us  [swap_faces(): behind = lax.ppermute(y_last, 'gy', ring(gy, 1))]
    ppermute x6 -> x5, starting transfers between devices: 7.92 us -> 6.38 us  [swap_faces(): ahead = lax.ppermute(y_first, 'gy', ring(gy, -1))]
    ppermute x6 -> x5, starting transfers between devices: 6.52 us -> 5.24 us  [swap_faces(): lax.ppermute(a, 'gx', ring(gx, by))]
    ppermute x25 -> x31, waiting for transfers between devices: 22.4 us -> 21.6 us  [pass_on(): return lax.ppermute(array, ('tm', 'gx', 'gy'), pairs)]
    pallas_call x14 -> x15, Pallas kernels: 36.2 us -> 37 us  [call(): pl.pallas_call(kernel, name=name, out_shape=[jax.ShapeDtypeStruct(dims, F...]
    ppermute x6 -> x5, starting transfers between devices: 5.09 us -> 4.6 us  [swap_faces(): behind = lax.ppermute(y_last, 'gy', ring(gy, 1))]
  transfers between devices with their start and end apart: 43 -> 46, of which waited for: 23 -> 21; matrix products, arithmetic and copies ran while one was open for 0% -> 0% of each run, Pallas kernels for 6% -> 6%
where the time goes in v10:
time: 142 us; the launch traced here: 141 us
  starting transfers between devices  55.2 us (39%)
  waiting for transfers between devices  47.8 us (34%)
  Pallas kernels  37 us (26%)
    ppermute x31, starting transfers between devices, pass_on(): return lax.ppermute(array, ('tm', 'gx', 'gy'), pairs)  38.9 us
    pallas_call x15, Pallas kernels, call(): pl.pallas_call(kernel, name=name, out_shape=[jax.ShapeDtypeStruct(dims, F...  37 us
    ppermute x31, waiting for transfers between devices, pass_on(): return lax.ppermute(array, ('tm', 'gx', 'gy'), pairs)  21.6 us
    ppermute x5, waiting for transfers between devices, swap_faces(): behind = lax.ppermute(y_last, 'gy', ring(gy, 1))  11.2 us
    ppermute x5, waiting for transfers between devices, swap_faces(): ahead = lax.ppermute(y_first, 'gy', ring(gy, -1))  11 us
    ppermute x5, starting transfers between devices, swap_faces(): ahead = lax.ppermute(y_first, 'gy', ring(gy, -1))  6.38 us
    ppermute x5, starting transfers between devices, swap_faces(): lax.ppermute(a, 'gx', ring(gx, by))  5.24 us
    ppermute x5, starting transfers between devices, swap_faces(): behind = lax.ppermute(y_last, 'gy', ring(gy, 1))  4.6 us
  transfers between devices with their start and end apart: 46, of which 21 were waited for; matrix products, arithmetic and copies ran while one was open for 0% of the time, Pallas kernels for 6%

profile of v10, /device:TPU:26, one launch (start us, length us, event | category | flops | bytes accessed | tf_op | source)
XLA Modules:
  0.0 141.4 jit_solution(14322179434837417361)
XLA Ops:
  0.0 4.1 %pack.1 = (f32[3,8,16,128]{3,2,1,0:T(8,128)}, f32[7,2,32,256]{3,2,1,0:T(8,128)}, f32[7,16,256]{2,1,0:T(8,128)}, f32[7,16,256]{2,1,0:T(8,128)}) custom-call(f32[3,16,32,256]{3,2,1,0:T(8,128)} %v.13, f32[3,16,32,256]{3,2,1,0:T(8,128)} %refs_16_.1, f32[3,16,32,256]{3,2,1,0:T(8,128)} %bitcast.4), custom_call_target="tpu_custom_call" | custom-call | flops 5000000 | bytes 4718592 | tf_op jit(solution)/shard_map/pack/pallas_call | solution.py:661
  10.3 2.8 %collective-permute-done.1.behind.w_b = f32[7,16,256]{2,1,0:T(8,128)S(1)} collective-permute-done((f32[7,16,256]{2,1,0:T(8,128)}, f32[7,16,256]{2,1,0:T(8,128)S(1)}, u32[]{:S(2)}, u32[]{:S(2)}) %collective-permute-start.1) | collective-permute-done | bytes 114720 | tf_op jit(solution)/shard_map/ppermute | solution.py:35
  13.1 3.6 %collective-permute-done.x_faces.w_x = f32[7,2,32,256]{3,2,1,0:T(8,128)} collective-permute-done((f32[7,2,32,256]{3,2,1,0:T(8,128)}, f32[7,2,32,256]{3,2,1,0:T(8,128)}, u32[]{:S(2)}, u32[]{:S(2)}) %collective-permute-start) | collective-permute-done | bytes 458784 | tf_op jit(solution)/shard_map/ppermute | solution.py:34
  16.7 5.4 %offset_start.1 = (f32[9,16,32,256]{3,2,1,0:T(8,128)S(1)}, f32[3,8,16,128]{3,2,1,0:T(8,128)S(1)}, f32[9,8,16,128]{3,2,1,0:T(8,128)S(1)}, f32[3,2,16,128]{3,2,1,0...) custom-call(f32[2]{0:T(128)S(1)} %add_convert_fusion.first.refs_0_, ...), custom_call_target="tpu_custom_call" | custom-call | flops 40000000 | bytes 5603328 | tf_op jit(solution)/shard_map/offset_start/pallas_call | solution.py:661
  30.7 6.7 %collective-permute-done.8.refs_2_.refs_6_ = f32[3,8,128]{2,1,0:T(8,128)S(1)} collective-permute-done((f32[3,8,128]{2,1,0:T(8,128)S(1)}, f32[3,8,128]{2,1,0:T(8,128)S(1)}, u32[]{:S(2)}, u32[]{:S(2)}) %collective-permute-start.8) | collective-permute-done | bytes 12320 | tf_op jit(solution)/shard_map/ppermute | solution.py:49
  48.6 2.9 %collective-permute-start.16 = (f32[4,16,256]{2,1,0:T(8,128)S(1)}, f32[4,16,256]{2,1,0:T(8,128)S(1)}, u32[]{:S(2)}, u32[]{:S(2)}) collective-permute-start(f32[4,16,256]{2,1,0:T(8,128)S(1)} %get-tuple-element.111), channel_id=1, source_target_pairs={{0,1},{1,2},{2,3},{3,0},{4,5},{5,6},{6,7},{7,4},{8,9},{9,10},{10,1... | collective-permute-start | bytes 196616 | tf_op jit(solution)/shard_map/ppermute | solution.py:35
  53.4 4.1 %collective-permute-done.17.m_a.refs_6_ = f32[4,16,256]{2,1,0:T(8,128)S(1)} collective-permute-done((f32[4,16,256]{2,1,0:T(8,128)S(1)}, f32[4,16,256]{2,1,0:T(8,128)S(1)}, u32[]{:S(2)}, u32[]{:S(2)}) %collective-permute-start.17) | collective-permute-done | bytes 65568 | tf_op jit(solution)/shard_map/ppermute | solution.py:36
  57.5 4.6 %middle.1 = (f32[3,16,32,256]{3,2,1,0:T(8,128)S(1)}, f32[3,2,32,256]{3,2,1,0:T(8,128)S(1)}, f32[3,16,256]{2,1,0:T(8,128)S(1)}, f32[3,16,256]{2,1,0:T(8,128)S(1)}...) custom-call(f32[2]{0:T(128)S(1)} %add_convert_fusion.first.refs_0_, ...), custom_call_target="tpu_custom_call" | custom-call | flops 60000000 | bytes 10985472 | tf_op jit(solution)/shard_map/middle/pallas_call | solution.py:661
  64.7 2.1 %collective-permute-done.19.a1_b.refs_9_ = f32[3,16,256]{2,1,0:T(8,128)S(1)} collective-permute-done((f32[3,16,256]{2,1,0:T(8,128)S(1)}, f32[3,16,256]{2,1,0:T(8,128)S(1)}, u32[]{:S(2)}, u32[]{:S(2)}) %collective-permute-start.19) | collective-permute-done | bytes 49184 | tf_op jit(solution)/shard_map/ppermute | solution.py:35
  66.8 3.2 %collective-permute-done.20.a1_a.refs_10_ = f32[3,16,256]{2,1,0:T(8,128)S(1)} collective-permute-done((f32[3,16,256]{2,1,0:T(8,128)S(1)}, f32[3,16,256]{2,1,0:T(8,128)S(1)}, u32[]{:S(2)}, u32[]{:S(2)}) %collective-permute-start.20) | collective-permute-done | bytes 49184 | tf_op jit(solution)/shard_map/ppermute | solution.py:36
  69.9 3.2 %finish.1 = (f32[3,16,32,256]{3,2,1,0:T(8,128)S(1)}, f32[3,2,32,256]{3,2,1,0:T(8,128)S(1)}, f32[3,16,256]{2,1,0:T(8,128)S(1)}, f32[3,16,256]{2,1,0:T(8,128)S(1)}, f32[3,8,16,128]{3,2,1,0:T(8,128)S(1)}) custom-call(f32[2]{0:T(128)S(1)} %add_convert_fusion.first.refs_0_, f32[3,16,32,256]{3,2,1,0:T(8,128)S(1)} %copy-done, ...), custom_call_target="tpu_custom_call" | custom-call | flops 40000000 | bytes 10027008 | tf_op jit(solution)/shard_map/finish/pallas_call | solution.py:661
  77.7 3.0 %collective-permute-start.24 = (f32[3,2,32,256]{3,2,1,0:T(8,128)S(1)}, f32[3,2,32,256]{3,2,1,0:T(8,128)S(1)}, u32[]{:S(2)}, u32[]{:S(2)}) collective-permute-start(f32[3,2,32,256]{3,2,1,0:T(8,128)S(1)} %get-tuple-element.132), channel_id=1, source_target_pairs={{16,20},{17,21},{18,22},{19,23},{20,16},{21,17},{22,18},{23,19},{2... | collective-permute-start | bytes 589832 | tf_op jit(solution)/shard_map/ppermute | solution.py:49
  80.7 2.0 %collective-permute-start.25 = (f32[3,16,256]{2,1,0:T(8,128)S(1)}, f32[3,16,256]{2,1,0:T(8,128)S(1)}, u32[]{:S(2)}, u32[]{:S(2)}) collective-permute-start(f32[3,16,256]{2,1,0:T(8,128)S(1)} %get-tuple-element.133), channel_id=1, source_target_pairs={{16,17},{17,18},{18,19},{19,16},{20,21},{21,22},{22,23},{23,20},{2... | collective-permute-start | bytes 147464 | tf_op jit(solution)/shard_map/ppermute | solution.py:49
  82.7 3.9 %collective-permute-start.26 = (f32[3,16,256]{2,1,0:T(8,128)S(1)}, f32[3,16,256]{2,1,0:T(8,128)S(1)}, u32[]{:S(2)}, u32[]{:S(2)}) collective-permute-start(f32[3,16,256]{2,1,0:T(8,128)S(1)} %get-tuple-element.134), channel_id=1, source_target_pairs={{16,19},{17,16},{18,17},{19,18},{20,23},{21,20},{22,21},{23,22},{2... | collective-permute-start | bytes 147464 | tf_op jit(solution)/shard_map/ppermute | solution.py:49
  87.2 3.2 %collective-permute-done.26.refs_14_ = f32[3,16,256]{2,1,0:T(8,128)S(1)} collective-permute-done((f32[3,16,256]{2,1,0:T(8,128)S(1)}, f32[3,16,256]{2,1,0:T(8,128)S(1)}, u32[]{:S(2)}, u32[]{:S(2)}) %collective-permute-start.26) | collective-permute-done | bytes 49184 | tf_op jit(solution)/shard_map/ppermute | solution.py:49
  90.5 5.5 %offset_late.1 = (f32[3,8,16,128]{3,2,1,0:T(8,128)S(1)}, f32[3,8,16,128]{3,2,1,0:T(8,128)S(1)}, f32[6,8,16,128]{3,2,1,0:T(8,128)S(1)}, f32[3,2,16,128]{3,2,1,0:T...) custom-call(f32[2]{0:T(128)S(1)} %add_convert_fusion.first.refs_0_, f32[3,16,32,256]{3,2,1,0:T(8,128)S(1)} %copy-done, ...), custom_call_target="tpu_custom_call" | custom-call | flops 60000000 | bytes 13246464 | tf_op jit(solution)/shard_map/offset_late/pallas_call | solution.py:661
  104.5 3.4 %collective-permute-done.32.refs_2_.refs_6_ = f32[3,8,128]{2,1,0:T(8,128)S(1)} collective-permute-done((f32[3,8,128]{2,1,0:T(8,128)S(1)}, f32[3,8,128]{2,1,0:T(8,128)S(1)}, u32[]{:S(2)}, u32[]{:S(2)}) %collective-permute-start.32) | collective-permute-done | bytes 12320 | tf_op jit(solution)/shard_map/ppermute | solution.py:49
  107.9 3.0 %collective-permute-done.33.refs_3_.refs_7_ = f32[3,8,128]{2,1,0:T(8,128)S(1)} collective-permute-done((f32[3,8,128]{2,1,0:T(8,128)S(1)}, f32[3,8,128]{2,1,0:T(8,128)S(1)}, u32[]{:S(2)}, u32[]{:S(2)}) %collective-permute-start.33) | collective-permute-done | bytes 12320 | tf_op jit(solution)/shard_map/ppermute | solution.py:49
  118.4 2.4 %settle.3 = (f32[3,16,32,256]{3,2,1,0:T(8,128)S(1)}, f32[3,2,32,256]{3,2,1,0:T(8,128)S(1)}, f32[3,16,256]{2,1,0:T(8,128)S(1)}, f32[3,16,256]{2,1,0:T(8,128)S(1)}...) custom-call(f32[2]{0:T(128)S(1)} %add_convert_fusion.first.refs_0_, ...), custom_call_target="tpu_custom_call" | custom-call | flops 10000000 | bytes 8675328 | tf_op jit(solution)/shard_map/settle/pallas_call | solution.py:661
  121.8 2.0 %collective-permute-start.42 = (f32[3,16,256]{2,1,0:T(8,128)S(1)}, f32[3,16,256]{2,1,0:T(8,128)S(1)}, u32[]{:S(2)}, u32[]{:S(2)}) collective-permute-start(f32[3,16,256]{2,1,0:T(8,128)S(1)} %get-tuple-element.159), channel_id=1, source_target_pairs={{0,3},{1,0},{2,1},{3,2},{4,7},{5,4},{6,5},{7,6},{8,11},{9,8},{10,9... | collective-permute-start | bytes 147464 | tf_op jit(solution)/shard_map/ppermute | solution.py:36
  123.8 2.1 %collective-permute-done.41.y_b = f32[3,16,256]{2,1,0:T(8,128)S(1)} collective-permute-done((f32[3,16,256]{2,1,0:T(8,128)S(1)}, f32[3,16,256]{2,1,0:T(8,128)S(1)}, u32[]{:S(2)}, u32[]{:S(2)}) %collective-permute-start.41) | collective-permute-done | bytes 49184 | tf_op jit(solution)/shard_map/ppermute | solution.py:35
  127.7 3.0 %stage.1 = (f32[3,16,32,256]{3,2,1,0:T(8,128)S(1)}, f32[3,16,32,256]{3,2,1,0:T(8,128)S(1)}, f32[3,2,32,256]{3,2,1,0:T(8,128)S(1)}, f32[3,16,256]{2,1,0:T(8,128)S(1)}, f32[3,16,256]{2,1,0:T(8,128)S(1)}) custom-call(f32[2]{0:T(128)S(1)} %add_convert_fusion.first.refs_0_, f32[3,16,32,256]{3,2,1,0:T(8,128)S(1)} %copy-done, ...), custom_call_target="tpu_custom_call" | custom-call | flops 40000000 | bytes 11304960 | tf_op jit(solution)/shard_map/stage/pallas_call | solution.py:661
  133.9 2.2 %collective-permute-done.44.y_b = f32[3,16,256]{2,1,0:T(8,128)S(1)} collective-permute-done((f32[3,16,256]{2,1,0:T(8,128)S(1)}, f32[3,16,256]{2,1,0:T(8,128)S(1)}, u32[]{:S(2)}, u32[]{:S(2)}) %collective-permute-start.44) | collective-permute-done | bytes 49184 | tf_op jit(solution)/shard_map/ppermute | solution.py:35
  138.5 2.9 %last_stage.1 = f32[3,16,32,256]{3,2,1,0:T(8,128)} custom-call(f32[3,16,32,256]{3,2,1,0:T(8,128)S(1)} %copy-done, f32[9,16,32,256]{3,2,1,0:T(8,128)S(1)} %get-tuple-element.91.grads.refs_2_, f32[3,16,32,256]{3,2,1,0:T(8,128)S(1)} %get-tuple-element.162.y, f32[3,2,32,256]{3,2,1,0:T(8,128)S(1)} %collective-permute-done.43.y_x, ...), custom_call_target="tpu_custom_call" | custom-call | flops 40000000 | bytes 9732096 | tf_op jit(solution)/shard_map/last_stage/pallas_call | solution.py:661
  (94 shorter events, 59.7 us)
Async XLA Ops:
  4.1 12.6 %collective-permute-start = (f32[7,2,32,256]{3,2,1,0:T(8,128)}, f32[7,2,32,256]{3,2,1,0:T(8,128)}, u32[]{:S(2)}, u32[]{:S(2)}) collective-permute-start(f32[7,2,32,256]{3,2,1,0:T(8,128)} %get-tuple-element.86), channel_id=1, source_target_pairs={{0,4},{4,0},{1,5},{5,1},{2,6},{6,2},{3,7},{7,3},{8,12},{12,8},{9,1... | collective-permute-start | bytes 1376264 | tf_op jit(solution)/shard_map/ppermute | solution.py:34
  5.6 7.5 %collective-permute-start.1 = (f32[7,16,256]{2,1,0:T(8,128)}, f32[7,16,256]{2,1,0:T(8,128)S(1)}, u32[]{:S(2)}, u32[]{:S(2)}) collective-permute-start(f32[7,16,256]{2,1,0:T(8,128)} %get-tuple-element.87), channel_id=1, source_target_pairs={{0,1},{1,2},{2,3},{3,0},{4,5},{5,6},{6,7},{7,4},{8,9},{9,10},{10,1... | collective-permute-start | bytes 344072 | tf_op jit(solution)/shard_map/ppermute | solution.py:35
  5.9 7.2 %collective-permute-start.2 = (f32[7,16,256]{2,1,0:T(8,128)}, f32[7,16,256]{2,1,0:T(8,128)S(1)}, u32[]{:S(2)}, u32[]{:S(2)}) collective-permute-start(f32[7,16,256]{2,1,0:T(8,128)} %get-tuple-element.88), channel_id=1, source_target_pairs={{0,3},{1,0},{2,1},{3,2},{4,7},{5,4},{6,5},{7,6},{8,11},{9,8},{10,9... | collective-permute-start | bytes 344072 | tf_op jit(solution)/shard_map/ppermute | solution.py:36
  25.5 13.6 %collective-permute-start.7 = (f32[3,8,16,128]{3,2,1,0:T(8,128)S(1)}, f32[3,8,16,128]{3,2,1,0:T(8,128)S(1)}, u32[]{:S(2)}, u32[]{:S(2)}) collective-permute-start(f32[3,8,16,128]{3,2,1,0:T(8,128)S(1)} %get-tuple-element.102), channel_id=1, source_target_pairs={{8,16},{9,17},{10,18},{11,19},{12,20},{13,21},{14,22},{15,23}} | collective-permute-start | bytes 589832 | tf_op jit(solution)/shard_map/ppermute | solution.py:49
  26.8 12.3 %collective-permute-start.10 = (f32[3,2,16,128]{3,2,1,0:T(8,128)S(1)}, f32[3,2,16,128]{3,2,1,0:T(8,128)S(1)}, u32[]{:S(2)}, u32[]{:S(2)}) collective-permute-start(f32[3,2,16,128]{3,2,1,0:T(8,128)S(1)} %get-tuple-element.105), channel_id=1, source_target_pairs={{8,20},{9,21},{10,22},{11,23},{12,16},{13,17},{14,18},{15,19}} | collective-permute-start | bytes 147464 | tf_op jit(solution)/shard_map/ppermute | solution.py:49
  28.1 9.3 %collective-permute-start.8 = (f32[3,8,128]{2,1,0:T(8,128)S(1)}, f32[3,8,128]{2,1,0:T(8,128)S(1)}, u32[]{:S(2)}, u32[]{:S(2)}) collective-permute-start(f32[3,8,128]{2,1,0:T(8,128)S(1)} %get-tuple-element.103), channel_id=1, source_target_pairs={{8,17},{9,18},{10,19},{11,16},{12,21},{13,22},{14,23},{15,20}} | collective-permute-start | bytes 36872 | tf_op jit(solution)/shard_map/ppermute | solution.py:49
  29.4 9.7 %collective-permute-start.9 = (f32[3,8,128]{2,1,0:T(8,128)S(1)}, f32[3,8,128]{2,1,0:T(8,128)S(1)}, u32[]{:S(2)}, u32[]{:S(2)}) collective-permute-start(f32[3,8,128]{2,1,0:T(8,128)S(1)} %get-tuple-element.104), channel_id=1, source_target_pairs={{8,19},{9,16},{10,17},{11,18},{12,23},{13,20},{14,21},{15,22}} | collective-permute-start | bytes 36872 | tf_op jit(solution)/shard_map/ppermute | solution.py:49
  40.0 6.6 %collective-permute-start.11 = (f32[3,8,16,128]{3,2,1,0:T(8,128)S(1)}, f32[3,8,16,128]{3,2,1,0:T(8,128)S(1)}, u32[]{:S(2)}, u32[]{:S(2)}) collective-permute-start(f32[3,8,16,128]{3,2,1,0:T(8,128)S(1)} %get-tuple-element.106), channel_id=1, source_target_pairs={{16,24},{17,25},{18,26},{19,27},{20,28},{21,29},{22,30},{23,31}} | collective-permute-start | bytes 589832 | tf_op jit(solution)/shard_map/ppermute | solution.py:49
  47.6 9.9 %collective-permute-start.15 = (f32[4,2,32,256]{3,2,1,0:T(8,128)S(1)}, f32[4,2,32,256]{3,2,1,0:T(8,128)S(1)}, u32[]{:S(2)}, u32[]{:S(2)}) collective-permute-start(f32[4,2,32,256]{3,2,1,0:T(8,128)S(1)} %get-tuple-element.110), channel_id=1, source_target_pairs={{0,4},{4,0},{1,5},{5,1},{2,6},{6,2},{3,7},{7,3},{8,12},{12,8},{9,1... | collective-permute-start | bytes 786440 | tf_op jit(solution)/shard_map/ppermute | solution.py:34
  51.5 6.1 %collective-permute-start.17 = (f32[4,16,256]{2,1,0:T(8,128)S(1)}, f32[4,16,256]{2,1,0:T(8,128)S(1)}, u32[]{:S(2)}, u32[]{:S(2)}) collective-permute-start(f32[4,16,256]{2,1,0:T(8,128)S(1)} %get-tuple-element.112), channel_id=1, source_target_pairs={{0,3},{1,0},{2,1},{3,2},{4,7},{5,4},{6,5},{7,6},{8,11},{9,8},{10,9... | collective-permute-start | bytes 196616 | tf_op jit(solution)/shard_map/ppermute | solution.py:36
  62.1 7.8 %collective-permute-start.18 = (f32[3,2,32,256]{3,2,1,0:T(8,128)S(1)}, f32[3,2,32,256]{3,2,1,0:T(8,128)S(1)}, u32[]{:S(2)}, u32[]{:S(2)}) collective-permute-start(f32[3,2,32,256]{3,2,1,0:T(8,128)S(1)} %get-tuple-element.119), channel_id=1, source_target_pairs={{0,4},{4,0},{1,5},{5,1},{2,6},{6,2},{3,7},{7,3},{8,12},{12,8},{9,1... | collective-permute-start | bytes 589832 | tf_op jit(solution)/shard_map/ppermute | solution.py:34
  64.1 5.9 %collective-permute-start.20 = (f32[3,16,256]{2,1,0:T(8,128)S(1)}, f32[3,16,256]{2,1,0:T(8,128)S(1)}, u32[]{:S(2)}, u32[]{:S(2)}) collective-permute-start(f32[3,16,256]{2,1,0:T(8,128)S(1)} %get-tuple-element.121), channel_id=1, source_target_pairs={{0,3},{1,0},{2,1},{3,2},{4,7},{5,4},{6,5},{7,6},{8,11},{9,8},{10,9... | collective-permute-start | bytes 147464 | tf_op jit(solution)/shard_map/ppermute | solution.py:36
  75.8 42.6 %collective-permute-start.39 = (f32[3,16,32,256]{3,2,1,0:T(8,128)S(1)}, f32[3,16,32,256]{3,2,1,0:T(8,128)S(1)}, u32[]{:S(2)}, u32[]{:S(2)}) collective-permute-start(f32[3,16,32,256]{3,2,1,0:T(8,128)S(1)} %get-tuple-element.155.refs_11_.refs_19_), channel_id=1, source_target_pairs={{0,8},{1,9},{2,10},{3,11},{4,12},{5,13},{6,14},{7,15},{8,16},{9,17... | collective-permute-start | bytes 4718600 | tf_op jit(solution)/shard_map/ppermute | solution.py:49
  77.7 12.8 %collective-permute-start.24 = (f32[3,2,32,256]{3,2,1,0:T(8,128)S(1)}, f32[3,2,32,256]{3,2,1,0:T(8,128)S(1)}, u32[]{:S(2)}, u32[]{:S(2)}) collective-permute-start(f32[3,2,32,256]{3,2,1,0:T(8,128)S(1)} %get-tuple-element.132), channel_id=1, source_target_pairs={{16,20},{17,21},{18,22},{19,23},{20,16},{21,17},{22,18},{23,19},{2... | collective-permute-start | bytes 589832 | tf_op jit(solution)/shard_map/ppermute | solution.py:49
  80.7 6.5 %collective-permute-start.25 = (f32[3,16,256]{2,1,0:T(8,128)S(1)}, f32[3,16,256]{2,1,0:T(8,128)S(1)}, u32[]{:S(2)}, u32[]{:S(2)}) collective-permute-start(f32[3,16,256]{2,1,0:T(8,128)S(1)} %get-tuple-element.133), channel_id=1, source_target_pairs={{16,17},{17,18},{18,19},{19,16},{20,21},{21,22},{22,23},{23,20},{2... | collective-permute-start | bytes 147464 | tf_op jit(solution)/shard_map/ppermute | solution.py:49
  82.7 7.8 %collective-permute-start.26 = (f32[3,16,256]{2,1,0:T(8,128)S(1)}, f32[3,16,256]{2,1,0:T(8,128)S(1)}, u32[]{:S(2)}, u32[]{:S(2)}) collective-permute-start(f32[3,16,256]{2,1,0:T(8,128)S(1)} %get-tuple-element.134), channel_id=1, source_target_pairs={{16,19},{17,16},{18,17},{19,18},{20,23},{21,20},{22,21},{23,22},{2... | collective-permute-start | bytes 147464 | tf_op jit(solution)/shard_map/ppermute | solution.py:49
  99.3 11.7 %collective-permute-start.31 = (f32[6,8,16,128]{3,2,1,0:T(8,128)S(1)}, f32[6,8,16,128]{3,2,1,0:T(8,128)S(1)}, u32[]{:S(2)}, u32[]{:S(2)}) collective-permute-start(f32[6,8,16,128]{3,2,1,0:T(8,128)S(1)} %get-tuple-element.147), channel_id=1, source_target_pairs={{8,16},{9,17},{10,18},{11,19},{12,20},{13,21},{14,22},{15,23}} | collective-permute-start | bytes 1179656 | tf_op jit(solution)/shard_map/ppermute | solution.py:49
  100.6 10.4 %collective-permute-start.34 = (f32[3,2,16,128]{3,2,1,0:T(8,128)S(1)}, f32[3,2,16,128]{3,2,1,0:T(8,128)S(1)}, u32[]{:S(2)}, u32[]{:S(2)}) collective-permute-start(f32[3,2,16,128]{3,2,1,0:T(8,128)S(1)} %get-tuple-element.150), channel_id=1, source_target_pairs={{8,20},{9,21},{10,22},{11,23},{12,16},{13,17},{14,18},{15,19}} | collective-permute-start | bytes 147464 | tf_op jit(solution)/shard_map/ppermute | solution.py:49
  101.9 6.0 %collective-permute-start.32 = (f32[3,8,128]{2,1,0:T(8,128)S(1)}, f32[3,8,128]{2,1,0:T(8,128)S(1)}, u32[]{:S(2)}, u32[]{:S(2)}) collective-permute-start(f32[3,8,128]{2,1,0:T(8,128)S(1)} %get-tuple-element.148), channel_id=1, source_target_pairs={{8,17},{9,18},{10,19},{11,16},{12,21},{13,22},{14,23},{15,20}} | collective-permute-start | bytes 36872 | tf_op jit(solution)/shard_map/ppermute | solution.py:49
  103.2 7.7 %collective-permute-start.33 = (f32[3,8,128]{2,1,0:T(8,128)S(1)}, f32[3,8,128]{2,1,0:T(8,128)S(1)}, u32[]{:S(2)}, u32[]{:S(2)}) collective-permute-start(f32[3,8,128]{2,1,0:T(8,128)S(1)} %get-tuple-element.149), channel_id=1, source_target_pairs={{8,19},{9,16},{10,17},{11,18},{12,23},{13,20},{14,21},{15,22}} | collective-permute-start | bytes 36872 | tf_op jit(solution)/shard_map/ppermute | solution.py:49
  111.8 6.6 %collective-permute-start.35 = (f32[6,8,16,128]{3,2,1,0:T(8,128)S(1)}, f32[6,8,16,128]{3,2,1,0:T(8,128)S(1)}, u32[]{:S(2)}, u32[]{:S(2)}) collective-permute-start(f32[6,8,16,128]{3,2,1,0:T(8,128)S(1)} %get-tuple-element.151), channel_id=1, source_target_pairs={{16,24},{17,25},{18,26},{19,27},{20,28},{21,29},{22,30},{23,31}} | collective-permute-start | bytes 1179656 | tf_op jit(solution)/shard_map/ppermute | solution.py:49
  120.8 6.9 %collective-permute-start.40 = (f32[3,2,32,256]{3,2,1,0:T(8,128)S(1)}, f32[3,2,32,256]{3,2,1,0:T(8,128)S(1)}, u32[]{:S(2)}, u32[]{:S(2)}) collective-permute-start(f32[3,2,32,256]{3,2,1,0:T(8,128)S(1)} %get-tuple-element.157), channel_id=1, source_target_pairs={{0,4},{4,0},{1,5},{5,1},{2,6},{6,2},{3,7},{7,3},{8,12},{12,8},{9,1... | collective-permute-start | bytes 589832 | tf_op jit(solution)/shard_map/ppermute | solution.py:34
  130.7 7.8 %collective-permute-start.43 = (f32[3,2,32,256]{3,2,1,0:T(8,128)S(1)}, f32[3,2,32,256]{3,2,1,0:T(8,128)S(1)}, u32[]{:S(2)}, u32[]{:S(2)}) collective-permute-start(f32[3,2,32,256]{3,2,1,0:T(8,128)S(1)} %get-tuple-element.163), channel_id=1, source_target_pairs={{0,4},{4,0},{1,5},{5,1},{2,6},{6,2},{3,7},{7,3},{8,12},{12,8},{9,1... | collective-permute-start | bytes 589832 | tf_op jit(solution)/shard_map/ppermute | solution.py:34
  132.0 6.1 %collective-permute-start.45 = (f32[3,16,256]{2,1,0:T(8,128)S(1)}, f32[3,16,256]{2,1,0:T(8,128)S(1)}, u32[]{:S(2)}, u32[]{:S(2)}) collective-permute-start(f32[3,16,256]{2,1,0:T(8,128)S(1)} %get-tuple-element.165), channel_id=1, source_target_pairs={{0,3},{1,0},{2,1},{3,2},{4,7},{5,4},{6,5},{7,6},{8,11},{9,8},{10,9... | collective-permute-start | bytes 147464 | tf_op jit(solution)/shard_map/ppermute | solution.py:36
  (27 other events, 111.2 us)

commit v11 on v9

--- a/solution.py
+++ b/solution.py
@@ -10,7 +10,7 @@
 VISCOSITY = 0.25
 TIME_STEP = 0.5
 PAD = 8
-CHUNK = 16
+CHUNK = 8
 ROOM = 4 << 20
 F32 = jnp.float32
 BF16 = jnp.bfloat16
@@ -37,24 +37,24 @@
     return before_after, behind, ahead
 
 
-def pass_on(slabs, array, dx=0, dy=0):
-    gx, gy = lax.axis_size("gx"), lax.axis_size("gy")
+def pass_on(array, dx=0, dy=0):
+    slabs, gx, gy = lax.axis_size("tm"), lax.axis_size("gx"), lax.axis_size("gy")
     pairs = []
-    for t in slabs:
+    for t in range(slabs):
         for x in range(gx):
             for y in range(gy):
                 source = (t * gx + x) * gy + y
-                target = ((t + 1) * gx + (x + dx) % gx) * gy + (y + dy) % gy
+                target = ((t + 1) % slabs * gx + (x + dx) % gx) * gy + (y + dy) % gy
                 pairs.append((source, target))
     return lax.ppermute(array, ("tm", "gx", "gy"), pairs)
 
 
-def hand_on(slabs, value, faces):
+def hand_on(value, faces):
     x_faces, y_last, y_first = faces
-    main = pass_on(slabs, value)
-    behind = pass_on(slabs, y_last, 0, 1)
-    ahead = pass_on(slabs, y_first, 0, -1)
-    before_after = both_faces(x_faces, lambda a, by: pass_on(slabs, a, by, 0), lax.axis_size("gx"))
+    main = pass_on(value)
+    behind = pass_on(y_last, 0, 1)
+    ahead = pass_on(y_first, 0, -1)
+    before_after = both_faces(x_faces, lambda a, by: pass_on(a, by, 0), lax.axis_size("gx"))
     return [main, behind, ahead, before_after]
 
 
@@ -410,6 +410,18 @@
     return main, x_faces, behind, ahead
 
 
+def own_round(first, arrived):
+    shares = [jnp.where(first[1] == float(k + 1), 1.0, 0.0) for k in range(len(arrived))]
+    return lambda read: total([share * read(group) for share, group in zip(shares, arrived)])
+
+
+def leave_empty(first, turn, outs):
+    @pl.when(first[1] != float(turn))
+    def _():
+        for out in outs:
+            out[...] = jnp.zeros(out.shape, F32)
+
+
 def pass_start_kernel(turn, first, *refs):
     arrived, zero = arrival(refs[:4]), refs[4:8]
     integral, speed, coarse_grads, end, end_x, end_l, end_f = refs[8:15]
@@ -427,6 +439,8 @@
             d0[k][...] = arrived[k][...] - zero[k][...]
         chain_step(base, speed, coarse_grads, d0, ext, store)
         emit_faces(end, (end_x, end_l, end_f))
+
+    leave_empty(first, turn, (end, end_x, end_l, end_f))
 
 
 def settle_start_kernel(count, first, *refs):
@@ -434,7 +448,7 @@
     refs = refs[4 * count :]
     zero, (integral, speed, coarse_grads, end_two, s) = refs[:4], refs[4:9]
     d0, d2, outs, ext = refs[9:13], refs[13], refs[14:17], refs[17]
-    rest = 1.0 - first[0]
+    rest, own = 1.0 - first[0], own_round(first, arrived)
 
     def base(a, x):
         return zero[0][a, x] + integral[a, x] - end_two[a, x]
@@ -443,7 +457,7 @@
         d2[a, x] = value
 
     for k in range(4):
-        d0[k][...] = rest * (total([group[k][...] for group in arrived]) - zero[k][...])
+        d0[k][...] = rest * (own(lambda group: group[k][...]) - zero[k][...])
     chain_step(base, speed, coarse_grads, d0, ext, store)
     emit_faces(s, outs, 0)
     emit_coarse_faces(d2, outs, 3)
@@ -465,22 +479,24 @@
         chain_step(base, speed, coarse_grads, arrived, ext, store)
         emit_faces(sent, (sent_x, sent_l, sent_f))
 
+    leave_empty(first, turn, (sent, sent_x, sent_l, sent_f))
+
 
 def settle_later_kernel(count, first, *refs):
     arrived = [arrival(refs[4 * k : 4 * k + 4]) for k in range(count)]
     own, speed, coarse_grads, s, u0, u1, u2, stage, stage_x, stage_l, stage_f, begin, rest = refs[4 * count : 4 * count + 13]
     d0, (d2, ext, wide0, wide2, rows) = refs[4 * count + 13 : 4 * count + 17], refs[4 * count + 17 :]
-    f = first[0]
+    f, picked = first[0], own_round(first, arrived)
 
     def base(a, x):
-        return own[a, x] + total([group[0][3 + a, x] for group in arrived])
+        return own[a, x] + picked(lambda group: group[0][3 + a, x])
 
     def store(a, x, value):
         d2[a, x] = value
 
-    d0[0][...] = total([group[0][0:3] for group in arrived])
+    d0[0][...] = picked(lambda group: group[0][0:3])
     for k in range(1, 4):
-        d0[k][...] = total([group[k][...] for group in arrived])
+        d0[k][...] = picked(lambda group: group[k][...])
     chain_step(base, speed, coarse_grads, d0, ext, store)
     prolong_own(d0[0], wide0, rows)
     prolong_own(d2, wide2, rows)
@@ -493,7 +509,7 @@
             toward_rest = 0.125 * (p2 - p0)
             for q in range(2):
                 x = 2 * i + q
-                start, one, two = f * s[c, x] + u0[c, x], u1[c, x], u2[c, x]
+                start, one, two = f * s[c, x] + (1.0 - f) * u0[c, x], u1[c, x], u2[c, x]
                 stage[c, x] = toward_stage + TIME_STEP * (start * (5.0 / 24.0) + one / 3.0 - two / 24.0)
                 begin[c, x] = start + p0
                 rest[c, x] = toward_rest + (two * (5.0 / 24.0) - one / 6.0 - start / 24.0)
@@ -682,7 +698,7 @@
     def chain(step, sent, outs, scratch, own_terms):
         arrivals = []
         for turn in range(1, slabs):
-            arrivals += hand_on([turn - 1], sent[0], sent[1:])
+            arrivals += hand_on(sent[0], sent[1:])
             if turn + 1 < slabs:
                 sent = call(
                     lambda *refs, turn=turn: step(turn, *refs), "chain", first,
@@ -711,7 +727,7 @@
         [fine] + fine_faces + [coarse], [ext, summed, rows], 40_000_000,
     )
     faces, end_two = results[:3], results[3]
-    u0 = pass_on(range(slabs - 1), value)
+    u0 = pass_on(value)
     u2 = [value, *swap_faces(faces)]
 
     own_part, following, *sent = call(

time: 139 us -> 138 us (level)
  starting transfers between devices: 47.6 us -> 43.2 us
  waiting for transfers between devices: 52.6 us -> 56.3 us
    ppermute x25, waiting for transfers between devices: 22.4 us -> 27.5 us  [pass_on(): return lax.ppermute(array, ('tm', 'gx', 'gy'), pairs)]
    ppermute x6, waiting for transfers between devices: 13.3 us -> 9.14 us  [swap_faces(): ahead = lax.ppermute(y_first, 'gy', ring(gy, -1))]
    ppermute x6, starting transfers between devices: 5.09 us -> 1.1 us  [swap_faces(): behind = lax.ppermute(y_last, 'gy', ring(gy, 1))]
    ppermute x25, starting transfers between devices: 28.1 us -> 24.6 us  [pass_on(): return lax.ppermute(array, ('tm', 'gx', 'gy'), pairs)]
    ppermute x6, starting transfers between devices: 7.92 us -> 11.1 us  [swap_faces(): ahead = lax.ppermute(y_first, 'gy', ring(gy, -1))]
    ppermute x6, waiting for transfers between devices: 3.85 us -> 5.7 us  [swap_faces(): lax.ppermute(a, 'gx', ring(gx, by))]
  transfers between devices with their start and end apart: 43 -> 43, of which waited for: 23 -> 30; matrix products, arithmetic and copies ran while one was open for 0% -> 0% of each run, Pallas kernels for 6% -> 6%
where the time goes in v11:
time: 138 us; the launch traced here: 137 us
  waiting for transfers between devices  56.3 us (41%)
  starting transfers between devices  43.2 us (31%)
  Pallas kernels  36.6 us (27%)
    pallas_call x14, Pallas kernels, call(): pl.pallas_call(kernel, name=name, out_shape=[jax.ShapeDtypeStruct(dims, F...  36.6 us
    ppermute x25, waiting for transfers between devices, pass_on(): return lax.ppermute(array, ('tm', 'gx', 'gy'), pairs)  27.5 us
    ppermute x25, starting transfers between devices, pass_on(): return lax.ppermute(array, ('tm', 'gx', 'gy'), pairs)  24.6 us
    ppermute x6, waiting for transfers between devices, swap_faces(): behind = lax.ppermute(y_last, 'gy', ring(gy, 1))  14 us
    ppermute x6, starting transfers between devices, swap_faces(): ahead = lax.ppermute(y_first, 'gy', ring(gy, -1))  11.1 us
    ppermute x6, waiting for transfers between devices, swap_faces(): ahead = lax.ppermute(y_first, 'gy', ring(gy, -1))  9.14 us
    ppermute x6, starting transfers between devices, swap_faces(): lax.ppermute(a, 'gx', ring(gx, by))  6.4 us
    ppermute x6, waiting for transfers between devices, swap_faces(): lax.ppermute(a, 'gx', ring(gx, by))  5.7 us
  transfers between devices with their start and end apart: 43, of which 30 were waited for; matrix products, arithmetic and copies ran while one was open for 0% of the time, Pallas kernels for 6%

profile of v11, /device:TPU:26, one launch (start us, length us, event | category | flops | bytes accessed | tf_op | source)
XLA Modules:
  0.0 137.3 jit_solution(5320656401331218823)
XLA Ops:
  0.0 4.1 %pack.1 = (f32[3,8,16,128]{3,2,1,0:T(8,128)}, f32[7,2,32,256]{3,2,1,0:T(8,128)}, f32[7,16,256]{2,1,0:T(8,128)}, f32[7,16,256]{2,1,0:T(8,128)}) custom-call(f32[3,16,32,256]{3,2,1,0:T(8,128)} %v.15, f32[3,16,32,256]{3,2,1,0:T(8,128)} %refs_16_.1, f32[3,16,32,256]{3,2,1,0:T(8,128)} %bitcast.4), custom_call_target="tpu_custom_call" | custom-call | flops 5000000 | bytes 4718592 | tf_op jit(solution)/shard_map/pack/pallas_call | solution.py:652
  10.3 2.8 %collective-permute-done.1.behind.w_b = f32[7,16,256]{2,1,0:T(8,128)S(1)} collective-permute-done((f32[7,16,256]{2,1,0:T(8,128)}, f32[7,16,256]{2,1,0:T(8,128)S(1)}, u32[]{:S(2)}, u32[]{:S(2)}) %collective-permute-start.1) | collective-permute-done | bytes 114720 | tf_op jit(solution)/shard_map/ppermute | solution.py:35
  13.1 3.6 %collective-permute-done.x_faces.w_x = f32[7,2,32,256]{3,2,1,0:T(8,128)} collective-permute-done((f32[7,2,32,256]{3,2,1,0:T(8,128)}, f32[7,2,32,256]{3,2,1,0:T(8,128)}, u32[]{:S(2)}, u32[]{:S(2)}) %collective-permute-start) | collective-permute-done | bytes 458784 | tf_op jit(solution)/shard_map/ppermute | solution.py:34
  16.7 5.4 %offset_start.1 = (f32[9,16,32,256]{3,2,1,0:T(8,128)S(1)}, f32[3,8,16,128]{3,2,1,0:T(8,128)S(1)}, f32[9,8,16,128]{3,2,1,0:T(8,128)S(1)}, f32[3,2,16,128]{3,2,1,0...) custom-call(f32[2]{0:T(128)S(1)} %add_convert_fusion.first.refs_0_, ...), custom_call_target="tpu_custom_call" | custom-call | flops 40000000 | bytes 5603328 | tf_op jit(solution)/shard_map/offset_start/pallas_call | solution.py:652
  23.9 2.7 %collective-permute-start.5 = (f32[3,8,128]{2,1,0:T(8,128)S(1)}, f32[3,8,128]{2,1,0:T(8,128)S(1)}, u32[]{:S(2)}, u32[]{:S(2)}) collective-permute-start(f32[3,8,128]{2,1,0:T(8,128)S(1)} %get-tuple-element.83), channel_id=1, source_target_pairs={{0,11},{1,8},{2,9},{3,10},{4,15},{5,12},{6,13},{7,14},{8,19},{9,16... | collective-permute-start | bytes 36872 | tf_op jit(solution)/shard_map/ppermute | solution.py:49
  33.8 2.3 %collective-permute-done.8.refs_2_.refs_6_ = f32[3,8,128]{2,1,0:T(8,128)S(1)} collective-permute-done((f32[3,8,128]{2,1,0:T(8,128)S(1)}, f32[3,8,128]{2,1,0:T(8,128)S(1)}, u32[]{:S(2)}, u32[]{:S(2)}) %collective-permute-start.8) | collective-permute-done | bytes 12320 | tf_op jit(solution)/shard_map/ppermute | solution.py:49
  40.3 2.9 %collective-permute-start.13 = (f32[3,8,128]{2,1,0:T(8,128)S(1)}, f32[3,8,128]{2,1,0:T(8,128)S(1)}, u32[]{:S(2)}, u32[]{:S(2)}) collective-permute-start(f32[3,8,128]{2,1,0:T(8,128)S(1)} %get-tuple-element.97), channel_id=1, source_target_pairs={{0,11},{1,8},{2,9},{3,10},{4,15},{5,12},{6,13},{7,14},{8,19},{9,16... | collective-permute-start | bytes 36872 | tf_op jit(solution)/shard_map/ppermute | solution.py:49
  49.8 2.3 %collective-permute-done.16.m_b.behind = f32[4,16,256]{2,1,0:T(8,128)S(1)} collective-permute-done((f32[4,16,256]{2,1,0:T(8,128)S(1)}, f32[4,16,256]{2,1,0:T(8,128)S(1)}, u32[]{:S(2)}, u32[]{:S(2)}) %collective-permute-start.16) | collective-permute-done | bytes 65568 | tf_op jit(solution)/shard_map/ppermute | solution.py:35
  52.1 2.3 %collective-permute-done.17.m_a.ahead = f32[4,16,256]{2,1,0:T(8,128)S(1)} collective-permute-done((f32[4,16,256]{2,1,0:T(8,128)S(1)}, f32[4,16,256]{2,1,0:T(8,128)S(1)}, u32[]{:S(2)}, u32[]{:S(2)}) %collective-permute-start.17) | collective-permute-done | bytes 65568 | tf_op jit(solution)/shard_map/ppermute | solution.py:36
  56.1 4.6 %middle.1 = (f32[3,16,32,256]{3,2,1,0:T(8,128)S(1)}, f32[3,2,32,256]{3,2,1,0:T(8,128)S(1)}, f32[3,16,256]{2,1,0:T(8,128)S(1)}, f32[3,16,256]{2,1,0:T(8,128)S(1)}...) custom-call(f32[2]{0:T(128)S(1)} %add_convert_fusion.first.refs_0_, ...), custom_call_target="tpu_custom_call" | custom-call | flops 60000000 | bytes 10985472 | tf_op jit(solution)/shard_map/middle/pallas_call | solution.py:652
  63.3 2.6 %collective-permute-done.19.a1_b.u1_b = f32[3,16,256]{2,1,0:T(8,128)S(1)} collective-permute-done((f32[3,16,256]{2,1,0:T(8,128)S(1)}, f32[3,16,256]{2,1,0:T(8,128)S(1)}, u32[]{:S(2)}, u32[]{:S(2)}) %collective-permute-start.19) | collective-permute-done | bytes 49184 | tf_op jit(solution)/shard_map/ppermute | solution.py:35
  67.3 3.2 %finish.1 = (f32[3,16,32,256]{3,2,1,0:T(8,128)S(1)}, f32[3,2,32,256]{3,2,1,0:T(8,128)S(1)}, f32[3,16,256]{2,1,0:T(8,128)S(1)}, f32[3,16,256]{2,1,0:T(8,128)S(1)}, f32[3,8,16,128]{3,2,1,0:T(8,128)S(1)}) custom-call(f32[2]{0:T(128)S(1)} %add_convert_fusion.first.refs_0_, f32[3,16,32,256]{3,2,1,0:T(8,128)S(1)} %copy-done, ...), custom_call_target="tpu_custom_call" | custom-call | flops 40000000 | bytes 10027008 | tf_op jit(solution)/shard_map/finish/pallas_call | solution.py:652
  74.1 2.1 %collective-permute-done.22.u2_b = f32[3,16,256]{2,1,0:T(8,128)S(1)} collective-permute-done((f32[3,16,256]{2,1,0:T(8,128)S(1)}, f32[3,16,256]{2,1,0:T(8,128)S(1)}, u32[]{:S(2)}, u32[]{:S(2)}) %collective-permute-start.22) | collective-permute-done | bytes 49184 | tf_op jit(solution)/shard_map/ppermute | solution.py:35
  76.2 2.0 %collective-permute-done.23.u2_a = f32[3,16,256]{2,1,0:T(8,128)S(1)} collective-permute-done((f32[3,16,256]{2,1,0:T(8,128)S(1)}, f32[3,16,256]{2,1,0:T(8,128)S(1)}, u32[]{:S(2)}, u32[]{:S(2)}) %collective-permute-start.23) | collective-permute-done | bytes 49184 | tf_op jit(solution)/shard_map/ppermute | solution.py:36
  78.4 5.4 %offset_later.1 = (f32[3,8,16,128]{3,2,1,0:T(8,128)S(1)}, f32[3,8,16,128]{3,2,1,0:T(8,128)S(1)}, f32[6,8,16,128]{3,2,1,0:T(8,128)S(1)}, f32[3,2,16,128]{3,2,1,0:...) custom-call(f32[2]{0:T(128)S(1)} %add_convert_fusion.first.refs_0_, f32[3,16,32,256]{3,2,1,0:T(8,128)S(1)} %copy-done, ...), custom_call_target="tpu_custom_call" | custom-call | flops 60000000 | bytes 12386304 | tf_op jit(solution)/shard_map/offset_later/pallas_call | solution.py:652
  85.3 2.7 %collective-permute-start.26 = (f32[3,8,128]{2,1,0:T(8,128)S(1)}, f32[3,8,128]{2,1,0:T(8,128)S(1)}, u32[]{:S(2)}, u32[]{:S(2)}) collective-permute-start(f32[3,8,128]{2,1,0:T(8,128)S(1)} %get-tuple-element.122), channel_id=1, source_target_pairs={{0,11},{1,8},{2,9},{3,10},{4,15},{5,12},{6,13},{7,14},{8,19},{9,16... | collective-permute-start | bytes 36872 | tf_op jit(solution)/shard_map/ppermute | solution.py:49
  91.2 5.1 %collective-permute-done.27.refs_4_ = f32[3,2,16,128]{3,2,1,0:T(8,128)S(1)} collective-permute-done((f32[3,2,16,128]{3,2,1,0:T(8,128)S(1)}, f32[3,2,16,128]{3,2,1,0:T(8,128)S(1)}, u32[]{:S(2)}, u32[]{:S(2)}) %collective-permute-start.27) | collective-permute-done | bytes 49184 | tf_op jit(solution)/shard_map/ppermute | solution.py:49
  98.1 2.4 %collective-permute-start.30 = (f32[3,8,128]{2,1,0:T(8,128)S(1)}, f32[3,8,128]{2,1,0:T(8,128)S(1)}, u32[]{:S(2)}, u32[]{:S(2)}) collective-permute-start(f32[3,8,128]{2,1,0:T(8,128)S(1)} %get-tuple-element.128), channel_id=1, source_target_pairs={{0,11},{1,8},{2,9},{3,10},{4,15},{5,12},{6,13},{7,14},{8,19},{9,16... | collective-permute-start | bytes 36872 | tf_op jit(solution)/shard_map/ppermute | solution.py:49
  107.4 2.8 %collective-permute-start.34 = (f32[3,8,128]{2,1,0:T(8,128)S(1)}, f32[3,8,128]{2,1,0:T(8,128)S(1)}, u32[]{:S(2)}, u32[]{:S(2)}) collective-permute-start(f32[3,8,128]{2,1,0:T(8,128)S(1)} %get-tuple-element.132), channel_id=1, source_target_pairs={{0,11},{1,8},{2,9},{3,10},{4,15},{5,12},{6,13},{7,14},{8,19},{9,16... | collective-permute-start | bytes 36872 | tf_op jit(solution)/shard_map/ppermute | solution.py:49
  114.7 2.4 %settle.3 = (f32[3,16,32,256]{3,2,1,0:T(8,128)S(1)}, f32[3,2,32,256]{3,2,1,0:T(8,128)S(1)}, f32[3,16,256]{2,1,0:T(8,128)S(1)}, f32[3,16,256]{2,1,0:T(8,128)S(1)}...) custom-call(f32[2]{0:T(128)S(1)} %add_convert_fusion.first.refs_0_, ...), custom_call_target="tpu_custom_call" | custom-call | flops 10000000 | bytes 8675328 | tf_op jit(solution)/shard_map/settle/pallas_call | solution.py:652
  119.9 2.2 %collective-permute-done.38.y_b = f32[3,16,256]{2,1,0:T(8,128)S(1)} collective-permute-done((f32[3,16,256]{2,1,0:T(8,128)S(1)}, f32[3,16,256]{2,1,0:T(8,128)S(1)}, u32[]{:S(2)}, u32[]{:S(2)}) %collective-permute-start.38) | collective-permute-done | bytes 49184 | tf_op jit(solution)/shard_map/ppermute | solution.py:35
  123.8 3.0 %stage.1 = (f32[3,16,32,256]{3,2,1,0:T(8,128)S(1)}, f32[3,16,32,256]{3,2,1,0:T(8,128)S(1)}, f32[3,2,32,256]{3,2,1,0:T(8,128)S(1)}, f32[3,16,256]{2,1,0:T(8,128)S(1)}, f32[3,16,256]{2,1,0:T(8,128)S(1)}) custom-call(f32[2]{0:T(128)S(1)} %add_convert_fusion.first.refs_0_, f32[3,16,32,256]{3,2,1,0:T(8,128)S(1)} %copy-done, ...), custom_call_target="tpu_custom_call" | custom-call | flops 40000000 | bytes 11304960 | tf_op jit(solution)/shard_map/stage/pallas_call | solution.py:652
  130.5 2.1 %collective-permute-done.41.y_b = f32[3,16,256]{2,1,0:T(8,128)S(1)} collective-permute-done((f32[3,16,256]{2,1,0:T(8,128)S(1)}, f32[3,16,256]{2,1,0:T(8,128)S(1)}, u32[]{:S(2)}, u32[]{:S(2)}) %collective-permute-start.41) | collective-permute-done | bytes 49184 | tf_op jit(solution)/shard_map/ppermute | solution.py:35
  134.3 2.9 %last_stage.1 = f32[3,16,32,256]{3,2,1,0:T(8,128)} custom-call(f32[3,16,32,256]{3,2,1,0:T(8,128)S(1)} %copy-done, f32[9,16,32,256]{3,2,1,0:T(8,128)S(1)} %get-tuple-element.80.grads, f32[3,16,32,256]{3,2,1,0:T(8,128)S(1)} %get-tuple-element.140.y, f32[3,2,32,256]{3,2,1,0:T(8,128)S(1)} %collective-permute-done.40.y_x, ...), custom_call_target="tpu_custom_call" | custom-call | flops 40000000 | bytes 9732096 | tf_op jit(solution)/shard_map/last_stage/pallas_call | solution.py:652
  (87 shorter events, 63.2 us)
Async XLA Ops:
  4.1 12.6 %collective-permute-start = (f32[7,2,32,256]{3,2,1,0:T(8,128)}, f32[7,2,32,256]{3,2,1,0:T(8,128)}, u32[]{:S(2)}, u32[]{:S(2)}) collective-permute-start(f32[7,2,32,256]{3,2,1,0:T(8,128)} %get-tuple-element.75), channel_id=1, source_target_pairs={{0,4},{4,0},{1,5},{5,1},{2,6},{6,2},{3,7},{7,3},{8,12},{12,8},{9,1... | collective-permute-start | bytes 1376264 | tf_op jit(solution)/shard_map/ppermute | solution.py:34
  5.6 7.5 %collective-permute-start.1 = (f32[7,16,256]{2,1,0:T(8,128)}, f32[7,16,256]{2,1,0:T(8,128)S(1)}, u32[]{:S(2)}, u32[]{:S(2)}) collective-permute-start(f32[7,16,256]{2,1,0:T(8,128)} %get-tuple-element.76), channel_id=1, source_target_pairs={{0,1},{1,2},{2,3},{3,0},{4,5},{5,6},{6,7},{7,4},{8,9},{9,10},{10,1... | collective-permute-start | bytes 344072 | tf_op jit(solution)/shard_map/ppermute | solution.py:35
  5.8 7.2 %collective-permute-start.2 = (f32[7,16,256]{2,1,0:T(8,128)}, f32[7,16,256]{2,1,0:T(8,128)S(1)}, u32[]{:S(2)}, u32[]{:S(2)}) collective-permute-start(f32[7,16,256]{2,1,0:T(8,128)} %get-tuple-element.77), channel_id=1, source_target_pairs={{0,3},{1,0},{2,1},{3,2},{4,7},{5,4},{6,5},{7,6},{8,11},{9,8},{10,9... | collective-permute-start | bytes 344072 | tf_op jit(solution)/shard_map/ppermute | solution.py:36
  22.1 7.7 %collective-permute-start.3 = (f32[3,8,16,128]{3,2,1,0:T(8,128)S(1)}, f32[3,8,16,128]{3,2,1,0:T(8,128)S(1)}, u32[]{:S(2)}, u32[]{:S(2)}) collective-permute-start(f32[3,8,16,128]{3,2,1,0:T(8,128)S(1)} %get-tuple-element.81), channel_id=1, source_target_pairs={{0,8},{1,9},{2,10},{3,11},{4,12},{5,13},{6,14},{7,15},{8,16},{9,17... | collective-permute-start | bytes 589832 | tf_op jit(solution)/shard_map/ppermute | solution.py:49
  22.1 7.6 %collective-permute-start.6 = (f32[3,2,16,128]{3,2,1,0:T(8,128)S(1)}, f32[3,2,16,128]{3,2,1,0:T(8,128)S(1)}, u32[]{:S(2)}, u32[]{:S(2)}) collective-permute-start(f32[3,2,16,128]{3,2,1,0:T(8,128)S(1)} %get-tuple-element.84), channel_id=1, source_target_pairs={{0,12},{1,13},{2,14},{3,15},{4,8},{5,9},{6,10},{7,11},{8,20},{9,21... | collective-permute-start | bytes 147464 | tf_op jit(solution)/shard_map/ppermute | solution.py:49
  30.3 7.6 %collective-permute-start.7 = (f32[3,8,16,128]{3,2,1,0:T(8,128)S(1)}, f32[3,8,16,128]{3,2,1,0:T(8,128)S(1)}, u32[]{:S(2)}, u32[]{:S(2)}) collective-permute-start(f32[3,8,16,128]{3,2,1,0:T(8,128)S(1)} %get-tuple-element.91), channel_id=1, source_target_pairs={{0,8},{1,9},{2,10},{3,11},{4,12},{5,13},{6,14},{7,15},{8,16},{9,17... | collective-permute-start | bytes 589832 | tf_op jit(solution)/shard_map/ppermute | solution.py:49
  30.7 7.2 %collective-permute-start.10 = (f32[3,2,16,128]{3,2,1,0:T(8,128)S(1)}, f32[3,2,16,128]{3,2,1,0:T(8,128)S(1)}, u32[]{:S(2)}, u32[]{:S(2)}) collective-permute-start(f32[3,2,16,128]{3,2,1,0:T(8,128)S(1)} %get-tuple-element.94), channel_id=1, source_target_pairs={{0,12},{1,13},{2,14},{3,15},{4,8},{5,9},{6,10},{7,11},{8,20},{9,21... | collective-permute-start | bytes 147464 | tf_op jit(solution)/shard_map/ppermute | solution.py:49
  38.8 7.4 %collective-permute-start.11 = (f32[3,8,16,128]{3,2,1,0:T(8,128)S(1)}, f32[3,8,16,128]{3,2,1,0:T(8,128)S(1)}, u32[]{:S(2)}, u32[]{:S(2)}) collective-permute-start(f32[3,8,16,128]{3,2,1,0:T(8,128)S(1)} %get-tuple-element.95), channel_id=1, source_target_pairs={{0,8},{1,9},{2,10},{3,11},{4,12},{5,13},{6,14},{7,15},{8,16},{9,17... | collective-permute-start | bytes 589832 | tf_op jit(solution)/shard_map/ppermute | solution.py:49
  38.8 7.3 %collective-permute-start.14 = (f32[3,2,16,128]{3,2,1,0:T(8,128)S(1)}, f32[3,2,16,128]{3,2,1,0:T(8,128)S(1)}, u32[]{:S(2)}, u32[]{:S(2)}) collective-permute-start(f32[3,2,16,128]{3,2,1,0:T(8,128)S(1)} %get-tuple-element.98), channel_id=1, source_target_pairs={{0,12},{1,13},{2,14},{3,15},{4,8},{5,9},{6,10},{7,11},{8,20},{9,21... | collective-permute-start | bytes 147464 | tf_op jit(solution)/shard_map/ppermute | solution.py:49
  47.2 8.9 %collective-permute-start.15 = (f32[4,2,32,256]{3,2,1,0:T(8,128)S(1)}, f32[4,2,32,256]{3,2,1,0:T(8,128)S(1)}, u32[]{:S(2)}, u32[]{:S(2)}) collective-permute-start(f32[4,2,32,256]{3,2,1,0:T(8,128)S(1)} %get-tuple-element.99), channel_id=1, source_target_pairs={{0,4},{4,0},{1,5},{5,1},{2,6},{6,2},{3,7},{7,3},{8,12},{12,8},{9,1... | collective-permute-start | bytes 786440 | tf_op jit(solution)/shard_map/ppermute | solution.py:34
  48.3 6.1 %collective-permute-start.17 = (f32[4,16,256]{2,1,0:T(8,128)S(1)}, f32[4,16,256]{2,1,0:T(8,128)S(1)}, u32[]{:S(2)}, u32[]{:S(2)}) collective-permute-start(f32[4,16,256]{2,1,0:T(8,128)S(1)} %get-tuple-element.101), channel_id=1, source_target_pairs={{0,3},{1,0},{2,1},{3,2},{4,7},{5,4},{6,5},{7,6},{8,11},{9,8},{10,9... | collective-permute-start | bytes 196616 | tf_op jit(solution)/shard_map/ppermute | solution.py:36
  60.7 6.7 %collective-permute-start.18 = (f32[3,2,32,256]{3,2,1,0:T(8,128)S(1)}, f32[3,2,32,256]{3,2,1,0:T(8,128)S(1)}, u32[]{:S(2)}, u32[]{:S(2)}) collective-permute-start(f32[3,2,32,256]{3,2,1,0:T(8,128)S(1)} %get-tuple-element.108), channel_id=1, source_target_pairs={{0,4},{4,0},{1,5},{5,1},{2,6},{6,2},{3,7},{7,3},{8,12},{12,8},{9,1... | collective-permute-start | bytes 589832 | tf_op jit(solution)/shard_map/ppermute | solution.py:34
  70.6 44.1 %collective-permute-start.36 = (f32[3,16,32,256]{3,2,1,0:T(8,128)S(1)}, f32[3,16,32,256]{3,2,1,0:T(8,128)S(1)}, u32[]{:S(2)}, u32[]{:S(2)}) collective-permute-start(f32[3,16,32,256]{3,2,1,0:T(8,128)S(1)} %get-tuple-element.115.u2.refs_19_), channel_id=1, source_target_pairs={{0,8},{1,9},{2,10},{3,11},{4,12},{5,13},{6,14},{7,15},{8,16},{9,17... | collective-permute-start | bytes 4718600 | tf_op jit(solution)/shard_map/ppermute | solution.py:49
  70.7 7.7 %collective-permute-start.21 = (f32[3,2,32,256]{3,2,1,0:T(8,128)S(1)}, f32[3,2,32,256]{3,2,1,0:T(8,128)S(1)}, u32[]{:S(2)}, u32[]{:S(2)}) collective-permute-start(f32[3,2,32,256]{3,2,1,0:T(8,128)S(1)} %get-tuple-element.116), channel_id=1, source_target_pairs={{0,4},{4,0},{1,5},{5,1},{2,6},{6,2},{3,7},{7,3},{8,12},{12,8},{9,1... | collective-permute-start | bytes 589832 | tf_op jit(solution)/shard_map/ppermute | solution.py:34
  83.8 12.5 %collective-permute-start.24 = (f32[6,8,16,128]{3,2,1,0:T(8,128)S(1)}, f32[6,8,16,128]{3,2,1,0:T(8,128)S(1)}, u32[]{:S(2)}, u32[]{:S(2)}) collective-permute-start(f32[6,8,16,128]{3,2,1,0:T(8,128)S(1)} %get-tuple-element.120), channel_id=1, source_target_pairs={{0,8},{1,9},{2,10},{3,11},{4,12},{5,13},{6,14},{7,15},{8,16},{9,17... | collective-permute-start | bytes 1179656 | tf_op jit(solution)/shard_map/ppermute | solution.py:49
  83.9 12.4 %collective-permute-start.27 = (f32[3,2,16,128]{3,2,1,0:T(8,128)S(1)}, f32[3,2,16,128]{3,2,1,0:T(8,128)S(1)}, u32[]{:S(2)}, u32[]{:S(2)}) collective-permute-start(f32[3,2,16,128]{3,2,1,0:T(8,128)S(1)} %get-tuple-element.123), channel_id=1, source_target_pairs={{0,12},{1,13},{2,14},{3,15},{4,8},{5,9},{6,10},{7,11},{8,20},{9,21... | collective-permute-start | bytes 147464 | tf_op jit(solution)/shard_map/ppermute | solution.py:49
  85.3 5.9 %collective-permute-start.26 = (f32[3,8,128]{2,1,0:T(8,128)S(1)}, f32[3,8,128]{2,1,0:T(8,128)S(1)}, u32[]{:S(2)}, u32[]{:S(2)}) collective-permute-start(f32[3,8,128]{2,1,0:T(8,128)S(1)} %get-tuple-element.122), channel_id=1, source_target_pairs={{0,11},{1,8},{2,9},{3,10},{4,15},{5,12},{6,13},{7,14},{8,19},{9,16... | collective-permute-start | bytes 36872 | tf_op jit(solution)/shard_map/ppermute | solution.py:49
  96.9 8.2 %collective-permute-start.28 = (f32[6,8,16,128]{3,2,1,0:T(8,128)S(1)}, f32[6,8,16,128]{3,2,1,0:T(8,128)S(1)}, u32[]{:S(2)}, u32[]{:S(2)}) collective-permute-start(f32[6,8,16,128]{3,2,1,0:T(8,128)S(1)} %get-tuple-element.126), channel_id=1, source_target_pairs={{0,8},{1,9},{2,10},{3,11},{4,12},{5,13},{6,14},{7,15},{8,16},{9,17... | collective-permute-start | bytes 1179656 | tf_op jit(solution)/shard_map/ppermute | solution.py:49
  96.9 8.1 %collective-permute-start.31 = (f32[3,2,16,128]{3,2,1,0:T(8,128)S(1)}, f32[3,2,16,128]{3,2,1,0:T(8,128)S(1)}, u32[]{:S(2)}, u32[]{:S(2)}) collective-permute-start(f32[3,2,16,128]{3,2,1,0:T(8,128)S(1)} %get-tuple-element.129), channel_id=1, source_target_pairs={{0,12},{1,13},{2,14},{3,15},{4,8},{5,9},{6,10},{7,11},{8,20},{9,21... | collective-permute-start | bytes 147464 | tf_op jit(solution)/shard_map/ppermute | solution.py:49
  98.1 5.9 %collective-permute-start.30 = (f32[3,8,128]{2,1,0:T(8,128)S(1)}, f32[3,8,128]{2,1,0:T(8,128)S(1)}, u32[]{:S(2)}, u32[]{:S(2)}) collective-permute-start(f32[3,8,128]{2,1,0:T(8,128)S(1)} %get-tuple-element.128), channel_id=1, source_target_pairs={{0,11},{1,8},{2,9},{3,10},{4,15},{5,12},{6,13},{7,14},{8,19},{9,16... | collective-permute-start | bytes 36872 | tf_op jit(solution)/shard_map/ppermute | solution.py:49
  105.9 8.8 %collective-permute-start.32 = (f32[6,8,16,128]{3,2,1,0:T(8,128)S(1)}, f32[6,8,16,128]{3,2,1,0:T(8,128)S(1)}, u32[]{:S(2)}, u32[]{:S(2)}) collective-permute-start(f32[6,8,16,128]{3,2,1,0:T(8,128)S(1)} %get-tuple-element.130), channel_id=1, source_target_pairs={{0,8},{1,9},{2,10},{3,11},{4,12},{5,13},{6,14},{7,15},{8,16},{9,17... | collective-permute-start | bytes 1179656 | tf_op jit(solution)/shard_map/ppermute | solution.py:49
  105.9 8.8 %collective-permute-start.35 = (f32[3,2,16,128]{3,2,1,0:T(8,128)S(1)}, f32[3,2,16,128]{3,2,1,0:T(8,128)S(1)}, u32[]{:S(2)}, u32[]{:S(2)}) collective-permute-start(f32[3,2,16,128]{3,2,1,0:T(8,128)S(1)} %get-tuple-element.133), channel_id=1, source_target_pairs={{0,12},{1,13},{2,14},{3,15},{4,8},{5,9},{6,10},{7,11},{8,20},{9,21... | collective-permute-start | bytes 147464 | tf_op jit(solution)/shard_map/ppermute | solution.py:49
  117.1 6.7 %collective-permute-start.37 = (f32[3,2,32,256]{3,2,1,0:T(8,128)S(1)}, f32[3,2,32,256]{3,2,1,0:T(8,128)S(1)}, u32[]{:S(2)}, u32[]{:S(2)}) collective-permute-start(f32[3,2,32,256]{3,2,1,0:T(8,128)S(1)} %get-tuple-element.135), channel_id=1, source_target_pairs={{0,4},{4,0},{1,5},{5,1},{2,6},{6,2},{3,7},{7,3},{8,12},{12,8},{9,1... | collective-permute-start | bytes 589832 | tf_op jit(solution)/shard_map/ppermute | solution.py:34
  126.8 7.5 %collective-permute-start.40 = (f32[3,2,32,256]{3,2,1,0:T(8,128)S(1)}, f32[3,2,32,256]{3,2,1,0:T(8,128)S(1)}, u32[]{:S(2)}, u32[]{:S(2)}) collective-permute-start(f32[3,2,32,256]{3,2,1,0:T(8,128)S(1)} %get-tuple-element.141), channel_id=1, source_target_pairs={{0,4},{4,0},{1,5},{5,1},{2,6},{6,2},{3,7},{7,3},{8,12},{12,8},{9,1... | collective-permute-start | bytes 589832 | tf_op jit(solution)/shard_map/ppermute | solution.py:34
  (24 other events, 141.4 us)

commit v12 on v11

--- a/solution.py
+++ b/solution.py
@@ -37,24 +37,26 @@
     return before_after, behind, ahead
 
 
-def pass_on(array, dx=0, dy=0):
+def pass_on(array, dx=0, dy=0, turn=0):
     slabs, gx, gy = lax.axis_size("tm"), lax.axis_size("gx"), lax.axis_size("gy")
     pairs = []
+    in_twos = turn % 2 == 1 and slabs % 2 == 0
     for t in range(slabs):
+        following = t + 1 - 2 * (t % 2) if in_twos else (t + 1) % slabs
         for x in range(gx):
             for y in range(gy):
                 source = (t * gx + x) * gy + y
-                target = ((t + 1) % slabs * gx + (x + dx) % gx) * gy + (y + dy) % gy
+                target = (following * gx + (x + dx) % gx) * gy + (y + dy) % gy
                 pairs.append((source, target))
     return lax.ppermute(array, ("tm", "gx", "gy"), pairs)
 
 
-def hand_on(value, faces):
+def hand_on(turn, value, faces):
     x_faces, y_last, y_first = faces
-    main = pass_on(value)
-    behind = pass_on(y_last, 0, 1)
-    ahead = pass_on(y_first, 0, -1)
-    before_after = both_faces(x_faces, lambda a, by: pass_on(a, by, 0), lax.axis_size("gx"))
+    main = pass_on(value, 0, 0, turn)
+    behind = pass_on(y_last, 0, 1, turn)
+    ahead = pass_on(y_first, 0, -1, turn)
+    before_after = both_faces(x_faces, lambda a, by: pass_on(a, by, 0, turn), lax.axis_size("gx"))
     return [main, behind, ahead, before_after]
 
 
@@ -698,7 +700,7 @@
     def chain(step, sent, outs, scratch, own_terms):
         arrivals = []
         for turn in range(1, slabs):
-            arrivals += hand_on(sent[0], sent[1:])
+            arrivals += hand_on(turn, sent[0], sent[1:])
             if turn + 1 < slabs:
                 sent = call(
                     lambda *refs, turn=turn: step(turn, *refs), "chain", first,

time: 138 us -> 128 us (0.928)
  waiting for transfers between devices: 56.3 us -> 50.1 us
  starting transfers between devices: 43.2 us -> 38.7 us
    ppermute x25, waiting for transfers between devices: 27.5 us -> 20.7 us  [pass_on(): return lax.ppermute(array, ('tm', 'gx', 'gy'), pairs)]
    ppermute x25, starting transfers between devices: 24.6 us -> 20.5 us  [pass_on(): return lax.ppermute(array, ('tm', 'gx', 'gy'), pairs)]
  transfers between devices with their start and end apart: 43 -> 43, of which waited for: 30 -> 27; matrix products, arithmetic and copies ran while one was open for 0% -> 0% of each run, Pallas kernels for 6% -> 7%
where the time goes in v12:
time: 128 us; the launch traced here: 127 us
  waiting for transfers between devices  50.1 us (39%)
  starting transfers between devices  38.7 us (30%)
  Pallas kernels  36.6 us (29%)
    pallas_call x14, Pallas kernels, call(): pl.pallas_call(kernel, name=name, out_shape=[jax.ShapeDtypeStruct(dims, F...  36.6 us
    ppermute x25, waiting for transfers between devices, pass_on(): return lax.ppermute(array, ('tm', 'gx', 'gy'), pairs)  20.7 us
    ppermute x25, starting transfers between devices, pass_on(): return lax.ppermute(array, ('tm', 'gx', 'gy'), pairs)  20.5 us
    ppermute x6, waiting for transfers between devices, swap_faces(): behind = lax.ppermute(y_last, 'gy', ring(gy, 1))  14.8 us
    ppermute x6, starting transfers between devices, swap_faces(): ahead = lax.ppermute(y_first, 'gy', ring(gy, -1))  10.5 us
    ppermute x6, waiting for transfers between devices, swap_faces(): ahead = lax.ppermute(y_first, 'gy', ring(gy, -1))  9.22 us
    ppermute x6, starting transfers between devices, swap_faces(): lax.ppermute(a, 'gx', ring(gx, by))  6.03 us
    ppermute x6, waiting for transfers between devices, swap_faces(): lax.ppermute(a, 'gx', ring(gx, by))  5.43 us
  transfers between devices with their start and end apart: 43, of which 27 were waited for; matrix products, arithmetic and copies ran while one was open for 0% of the time, Pallas kernels for 7%

profile of v12, /device:TPU:26, one launch (start us, length us, event | category | flops | bytes accessed | tf_op | source)
XLA Modules:
  0.0 126.5 jit_solution(6796443379518016363)
XLA Ops:
  0.0 4.1 %pack.1 = (f32[3,8,16,128]{3,2,1,0:T(8,128)}, f32[7,2,32,256]{3,2,1,0:T(8,128)}, f32[7,16,256]{2,1,0:T(8,128)}, f32[7,16,256]{2,1,0:T(8,128)}) custom-call(f32[3,16,32,256]{3,2,1,0:T(8,128)} %v.15, f32[3,16,32,256]{3,2,1,0:T(8,128)} %refs_16_.1, f32[3,16,32,256]{3,2,1,0:T(8,128)} %bitcast.4), custom_call_target="tpu_custom_call" | custom-call | flops 5000000 | bytes 4718592 | tf_op jit(solution)/shard_map/pack/pallas_call | solution.py:654
  10.3 2.8 %collective-permute-done.1.behind.w_b = f32[7,16,256]{2,1,0:T(8,128)S(1)} collective-permute-done((f32[7,16,256]{2,1,0:T(8,128)}, f32[7,16,256]{2,1,0:T(8,128)S(1)}, u32[]{:S(2)}, u32[]{:S(2)}) %collective-permute-start.1) | collective-permute-done | bytes 114720 | tf_op jit(solution)/shard_map/ppermute | solution.py:35
  13.1 3.6 %collective-permute-done.x_faces.w_x = f32[7,2,32,256]{3,2,1,0:T(8,128)} collective-permute-done((f32[7,2,32,256]{3,2,1,0:T(8,128)}, f32[7,2,32,256]{3,2,1,0:T(8,128)}, u32[]{:S(2)}, u32[]{:S(2)}) %collective-permute-start) | collective-permute-done | bytes 458784 | tf_op jit(solution)/shard_map/ppermute | solution.py:34
  16.7 5.4 %offset_start.1 = (f32[9,16,32,256]{3,2,1,0:T(8,128)S(1)}, f32[3,8,16,128]{3,2,1,0:T(8,128)S(1)}, f32[9,8,16,128]{3,2,1,0:T(8,128)S(1)}, f32[3,2,16,128]{3,2,1,0...) custom-call(f32[2]{0:T(128)S(1)} %add_convert_fusion.first.refs_0_, ...), custom_call_target="tpu_custom_call" | custom-call | flops 40000000 | bytes 5603328 | tf_op jit(solution)/shard_map/offset_start/pallas_call | solution.py:654
  30.2 2.6 %collective-permute-start.9 = (f32[3,8,128]{2,1,0:T(8,128)S(1)}, f32[3,8,128]{2,1,0:T(8,128)S(1)}, u32[]{:S(2)}, u32[]{:S(2)}) collective-permute-start(f32[3,8,128]{2,1,0:T(8,128)S(1)} %get-tuple-element.93), channel_id=1, source_target_pairs={{0,11},{1,8},{2,9},{3,10},{4,15},{5,12},{6,13},{7,14},{8,19},{9,16... | collective-permute-start | bytes 36872 | tf_op jit(solution)/shard_map/ppermute | solution.py:51
  47.2 2.2 %collective-permute-done.16.m_b.behind = f32[4,16,256]{2,1,0:T(8,128)S(1)} collective-permute-done((f32[4,16,256]{2,1,0:T(8,128)S(1)}, f32[4,16,256]{2,1,0:T(8,128)S(1)}, u32[]{:S(2)}, u32[]{:S(2)}) %collective-permute-start.16) | collective-permute-done | bytes 65568 | tf_op jit(solution)/shard_map/ppermute | solution.py:35
  49.4 2.0 %collective-permute-done.17.m_a.ahead = f32[4,16,256]{2,1,0:T(8,128)S(1)} collective-permute-done((f32[4,16,256]{2,1,0:T(8,128)S(1)}, f32[4,16,256]{2,1,0:T(8,128)S(1)}, u32[]{:S(2)}, u32[]{:S(2)}) %collective-permute-start.17) | collective-permute-done | bytes 65568 | tf_op jit(solution)/shard_map/ppermute | solution.py:36
  53.2 4.6 %middle.1 = (f32[3,16,32,256]{3,2,1,0:T(8,128)S(1)}, f32[3,2,32,256]{3,2,1,0:T(8,128)S(1)}, f32[3,16,256]{2,1,0:T(8,128)S(1)}, f32[3,16,256]{2,1,0:T(8,128)S(1)}...) custom-call(f32[2]{0:T(128)S(1)} %add_convert_fusion.first.refs_0_, ...), custom_call_target="tpu_custom_call" | custom-call | flops 60000000 | bytes 10985472 | tf_op jit(solution)/shard_map/middle/pallas_call | solution.py:654
  58.5 1.8 %collective-permute-start.20 = (f32[3,16,256]{2,1,0:T(8,128)S(1)}, f32[3,16,256]{2,1,0:T(8,128)S(1)}, u32[]{:S(2)}, u32[]{:S(2)}) collective-permute-start(f32[3,16,256]{2,1,0:T(8,128)S(1)} %get-tuple-element.110), channel_id=1, source_target_pairs={{0,3},{1,0},{2,1},{3,2},{4,7},{5,4},{6,5},{7,6},{8,11},{9,8},{10,9... | collective-permute-start | bytes 147464 | tf_op jit(solution)/shard_map/ppermute | solution.py:36
  60.3 2.6 %collective-permute-done.19.a1_b.u1_b = f32[3,16,256]{2,1,0:T(8,128)S(1)} collective-permute-done((f32[3,16,256]{2,1,0:T(8,128)S(1)}, f32[3,16,256]{2,1,0:T(8,128)S(1)}, u32[]{:S(2)}, u32[]{:S(2)}) %collective-permute-start.19) | collective-permute-done | bytes 49184 | tf_op jit(solution)/shard_map/ppermute | solution.py:35
  64.4 3.2 %finish.1 = (f32[3,16,32,256]{3,2,1,0:T(8,128)S(1)}, f32[3,2,32,256]{3,2,1,0:T(8,128)S(1)}, f32[3,16,256]{2,1,0:T(8,128)S(1)}, f32[3,16,256]{2,1,0:T(8,128)S(1)}, f32[3,8,16,128]{3,2,1,0:T(8,128)S(1)}) custom-call(f32[2]{0:T(128)S(1)} %add_convert_fusion.first.refs_0_, f32[3,16,32,256]{3,2,1,0:T(8,128)S(1)} %copy-done, ...), custom_call_target="tpu_custom_call" | custom-call | flops 40000000 | bytes 10027008 | tf_op jit(solution)/shard_map/finish/pallas_call | solution.py:654
  71.3 2.5 %collective-permute-done.22.u2_b = f32[3,16,256]{2,1,0:T(8,128)S(1)} collective-permute-done((f32[3,16,256]{2,1,0:T(8,128)S(1)}, f32[3,16,256]{2,1,0:T(8,128)S(1)}, u32[]{:S(2)}, u32[]{:S(2)}) %collective-permute-start.22) | collective-permute-done | bytes 49184 | tf_op jit(solution)/shard_map/ppermute | solution.py:35
  73.8 2.1 %collective-permute-done.23.u2_a = f32[3,16,256]{2,1,0:T(8,128)S(1)} collective-permute-done((f32[3,16,256]{2,1,0:T(8,128)S(1)}, f32[3,16,256]{2,1,0:T(8,128)S(1)}, u32[]{:S(2)}, u32[]{:S(2)}) %collective-permute-start.23) | collective-permute-done | bytes 49184 | tf_op jit(solution)/shard_map/ppermute | solution.py:36
  75.9 5.4 %offset_later.1 = (f32[3,8,16,128]{3,2,1,0:T(8,128)S(1)}, f32[3,8,16,128]{3,2,1,0:T(8,128)S(1)}, f32[6,8,16,128]{3,2,1,0:T(8,128)S(1)}, f32[3,2,16,128]{3,2,1,0:...) custom-call(f32[2]{0:T(128)S(1)} %add_convert_fusion.first.refs_0_, f32[3,16,32,256]{3,2,1,0:T(8,128)S(1)} %copy-done, ...), custom_call_target="tpu_custom_call" | custom-call | flops 60000000 | bytes 12386304 | tf_op jit(solution)/shard_map/offset_later/pallas_call | solution.py:654
  85.7 2.1 %collective-permute-done.26.refs_3_ = f32[3,8,128]{2,1,0:T(8,128)S(1)} collective-permute-done((f32[3,8,128]{2,1,0:T(8,128)S(1)}, f32[3,8,128]{2,1,0:T(8,128)S(1)}, u32[]{:S(2)}, u32[]{:S(2)}) %collective-permute-start.26) | collective-permute-done | bytes 12320 | tf_op jit(solution)/shard_map/ppermute | solution.py:51
  90.0 2.1 %collective-permute-start.30 = (f32[3,8,128]{2,1,0:T(8,128)S(1)}, f32[3,8,128]{2,1,0:T(8,128)S(1)}, u32[]{:S(2)}, u32[]{:S(2)}) collective-permute-start(f32[3,8,128]{2,1,0:T(8,128)S(1)} %get-tuple-element.128), channel_id=1, source_target_pairs={{0,11},{1,8},{2,9},{3,10},{4,15},{5,12},{6,13},{7,14},{8,19},{9,16... | collective-permute-start | bytes 36872 | tf_op jit(solution)/shard_map/ppermute | solution.py:51
  92.1 1.8 %collective-permute-done.29.refs_2_.refs_6_ = f32[3,8,128]{2,1,0:T(8,128)S(1)} collective-permute-done((f32[3,8,128]{2,1,0:T(8,128)S(1)}, f32[3,8,128]{2,1,0:T(8,128)S(1)}, u32[]{:S(2)}, u32[]{:S(2)}) %collective-permute-start.29) | collective-permute-done | bytes 12320 | tf_op jit(solution)/shard_map/ppermute | solution.py:51
  93.9 2.0 %collective-permute-done.30.refs_3_.refs_7_ = f32[3,8,128]{2,1,0:T(8,128)S(1)} collective-permute-done((f32[3,8,128]{2,1,0:T(8,128)S(1)}, f32[3,8,128]{2,1,0:T(8,128)S(1)}, u32[]{:S(2)}, u32[]{:S(2)}) %collective-permute-start.30) | collective-permute-done | bytes 12320 | tf_op jit(solution)/shard_map/ppermute | solution.py:51
  103.9 2.4 %settle.3 = (f32[3,16,32,256]{3,2,1,0:T(8,128)S(1)}, f32[3,2,32,256]{3,2,1,0:T(8,128)S(1)}, f32[3,16,256]{2,1,0:T(8,128)S(1)}, f32[3,16,256]{2,1,0:T(8,128)S(1)}...) custom-call(f32[2]{0:T(128)S(1)} %add_convert_fusion.first.refs_0_, ...), custom_call_target="tpu_custom_call" | custom-call | flops 10000000 | bytes 8675328 | tf_op jit(solution)/shard_map/settle/pallas_call | solution.py:654
  109.0 2.1 %collective-permute-done.38.y_b = f32[3,16,256]{2,1,0:T(8,128)S(1)} collective-permute-done((f32[3,16,256]{2,1,0:T(8,128)S(1)}, f32[3,16,256]{2,1,0:T(8,128)S(1)}, u32[]{:S(2)}, u32[]{:S(2)}) %collective-permute-start.38) | collective-permute-done | bytes 49184 | tf_op jit(solution)/shard_map/ppermute | solution.py:35
  111.1 2.2 %collective-permute-done.39.y_a = f32[3,16,256]{2,1,0:T(8,128)S(1)} collective-permute-done((f32[3,16,256]{2,1,0:T(8,128)S(1)}, f32[3,16,256]{2,1,0:T(8,128)S(1)}, u32[]{:S(2)}, u32[]{:S(2)}) %collective-permute-start.39) | collective-permute-done | bytes 49184 | tf_op jit(solution)/shard_map/ppermute | solution.py:36
  113.4 3.0 %stage.1 = (f32[3,16,32,256]{3,2,1,0:T(8,128)S(1)}, f32[3,16,32,256]{3,2,1,0:T(8,128)S(1)}, f32[3,2,32,256]{3,2,1,0:T(8,128)S(1)}, f32[3,16,256]{2,1,0:T(8,128)S(1)}, f32[3,16,256]{2,1,0:T(8,128)S(1)}) custom-call(f32[2]{0:T(128)S(1)} %add_convert_fusion.first.refs_0_, f32[3,16,32,256]{3,2,1,0:T(8,128)S(1)} %copy-done, ...), custom_call_target="tpu_custom_call" | custom-call | flops 40000000 | bytes 11304960 | tf_op jit(solution)/shard_map/stage/pallas_call | solution.py:654
  119.5 2.6 %collective-permute-done.41.y_b = f32[3,16,256]{2,1,0:T(8,128)S(1)} collective-permute-done((f32[3,16,256]{2,1,0:T(8,128)S(1)}, f32[3,16,256]{2,1,0:T(8,128)S(1)}, u32[]{:S(2)}, u32[]{:S(2)}) %collective-permute-start.41) | collective-permute-done | bytes 49184 | tf_op jit(solution)/shard_map/ppermute | solution.py:35
  123.6 2.9 %last_stage.1 = f32[3,16,32,256]{3,2,1,0:T(8,128)} custom-call(f32[3,16,32,256]{3,2,1,0:T(8,128)S(1)} %copy-done, f32[9,16,32,256]{3,2,1,0:T(8,128)S(1)} %get-tuple-element.80.grads, f32[3,16,32,256]{3,2,1,0:T(8,128)S(1)} %get-tuple-element.140.y, f32[3,2,32,256]{3,2,1,0:T(8,128)S(1)} %collective-permute-done.40.y_x, ...), custom_call_target="tpu_custom_call" | custom-call | flops 40000000 | bytes 9732096 | tf_op jit(solution)/shard_map/last_stage/pallas_call | solution.py:654
  (87 shorter events, 58.2 us)
Async XLA Ops:
  4.1 12.6 %collective-permute-start = (f32[7,2,32,256]{3,2,1,0:T(8,128)}, f32[7,2,32,256]{3,2,1,0:T(8,128)}, u32[]{:S(2)}, u32[]{:S(2)}) collective-permute-start(f32[7,2,32,256]{3,2,1,0:T(8,128)} %get-tuple-element.75), channel_id=1, source_target_pairs={{0,4},{4,0},{1,5},{5,1},{2,6},{6,2},{3,7},{7,3},{8,12},{12,8},{9,1... | collective-permute-start | bytes 1376264 | tf_op jit(solution)/shard_map/ppermute | solution.py:34
  5.6 7.5 %collective-permute-start.1 = (f32[7,16,256]{2,1,0:T(8,128)}, f32[7,16,256]{2,1,0:T(8,128)S(1)}, u32[]{:S(2)}, u32[]{:S(2)}) collective-permute-start(f32[7,16,256]{2,1,0:T(8,128)} %get-tuple-element.76), channel_id=1, source_target_pairs={{0,1},{1,2},{2,3},{3,0},{4,5},{5,6},{6,7},{7,4},{8,9},{9,10},{10,1... | collective-permute-start | bytes 344072 | tf_op jit(solution)/shard_map/ppermute | solution.py:35
  5.8 7.2 %collective-permute-start.2 = (f32[7,16,256]{2,1,0:T(8,128)}, f32[7,16,256]{2,1,0:T(8,128)S(1)}, u32[]{:S(2)}, u32[]{:S(2)}) collective-permute-start(f32[7,16,256]{2,1,0:T(8,128)} %get-tuple-element.77), channel_id=1, source_target_pairs={{0,3},{1,0},{2,1},{3,2},{4,7},{5,4},{6,5},{7,6},{8,11},{9,8},{10,9... | collective-permute-start | bytes 344072 | tf_op jit(solution)/shard_map/ppermute | solution.py:36
  22.1 6.6 %collective-permute-start.3 = (f32[3,8,16,128]{3,2,1,0:T(8,128)S(1)}, f32[3,8,16,128]{3,2,1,0:T(8,128)S(1)}, u32[]{:S(2)}, u32[]{:S(2)}) collective-permute-start(f32[3,8,16,128]{3,2,1,0:T(8,128)S(1)} %get-tuple-element.81), channel_id=1, source_target_pairs={{0,8},{1,9},{2,10},{3,11},{4,12},{5,13},{6,14},{7,15},{8,0},{9,1},... | collective-permute-start | bytes 589832 | tf_op jit(solution)/shard_map/ppermute | solution.py:51
  22.2 6.6 %collective-permute-start.6 = (f32[3,2,16,128]{3,2,1,0:T(8,128)S(1)}, f32[3,2,16,128]{3,2,1,0:T(8,128)S(1)}, u32[]{:S(2)}, u32[]{:S(2)}) collective-permute-start(f32[3,2,16,128]{3,2,1,0:T(8,128)S(1)} %get-tuple-element.84), channel_id=1, source_target_pairs={{0,12},{1,13},{2,14},{3,15},{4,8},{5,9},{6,10},{7,11},{8,4},{9,5},... | collective-permute-start | bytes 147464 | tf_op jit(solution)/shard_map/ppermute | solution.py:51
  29.3 6.7 %collective-permute-start.7 = (f32[3,8,16,128]{3,2,1,0:T(8,128)S(1)}, f32[3,8,16,128]{3,2,1,0:T(8,128)S(1)}, u32[]{:S(2)}, u32[]{:S(2)}) collective-permute-start(f32[3,8,16,128]{3,2,1,0:T(8,128)S(1)} %get-tuple-element.91), channel_id=1, source_target_pairs={{0,8},{1,9},{2,10},{3,11},{4,12},{5,13},{6,14},{7,15},{8,16},{9,17... | collective-permute-start | bytes 589832 | tf_op jit(solution)/shard_map/ppermute | solution.py:51
  29.7 6.4 %collective-permute-start.10 = (f32[3,2,16,128]{3,2,1,0:T(8,128)S(1)}, f32[3,2,16,128]{3,2,1,0:T(8,128)S(1)}, u32[]{:S(2)}, u32[]{:S(2)}) collective-permute-start(f32[3,2,16,128]{3,2,1,0:T(8,128)S(1)} %get-tuple-element.94), channel_id=1, source_target_pairs={{0,12},{1,13},{2,14},{3,15},{4,8},{5,9},{6,10},{7,11},{8,20},{9,21... | collective-permute-start | bytes 147464 | tf_op jit(solution)/shard_map/ppermute | solution.py:51
  36.9 6.6 %collective-permute-start.11 = (f32[3,8,16,128]{3,2,1,0:T(8,128)S(1)}, f32[3,8,16,128]{3,2,1,0:T(8,128)S(1)}, u32[]{:S(2)}, u32[]{:S(2)}) collective-permute-start(f32[3,8,16,128]{3,2,1,0:T(8,128)S(1)} %get-tuple-element.95), channel_id=1, source_target_pairs={{0,8},{1,9},{2,10},{3,11},{4,12},{5,13},{6,14},{7,15},{8,0},{9,1},... | collective-permute-start | bytes 589832 | tf_op jit(solution)/shard_map/ppermute | solution.py:51
  37.0 6.6 %collective-permute-start.14 = (f32[3,2,16,128]{3,2,1,0:T(8,128)S(1)}, f32[3,2,16,128]{3,2,1,0:T(8,128)S(1)}, u32[]{:S(2)}, u32[]{:S(2)}) collective-permute-start(f32[3,2,16,128]{3,2,1,0:T(8,128)S(1)} %get-tuple-element.98), channel_id=1, source_target_pairs={{0,12},{1,13},{2,14},{3,15},{4,8},{5,9},{6,10},{7,11},{8,4},{9,5},... | collective-permute-start | bytes 147464 | tf_op jit(solution)/shard_map/ppermute | solution.py:51
  44.6 8.6 %collective-permute-start.15 = (f32[4,2,32,256]{3,2,1,0:T(8,128)S(1)}, f32[4,2,32,256]{3,2,1,0:T(8,128)S(1)}, u32[]{:S(2)}, u32[]{:S(2)}) collective-permute-start(f32[4,2,32,256]{3,2,1,0:T(8,128)S(1)} %get-tuple-element.99), channel_id=1, source_target_pairs={{0,4},{4,0},{1,5},{5,1},{2,6},{6,2},{3,7},{7,3},{8,12},{12,8},{9,1... | collective-permute-start | bytes 786440 | tf_op jit(solution)/shard_map/ppermute | solution.py:34
  45.4 6.1 %collective-permute-start.17 = (f32[4,16,256]{2,1,0:T(8,128)S(1)}, f32[4,16,256]{2,1,0:T(8,128)S(1)}, u32[]{:S(2)}, u32[]{:S(2)}) collective-permute-start(f32[4,16,256]{2,1,0:T(8,128)S(1)} %get-tuple-element.101), channel_id=1, source_target_pairs={{0,3},{1,0},{2,1},{3,2},{4,7},{5,4},{6,5},{7,6},{8,11},{9,8},{10,9... | collective-permute-start | bytes 196616 | tf_op jit(solution)/shard_map/ppermute | solution.py:36
  57.8 6.7 %collective-permute-start.18 = (f32[3,2,32,256]{3,2,1,0:T(8,128)S(1)}, f32[3,2,32,256]{3,2,1,0:T(8,128)S(1)}, u32[]{:S(2)}, u32[]{:S(2)}) collective-permute-start(f32[3,2,32,256]{3,2,1,0:T(8,128)S(1)} %get-tuple-element.108), channel_id=1, source_target_pairs={{0,4},{4,0},{1,5},{5,1},{2,6},{6,2},{3,7},{7,3},{8,12},{12,8},{9,1... | collective-permute-start | bytes 589832 | tf_op jit(solution)/shard_map/ppermute | solution.py:34
  67.7 36.2 %collective-permute-start.36 = (f32[3,16,32,256]{3,2,1,0:T(8,128)S(1)}, f32[3,16,32,256]{3,2,1,0:T(8,128)S(1)}, u32[]{:S(2)}, u32[]{:S(2)}) collective-permute-start(f32[3,16,32,256]{3,2,1,0:T(8,128)S(1)} %get-tuple-element.115.u2.refs_19_), channel_id=1, source_target_pairs={{0,8},{1,9},{2,10},{3,11},{4,12},{5,13},{6,14},{7,15},{8,16},{9,17... | collective-permute-start | bytes 4718600 | tf_op jit(solution)/shard_map/ppermute | solution.py:51
  67.7 8.1 %collective-permute-start.21 = (f32[3,2,32,256]{3,2,1,0:T(8,128)S(1)}, f32[3,2,32,256]{3,2,1,0:T(8,128)S(1)}, u32[]{:S(2)}, u32[]{:S(2)}) collective-permute-start(f32[3,2,32,256]{3,2,1,0:T(8,128)S(1)} %get-tuple-element.116), channel_id=1, source_target_pairs={{0,4},{4,0},{1,5},{5,1},{2,6},{6,2},{3,7},{7,3},{8,12},{12,8},{9,1... | collective-permute-start | bytes 589832 | tf_op jit(solution)/shard_map/ppermute | solution.py:34
  69.7 6.1 %collective-permute-start.23 = (f32[3,16,256]{2,1,0:T(8,128)S(1)}, f32[3,16,256]{2,1,0:T(8,128)S(1)}, u32[]{:S(2)}, u32[]{:S(2)}) collective-permute-start(f32[3,16,256]{2,1,0:T(8,128)S(1)} %get-tuple-element.118), channel_id=1, source_target_pairs={{0,3},{1,0},{2,1},{3,2},{4,7},{5,4},{6,5},{7,6},{8,11},{9,8},{10,9... | collective-permute-start | bytes 147464 | tf_op jit(solution)/shard_map/ppermute | solution.py:36
  81.3 6.5 %collective-permute-start.24 = (f32[6,8,16,128]{3,2,1,0:T(8,128)S(1)}, f32[6,8,16,128]{3,2,1,0:T(8,128)S(1)}, u32[]{:S(2)}, u32[]{:S(2)}) collective-permute-start(f32[6,8,16,128]{3,2,1,0:T(8,128)S(1)} %get-tuple-element.120), channel_id=1, source_target_pairs={{0,8},{1,9},{2,10},{3,11},{4,12},{5,13},{6,14},{7,15},{8,0},{9,1},... | collective-permute-start | bytes 1179656 | tf_op jit(solution)/shard_map/ppermute | solution.py:51
  81.4 6.4 %collective-permute-start.27 = (f32[3,2,16,128]{3,2,1,0:T(8,128)S(1)}, f32[3,2,16,128]{3,2,1,0:T(8,128)S(1)}, u32[]{:S(2)}, u32[]{:S(2)}) collective-permute-start(f32[3,2,16,128]{3,2,1,0:T(8,128)S(1)} %get-tuple-element.123), channel_id=1, source_target_pairs={{0,12},{1,13},{2,14},{3,15},{4,8},{5,9},{6,10},{7,11},{8,4},{9,5},... | collective-permute-start | bytes 147464 | tf_op jit(solution)/shard_map/ppermute | solution.py:51
  88.4 8.1 %collective-permute-start.28 = (f32[6,8,16,128]{3,2,1,0:T(8,128)S(1)}, f32[6,8,16,128]{3,2,1,0:T(8,128)S(1)}, u32[]{:S(2)}, u32[]{:S(2)}) collective-permute-start(f32[6,8,16,128]{3,2,1,0:T(8,128)S(1)} %get-tuple-element.126), channel_id=1, source_target_pairs={{0,8},{1,9},{2,10},{3,11},{4,12},{5,13},{6,14},{7,15},{8,16},{9,17... | collective-permute-start | bytes 1179656 | tf_op jit(solution)/shard_map/ppermute | solution.py:51
  88.6 7.9 %collective-permute-start.31 = (f32[3,2,16,128]{3,2,1,0:T(8,128)S(1)}, f32[3,2,16,128]{3,2,1,0:T(8,128)S(1)}, u32[]{:S(2)}, u32[]{:S(2)}) collective-permute-start(f32[3,2,16,128]{3,2,1,0:T(8,128)S(1)} %get-tuple-element.129), channel_id=1, source_target_pairs={{0,12},{1,13},{2,14},{3,15},{4,8},{5,9},{6,10},{7,11},{8,20},{9,21... | collective-permute-start | bytes 147464 | tf_op jit(solution)/shard_map/ppermute | solution.py:51
  90.0 5.9 %collective-permute-start.30 = (f32[3,8,128]{2,1,0:T(8,128)S(1)}, f32[3,8,128]{2,1,0:T(8,128)S(1)}, u32[]{:S(2)}, u32[]{:S(2)}) collective-permute-start(f32[3,8,128]{2,1,0:T(8,128)S(1)} %get-tuple-element.128), channel_id=1, source_target_pairs={{0,11},{1,8},{2,9},{3,10},{4,15},{5,12},{6,13},{7,14},{8,19},{9,16... | collective-permute-start | bytes 36872 | tf_op jit(solution)/shard_map/ppermute | solution.py:51
  97.3 6.6 %collective-permute-start.32 = (f32[6,8,16,128]{3,2,1,0:T(8,128)S(1)}, f32[6,8,16,128]{3,2,1,0:T(8,128)S(1)}, u32[]{:S(2)}, u32[]{:S(2)}) collective-permute-start(f32[6,8,16,128]{3,2,1,0:T(8,128)S(1)} %get-tuple-element.130), channel_id=1, source_target_pairs={{0,8},{1,9},{2,10},{3,11},{4,12},{5,13},{6,14},{7,15},{8,0},{9,1},... | collective-permute-start | bytes 1179656 | tf_op jit(solution)/shard_map/ppermute | solution.py:51
  97.4 6.5 %collective-permute-start.35 = (f32[3,2,16,128]{3,2,1,0:T(8,128)S(1)}, f32[3,2,16,128]{3,2,1,0:T(8,128)S(1)}, u32[]{:S(2)}, u32[]{:S(2)}) collective-permute-start(f32[3,2,16,128]{3,2,1,0:T(8,128)S(1)} %get-tuple-element.133), channel_id=1, source_target_pairs={{0,12},{1,13},{2,14},{3,15},{4,8},{5,9},{6,10},{7,11},{8,4},{9,5},... | collective-permute-start | bytes 147464 | tf_op jit(solution)/shard_map/ppermute | solution.py:51
  106.3 7.0 %collective-permute-start.37 = (f32[3,2,32,256]{3,2,1,0:T(8,128)S(1)}, f32[3,2,32,256]{3,2,1,0:T(8,128)S(1)}, u32[]{:S(2)}, u32[]{:S(2)}) collective-permute-start(f32[3,2,32,256]{3,2,1,0:T(8,128)S(1)} %get-tuple-element.135), channel_id=1, source_target_pairs={{0,4},{4,0},{1,5},{5,1},{2,6},{6,2},{3,7},{7,3},{8,12},{12,8},{9,1... | collective-permute-start | bytes 589832 | tf_op jit(solution)/shard_map/ppermute | solution.py:34
  116.4 7.2 %collective-permute-start.40 = (f32[3,2,32,256]{3,2,1,0:T(8,128)S(1)}, f32[3,2,32,256]{3,2,1,0:T(8,128)S(1)}, u32[]{:S(2)}, u32[]{:S(2)}) collective-permute-start(f32[3,2,32,256]{3,2,1,0:T(8,128)S(1)} %get-tuple-element.141), channel_id=1, source_target_pairs={{0,4},{4,0},{1,5},{5,1},{2,6},{6,2},{3,7},{7,3},{8,12},{12,8},{9,1... | collective-permute-start | bytes 589832 | tf_op jit(solution)/shard_map/ppermute | solution.py:34
  (24 other events, 131.9 us)

commit v13 on v12

--- a/solution.py
+++ b/solution.py
@@ -40,9 +40,9 @@
 def pass_on(array, dx=0, dy=0, turn=0):
     slabs, gx, gy = lax.axis_size("tm"), lax.axis_size("gx"), lax.axis_size("gy")
     pairs = []
-    in_twos = turn % 2 == 1 and slabs % 2 == 0
+    in_twos = turn > 0 and slabs % 2 == 0
     for t in range(slabs):
-        following = t + 1 - 2 * (t % 2) if in_twos else (t + 1) % slabs
+        following = (t - 1 if in_twos and (t - turn) % 2 == 0 else t + 1) % slabs
         for x in range(gx):
             for y in range(gy):
                 source = (t * gx + x) * gy + y

time: 128 us -> 134 us (1.047)
  waiting for transfers between devices: 50.1 us -> 54.7 us
    ppermute x25, waiting for transfers between devices: 20.7 us -> 25.2 us  [pass_on(): return lax.ppermute(array, ('tm', 'gx', 'gy'), pairs)]
    ppermute x25, starting transfers between devices: 20.5 us -> 22.1 us  [pass_on(): return lax.ppermute(array, ('tm', 'gx', 'gy'), pairs)]
  transfers between devices with their start and end apart: 43 -> 43, of which waited for: 27 -> 29; matrix products, arithmetic and copies ran while one was open for 0% -> 0% of each run, Pallas kernels for 7% -> 6%
where the time goes in v13:
time: 134 us; the launch traced here: 133 us
  waiting for transfers between devices  54.7 us (41%)
  starting transfers between devices  40 us (30%)
  Pallas kernels  36.6 us (27%)
    pallas_call x14, Pallas kernels, call(): pl.pallas_call(kernel, name=name, out_shape=[jax.ShapeDtypeStruct(dims, F...  36.6 us
    ppermute x25, waiting for transfers between devices, pass_on(): return lax.ppermute(array, ('tm', 'gx', 'gy'), pairs)  25.2 us
    ppermute x25, starting transfers between devices, pass_on(): return lax.ppermute(array, ('tm', 'gx', 'gy'), pairs)  22.1 us
    ppermute x6, waiting for transfers between devices, swap_faces(): behind = lax.ppermute(y_last, 'gy', ring(gy, 1))  14.2 us
    ppermute x6, starting transfers between devices, swap_faces(): ahead = lax.ppermute(y_first, 'gy', ring(gy, -1))  11.2 us
    ppermute x6, waiting for transfers between devices, swap_faces(): ahead = lax.ppermute(y_first, 'gy', ring(gy, -1))  8.84 us
    ppermute x6, waiting for transfers between devices, swap_faces(): lax.ppermute(a, 'gx', ring(gx, by))  6.5 us
    ppermute x6, starting transfers between devices, swap_faces(): lax.ppermute(a, 'gx', ring(gx, by))  5.74 us
  transfers between devices with their start and end apart: 43, of which 29 were waited for; matrix products, arithmetic and copies ran while one was open for 0% of the time, Pallas kernels for 6%

profile of v13, /device:TPU:26, one launch (start us, length us, event | category | flops | bytes accessed | tf_op | source)
XLA Modules:
  0.0 132.5 jit_solution(7543684917134614396)
XLA Ops:
  0.0 4.1 %pack.1 = (f32[3,8,16,128]{3,2,1,0:T(8,128)}, f32[7,2,32,256]{3,2,1,0:T(8,128)}, f32[7,16,256]{2,1,0:T(8,128)}, f32[7,16,256]{2,1,0:T(8,128)}) custom-call(f32[3,16,32,256]{3,2,1,0:T(8,128)} %v.15, f32[3,16,32,256]{3,2,1,0:T(8,128)} %refs_16_.1, f32[3,16,32,256]{3,2,1,0:T(8,128)} %bitcast.4), custom_call_target="tpu_custom_call" | custom-call | flops 5000000 | bytes 4718592 | tf_op jit(solution)/shard_map/pack/pallas_call | solution.py:654
  10.3 2.8 %collective-permute-done.1.behind.w_b = f32[7,16,256]{2,1,0:T(8,128)S(1)} collective-permute-done((f32[7,16,256]{2,1,0:T(8,128)}, f32[7,16,256]{2,1,0:T(8,128)S(1)}, u32[]{:S(2)}, u32[]{:S(2)}) %collective-permute-start.1) | collective-permute-done | bytes 114720 | tf_op jit(solution)/shard_map/ppermute | solution.py:35
  13.1 3.6 %collective-permute-done.x_faces.w_x = f32[7,2,32,256]{3,2,1,0:T(8,128)} collective-permute-done((f32[7,2,32,256]{3,2,1,0:T(8,128)}, f32[7,2,32,256]{3,2,1,0:T(8,128)}, u32[]{:S(2)}, u32[]{:S(2)}) %collective-permute-start) | collective-permute-done | bytes 458784 | tf_op jit(solution)/shard_map/ppermute | solution.py:34
  16.7 5.4 %offset_start.1 = (f32[9,16,32,256]{3,2,1,0:T(8,128)S(1)}, f32[3,8,16,128]{3,2,1,0:T(8,128)S(1)}, f32[9,8,16,128]{3,2,1,0:T(8,128)S(1)}, f32[3,2,16,128]{3,2,1,0...) custom-call(f32[2]{0:T(128)S(1)} %add_convert_fusion.first.refs_0_, ...), custom_call_target="tpu_custom_call" | custom-call | flops 40000000 | bytes 5603328 | tf_op jit(solution)/shard_map/offset_start/pallas_call | solution.py:654
  31.3 2.4 %collective-permute-start.9 = (f32[3,8,128]{2,1,0:T(8,128)S(1)}, f32[3,8,128]{2,1,0:T(8,128)S(1)}, u32[]{:S(2)}, u32[]{:S(2)}) collective-permute-start(f32[3,8,128]{2,1,0:T(8,128)S(1)} %get-tuple-element.93), channel_id=1, source_target_pairs={{0,27},{1,24},{2,25},{3,26},{4,31},{5,28},{6,29},{7,30},{8,19},{9,... | collective-permute-start | bytes 36872 | tf_op jit(solution)/shard_map/ppermute | solution.py:51
  35.2 2.0 %collective-permute-done.9.refs_3_.refs_7_ = f32[3,8,128]{2,1,0:T(8,128)S(1)} collective-permute-done((f32[3,8,128]{2,1,0:T(8,128)S(1)}, f32[3,8,128]{2,1,0:T(8,128)S(1)}, u32[]{:S(2)}, u32[]{:S(2)}) %collective-permute-start.9) | collective-permute-done | bytes 12320 | tf_op jit(solution)/shard_map/ppermute | solution.py:51
  48.6 2.2 %collective-permute-done.16.m_b.behind = f32[4,16,256]{2,1,0:T(8,128)S(1)} collective-permute-done((f32[4,16,256]{2,1,0:T(8,128)S(1)}, f32[4,16,256]{2,1,0:T(8,128)S(1)}, u32[]{:S(2)}, u32[]{:S(2)}) %collective-permute-start.16) | collective-permute-done | bytes 65568 | tf_op jit(solution)/shard_map/ppermute | solution.py:35
  52.8 2.2 %collective-permute-done.15.m_x.x_faces = f32[4,2,32,256]{3,2,1,0:T(8,128)S(1)} collective-permute-done((f32[4,2,32,256]{3,2,1,0:T(8,128)S(1)}, f32[4,2,32,256]{3,2,1,0:T(8,128)S(1)}, u32[]{:S(2)}, u32[]{:S(2)}) %collective-permute-start.15) | collective-permute-done | bytes 262176 | tf_op jit(solution)/shard_map/ppermute | solution.py:34
  54.9 4.6 %middle.1 = (f32[3,16,32,256]{3,2,1,0:T(8,128)S(1)}, f32[3,2,32,256]{3,2,1,0:T(8,128)S(1)}, f32[3,16,256]{2,1,0:T(8,128)S(1)}, f32[3,16,256]{2,1,0:T(8,128)S(1)}...) custom-call(f32[2]{0:T(128)S(1)} %add_convert_fusion.first.refs_0_, ...), custom_call_target="tpu_custom_call" | custom-call | flops 60000000 | bytes 10985472 | tf_op jit(solution)/shard_map/middle/pallas_call | solution.py:654
  59.9 2.0 %collective-permute-start.20 = (f32[3,16,256]{2,1,0:T(8,128)S(1)}, f32[3,16,256]{2,1,0:T(8,128)S(1)}, u32[]{:S(2)}, u32[]{:S(2)}) collective-permute-start(f32[3,16,256]{2,1,0:T(8,128)S(1)} %get-tuple-element.110), channel_id=1, source_target_pairs={{0,3},{1,0},{2,1},{3,2},{4,7},{5,4},{6,5},{7,6},{8,11},{9,8},{10,9... | collective-permute-start | bytes 147464 | tf_op jit(solution)/shard_map/ppermute | solution.py:36
  61.9 2.6 %collective-permute-done.19.a1_b.u1_b = f32[3,16,256]{2,1,0:T(8,128)S(1)} collective-permute-done((f32[3,16,256]{2,1,0:T(8,128)S(1)}, f32[3,16,256]{2,1,0:T(8,128)S(1)}, u32[]{:S(2)}, u32[]{:S(2)}) %collective-permute-start.19) | collective-permute-done | bytes 49184 | tf_op jit(solution)/shard_map/ppermute | solution.py:35
  66.0 3.2 %finish.1 = (f32[3,16,32,256]{3,2,1,0:T(8,128)S(1)}, f32[3,2,32,256]{3,2,1,0:T(8,128)S(1)}, f32[3,16,256]{2,1,0:T(8,128)S(1)}, f32[3,16,256]{2,1,0:T(8,128)S(1)}, f32[3,8,16,128]{3,2,1,0:T(8,128)S(1)}) custom-call(f32[2]{0:T(128)S(1)} %add_convert_fusion.first.refs_0_, f32[3,16,32,256]{3,2,1,0:T(8,128)S(1)} %copy-done, ...), custom_call_target="tpu_custom_call" | custom-call | flops 40000000 | bytes 10027008 | tf_op jit(solution)/shard_map/finish/pallas_call | solution.py:654
  72.9 2.1 %collective-permute-done.22.u2_b = f32[3,16,256]{2,1,0:T(8,128)S(1)} collective-permute-done((f32[3,16,256]{2,1,0:T(8,128)S(1)}, f32[3,16,256]{2,1,0:T(8,128)S(1)}, u32[]{:S(2)}, u32[]{:S(2)}) %collective-permute-start.22) | collective-permute-done | bytes 49184 | tf_op jit(solution)/shard_map/ppermute | solution.py:35
  75.0 2.2 %collective-permute-done.23.u2_a = f32[3,16,256]{2,1,0:T(8,128)S(1)} collective-permute-done((f32[3,16,256]{2,1,0:T(8,128)S(1)}, f32[3,16,256]{2,1,0:T(8,128)S(1)}, u32[]{:S(2)}, u32[]{:S(2)}) %collective-permute-start.23) | collective-permute-done | bytes 49184 | tf_op jit(solution)/shard_map/ppermute | solution.py:36
  77.2 5.4 %offset_later.1 = (f32[3,8,16,128]{3,2,1,0:T(8,128)S(1)}, f32[3,8,16,128]{3,2,1,0:T(8,128)S(1)}, f32[6,8,16,128]{3,2,1,0:T(8,128)S(1)}, f32[3,2,16,128]{3,2,1,0:...) custom-call(f32[2]{0:T(128)S(1)} %add_convert_fusion.first.refs_0_, f32[3,16,32,256]{3,2,1,0:T(8,128)S(1)} %copy-done, ...), custom_call_target="tpu_custom_call" | custom-call | flops 60000000 | bytes 12386304 | tf_op jit(solution)/shard_map/offset_later/pallas_call | solution.py:654
  86.9 2.0 %collective-permute-done.26.refs_3_ = f32[3,8,128]{2,1,0:T(8,128)S(1)} collective-permute-done((f32[3,8,128]{2,1,0:T(8,128)S(1)}, f32[3,8,128]{2,1,0:T(8,128)S(1)}, u32[]{:S(2)}, u32[]{:S(2)}) %collective-permute-start.26) | collective-permute-done | bytes 12320 | tf_op jit(solution)/shard_map/ppermute | solution.py:51
  95.8 2.8 %collective-permute-done.30.refs_3_.refs_7_ = f32[3,8,128]{2,1,0:T(8,128)S(1)} collective-permute-done((f32[3,8,128]{2,1,0:T(8,128)S(1)}, f32[3,8,128]{2,1,0:T(8,128)S(1)}, u32[]{:S(2)}, u32[]{:S(2)}) %collective-permute-start.30) | collective-permute-done | bytes 12320 | tf_op jit(solution)/shard_map/ppermute | solution.py:51
  98.5 4.0 %collective-permute-done.31.refs_4_.refs_8_ = f32[3,2,16,128]{3,2,1,0:T(8,128)S(1)} collective-permute-done((f32[3,2,16,128]{3,2,1,0:T(8,128)S(1)}, f32[3,2,16,128]{3,2,1,0:T(8,128)S(1)}, u32[]{:S(2)}, u32[]{:S(2)}) %collective-permute-start.31) | collective-permute-done | bytes 49184 | tf_op jit(solution)/shard_map/ppermute | solution.py:51
  107.6 2.1 %collective-permute-done.34.refs_11_ = f32[3,8,128]{2,1,0:T(8,128)S(1)} collective-permute-done((f32[3,8,128]{2,1,0:T(8,128)S(1)}, f32[3,8,128]{2,1,0:T(8,128)S(1)}, u32[]{:S(2)}, u32[]{:S(2)}) %collective-permute-start.34) | collective-permute-done | bytes 12320 | tf_op jit(solution)/shard_map/ppermute | solution.py:51
  109.8 2.4 %settle.3 = (f32[3,16,32,256]{3,2,1,0:T(8,128)S(1)}, f32[3,2,32,256]{3,2,1,0:T(8,128)S(1)}, f32[3,16,256]{2,1,0:T(8,128)S(1)}, f32[3,16,256]{2,1,0:T(8,128)S(1)}...) custom-call(f32[2]{0:T(128)S(1)} %add_convert_fusion.first.refs_0_, ...), custom_call_target="tpu_custom_call" | custom-call | flops 10000000 | bytes 8675328 | tf_op jit(solution)/shard_map/settle/pallas_call | solution.py:654
  115.1 2.1 %collective-permute-done.38.y_b = f32[3,16,256]{2,1,0:T(8,128)S(1)} collective-permute-done((f32[3,16,256]{2,1,0:T(8,128)S(1)}, f32[3,16,256]{2,1,0:T(8,128)S(1)}, u32[]{:S(2)}, u32[]{:S(2)}) %collective-permute-start.38) | collective-permute-done | bytes 49184 | tf_op jit(solution)/shard_map/ppermute | solution.py:35
  119.5 3.0 %stage.1 = (f32[3,16,32,256]{3,2,1,0:T(8,128)S(1)}, f32[3,16,32,256]{3,2,1,0:T(8,128)S(1)}, f32[3,2,32,256]{3,2,1,0:T(8,128)S(1)}, f32[3,16,256]{2,1,0:T(8,128)S(1)}, f32[3,16,256]{2,1,0:T(8,128)S(1)}) custom-call(f32[2]{0:T(128)S(1)} %add_convert_fusion.first.refs_0_, f32[3,16,32,256]{3,2,1,0:T(8,128)S(1)} %copy-done, ...), custom_call_target="tpu_custom_call" | custom-call | flops 40000000 | bytes 11304960 | tf_op jit(solution)/shard_map/stage/pallas_call | solution.py:654
  125.7 2.4 %collective-permute-done.41.y_b = f32[3,16,256]{2,1,0:T(8,128)S(1)} collective-permute-done((f32[3,16,256]{2,1,0:T(8,128)S(1)}, f32[3,16,256]{2,1,0:T(8,128)S(1)}, u32[]{:S(2)}, u32[]{:S(2)}) %collective-permute-start.41) | collective-permute-done | bytes 49184 | tf_op jit(solution)/shard_map/ppermute | solution.py:35
  129.6 2.9 %last_stage.1 = f32[3,16,32,256]{3,2,1,0:T(8,128)} custom-call(f32[3,16,32,256]{3,2,1,0:T(8,128)S(1)} %copy-done, f32[9,16,32,256]{3,2,1,0:T(8,128)S(1)} %get-tuple-element.80.grads, f32[3,16,32,256]{3,2,1,0:T(8,128)S(1)} %get-tuple-element.140.y, f32[3,2,32,256]{3,2,1,0:T(8,128)S(1)} %collective-permute-done.40.y_x, ...), custom_call_target="tpu_custom_call" | custom-call | flops 40000000 | bytes 9732096 | tf_op jit(solution)/shard_map/last_stage/pallas_call | solution.py:654
  (87 shorter events, 61.8 us)
Async XLA Ops:
  4.1 12.6 %collective-permute-start = (f32[7,2,32,256]{3,2,1,0:T(8,128)}, f32[7,2,32,256]{3,2,1,0:T(8,128)}, u32[]{:S(2)}, u32[]{:S(2)}) collective-permute-start(f32[7,2,32,256]{3,2,1,0:T(8,128)} %get-tuple-element.75), channel_id=1, source_target_pairs={{0,4},{4,0},{1,5},{5,1},{2,6},{6,2},{3,7},{7,3},{8,12},{12,8},{9,1... | collective-permute-start | bytes 1376264 | tf_op jit(solution)/shard_map/ppermute | solution.py:34
  5.6 7.5 %collective-permute-start.1 = (f32[7,16,256]{2,1,0:T(8,128)}, f32[7,16,256]{2,1,0:T(8,128)S(1)}, u32[]{:S(2)}, u32[]{:S(2)}) collective-permute-start(f32[7,16,256]{2,1,0:T(8,128)} %get-tuple-element.76), channel_id=1, source_target_pairs={{0,1},{1,2},{2,3},{3,0},{4,5},{5,6},{6,7},{7,4},{8,9},{9,10},{10,1... | collective-permute-start | bytes 344072 | tf_op jit(solution)/shard_map/ppermute | solution.py:35
  5.8 7.2 %collective-permute-start.2 = (f32[7,16,256]{2,1,0:T(8,128)}, f32[7,16,256]{2,1,0:T(8,128)S(1)}, u32[]{:S(2)}, u32[]{:S(2)}) collective-permute-start(f32[7,16,256]{2,1,0:T(8,128)} %get-tuple-element.77), channel_id=1, source_target_pairs={{0,3},{1,0},{2,1},{3,2},{4,7},{5,4},{6,5},{7,6},{8,11},{9,8},{10,9... | collective-permute-start | bytes 344072 | tf_op jit(solution)/shard_map/ppermute | solution.py:36
  22.1 6.6 %collective-permute-start.3 = (f32[3,8,16,128]{3,2,1,0:T(8,128)S(1)}, f32[3,8,16,128]{3,2,1,0:T(8,128)S(1)}, u32[]{:S(2)}, u32[]{:S(2)}) collective-permute-start(f32[3,8,16,128]{3,2,1,0:T(8,128)S(1)} %get-tuple-element.81), channel_id=1, source_target_pairs={{0,8},{1,9},{2,10},{3,11},{4,12},{5,13},{6,14},{7,15},{8,0},{9,1},... | collective-permute-start | bytes 589832 | tf_op jit(solution)/shard_map/ppermute | solution.py:51
  22.2 6.6 %collective-permute-start.6 = (f32[3,2,16,128]{3,2,1,0:T(8,128)S(1)}, f32[3,2,16,128]{3,2,1,0:T(8,128)S(1)}, u32[]{:S(2)}, u32[]{:S(2)}) collective-permute-start(f32[3,2,16,128]{3,2,1,0:T(8,128)S(1)} %get-tuple-element.84), channel_id=1, source_target_pairs={{0,12},{1,13},{2,14},{3,15},{4,8},{5,9},{6,10},{7,11},{8,4},{9,5},... | collective-permute-start | bytes 147464 | tf_op jit(solution)/shard_map/ppermute | solution.py:51
  29.3 8.1 %collective-permute-start.7 = (f32[3,8,16,128]{3,2,1,0:T(8,128)S(1)}, f32[3,8,16,128]{3,2,1,0:T(8,128)S(1)}, u32[]{:S(2)}, u32[]{:S(2)}) collective-permute-start(f32[3,8,16,128]{3,2,1,0:T(8,128)S(1)} %get-tuple-element.91), channel_id=1, source_target_pairs={{0,24},{1,25},{2,26},{3,27},{4,28},{5,29},{6,30},{7,31},{8,16},{9,... | collective-permute-start | bytes 589832 | tf_op jit(solution)/shard_map/ppermute | solution.py:51
  30.1 7.3 %collective-permute-start.10 = (f32[3,2,16,128]{3,2,1,0:T(8,128)S(1)}, f32[3,2,16,128]{3,2,1,0:T(8,128)S(1)}, u32[]{:S(2)}, u32[]{:S(2)}) collective-permute-start(f32[3,2,16,128]{3,2,1,0:T(8,128)S(1)} %get-tuple-element.94), channel_id=1, source_target_pairs={{0,28},{1,29},{2,30},{3,31},{4,24},{5,25},{6,26},{7,27},{8,20},{9,... | collective-permute-start | bytes 147464 | tf_op jit(solution)/shard_map/ppermute | solution.py:51
  31.3 5.9 %collective-permute-start.9 = (f32[3,8,128]{2,1,0:T(8,128)S(1)}, f32[3,8,128]{2,1,0:T(8,128)S(1)}, u32[]{:S(2)}, u32[]{:S(2)}) collective-permute-start(f32[3,8,128]{2,1,0:T(8,128)S(1)} %get-tuple-element.93), channel_id=1, source_target_pairs={{0,27},{1,24},{2,25},{3,26},{4,31},{5,28},{6,29},{7,30},{8,19},{9,... | collective-permute-start | bytes 36872 | tf_op jit(solution)/shard_map/ppermute | solution.py:51
  38.2 6.9 %collective-permute-start.11 = (f32[3,8,16,128]{3,2,1,0:T(8,128)S(1)}, f32[3,8,16,128]{3,2,1,0:T(8,128)S(1)}, u32[]{:S(2)}, u32[]{:S(2)}) collective-permute-start(f32[3,8,16,128]{3,2,1,0:T(8,128)S(1)} %get-tuple-element.95), channel_id=1, source_target_pairs={{0,8},{1,9},{2,10},{3,11},{4,12},{5,13},{6,14},{7,15},{8,0},{9,1},... | collective-permute-start | bytes 589832 | tf_op jit(solution)/shard_map/ppermute | solution.py:51
  38.3 6.8 %collective-permute-start.14 = (f32[3,2,16,128]{3,2,1,0:T(8,128)S(1)}, f32[3,2,16,128]{3,2,1,0:T(8,128)S(1)}, u32[]{:S(2)}, u32[]{:S(2)}) collective-permute-start(f32[3,2,16,128]{3,2,1,0:T(8,128)S(1)} %get-tuple-element.98), channel_id=1, source_target_pairs={{0,12},{1,13},{2,14},{3,15},{4,8},{5,9},{6,10},{7,11},{8,4},{9,5},... | collective-permute-start | bytes 147464 | tf_op jit(solution)/shard_map/ppermute | solution.py:51
  46.2 8.7 %collective-permute-start.15 = (f32[4,2,32,256]{3,2,1,0:T(8,128)S(1)}, f32[4,2,32,256]{3,2,1,0:T(8,128)S(1)}, u32[]{:S(2)}, u32[]{:S(2)}) collective-permute-start(f32[4,2,32,256]{3,2,1,0:T(8,128)S(1)} %get-tuple-element.99), channel_id=1, source_target_pairs={{0,4},{4,0},{1,5},{5,1},{2,6},{6,2},{3,7},{7,3},{8,12},{12,8},{9,1... | collective-permute-start | bytes 786440 | tf_op jit(solution)/shard_map/ppermute | solution.py:34
  46.7 6.1 %collective-permute-start.17 = (f32[4,16,256]{2,1,0:T(8,128)S(1)}, f32[4,16,256]{2,1,0:T(8,128)S(1)}, u32[]{:S(2)}, u32[]{:S(2)}) collective-permute-start(f32[4,16,256]{2,1,0:T(8,128)S(1)} %get-tuple-element.101), channel_id=1, source_target_pairs={{0,3},{1,0},{2,1},{3,2},{4,7},{5,4},{6,5},{7,6},{8,11},{9,8},{10,9... | collective-permute-start | bytes 196616 | tf_op jit(solution)/shard_map/ppermute | solution.py:36
  59.5 6.5 %collective-permute-start.18 = (f32[3,2,32,256]{3,2,1,0:T(8,128)S(1)}, f32[3,2,32,256]{3,2,1,0:T(8,128)S(1)}, u32[]{:S(2)}, u32[]{:S(2)}) collective-permute-start(f32[3,2,32,256]{3,2,1,0:T(8,128)S(1)} %get-tuple-element.108), channel_id=1, source_target_pairs={{0,4},{4,0},{1,5},{5,1},{2,6},{6,2},{3,7},{7,3},{8,12},{12,8},{9,1... | collective-permute-start | bytes 589832 | tf_op jit(solution)/shard_map/ppermute | solution.py:34
  69.3 40.5 %collective-permute-start.36 = (f32[3,16,32,256]{3,2,1,0:T(8,128)S(1)}, f32[3,16,32,256]{3,2,1,0:T(8,128)S(1)}, u32[]{:S(2)}, u32[]{:S(2)}) collective-permute-start(f32[3,16,32,256]{3,2,1,0:T(8,128)S(1)} %get-tuple-element.115.u2.refs_19_), channel_id=1, source_target_pairs={{0,8},{1,9},{2,10},{3,11},{4,12},{5,13},{6,14},{7,15},{8,16},{9,17... | collective-permute-start | bytes 4718600 | tf_op jit(solution)/shard_map/ppermute | solution.py:51
  69.4 7.9 %collective-permute-start.21 = (f32[3,2,32,256]{3,2,1,0:T(8,128)S(1)}, f32[3,2,32,256]{3,2,1,0:T(8,128)S(1)}, u32[]{:S(2)}, u32[]{:S(2)}) collective-permute-start(f32[3,2,32,256]{3,2,1,0:T(8,128)S(1)} %get-tuple-element.116), channel_id=1, source_target_pairs={{0,4},{4,0},{1,5},{5,1},{2,6},{6,2},{3,7},{7,3},{8,12},{12,8},{9,1... | collective-permute-start | bytes 589832 | tf_op jit(solution)/shard_map/ppermute | solution.py:34
  82.7 6.3 %collective-permute-start.24 = (f32[6,8,16,128]{3,2,1,0:T(8,128)S(1)}, f32[6,8,16,128]{3,2,1,0:T(8,128)S(1)}, u32[]{:S(2)}, u32[]{:S(2)}) collective-permute-start(f32[6,8,16,128]{3,2,1,0:T(8,128)S(1)} %get-tuple-element.120), channel_id=1, source_target_pairs={{0,8},{1,9},{2,10},{3,11},{4,12},{5,13},{6,14},{7,15},{8,0},{9,1},... | collective-permute-start | bytes 1179656 | tf_op jit(solution)/shard_map/ppermute | solution.py:51
  82.7 6.2 %collective-permute-start.27 = (f32[3,2,16,128]{3,2,1,0:T(8,128)S(1)}, f32[3,2,16,128]{3,2,1,0:T(8,128)S(1)}, u32[]{:S(2)}, u32[]{:S(2)}) collective-permute-start(f32[3,2,16,128]{3,2,1,0:T(8,128)S(1)} %get-tuple-element.123), channel_id=1, source_target_pairs={{0,12},{1,13},{2,14},{3,15},{4,8},{5,9},{6,10},{7,11},{8,4},{9,5},... | collective-permute-start | bytes 147464 | tf_op jit(solution)/shard_map/ppermute | solution.py:51
  89.5 13.0 %collective-permute-start.28 = (f32[6,8,16,128]{3,2,1,0:T(8,128)S(1)}, f32[6,8,16,128]{3,2,1,0:T(8,128)S(1)}, u32[]{:S(2)}, u32[]{:S(2)}) collective-permute-start(f32[6,8,16,128]{3,2,1,0:T(8,128)S(1)} %get-tuple-element.126), channel_id=1, source_target_pairs={{0,24},{1,25},{2,26},{3,27},{4,28},{5,29},{6,30},{7,31},{8,16},{9,... | collective-permute-start | bytes 1179656 | tf_op jit(solution)/shard_map/ppermute | solution.py:51
  90.5 12.0 %collective-permute-start.31 = (f32[3,2,16,128]{3,2,1,0:T(8,128)S(1)}, f32[3,2,16,128]{3,2,1,0:T(8,128)S(1)}, u32[]{:S(2)}, u32[]{:S(2)}) collective-permute-start(f32[3,2,16,128]{3,2,1,0:T(8,128)S(1)} %get-tuple-element.129), channel_id=1, source_target_pairs={{0,28},{1,29},{2,30},{3,31},{4,24},{5,25},{6,26},{7,27},{8,20},{9,... | collective-permute-start | bytes 147464 | tf_op jit(solution)/shard_map/ppermute | solution.py:51
  92.5 6.1 %collective-permute-start.30 = (f32[3,8,128]{2,1,0:T(8,128)S(1)}, f32[3,8,128]{2,1,0:T(8,128)S(1)}, u32[]{:S(2)}, u32[]{:S(2)}) collective-permute-start(f32[3,8,128]{2,1,0:T(8,128)S(1)} %get-tuple-element.128), channel_id=1, source_target_pairs={{0,27},{1,24},{2,25},{3,26},{4,31},{5,28},{6,29},{7,30},{8,19},{9,... | collective-permute-start | bytes 36872 | tf_op jit(solution)/shard_map/ppermute | solution.py:51
  103.4 6.4 %collective-permute-start.32 = (f32[6,8,16,128]{3,2,1,0:T(8,128)S(1)}, f32[6,8,16,128]{3,2,1,0:T(8,128)S(1)}, u32[]{:S(2)}, u32[]{:S(2)}) collective-permute-start(f32[6,8,16,128]{3,2,1,0:T(8,128)S(1)} %get-tuple-element.130), channel_id=1, source_target_pairs={{0,8},{1,9},{2,10},{3,11},{4,12},{5,13},{6,14},{7,15},{8,0},{9,1},... | collective-permute-start | bytes 1179656 | tf_op jit(solution)/shard_map/ppermute | solution.py:51
  103.5 6.3 %collective-permute-start.35 = (f32[3,2,16,128]{3,2,1,0:T(8,128)S(1)}, f32[3,2,16,128]{3,2,1,0:T(8,128)S(1)}, u32[]{:S(2)}, u32[]{:S(2)}) collective-permute-start(f32[3,2,16,128]{3,2,1,0:T(8,128)S(1)} %get-tuple-element.133), channel_id=1, source_target_pairs={{0,12},{1,13},{2,14},{3,15},{4,8},{5,9},{6,10},{7,11},{8,4},{9,5},... | collective-permute-start | bytes 147464 | tf_op jit(solution)/shard_map/ppermute | solution.py:51
  112.2 7.3 %collective-permute-start.37 = (f32[3,2,32,256]{3,2,1,0:T(8,128)S(1)}, f32[3,2,32,256]{3,2,1,0:T(8,128)S(1)}, u32[]{:S(2)}, u32[]{:S(2)}) collective-permute-start(f32[3,2,32,256]{3,2,1,0:T(8,128)S(1)} %get-tuple-element.135), channel_id=1, source_target_pairs={{0,4},{4,0},{1,5},{5,1},{2,6},{6,2},{3,7},{7,3},{8,12},{12,8},{9,1... | collective-permute-start | bytes 589832 | tf_op jit(solution)/shard_map/ppermute | solution.py:34
  122.5 7.0 %collective-permute-start.40 = (f32[3,2,32,256]{3,2,1,0:T(8,128)S(1)}, f32[3,2,32,256]{3,2,1,0:T(8,128)S(1)}, u32[]{:S(2)}, u32[]{:S(2)}) collective-permute-start(f32[3,2,32,256]{3,2,1,0:T(8,128)S(1)} %get-tuple-element.141), channel_id=1, source_target_pairs={{0,4},{4,0},{1,5},{5,1},{2,6},{6,2},{3,7},{7,3},{8,12},{12,8},{9,1... | collective-permute-start | bytes 589832 | tf_op jit(solution)/shard_map/ppermute | solution.py:34
  (24 other events, 133.0 us)
